TPU v7x, 256 devices: a whole 4x4x8 slice. The times are simulated.
256 devices in a mesh: row: 16 (over z, core), col: 16 (over y, x).
Axes of the slice: x: 4, y: 4, z: 8, core: 2. Of those that a mesh axis runs over, the one named last changes fastest.
Arguments:
- points: bfloat16 [16384, 1024], P(('row', 'col')), may hold values from -6 to 6
- factor: float32 [16384, 256], P(('row', 'col')), may hold values from 0 to 1
Outputs:
- factor_out: float32 [16384, 256], P(('row', 'col'))
All inputs are finite; a program needn't handle non-finite values.
Results may differ from a plain program's by a relative error of at most 0.002.
The roundings to bfloat16 on the way count: a program that leaves them out, or rounds other values in their place, can miss the bound.
Values may be sent and summed in bfloat16 or wider, within the bound.
No kernel may reach another device: no remote copies, remote signals or barrier semaphores. Data moves between devices by JAX's collectives and lax.ppermute only.
A program may use at most 64 MiB of HBM per device.

v0:
```python
import math

import jax
import jax.numpy as jnp
from jax import lax
from jax.sharding import Mesh
from jax.sharding import PartitionSpec as P

EMBED_WIDTH = 1024
ITERS = 2
Z, CORE, Y, X = "row_0", "row_1", "col_0", "col_1"
ROW = (Z, CORE)
COL = (Y, X)
ROW_COL = (Z, CORE, Y, X)


def from_ahead(value, axis, steps):
    length = lax.axis_size(axis)
    return lax.ppermute(value, axis, [((i + steps) % length, i) for i in range(length)])


def to_ahead(value, axis, steps):
    length = lax.axis_size(axis)
    return lax.ppermute(value, axis, [(i, (i + steps) % length) for i in range(length)])


def all_ahead(value, axis):
    length = lax.axis_size(axis)
    return jnp.stack([value] + [from_ahead(value, axis, s) for s in range(1, length)])


def sent_to_all(value, axes):
    length = math.prod(lax.axis_size(a) for a in axes)
    copies = jnp.broadcast_to(value, (length, *value.shape))
    return lax.all_to_all(copies, axes, split_axis=0, concat_axis=0, tiled=True)


def to_own_place(value, dim, axis):
    return jnp.roll(value, lax.axis_index(axis), dim)


def from_own_place(value, dim, axis):
    return jnp.roll(value, -lax.axis_index(axis), dim)


def column_order(value):
    half = value.shape[2] // 2
    first = value[:, :, :half]
    second = jnp.swapaxes(value[:, :, half:], 0, 1)
    rest = value.shape[3:]
    return jnp.concatenate([first.reshape(-1, *rest), second.reshape(-1, *rest)])


def shards(points, factor):
    nz, ncore, ny, nx = (lax.axis_size(a) for a in ROW_COL)
    nrow, ncol = nz * ncore, ny * nx
    pts, rank = factor.shape
    total = pts * nrow * ncol
    unit = 2.0 / math.sqrt(total * rank)
    h = factor * unit
    hb = h.astype(jnp.bfloat16)
    width = points.shape[1]
    half = pts // 2

    both = jnp.concatenate([points, hb], axis=1)
    first, second = both[:half], both[half:]
    by_x = [from_ahead(first, X, s) for s in (1, 3, 2)]
    by_y = [from_ahead(second, Y, s) for s in (1, 3, 2)]
    z1, z7 = from_ahead(points, Z, 1), from_ahead(points, Z, -1)
    by_x, by_y, z1, z7 = lax.optimization_barrier((by_x, by_y, z1, z7))
    by_x = jnp.stack([first, by_x[0], by_x[2], by_x[1]])
    by_y = jnp.stack([second, by_y[0], by_y[2], by_y[1]])
    z23 = from_ahead(jnp.stack([points, z1]), Z, 2)
    z65 = from_ahead(jnp.stack([points, z7]), Z, -2)
    z4 = from_ahead(z23[1], Z, 1)
    cols = [by_x] + [from_ahead(by_x, Y, s) for s in (1, 3, 2)]
    cols += [by_y] + [from_ahead(by_y, X, s) for s in (1, 3, 2)]
    cols = [cols[i].reshape(-1, width + rank) for i in (0, 1, 3, 2, 4, 5, 7, 6)]
    cols = jnp.concatenate(cols)
    along_z = jnp.stack([points, z1, z23[0], z23[1], z4, z65[1], z65[0], z7])
    along_z = to_own_place(along_z, 0, Z)
    other = from_ahead(along_z, CORE, 1)
    rows = jnp.stack([along_z, other]).reshape(-1, width)
    col_pts, hb_cols = cols[:, :width], cols[:, width:]

    gram_matrix = lax.dot_general(
        rows, col_pts, (((1,), (1,)), ((), ())), preferred_element_type=jnp.float32
    )
    row_sq = jnp.sum(jnp.square(rows.astype(jnp.float32)), axis=1)
    col_sq = jnp.sum(jnp.square(col_pts.astype(jnp.float32)), axis=1)
    kern = jnp.exp((2.0 * gram_matrix - row_sq[:, None] - col_sq[None, :]) * (0.5 / EMBED_WIDTH))

    own_col = lax.axis_index(COL)
    own_row = lax.axis_index(ROW)
    part = rank // ncol

    def gram_part(cols_b):
        whole = lax.dot_general(
            cols_b, cols_b, (((0,), (0,)), ((), ())), preferred_element_type=jnp.float32
        )
        return lax.dynamic_slice_in_dim(whole, own_col * part, part, 0)

    row_sum = jnp.sum(kern, axis=1).reshape(ncore, nz, pts)
    placed = jnp.swapaxes(to_own_place(row_sum, 0, CORE), 0, 1)
    message = jnp.concatenate([placed.reshape(-1, rank), gram_part(hb_cols)])
    summed = jnp.sum(sent_to_all(message, ROW), axis=0)
    lines = nrow * pts // rank
    mean_rows = summed[:lines].reshape(nz, ncore, pts) / total
    own_mean = lax.dynamic_slice_in_dim(mean_rows.reshape(nrow, pts), own_row, 1, 0)
    band = jnp.full((1, rank - pts), jnp.sum(mean_rows))
    message = jnp.concatenate([jnp.concatenate([own_mean, band], axis=1), summed[lines:]])
    gathered = sent_to_all(message, COL)
    hh = gathered[:, 1:].reshape(rank, rank)
    grand = jnp.sum(gathered[:, 0, pts]) / total
    mean_cols = gathered[:, 0, :pts].reshape(ny, nx, pts)
    mean_cols = column_order(from_own_place(from_own_place(mean_cols, 0, Y), 1, X))
    mean_rows = from_own_place(jnp.swapaxes(mean_rows, 0, 1), 0, CORE)
    affinity = (kern - mean_rows.reshape(-1)[:, None] - mean_cols[None, :] + grand).astype(
        jnp.bfloat16
    )

    def summed_rows(partial, extra):
        partial = partial.reshape(ncore, nz, pts, rank)
        if extra is None:
            mine = partial[0] + from_ahead(partial[1], CORE, 1)
        else:
            sent = jnp.concatenate([partial[1].reshape(-1, rank), extra])
            got = from_ahead(sent, CORE, 1)
            mine = partial[0] + got[: nz * pts].reshape(nz, pts, rank)
            extra = jnp.broadcast_to(extra + got[nz * pts :], (nz, *extra.shape))
            mine = jnp.concatenate([mine, extra], axis=1)
        own = jnp.sum(lax.all_to_all(mine, Z, 0, 0, tiled=True), axis=0)
        return own[:pts], own[pts:]

    for step in range(ITERS):
        partial = jnp.dot(affinity, hb_cols, preferred_element_type=jnp.float32)
        if step == 0:
            ah, _ = summed_rows(partial, None)
        else:
            ah, own_part = summed_rows(partial, gram_part(hb_cols))
            hh = sent_to_all(own_part, COL).reshape(rank, rank)
        scale = 0.5 / jnp.sqrt(jnp.sum(hh * hh) + 1e-06)
        h = jnp.maximum(h - scale * (jnp.dot(h, hh, precision=lax.Precision.HIGHEST) - ah), 0.0)
        if step + 1 < ITERS:
            hb_cols = column_order(all_ahead(all_ahead(h.astype(jnp.bfloat16), X), Y))
    return h / unit


def solution(mesh):
    split = Mesh(mesh.devices.reshape(8, 2, 4, 4), ROW_COL)
    return jax.shard_map(
        shards,
        mesh=split,
        in_specs=(P(ROW_COL, None), P(ROW_COL, None)),
        out_specs=P(ROW_COL, None),
        check_vma=False,
    )
```

profile of v0, /device:TPU:1, one launch (start us, length us, event | category | flops | bytes accessed | tf_op | source)
XLA Modules:
  0.0 193.2 jit_solution(17189325724903074852)
XLA Ops:
  1.7 3.4 %collective-permute-start = (bf16[32,1280]{1,0:T(8,128)(2,1)S(1)}, bf16[32,1280]{1,0:T(8,128)(2,1)S(1)}, u32[]{:S(2)}, u32[]{:S(2)}) collective-permute-start(bf16[32,1280]{1,0:T(8,128)(2,1)S(1)} %get-tuple-element.29), channel_id=1, source_target_pairs={{1,0},{2,1},{3,2},{0,3},{5,4},{6,5},{7,6},{4,7},{9,8},{10,9},{11,1... | collective-permute-start | bytes 245768 | tf_op jit(solution)/shard_map/ppermute | solution.py:19
  5.1 1.7 collective-permute-start.2
  6.8 2.7 %collective-permute-start.3 = (bf16[32,1280]{1,0:T(8,128)(2,1)S(1)}, bf16[32,1280]{1,0:T(8,128)(2,1)S(1)}, u32[]{:S(2)}, u32[]{:S(2)}) collective-permute-start(bf16[32,1280]{1,0:T(8,128)(2,1)S(1)} %get-tuple-element.28), channel_id=1, source_target_pairs={{4,0},{8,4},{12,8},{0,12},{5,1},{9,5},{13,9},{1,13},{6,2},{10,6},{... | collective-permute-start | bytes 245768 | tf_op jit(solution)/shard_map/ppermute | solution.py:19
  9.6 1.6 collective-permute-start.5
  11.2 5.6 %collective-permute-start.6 = (bf16[64,1024]{1,0:T(8,128)(2,1)}, bf16[64,1024]{1,0:T(8,128)(2,1)S(1)}, u32[]{:S(2)}, u32[]{:S(2)}) collective-permute-start(bf16[64,1024]{1,0:T(8,128)(2,1)} %param.4), channel_id=1, source_target_pairs={{32,0},{64,32},{96,64},{128,96},{160,128},{192,160},{224,192},{0,2... | collective-permute-start | bytes 393224 | tf_op jit(solution)/shard_map/ppermute | solution.py:19
  19.1 3.0 %collective-permute-done.7 = bf16[64,1024]{1,0:T(8,128)(2,1)S(1)} collective-permute-done((bf16[64,1024]{1,0:T(8,128)(2,1)}, bf16[64,1024]{1,0:T(8,128)(2,1)S(1)}, u32[]{:S(2)}, u32[]{:S(2)}) %collective-permute-start.7) | collective-permute-done | bytes 131104 | tf_op jit(solution)/shard_map/ppermute | solution.py:19
  22.1 2.3 %collective-permute-start.12 = (bf16[4,32,1280]{2,1,0:T(8,128)(2,1)S(1)}, bf16[4,32,1280]{2,1,0:T(8,128)(2,1)S(1)}, u32[]{:S(2)}, u32[]{:S(2)}) collective-permute-start(bf16[4,32,1280]{2,1,0:T(8,128)(2,1)S(1)} %pad_maximum_fusion.7), channel_id=1, source_target_pairs={{4,0},{8,4},{12,8},{0,12},{5,1},{9,5},{13,9},{1,13},{6,2},{10,6},{... | collective-permute-start | bytes 983048 | tf_op jit(solution)/shard_map/ppermute | solution.py:19
  28.0 9.4 %collective-permute-done.8 = bf16[2,64,1024]{2,1,0:T(8,128)(2,1)S(1)} collective-permute-done((bf16[2,64,1024]{2,1,0:T(8,128)(2,1)S(1)}, bf16[2,64,1024]{2,1,0:T(8,128)(2,1)S(1)}, u32[]{:S(2)}, u32[]{:S(2)}) %collective-permute-start.8) | collective-permute-done | bytes 262176 | tf_op jit(solution)/shard_map/ppermute | solution.py:19
  37.4 2.2 %collective-permute-start.16 = (bf16[4,32,1280]{2,1,0:T(8,128)(2,1)S(1)}, bf16[4,32,1280]{2,1,0:T(8,128)(2,1)S(1)}, u32[]{:S(2)}, u32[]{:S(2)}) collective-permute-start(bf16[4,32,1280]{2,1,0:T(8,128)(2,1)S(1)} %pad_maximum_fusion.8), channel_id=1, source_target_pairs={{2,0},{3,1},{0,2},{1,3},{6,4},{7,5},{4,6},{5,7},{10,8},{11,9},{8,1... | collective-permute-start | bytes 983048 | tf_op jit(solution)/shard_map/ppermute | solution.py:19
  42.1 2.8 %collective-permute-done.9 = bf16[64,1024]{1,0:T(8,128)(2,1)S(1)} collective-permute-done((bf16[64,1024]{1,0:T(8,128)(2,1)S(1)}, bf16[64,1024]{1,0:T(8,128)(2,1)S(1)}, u32[]{:S(2)}, u32[]{:S(2)}) %collective-permute-start.9) | collective-permute-done | bytes 131104 | tf_op jit(solution)/shard_map/ppermute | solution.py:19
  44.9 2.6 %collective-permute-done.10 = bf16[2,64,1024]{2,1,0:T(8,128)(2,1)S(1)} collective-permute-done((bf16[2,64,1024]{2,1,0:T(8,128)(2,1)S(1)}, bf16[2,64,1024]{2,1,0:T(8,128)(2,1)S(1)}, u32[]{:S(2)}, u32[]{:S(2)}) %collective-permute-start.10) | collective-permute-done | bytes 262176 | tf_op jit(solution)/shard_map/ppermute | solution.py:19
  47.8 7.2 %collective-permute-start.11 = (bf16[8,64,1024]{2,1,0:T(8,128)(2,1)S(1)}, bf16[8,64,1024]{2,1,0:T(8,128)(2,1)S(1)}, u32[]{:S(2)}, u32[]{:S(2)}) collective-permute-start(bf16[8,64,1024]{2,1,0:T(8,128)(2,1)S(1)} %constant_dynamic-slice_fusion.3), channel_id=1, source_target_pairs={{16,0},{0,16},{17,1},{1,17},{18,2},{2,18},{19,3},{3,19},{20,4},{4,... | collective-permute-start | bytes 3145736 | tf_op jit(solution)/shard_map/ppermute | solution.py:19
  57.3 1.5 pad_maximum_fusion
  59.8 6.2 %fusion = (f32[1024]{0:T(1024)S(1)}, f32[1024,1024]{0,1:T(8,128)}) fusion(f32[1024]{0:T(1024)S(1)} %multiply_reduce_fusion, f32[1024]{0:T(1024)S(1)} %sub.64, bf16[1024,1024]{1,0:T(8,128)(2,1)} %bitcast.69, bf16[1024,1280]{1,0:T(8,128)(2,1)S(1)} %copy-done.1), kind=kOutput, calls=%fused_computation.4 | convolution fusion | flops 2152725504 | bytes 8400896 | tf_op jit(solution)/shard_map/dot_general | solution.py:86
  66.9 4.3 %all-to-all-start = ((f32[16,20,256]{2,1,0:T(8,128)}), f32[16,20,256]{2,1,0:T(8,128)S(1)}, u32[]{:S(2)}, u32[]{:S(2)}) async-start(f32[16,20,256]{2,1,0:T(8,128)} %broadcast_in_dim.16), calls=%async_computation | async-start | bytes 786432 | tf_op jit(solution)/shard_map/all_to_all | solution.py:35
  71.3 14.5 %all-to-all-done = f32[16,20,256]{2,1,0:T(8,128)S(1)} async-done(((f32[16,20,256]{2,1,0:T(8,128)}), f32[16,20,256]{2,1,0:T(8,128)S(1)}, u32[]{:S(2)}, u32[]{:S(2)}) %all-to-all-start) | async-done | bytes 327712 | tf_op jit(solution)/shard_map/all_to_all | solution.py:35
  88.0 7.0 %all-to-all-start.1 = ((f32[16,17,256]{2,1,0:T(8,128)}), f32[16,17,256]{2,1,0:T(8,128)S(1)}, u32[]{:S(2)}, u32[]{:S(2)}) async-start(f32[16,17,256]{2,1,0:T(8,128)} %broadcast_in_dim.17), calls=%async_computation.1 | async-start | bytes 786432 | tf_op jit(solution)/shard_map/all_to_all | solution.py:35
  95.3 10.3 %all-to-all-done.1 = f32[16,17,256]{2,1,0:T(8,128)S(1)} async-done(((f32[16,17,256]{2,1,0:T(8,128)}), f32[16,17,256]{2,1,0:T(8,128)S(1)}, u32[]{:S(2)}, u32[]{:S(2)}) %all-to-all-start.1) | async-done | bytes 278560 | tf_op jit(solution)/shard_map/all_to_all | solution.py:35
  107.3 3.1 %add_convert_fusion = bf16[1024,1024]{0,1:T(8,128)(2,1)S(1)} fusion(f32[1024,1024]{0,1:T(8,128)} %get-tuple-element.39, f32[]{:T(128)S(6)} %div.27, f32[1024]{0:T(1024)S(1)} %pad_maximum_fusion.14, f32[1024]{0:T(1024)S(1)} %sub.69, f32[1024]{0:T(1024)S(1)} %multiply_reduce_fusion, f32[1024]{0:T(1024)S(1)} %sub.64), kind=kLoop, calls=%fused_computation | loop fusion | flops 8388608 | bytes 6307844 | tf_op jit(solution)/shard_map/convert_element_type | solution.py:118
  112.3 1.5 collective-permute-done.18
  114.7 3.5 %all-to-all-start.2 = ((f32[8,64,256]{2,1,0:T(8,128)}), f32[8,64,256]{2,1,0:T(8,128)S(1)}, u32[]{:S(2)}, u32[]{:S(2)}) async-start(f32[8,64,256]{2,1,0:T(8,128)} %add.87), calls=%async_computation.2 | async-start | bytes 1048576 | tf_op jit(solution)/shard_map/all_to_all | solution.py:132
  119.7 16.4 %all-to-all-done.2 = f32[8,64,256]{2,1,0:T(8,128)S(1)} async-done(((f32[8,64,256]{2,1,0:T(8,128)}), f32[8,64,256]{2,1,0:T(8,128)S(1)}, u32[]{:S(2)}, u32[]{:S(2)}) %all-to-all-start.2) | async-done | bytes 524320 | tf_op jit(solution)/shard_map/all_to_all | solution.py:132
  136.8 1.8 collective-permute-start.20
  139.3 1.7 collective-permute-done.20
  141.0 1.6 collective-permute-done.21
  144.5 2.1 %collective-permute-done.22 = bf16[4,64,256]{2,1,0:T(8,128)(2,1)S(1)} collective-permute-done((bf16[4,64,256]{2,1,0:T(8,128)(2,1)S(1)}, bf16[4,64,256]{2,1,0:T(8,128)(2,1)S(1)}, u32[]{:S(2)}, u32[]{:S(2)}) %collective-permute-start.22) | collective-permute-done | bytes 131104 | tf_op jit(solution)/shard_map/ppermute | solution.py:19
  146.5 2.7 %collective-permute-done.23 = bf16[4,64,256]{2,1,0:T(8,128)(2,1)S(1)} collective-permute-done((bf16[4,64,256]{2,1,0:T(8,128)(2,1)S(1)}, bf16[4,64,256]{2,1,0:T(8,128)(2,1)S(1)}, u32[]{:S(2)}, u32[]{:S(2)}) %collective-permute-start.23) | collective-permute-done | bytes 131104 | tf_op jit(solution)/shard_map/ppermute | solution.py:19
  149.2 1.8 collective-permute-done.24
  152.4 3.0 %collective-permute-start.25 = (f32[528,256]{1,0:T(8,128)S(1)}, f32[528,256]{1,0:T(8,128)S(1)}, u32[]{:S(2)}, u32[]{:S(2)}) collective-permute-start(f32[528,256]{1,0:T(8,128)S(1)} %pad_maximum_fusion.2), channel_id=1, source_target_pairs={{16,0},{0,16},{17,1},{1,17},{18,2},{2,18},{19,3},{3,19},{20,4},{4,... | collective-permute-start | bytes 1622024 | tf_op jit(solution)/shard_map/ppermute | solution.py:19
  155.4 1.6 collective-permute-done.25
  157.1 23.2 %all_to_all.25 = f32[8,80,256]{2,1,0:T(8,128)S(1)} all-to-all(f32[8,80,256]{2,1,0:T(8,128)S(1)} %pad_maximum_fusion.1), channel_id=1, replica_groups=mesh['row_0'=8,'row_1'=2,'col_0'=4,'col_1'=4] {'row_0'}, dimensions={0} | all-to-all | bytes 1310720 | tf_op jit(solution)/shard_map/all_to_all | solution.py:132
  180.4 10.6 %all_to_all.26 = f32[16,16,256]{2,1,0:T(8,128)S(1)} all-to-all(f32[16,16,256]{2,1,0:T(8,128)S(1)} %broadcast_in_dim.19), channel_id=1, replica_groups=mesh['row_0'=8,'row_1'=2,'col_0'=4,'col_1'=4] {'col_0','col_1'}, dimensions={0} | all-to-all | bytes 524288 | tf_op jit(solution)/shard_map/all_to_all | solution.py:35
  (128 shorter events, 27.3 us)
Async XLA Ops:
  1.7 7.9 %collective-permute-start = (bf16[32,1280]{1,0:T(8,128)(2,1)S(1)}, bf16[32,1280]{1,0:T(8,128)(2,1)S(1)}, u32[]{:S(2)}, u32[]{:S(2)}) collective-permute-start(bf16[32,1280]{1,0:T(8,128)(2,1)S(1)} %get-tuple-element.29), channel_id=1, source_target_pairs={{1,0},{2,1},{3,2},{0,3},{5,4},{6,5},{7,6},{4,7},{9,8},{10,9},{11,1... | collective-permute-start | bytes 245768 | tf_op jit(solution)/shard_map/ppermute | solution.py:19
  5.1 6.1 %collective-permute-start.1 = (bf16[32,1280]{1,0:T(8,128)(2,1)S(1)}, bf16[32,1280]{1,0:T(8,128)(2,1)S(1)}, u32[]{:S(2)}, u32[]{:S(2)}) collective-permute-start(bf16[32,1280]{1,0:T(8,128)(2,1)S(1)} %get-tuple-element.29), channel_id=1, source_target_pairs={{3,0},{0,1},{1,2},{2,3},{7,4},{4,5},{5,6},{6,7},{11,8},{8,9},{9,10... | collective-permute-start | bytes 245768 | tf_op jit(solution)/shard_map/ppermute | solution.py:19
  5.1 11.7 %collective-permute-start.2 = (bf16[32,1280]{1,0:T(8,128)(2,1)S(1)}, bf16[32,1280]{1,0:T(8,128)(2,1)S(1)}, u32[]{:S(2)}, u32[]{:S(2)}) collective-permute-start(bf16[32,1280]{1,0:T(8,128)(2,1)S(1)} %get-tuple-element.29), channel_id=1, source_target_pairs={{2,0},{3,1},{0,2},{1,3},{6,4},{7,5},{4,6},{5,7},{10,8},{11,9},{8,1... | collective-permute-start | bytes 245768 | tf_op jit(solution)/shard_map/ppermute | solution.py:19
  6.8 11.0 %collective-permute-start.3 = (bf16[32,1280]{1,0:T(8,128)(2,1)S(1)}, bf16[32,1280]{1,0:T(8,128)(2,1)S(1)}, u32[]{:S(2)}, u32[]{:S(2)}) collective-permute-start(bf16[32,1280]{1,0:T(8,128)(2,1)S(1)} %get-tuple-element.28), channel_id=1, source_target_pairs={{4,0},{8,4},{12,8},{0,12},{5,1},{9,5},{13,9},{1,13},{6,2},{10,6},{... | collective-permute-start | bytes 245768 | tf_op jit(solution)/shard_map/ppermute | solution.py:19
  9.6 8.3 %collective-permute-start.4 = (bf16[32,1280]{1,0:T(8,128)(2,1)S(1)}, bf16[32,1280]{1,0:T(8,128)(2,1)S(1)}, u32[]{:S(2)}, u32[]{:S(2)}) collective-permute-start(bf16[32,1280]{1,0:T(8,128)(2,1)S(1)} %get-tuple-element.28), channel_id=1, source_target_pairs={{12,0},{0,4},{4,8},{8,12},{13,1},{1,5},{5,9},{9,13},{14,2},{2,6},{... | collective-permute-start | bytes 245768 | tf_op jit(solution)/shard_map/ppermute | solution.py:19
  9.6 8.3 %collective-permute-start.5 = (bf16[32,1280]{1,0:T(8,128)(2,1)S(1)}, bf16[32,1280]{1,0:T(8,128)(2,1)S(1)}, u32[]{:S(2)}, u32[]{:S(2)}) collective-permute-start(bf16[32,1280]{1,0:T(8,128)(2,1)S(1)} %get-tuple-element.28), channel_id=1, source_target_pairs={{8,0},{12,4},{0,8},{4,12},{9,1},{13,5},{1,9},{5,13},{10,2},{14,6},... | collective-permute-start | bytes 245768 | tf_op jit(solution)/shard_map/ppermute | solution.py:19
  11.2 7.8 %collective-permute-start.6 = (bf16[64,1024]{1,0:T(8,128)(2,1)}, bf16[64,1024]{1,0:T(8,128)(2,1)S(1)}, u32[]{:S(2)}, u32[]{:S(2)}) collective-permute-start(bf16[64,1024]{1,0:T(8,128)(2,1)} %param.4), channel_id=1, source_target_pairs={{32,0},{64,32},{96,64},{128,96},{160,128},{192,160},{224,192},{0,2... | collective-permute-start | bytes 393224 | tf_op jit(solution)/shard_map/ppermute | solution.py:19
  16.8 5.2 %collective-permute-start.7 = (bf16[64,1024]{1,0:T(8,128)(2,1)}, bf16[64,1024]{1,0:T(8,128)(2,1)S(1)}, u32[]{:S(2)}, u32[]{:S(2)}) collective-permute-start(bf16[64,1024]{1,0:T(8,128)(2,1)} %param.4), channel_id=1, source_target_pairs={{224,0},{0,32},{32,64},{64,96},{96,128},{128,160},{160,192},{192,2... | collective-permute-start | bytes 393224 | tf_op jit(solution)/shard_map/ppermute | solution.py:19
  22.1 17.5 %collective-permute-start.12 = (bf16[4,32,1280]{2,1,0:T(8,128)(2,1)S(1)}, bf16[4,32,1280]{2,1,0:T(8,128)(2,1)S(1)}, u32[]{:S(2)}, u32[]{:S(2)}) collective-permute-start(bf16[4,32,1280]{2,1,0:T(8,128)(2,1)S(1)} %pad_maximum_fusion.7), channel_id=1, source_target_pairs={{4,0},{8,4},{12,8},{0,12},{5,1},{9,5},{13,9},{1,13},{6,2},{10,6},{... | collective-permute-start | bytes 983048 | tf_op jit(solution)/shard_map/ppermute | solution.py:19
  24.4 15.4 %collective-permute-start.13 = (bf16[4,32,1280]{2,1,0:T(8,128)(2,1)S(1)}, bf16[4,32,1280]{2,1,0:T(8,128)(2,1)S(1)}, u32[]{:S(2)}, u32[]{:S(2)}) collective-permute-start(bf16[4,32,1280]{2,1,0:T(8,128)(2,1)S(1)} %pad_maximum_fusion.7), channel_id=1, source_target_pairs={{8,0},{12,4},{0,8},{4,12},{9,1},{13,5},{1,9},{5,13},{10,2},{14,6},... | collective-permute-start | bytes 983048 | tf_op jit(solution)/shard_map/ppermute | solution.py:19
  25.6 15.5 %collective-permute-start.14 = (bf16[4,32,1280]{2,1,0:T(8,128)(2,1)S(1)}, bf16[4,32,1280]{2,1,0:T(8,128)(2,1)S(1)}, u32[]{:S(2)}, u32[]{:S(2)}) collective-permute-start(bf16[4,32,1280]{2,1,0:T(8,128)(2,1)S(1)} %pad_maximum_fusion.7), channel_id=1, source_target_pairs={{12,0},{0,4},{4,8},{8,12},{13,1},{1,5},{5,9},{9,13},{14,2},{2,6},{... | collective-permute-start | bytes 983048 | tf_op jit(solution)/shard_map/ppermute | solution.py:19
  26.5 10.9 %collective-permute-start.8 = (bf16[2,64,1024]{2,1,0:T(8,128)(2,1)S(1)}, bf16[2,64,1024]{2,1,0:T(8,128)(2,1)S(1)}, u32[]{:S(2)}, u32[]{:S(2)}) collective-permute-start(bf16[2,64,1024]{2,1,0:T(8,128)(2,1)S(1)} %get-tuple-element.33), channel_id=1, source_target_pairs={{64,0},{96,32},{128,64},{160,96},{192,128},{224,160},{0,192},{32,2... | collective-permute-start | bytes 786440 | tf_op jit(solution)/shard_map/ppermute | solution.py:19
  26.8 15.2 %collective-permute-start.15 = (bf16[4,32,1280]{2,1,0:T(8,128)(2,1)S(1)}, bf16[4,32,1280]{2,1,0:T(8,128)(2,1)S(1)}, u32[]{:S(2)}, u32[]{:S(2)}) collective-permute-start(bf16[4,32,1280]{2,1,0:T(8,128)(2,1)S(1)} %pad_maximum_fusion.8), channel_id=1, source_target_pairs={{1,0},{2,1},{3,2},{0,3},{5,4},{6,5},{7,6},{4,7},{9,8},{10,9},{11,1... | collective-permute-start | bytes 983048 | tf_op jit(solution)/shard_map/ppermute | solution.py:19
  37.4 17.6 %collective-permute-start.16 = (bf16[4,32,1280]{2,1,0:T(8,128)(2,1)S(1)}, bf16[4,32,1280]{2,1,0:T(8,128)(2,1)S(1)}, u32[]{:S(2)}, u32[]{:S(2)}) collective-permute-start(bf16[4,32,1280]{2,1,0:T(8,128)(2,1)S(1)} %pad_maximum_fusion.8), channel_id=1, source_target_pairs={{2,0},{3,1},{0,2},{1,3},{6,4},{7,5},{4,6},{5,7},{10,8},{11,9},{8,1... | collective-permute-start | bytes 983048 | tf_op jit(solution)/shard_map/ppermute | solution.py:19
  39.7 15.4 %collective-permute-start.17 = (bf16[4,32,1280]{2,1,0:T(8,128)(2,1)S(1)}, bf16[4,32,1280]{2,1,0:T(8,128)(2,1)S(1)}, u32[]{:S(2)}, u32[]{:S(2)}) collective-permute-start(bf16[4,32,1280]{2,1,0:T(8,128)(2,1)S(1)} %pad_maximum_fusion.8), channel_id=1, source_target_pairs={{3,0},{0,1},{1,2},{2,3},{7,4},{4,5},{5,6},{6,7},{11,8},{8,9},{9,10... | collective-permute-start | bytes 983048 | tf_op jit(solution)/shard_map/ppermute | solution.py:19
  39.8 7.8 %copy-start.4 = (bf16[64,1024]{1,0:T(8,128)(2,1)S(1)}, bf16[64,1024]{1,0:T(8,128)(2,1)}, u32[]{:S(2)}) copy-start(bf16[64,1024]{1,0:T(8,128)(2,1)} %param.4) | copy-start | bytes 393220
  39.8 7.7 %collective-permute-start.10 = (bf16[2,64,1024]{2,1,0:T(8,128)(2,1)S(1)}, bf16[2,64,1024]{2,1,0:T(8,128)(2,1)S(1)}, u32[]{:S(2)}, u32[]{:S(2)}) collective-permute-start(bf16[2,64,1024]{2,1,0:T(8,128)(2,1)S(1)} %get-tuple-element.32), channel_id=1, source_target_pairs={{192,0},{224,32},{0,64},{32,96},{64,128},{96,160},{128,192},{160,2... | collective-permute-start | bytes 786440 | tf_op jit(solution)/shard_map/ppermute | solution.py:19
  41.1 3.8 %collective-permute-start.9 = (bf16[64,1024]{1,0:T(8,128)(2,1)S(1)}, bf16[64,1024]{1,0:T(8,128)(2,1)S(1)}, u32[]{:S(2)}, u32[]{:S(2)}) collective-permute-start(bf16[64,1024]{1,0:T(8,128)(2,1)S(1)} %slice_bitcast_fusion.1), channel_id=1, source_target_pairs={{32,0},{64,32},{96,64},{128,96},{160,128},{192,160},{224,192},{0,2... | collective-permute-start | bytes 393224 | tf_op jit(solution)/shard_map/ppermute | solution.py:19
  47.8 9.5 %collective-permute-start.11 = (bf16[8,64,1024]{2,1,0:T(8,128)(2,1)S(1)}, bf16[8,64,1024]{2,1,0:T(8,128)(2,1)S(1)}, u32[]{:S(2)}, u32[]{:S(2)}) collective-permute-start(bf16[8,64,1024]{2,1,0:T(8,128)(2,1)S(1)} %constant_dynamic-slice_fusion.3), channel_id=1, source_target_pairs={{16,0},{0,16},{17,1},{1,17},{18,2},{2,18},{19,3},{3,19},{20,4},{4,... | collective-permute-start | bytes 3145736 | tf_op jit(solution)/shard_map/ppermute | solution.py:19
  66.9 18.9 %all-to-all-start = ((f32[16,20,256]{2,1,0:T(8,128)}), f32[16,20,256]{2,1,0:T(8,128)S(1)}, u32[]{:S(2)}, u32[]{:S(2)}) async-start(f32[16,20,256]{2,1,0:T(8,128)} %broadcast_in_dim.16), calls=%async_computation | async-start | bytes 786432 | tf_op jit(solution)/shard_map/all_to_all | solution.py:35
  88.0 17.6 %all-to-all-start.1 = ((f32[16,17,256]{2,1,0:T(8,128)}), f32[16,17,256]{2,1,0:T(8,128)S(1)}, u32[]{:S(2)}, u32[]{:S(2)}) async-start(f32[16,17,256]{2,1,0:T(8,128)} %broadcast_in_dim.17), calls=%async_computation.1 | async-start | bytes 786432 | tf_op jit(solution)/shard_map/all_to_all | solution.py:35
  111.8 24.4 %copy-start.5 = (f32[64,256]{1,0:T(8,128)S(1)}, f32[64,256]{1,0:T(8,128)}, u32[]{:S(2)}) copy-start(f32[64,256]{1,0:T(8,128)} %param.5) | copy-start | bytes 196612
  111.8 2.0 %collective-permute-start.18 = (f32[8,64,256]{2,1,0:T(8,128)S(1)}, f32[8,64,256]{2,1,0:T(8,128)S(1)}, u32[]{:S(2)}, u32[]{:S(2)}) collective-permute-start(f32[8,64,256]{2,1,0:T(8,128)S(1)} %bitcast.76), channel_id=1, source_target_pairs={{16,0},{0,16},{17,1},{1,17},{18,2},{2,18},{19,3},{3,19},{20,4},{4,... | collective-permute-start | bytes 1572872 | tf_op jit(solution)/shard_map/ppermute | solution.py:19
  114.7 21.4 %all-to-all-start.2 = ((f32[8,64,256]{2,1,0:T(8,128)}), f32[8,64,256]{2,1,0:T(8,128)S(1)}, u32[]{:S(2)}, u32[]{:S(2)}) async-start(f32[8,64,256]{2,1,0:T(8,128)} %add.87), calls=%async_computation.2 | async-start | bytes 1048576 | tf_op jit(solution)/shard_map/all_to_all | solution.py:132
  118.9 32.3 %copy-start.3 = (bf16[1024,1024]{0,1:T(8,128)(2,1)S(1)}, bf16[1024,1024]{0,1:T(8,128)(2,1)}, u32[]{:S(2)}) copy-start(bf16[1024,1024]{0,1:T(8,128)(2,1)} %copy-done.2) | copy-start | bytes 6291460
  136.4 2.8 %collective-permute-start.19 = (bf16[64,256]{1,0:T(8,128)(2,1)S(1)}, bf16[64,256]{1,0:T(8,128)(2,1)S(1)}, u32[]{:S(2)}, u32[]{:S(2)}) collective-permute-start(bf16[64,256]{1,0:T(8,128)(2,1)S(1)} %get-tuple-element.40), channel_id=1, source_target_pairs={{1,0},{2,1},{3,2},{0,3},{5,4},{6,5},{7,6},{4,7},{9,8},{10,9},{11,1... | collective-permute-start | bytes 98312 | tf_op jit(solution)/shard_map/ppermute | solution.py:19
  136.8 4.3 %collective-permute-start.20 = (bf16[64,256]{1,0:T(8,128)(2,1)S(1)}, bf16[64,256]{1,0:T(8,128)(2,1)S(1)}, u32[]{:S(2)}, u32[]{:S(2)}) collective-permute-start(bf16[64,256]{1,0:T(8,128)(2,1)S(1)} %get-tuple-element.40), channel_id=1, source_target_pairs={{2,0},{3,1},{0,2},{1,3},{6,4},{7,5},{4,6},{5,7},{10,8},{11,9},{8,1... | collective-permute-start | bytes 98312 | tf_op jit(solution)/shard_map/ppermute | solution.py:19
  138.6 4.0 %collective-permute-start.21 = (bf16[64,256]{1,0:T(8,128)(2,1)S(1)}, bf16[64,256]{1,0:T(8,128)(2,1)S(1)}, u32[]{:S(2)}, u32[]{:S(2)}) collective-permute-start(bf16[64,256]{1,0:T(8,128)(2,1)S(1)} %get-tuple-element.40), channel_id=1, source_target_pairs={{3,0},{0,1},{1,2},{2,3},{7,4},{4,5},{5,6},{6,7},{11,8},{8,9},{9,10... | collective-permute-start | bytes 98312 | tf_op jit(solution)/shard_map/ppermute | solution.py:19
  142.6 3.9 %collective-permute-start.22 = (bf16[4,64,256]{2,1,0:T(8,128)(2,1)S(1)}, bf16[4,64,256]{2,1,0:T(8,128)(2,1)S(1)}, u32[]{:S(2)}, u32[]{:S(2)}) collective-permute-start(bf16[4,64,256]{2,1,0:T(8,128)(2,1)S(1)} %get-tuple-element.31), channel_id=1, source_target_pairs={{4,0},{8,4},{12,8},{0,12},{5,1},{9,5},{13,9},{1,13},{6,2},{10,6},{... | collective-permute-start | bytes 393224 | tf_op jit(solution)/shard_map/ppermute | solution.py:19
  143.8 5.4 %collective-permute-start.23 = (bf16[4,64,256]{2,1,0:T(8,128)(2,1)S(1)}, bf16[4,64,256]{2,1,0:T(8,128)(2,1)S(1)}, u32[]{:S(2)}, u32[]{:S(2)}) collective-permute-start(bf16[4,64,256]{2,1,0:T(8,128)(2,1)S(1)} %get-tuple-element.31), channel_id=1, source_target_pairs={{8,0},{12,4},{0,8},{4,12},{9,1},{13,5},{1,9},{5,13},{10,2},{14,6},... | collective-permute-start | bytes 393224 | tf_op jit(solution)/shard_map/ppermute | solution.py:19
  144.0 7.0 %collective-permute-start.24 = (bf16[4,64,256]{2,1,0:T(8,128)(2,1)S(1)}, bf16[4,64,256]{2,1,0:T(8,128)(2,1)S(1)}, u32[]{:S(2)}, u32[]{:S(2)}) collective-permute-start(bf16[4,64,256]{2,1,0:T(8,128)(2,1)S(1)} %get-tuple-element.31), channel_id=1, source_target_pairs={{12,0},{0,4},{4,8},{8,12},{13,1},{1,5},{5,9},{9,13},{14,2},{2,6},{... | collective-permute-start | bytes 393224 | tf_op jit(solution)/shard_map/ppermute | solution.py:19
  152.4 4.6 %collective-permute-start.25 = (f32[528,256]{1,0:T(8,128)S(1)}, f32[528,256]{1,0:T(8,128)S(1)}, u32[]{:S(2)}, u32[]{:S(2)}) collective-permute-start(f32[528,256]{1,0:T(8,128)S(1)} %pad_maximum_fusion.2), channel_id=1, source_target_pairs={{16,0},{0,16},{17,1},{1,17},{18,2},{2,18},{19,3},{3,19},{20,4},{4,... | collective-permute-start | bytes 1622024 | tf_op jit(solution)/shard_map/ppermute | solution.py:19
  (3 other events, 5.3 us)
where the time goes:
time: 194 us; the launch traced here: 193 us
  waiting for transfers between devices  75.3 us (39%)
  starting transfers between devices  53.2 us (27%)
  blocking collectives  33.8 us (17%)
  other arithmetic  13 us (7%)
  matrix products  9.48 us (5%)
  local copies, waits for them, and re-layouts  5.56 us (3%)
  between operations  2.84 us (1%)
    ppermute x26, starting transfers between devices, from_ahead(): lax.ppermute(value, axis, [((i + steps) % length, i) for i in range(lengt...  38.4 us
    ppermute x26, waiting for transfers between devices, from_ahead(): lax.ppermute(value, axis, [((i + steps) % length, i) for i in range(lengt...  34 us
    all_to_all x2, waiting for transfers between devices, sent_to_all(): return lax.all_to_all(copies, axes, split_axis=0, concat_axis=0, tiled=True)  24.9 us
    all_to_all x1, blocking collectives, summed_rows(): own = jnp.sum(lax.all_to_all(mine, Z, 0, 0, tiled=True), axis=0)  23.2 us
    all_to_all x1, waiting for transfers between devices, summed_rows(): own = jnp.sum(lax.all_to_all(mine, Z, 0, 0, tiled=True), axis=0)  16.4 us
    all_to_all x2, starting transfers between devices, sent_to_all(): return lax.all_to_all(copies, axes, split_axis=0, concat_axis=0, tiled=True)  11.3 us
    all_to_all x1, blocking collectives, sent_to_all(): return lax.all_to_all(copies, axes, split_axis=0, concat_axis=0, tiled=True)  10.6 us
    dot_general x1, matrix products, shards(): lax.dot_general(rows, col_pts, (((1,), (1,)), ((), ())), preferred_elemen...  6.17 us
  transfers between devices with their start and end apart: 29, of which 18 were waited for; matrix products, arithmetic and copies ran while one was open for 2% of the time, Pallas kernels for 0%

commit v1 on v0

v1 whole, which is shorter than its diff:
```python
import functools
import math

import jax
import jax.numpy as jnp
from jax import lax
from jax.experimental import pallas as pl
from jax.experimental.pallas import tpu as pltpu
from jax.sharding import Mesh
from jax.sharding import PartitionSpec as P

EMBED_WIDTH = 1024
Z, CORE, Y, X = "row_0", "row_1", "col_0", "col_1"
ROW = (Z, CORE)
COL = (Y, X)
ROW_COL = (Z, CORE, Y, X)


def from_ahead(value, axis, steps):
    length = lax.axis_size(axis)
    return lax.ppermute(value, axis, [((i + steps) % length, i) for i in range(length)])


def sent_to_all(value, axes):
    length = math.prod(lax.axis_size(a) for a in axes)
    copies = jnp.broadcast_to(value, (length, *value.shape))
    return lax.all_to_all(copies, axes, split_axis=0, concat_axis=0, tiled=True)


F32, BF16 = jnp.float32, jnp.bfloat16
VMEM = pl.BlockSpec(memory_space=pltpu.VMEM)
LANES = 128


def call(kernel, outs, args, flops, scratch=(), vmem=24):
    size = sum(math.prod(a.shape) * a.dtype.itemsize for a in (*outs, *args))
    return pl.pallas_call(
        kernel,
        out_shape=outs,
        in_specs=[VMEM] * len(args),
        out_specs=[VMEM] * len(outs),
        scratch_shapes=list(scratch),
        compiler_params=pltpu.CompilerParams(vmem_limit_bytes=vmem << 20),
        cost_estimate=pl.CostEstimate(flops=flops, bytes_accessed=size, transcendentals=0),
    )(*args)


def rows_dot(a, b):
    return lax.dot_general(a, b, (((1,), (1,)), ((), ())), preferred_element_type=F32)


def squares(rows):
    wide = rows.astype(F32)
    groups = [wide[:, g : g + LANES] for g in range(0, rows.shape[1], LANES)]
    return sum(g * g for g in groups)


def columns_kernel(by_x, y1, y2, y3, by_y, x1, x2, x3, pts_ref, hb_ref, sq_ref, part_ref, gram_ref):
    ny, nx = lax.axis_size(Y), lax.axis_size(X)
    y, x = lax.axis_index(Y), lax.axis_index(X)
    half = by_x.shape[1]
    width = pts_ref.shape[1]
    for far, ref in enumerate((by_x, y1, y2, y3)):
        for near in range(nx):
            at = lax.rem(y + far, ny) * nx + lax.rem(x + near, nx)
            at = pl.multiple_of(at * 2 * half, half)
            pts_ref[pl.ds(at, half), :] = ref[near, :, :width]
            hb_ref[pl.ds(at, half), :] = ref[near, :, width:]
    for far, ref in enumerate((by_y, x1, x2, x3)):
        for near in range(ny):
            at = lax.rem(y + near, ny) * nx + lax.rem(x + far, nx)
            at = pl.multiple_of(at * 2 * half + half, half)
            pts_ref[pl.ds(at, half), :] = ref[near, :, :width]
            hb_ref[pl.ds(at, half), :] = ref[near, :, width:]
    for block in range(pts_ref.shape[0] // LANES):
        sums = squares(pts_ref[block * LANES : (block + 1) * LANES, :])
        sq_ref[block : block + 1, :] = jnp.sum(sums.T, axis=0, keepdims=True)
    gram_ref[...] = lax.dot_general(
        hb_ref[...], hb_ref[...], (((0,), (0,)), ((), ())), preferred_element_type=F32
    )
    part = part_ref.shape[0]
    at = pl.multiple_of((y * nx + x) * part, part)
    part_ref[...] = gram_ref[pl.ds(at, part), :]


def rows_kernel(
    p0, p1, p23, p4, p65, p7, o0, o1, o23, o4, o65, o7, cols, sq, kern, sums, held
):
    z, core = lax.axis_index(Z), lax.axis_index(CORE)
    nz, pts = lax.axis_size(Z), p0.shape[0]

    def put(which, steps, value):
        at = (which * nz + lax.rem(z + steps, nz)) * pts
        held[pl.ds(pl.multiple_of(at, pts), pts), :] = value

    for which, refs in ((core, (p0, p1, p23, p4, p65, p7)), (1 - core, (o0, o1, o23, o4, o65, o7))):
        put(which, 0, refs[0][...])
        put(which, 1, refs[1][...])
        put(which, 2, refs[2][0])
        put(which, 3, refs[2][1])
        put(which, 4, refs[3][...])
        put(which, 5, refs[4][1])
        put(which, 6, refs[4][0])
        put(which, 7, refs[5][...])
    col_sq = jnp.concatenate([sq[g : g + 1, :] for g in range(sq.shape[0])], axis=1)
    tall = 2 * LANES

    def block(i, _):
        at = pl.ds(pl.multiple_of(i * tall, tall), tall)
        rows = held[at, :]
        row_sq = jnp.sum(squares(rows), axis=1, keepdims=True)
        gram = rows_dot(rows, cols[...])
        values = jnp.exp((2.0 * gram - row_sq - col_sq) * (0.5 / EMBED_WIDTH))
        kern[at, :] = values
        total = sum(values[:, g : g + LANES] for g in range(0, values.shape[1], LANES))
        for j in range(2):
            line = jnp.sum(total[j * LANES : (j + 1) * LANES].T, axis=0, keepdims=True)
            sums[pl.ds(i * 2 + j, 1), :] = line
        return 0

    lax.fori_loop(0, held.shape[0] // tall, block, 0)


def means_kernel(got, mean_ref, out):
    z, core = lax.axis_index(Z), lax.axis_index(CORE)
    n = got.shape[0]
    lines = mean_ref.shape[0]
    total = lines * LANES * n
    even, odd = got[0], got[1]
    for i in range(2, n, 2):
        even, odd = even + got[i], odd + got[i + 1]
    sums = even + odd
    means = sums[:lines] / total
    mean_ref[...] = means
    own = mean_ref[pl.ds((core * lax.axis_size(Z) + z) // 2, 1), :]
    band = jnp.broadcast_to(jnp.sum(means, keepdims=True), (1, LANES))
    fill = jnp.zeros((lines - 2, LANES), F32)
    deep = (got.shape[1] - lines) // 2
    pieces = [own, band, fill]
    for at in (lines, lines + deep):
        pieces += [even[at : at + deep], odd[at : at + deep]]
    whole = jnp.concatenate(pieces, axis=0)
    for i in range(out.shape[0]):
        out[i] = whole


def centred_kernel(own, kern, mean_ref, got, hb, aff, partial, *hh):
    z, core = lax.axis_index(Z), lax.axis_index(CORE)
    n = got.shape[0]
    total = mean_ref.shape[0] * LANES * n
    which = core if own else 1 - core
    grand = got[0, 1:2, :]
    for i in range(1, n):
        grand = grand + got[i, 1:2, :]
    grand = grand / total
    lane = lax.broadcasted_iota(jnp.int32, (1, LANES), 1)
    odd = lax.rem(z, 2) == 1
    places = []
    for i in range(0, n, 2):
        pair = []
        for j in range(2):
            line = got[i + j, 0:1, :]
            swapped = pltpu.roll(line, LANES // 2, 1)
            pair.append(jnp.where(odd if j == 0 else jnp.logical_not(odd), swapped, line))
        places.append(jnp.where(lane < LANES // 2, pair[0], pair[1]))
    lines = mean_ref.shape[0] // 2
    rows = aff.shape[0]
    for i in range(lines):
        line = mean_ref[pl.ds(which * lines + i, 1), :]
        mine = jnp.broadcast_to(line, (LANES, LANES)).T
        at = pl.ds(pl.multiple_of(which * rows + i * LANES, LANES), LANES)
        for g, place in enumerate(places):
            values = kern[at, g * LANES : (g + 1) * LANES]
            values = values - mine - place + grand
            aff[i * LANES : (i + 1) * LANES, g * LANES : (g + 1) * LANES] = values.astype(BF16)
    partial[...] = jnp.dot(aff[...], hb[...], preferred_element_type=F32)
    if hh:
        deep = (got.shape[1] - 8) // 2
        for i in range(n):
            hh[0][i * deep : (i + 1) * deep, :LANES] = got[i, 8 : 8 + deep, :]
            hh[0][i * deep : (i + 1) * deep, LANES:] = got[i, 8 + deep :, :]


def shards(points, factor):
    nz, ncore, ny, nx = (lax.axis_size(a) for a in ROW_COL)
    nrow, ncol = nz * ncore, ny * nx
    pts, rank = factor.shape
    total = pts * nrow * ncol
    unit = 2.0 / math.sqrt(total * rank)
    h = factor * unit
    hb = h.astype(BF16)
    width = points.shape[1]
    half = pts // 2
    shape = jax.ShapeDtypeStruct

    both = jnp.concatenate([points, hb], axis=1)
    first, second = both[:half], both[half:]
    by_x = [from_ahead(first, X, s) for s in (1, 3, 2)]
    by_y = [from_ahead(second, Y, s) for s in (1, 3, 2)]
    z1, z7 = from_ahead(points, Z, 1), from_ahead(points, Z, -1)
    by_x, by_y, z1, z7 = lax.optimization_barrier((by_x, by_y, z1, z7))
    by_x = jnp.stack([first, by_x[0], by_x[2], by_x[1]])
    by_y = jnp.stack([second, by_y[0], by_y[2], by_y[1]])
    z23 = from_ahead(jnp.stack([points, z1]), Z, 2)
    z65 = from_ahead(jnp.stack([points, z7]), Z, -2)
    z4 = from_ahead(z23[1], Z, 1)
    cols = [by_x] + [from_ahead(by_x, Y, s) for s in (1, 2, 3)]
    cols += [by_y] + [from_ahead(by_y, X, s) for s in (1, 2, 3)]
    along_z = [points, z1, z23, z4, z65, z7]
    other = [from_ahead(v, CORE, 1) for v in along_z]

    part = rank // ncol
    group = nrow * pts
    col_pts, hb_cols, col_sq, own_part = call(
        columns_kernel,
        [
            shape((group, width), BF16),
            shape((group, rank), BF16),
            shape((group // LANES, LANES), F32),
            shape((part, rank), F32),
        ],
        cols,
        2 * group * rank * rank,
        [pltpu.VMEM((rank, rank), F32)],
    )
    own_part = own_part + from_ahead(own_part, CORE, 1)
    kern, row_sum = call(
        rows_kernel,
        [shape((group, group), F32), shape((group // LANES, LANES), F32)],
        [*along_z, *other, col_pts, col_sq],
        2 * group * group * width,
        [pltpu.VMEM((group, width), BF16)],
    )
    core_part = lax.dynamic_slice_in_dim(own_part, lax.axis_index(CORE) * (part // 2), part // 2, 0)
    message = jnp.concatenate([row_sum, core_part[:, :LANES], core_part[:, LANES:]])
    mean_rows, message = call(
        means_kernel,
        [shape(row_sum.shape, F32), shape((ncol, 8 + 2 * part, LANES), F32)],
        [sent_to_all(message, ROW)],
        1,
    )
    gathered = lax.all_to_all(message, COL, 0, 0, tiled=True)

    def centred(own):
        outs = [shape((group // 2, group), BF16), shape((group // 2, rank), F32)]
        if own:
            outs.append(shape((rank, rank), F32))
        return call(
            functools.partial(centred_kernel, own),
            outs,
            [kern, mean_rows, gathered, hb_cols],
            group * group * rank,
        )

    aff_other, partial_other = centred(False)
    got = from_ahead(partial_other, CORE, 1)
    aff_own, partial_own, hh = centred(True)

    def over_z(mine):
        return jnp.sum(lax.all_to_all(mine, Z, 0, 0, tiled=True), axis=0)

    def stepped(h, ah, hh):
        scale = 0.5 / jnp.sqrt(jnp.sum(hh * hh) + 1e-06)
        return jnp.maximum(h - scale * (jnp.dot(h, hh, precision=lax.Precision.HIGHEST) - ah), 0.0)

    ah = over_z((partial_own + got).reshape(nz, pts, rank))
    h = stepped(h, ah, hh)

    hb_cols = sent_to_all(h.astype(BF16), COL).reshape(group, rank)
    gram = lax.dot_general(hb_cols, hb_cols, (((0,), (0,)), ((), ())), preferred_element_type=F32)
    own_part = lax.dynamic_slice_in_dim(gram, lax.axis_index(COL) * part, part, 0)
    partial_other = jnp.dot(aff_other, hb_cols, preferred_element_type=F32)
    got = from_ahead(jnp.concatenate([partial_other, own_part]), CORE, 1)
    partial_own = jnp.dot(aff_own, hb_cols, preferred_element_type=F32)
    mine = (partial_own + got[: group // 2]).reshape(nz, pts, rank)
    extra = jnp.broadcast_to(own_part + got[group // 2 :], (nz, part, rank))
    own = over_z(jnp.concatenate([mine, extra], axis=1))
    hh = sent_to_all(own[pts:], COL).reshape(rank, rank)
    return stepped(h, own[:pts], hh) / unit


def solution(mesh):
    split = Mesh(mesh.devices.reshape(8, 2, 4, 4), ROW_COL)
    return jax.shard_map(
        shards,
        mesh=split,
        in_specs=(P(ROW_COL, None), P(ROW_COL, None)),
        out_specs=P(ROW_COL, None),
        check_vma=False,
    )
```

time: 194 us -> 179 us (0.923)
  blocking collectives: 33.8 us -> 66.4 us
  waiting for transfers between devices: 75.3 us -> 47.6 us
  starting transfers between devices: 53.2 us -> 43.8 us
  Pallas kernels: 0 us -> 7.42 us
  matrix products: 9.48 us -> 2.36 us
  other arithmetic: 13 us -> 6.58 us
  local copies, waits for them, and re-layouts: 5.56 us -> 2.87 us
    all_to_all x1 -> x2, blocking collectives: 10.6 us -> 27.7 us  [sent_to_all(): return lax.all_to_all(copies, axes, split_axis=0, concat_axis=0, tiled=True)]
    all_to_all x1 -> x2, blocking collectives: 23.2 us -> 38.7 us  [the longest x1 23.2 us: over_z(): return jnp.sum(lax.all_to_all(mine, Z, 0, 0, tiled=True), axis=0)]
    all_to_all x2 -> x1, waiting for transfers between devices: 24.9 us -> 10.8 us  [sent_to_all(): return lax.all_to_all(copies, axes, split_axis=0, concat_axis=0, tiled=True)]
    ppermute x26, waiting for transfers between devices: 34 us -> 20.2 us  [from_ahead(): lax.ppermute(value, axis, [((i + steps) % length, i) for i in range(lengt...]
    all_to_all x2 -> x1, starting transfers between devices: 11.3 us -> 3.57 us  [sent_to_all(): return lax.all_to_all(copies, axes, split_axis=0, concat_axis=0, tiled=True)]
    pallas_call x0 -> x5, Pallas kernels: none -> 7.42 us  [call(): pl.pallas_call(kernel, out_shape=outs, in_specs=[VMEM] * len(args), out_s...]
    dot_general x7 -> x5, matrix products: 9.48 us -> 2.36 us  [the longest x2 1.14 us: stepped(): jnp.dot(h, hh, precision=lax.Precision.HIGHEST) - ah]
    convert_element_type x2 -> x1, other arithmetic: 3.95 us -> 0.88 us  [shards(): hb = h.astype(BF16)]
  transfers between devices with their start and end apart: 29 -> 28, of which waited for: 18 -> 12; matrix products, arithmetic and copies ran while one was open for 2% -> 2% of each run, Pallas kernels for 0% -> 1%
where the time goes in v1:
time: 179 us
  blocking collectives  66.4 us (37%)
  waiting for transfers between devices  47.6 us (27%)
  starting transfers between devices  43.8 us (24%)
  Pallas kernels  7.42 us (4%)
  other arithmetic  6.58 us (4%)
  local copies, waits for them, and re-layouts  2.87 us (2%)
  matrix products  2.36 us (1%)
    ppermute x26, starting transfers between devices, from_ahead(): lax.ppermute(value, axis, [((i + steps) % length, i) for i in range(lengt...  36.7 us
    all_to_all x2, blocking collectives, sent_to_all(): return lax.all_to_all(copies, axes, split_axis=0, concat_axis=0, tiled=True)  27.7 us
    all_to_all x1, blocking collectives, over_z(): return jnp.sum(lax.all_to_all(mine, Z, 0, 0, tiled=True), axis=0)  23.2 us
    ppermute x26, waiting for transfers between devices, from_ahead(): lax.ppermute(value, axis, [((i + steps) % length, i) for i in range(lengt...  20.2 us
    all_to_all x1, waiting for transfers between devices, over_z(): return jnp.sum(lax.all_to_all(mine, Z, 0, 0, tiled=True), axis=0)  16.6 us
    all_to_all x1, blocking collectives, shards(): gathered = lax.all_to_all(message, COL, 0, 0, tiled=True)  15.6 us
    all_to_all x1, waiting for transfers between devices, sent_to_all(): return lax.all_to_all(copies, axes, split_axis=0, concat_axis=0, tiled=True)  10.8 us
    pallas_call x5, Pallas kernels, call(): pl.pallas_call(kernel, out_shape=outs, in_specs=[VMEM] * len(args), out_s...  7.42 us
  transfers between devices with their start and end apart: 28, of which 12 were waited for; matrix products, arithmetic and copies ran while one was open for 2% of the time, Pallas kernels for 1%

profile of v1, /device:TPU:1, one launch (start us, length us, event | category | flops | bytes accessed | tf_op | source)
XLA Modules:
  0.0 178.6 jit_solution(14627479790426059720)
XLA Ops:
  0.0 0.9 multiply_convert_fusion
  0.9 0.9 pad_maximum_fusion.6
  1.8 3.8 %collective-permute-start.5 = (bf16[32,1280]{1,0:T(8,128)(2,1)S(1)}, bf16[32,1280]{1,0:T(8,128)(2,1)S(1)}, u32[]{:S(2)}, u32[]{:S(2)}) collective-permute-start(bf16[32,1280]{1,0:T(8,128)(2,1)S(1)} %get-tuple-element.47), channel_id=1, source_target_pairs={{8,0},{12,4},{0,8},{4,12},{9,1},{13,5},{1,9},{5,13},{10,2},{14,6},... | collective-permute-start | bytes 245768 | tf_op jit(solution)/shard_map/ppermute | solution.py:21
  6.0 2.3 %collective-permute-start.3 = (bf16[32,1280]{1,0:T(8,128)(2,1)S(1)}, bf16[32,1280]{1,0:T(8,128)(2,1)S(1)}, u32[]{:S(2)}, u32[]{:S(2)}) collective-permute-start(bf16[32,1280]{1,0:T(8,128)(2,1)S(1)} %get-tuple-element.47), channel_id=1, source_target_pairs={{4,0},{8,4},{12,8},{0,12},{5,1},{9,5},{13,9},{1,13},{6,2},{10,6},{... | collective-permute-start | bytes 245768 | tf_op jit(solution)/shard_map/ppermute | solution.py:21
  8.3 1.6 collective-permute-start.7
  9.9 3.9 %collective-permute-start.6 = (bf16[64,1024]{1,0:T(8,128)(2,1)}, bf16[64,1024]{1,0:T(8,128)(2,1)S(1)}, u32[]{:S(2)}, u32[]{:S(2)}) collective-permute-start(bf16[64,1024]{1,0:T(8,128)(2,1)} %p0.1), channel_id=1, source_target_pairs={{32,0},{64,32},{96,64},{128,96},{160,128},{192,160},{224,192},{0,2... | collective-permute-start | bytes 393224 | tf_op jit(solution)/shard_map/ppermute | solution.py:21
  13.9 2.7 %collective-permute-start.2 = (bf16[32,1280]{1,0:T(8,128)(2,1)S(1)}, bf16[32,1280]{1,0:T(8,128)(2,1)S(1)}, u32[]{:S(2)}, u32[]{:S(2)}) collective-permute-start(bf16[32,1280]{1,0:T(8,128)(2,1)S(1)} %get-tuple-element.48), channel_id=1, source_target_pairs={{2,0},{3,1},{0,2},{1,3},{6,4},{7,5},{4,6},{5,7},{10,8},{11,9},{8,1... | collective-permute-start | bytes 245768 | tf_op jit(solution)/shard_map/ppermute | solution.py:21
  16.9 2.4 %collective-permute-start = (bf16[32,1280]{1,0:T(8,128)(2,1)S(1)}, bf16[32,1280]{1,0:T(8,128)(2,1)S(1)}, u32[]{:S(2)}, u32[]{:S(2)}) collective-permute-start(bf16[32,1280]{1,0:T(8,128)(2,1)S(1)} %get-tuple-element.48), channel_id=1, source_target_pairs={{1,0},{2,1},{3,2},{0,3},{5,4},{6,5},{7,6},{4,7},{9,8},{10,9},{11,1... | collective-permute-start | bytes 245768 | tf_op jit(solution)/shard_map/ppermute | solution.py:21
  19.3 2.6 %collective-permute-done.1 = bf16[32,1280]{1,0:T(8,128)(2,1)S(1)} collective-permute-done((bf16[32,1280]{1,0:T(8,128)(2,1)S(1)}, bf16[32,1280]{1,0:T(8,128)(2,1)S(1)}, u32[]{:S(2)}, u32[]{:S(2)}) %collective-permute-start.1) | collective-permute-done | bytes 81952 | tf_op jit(solution)/shard_map/ppermute | solution.py:21
  22.0 1.6 pad_maximum_fusion.4
  23.7 2.0 %collective-permute-start.8 = (bf16[2,64,1024]{2,1,0:T(8,128)(2,1)S(1)}, bf16[2,64,1024]{2,1,0:T(8,128)(2,1)S(1)}, u32[]{:S(2)}, u32[]{:S(2)}) collective-permute-start(bf16[2,64,1024]{2,1,0:T(8,128)(2,1)S(1)} %get-tuple-element.50), channel_id=1, source_target_pairs={{64,0},{96,32},{128,64},{160,96},{192,128},{224,160},{0,192},{32,2... | collective-permute-start | bytes 786440 | tf_op jit(solution)/shard_map/ppermute | solution.py:21
  25.7 3.7 %collective-permute-start.21 = (bf16[4,32,1280]{2,1,0:T(8,128)(2,1)S(1)}, bf16[4,32,1280]{2,1,0:T(8,128)(2,1)S(1)}, u32[]{:S(2)}, u32[]{:S(2)}) collective-permute-start(bf16[4,32,1280]{2,1,0:T(8,128)(2,1)S(1)} %pad_maximum_fusion.3.by_y), channel_id=1, source_target_pairs={{2,0},{3,1},{0,2},{1,3},{6,4},{7,5},{4,6},{5,7},{10,8},{11,9},{8,1... | collective-permute-start | bytes 983048 | tf_op jit(solution)/shard_map/ppermute | solution.py:21
  29.6 7.2 %collective-permute-done.8.p23 = bf16[2,64,1024]{2,1,0:T(8,128)(2,1)S(1)} collective-permute-done((bf16[2,64,1024]{2,1,0:T(8,128)(2,1)S(1)}, bf16[2,64,1024]{2,1,0:T(8,128)(2,1)S(1)}, u32[]{:S(2)}, u32[]{:S(2)}) %collective-permute-start.8) | collective-permute-done | bytes 262176 | tf_op jit(solution)/shard_map/ppermute | solution.py:21
  36.7 1.6 collective-permute-start.17
  38.3 2.9 %collective-permute-start.10 = (bf16[2,64,1024]{2,1,0:T(8,128)(2,1)}, bf16[2,64,1024]{2,1,0:T(8,128)(2,1)S(1)}, u32[]{:S(2)}, u32[]{:S(2)}) collective-permute-start(bf16[2,64,1024]{2,1,0:T(8,128)(2,1)} %get-tuple-element.49), channel_id=1, source_target_pairs={{192,0},{224,32},{0,64},{32,96},{64,128},{96,160},{128,192},{160,2... | collective-permute-start | bytes 786440 | tf_op jit(solution)/shard_map/ppermute | solution.py:21
  42.4 2.3 %collective-permute-start.11 = (bf16[64,1024]{1,0:T(8,128)(2,1)}, bf16[64,1024]{1,0:T(8,128)(2,1)}, u32[]{:S(2)}, u32[]{:S(2)}) collective-permute-start(bf16[64,1024]{1,0:T(8,128)(2,1)} %p0.1), channel_id=1, source_target_pairs={{16,0},{0,16},{17,1},{1,17},{18,2},{2,18},{19,3},{3,19},{20,4},{4,... | collective-permute-start | bytes 393224 | tf_op jit(solution)/shard_map/ppermute | solution.py:21
  46.0 5.4 %collective-permute-done.17.y1 = bf16[4,32,1280]{2,1,0:T(8,128)(2,1)S(1)} collective-permute-done((bf16[4,32,1280]{2,1,0:T(8,128)(2,1)S(1)}, bf16[4,32,1280]{2,1,0:T(8,128)(2,1)S(1)}, u32[]{:S(2)}, u32[]{:S(2)}) %collective-permute-start.17) | collective-permute-done | bytes 327712 | tf_op jit(solution)/shard_map/ppermute | solution.py:21
  52.7 1.6 collective-permute-start.23
  58.7 4.9 %shard_map.29 = (f32[1024,1024]{1,0:T(8,128)S(1)}, f32[8,128]{1,0:T(8,128)S(1)}) custom-call(bf16[64,1024]{1,0:T(8,128)(2,1)S(1)} %copy-done, bf16[64,1024]{1,0:T(8,128)(2,1)S(1)} %collective-permute-done.6.p1, bf16[2,64,1024]{2,1,0:T(8,128)(2,1)S(1)} %collective-permute-done.8.p23, bf16[64,1024]{1,0:T(8,128)(2,1)} %collective-permute-done.9.p4, ...), custom_call_target="tpu_custom_call" | custom-call | flops 2147483648 | bytes 8396800 | tf_op jit(solution)/shard_map/pallas_call | solution.py:37
  63.6 17.0 %all_to_all.30.got = f32[16,24,128]{2,1,0:T(8,128)S(1)} all-to-all(f32[16,24,128]{2,1,0:T(8,128)S(1)} %broadcast_in_dim.12), channel_id=1, replica_groups=mesh['row_0'=8,'row_1'=2,'col_0'=4,'col_1'=4] {'row_0','row_1'}, dimensions={0} | all-to-all | bytes 393216 | tf_op jit(solution)/shard_map/all_to_all | solution.py:27
  80.8 15.6 %all_to_all.31.got = f32[16,40,128]{2,1,0:T(8,128)S(1)} all-to-all(f32[16,40,128]{2,1,0:T(8,128)S(1)} %get-tuple-element.40), channel_id=1, replica_groups=mesh['row_0'=8,'row_1'=2,'col_0'=4,'col_1'=4] {'col_0','col_1'}, dimensions={0} | all-to-all | bytes 655360 | tf_op jit(solution)/shard_map/all_to_all | solution.py:242
  97.2 1.2 collective-permute-start.24
  99.9 0.9 add.30
  100.8 3.5 %all-to-all-start.2 = ((f32[8,64,256]{2,1,0:T(8,128)}), f32[8,64,256]{2,1,0:T(8,128)S(1)}, u32[]{:S(2)}, u32[]{:S(2)}) async-start(f32[8,64,256]{2,1,0:T(8,128)} %bitcast.12), calls=%async_computation.2 | async-start | bytes 1048576 | tf_op jit(solution)/shard_map/all_to_all | solution.py:260
  105.6 16.6 %all-to-all-done.2 = f32[8,64,256]{2,1,0:T(8,128)S(1)} async-done(((f32[8,64,256]{2,1,0:T(8,128)}), f32[8,64,256]{2,1,0:T(8,128)S(1)}, u32[]{:S(2)}, u32[]{:S(2)}) %all-to-all-start.2) | async-done | bytes 524320 | tf_op jit(solution)/shard_map/all_to_all | solution.py:260
  123.4 3.6 %all-to-all-start.3 = ((bf16[16,64,256]{2,1,0:T(8,128)(2,1)}), bf16[16,64,256]{2,1,0:T(8,128)(2,1)S(1)}, u32[]{:S(2)}, u32[]{:S(2)}) async-start(bf16[16,64,256]{2,1,0:T(8,128)(2,1)} %broadcast_in_dim.13), calls=%async_computation.3 | async-start | bytes 1048576 | tf_op jit(solution)/shard_map/all_to_all | solution.py:27
  127.0 10.8 %all-to-all-done.3 = bf16[16,64,256]{2,1,0:T(8,128)(2,1)S(1)} async-done(((bf16[16,64,256]{2,1,0:T(8,128)(2,1)}), bf16[16,64,256]{2,1,0:T(8,128)(2,1)S(1)}, u32[]{:S(2)}, u32[]{:S(2)}) %all-to-all-start.3) | async-done | bytes 524320 | tf_op jit(solution)/shard_map/all_to_all | solution.py:27
  138.6 1.7 collective-permute-start.25
  140.3 1.6 collective-permute-done.25
  142.4 23.2 %all_to_all.32 = f32[8,80,256]{2,1,0:T(8,128)S(1)} all-to-all(f32[8,80,256]{2,1,0:T(8,128)S(1)} %pad_maximum_fusion), channel_id=1, replica_groups=mesh['row_0'=8,'row_1'=2,'col_0'=4,'col_1'=4] {'row_0'}, dimensions={0} | all-to-all | bytes 1310720 | tf_op jit(solution)/shard_map/all_to_all | solution.py:260
  165.7 10.7 %all_to_all.33 = f32[16,16,256]{2,1,0:T(8,128)S(1)} all-to-all(f32[16,16,256]{2,1,0:T(8,128)S(1)} %broadcast_in_dim.15), channel_id=1, replica_groups=mesh['row_0'=8,'row_1'=2,'col_0'=4,'col_1'=4] {'col_0','col_1'}, dimensions={0} | all-to-all | bytes 524288 | tf_op jit(solution)/shard_map/all_to_all | solution.py:27
  177.7 0.9 fusion.3
  (69 shorter events, 15.7 us)
Async XLA Ops:
  0.0 58.0 %copy-start = (bf16[64,1024]{1,0:T(8,128)(2,1)S(1)}, bf16[64,1024]{1,0:T(8,128)(2,1)}, u32[]{:S(2)}) copy-start(bf16[64,1024]{1,0:T(8,128)(2,1)} %p0.1) | copy-start | bytes 393220
  1.8 12.1 %collective-permute-start.5 = (bf16[32,1280]{1,0:T(8,128)(2,1)S(1)}, bf16[32,1280]{1,0:T(8,128)(2,1)S(1)}, u32[]{:S(2)}, u32[]{:S(2)}) collective-permute-start(bf16[32,1280]{1,0:T(8,128)(2,1)S(1)} %get-tuple-element.47), channel_id=1, source_target_pairs={{8,0},{12,4},{0,8},{4,12},{9,1},{13,5},{1,9},{5,13},{10,2},{14,6},... | collective-permute-start | bytes 245768 | tf_op jit(solution)/shard_map/ppermute | solution.py:21
  5.6 11.0 %collective-permute-start.4 = (bf16[32,1280]{1,0:T(8,128)(2,1)S(1)}, bf16[32,1280]{1,0:T(8,128)(2,1)S(1)}, u32[]{:S(2)}, u32[]{:S(2)}) collective-permute-start(bf16[32,1280]{1,0:T(8,128)(2,1)S(1)} %get-tuple-element.47), channel_id=1, source_target_pairs={{12,0},{0,4},{4,8},{8,12},{13,1},{1,5},{5,9},{9,13},{14,2},{2,6},{... | collective-permute-start | bytes 245768 | tf_op jit(solution)/shard_map/ppermute | solution.py:21
  6.0 10.9 %collective-permute-start.3 = (bf16[32,1280]{1,0:T(8,128)(2,1)S(1)}, bf16[32,1280]{1,0:T(8,128)(2,1)S(1)}, u32[]{:S(2)}, u32[]{:S(2)}) collective-permute-start(bf16[32,1280]{1,0:T(8,128)(2,1)S(1)} %get-tuple-element.47), channel_id=1, source_target_pairs={{4,0},{8,4},{12,8},{0,12},{5,1},{9,5},{13,9},{1,13},{6,2},{10,6},{... | collective-permute-start | bytes 245768 | tf_op jit(solution)/shard_map/ppermute | solution.py:21
  8.3 13.6 %collective-permute-start.7 = (bf16[64,1024]{1,0:T(8,128)(2,1)}, bf16[64,1024]{1,0:T(8,128)(2,1)S(1)}, u32[]{:S(2)}, u32[]{:S(2)}) collective-permute-start(bf16[64,1024]{1,0:T(8,128)(2,1)} %p0.1), channel_id=1, source_target_pairs={{224,0},{0,32},{32,64},{64,96},{96,128},{128,160},{160,192},{192,2... | collective-permute-start | bytes 393224 | tf_op jit(solution)/shard_map/ppermute | solution.py:21
  9.9 11.9 %collective-permute-start.6 = (bf16[64,1024]{1,0:T(8,128)(2,1)}, bf16[64,1024]{1,0:T(8,128)(2,1)S(1)}, u32[]{:S(2)}, u32[]{:S(2)}) collective-permute-start(bf16[64,1024]{1,0:T(8,128)(2,1)} %p0.1), channel_id=1, source_target_pairs={{32,0},{64,32},{96,64},{128,96},{160,128},{192,160},{224,192},{0,2... | collective-permute-start | bytes 393224 | tf_op jit(solution)/shard_map/ppermute | solution.py:21
  13.9 5.4 %collective-permute-start.2 = (bf16[32,1280]{1,0:T(8,128)(2,1)S(1)}, bf16[32,1280]{1,0:T(8,128)(2,1)S(1)}, u32[]{:S(2)}, u32[]{:S(2)}) collective-permute-start(bf16[32,1280]{1,0:T(8,128)(2,1)S(1)} %get-tuple-element.48), channel_id=1, source_target_pairs={{2,0},{3,1},{0,2},{1,3},{6,4},{7,5},{4,6},{5,7},{10,8},{11,9},{8,1... | collective-permute-start | bytes 245768 | tf_op jit(solution)/shard_map/ppermute | solution.py:21
  16.6 5.2 %collective-permute-start.1 = (bf16[32,1280]{1,0:T(8,128)(2,1)S(1)}, bf16[32,1280]{1,0:T(8,128)(2,1)S(1)}, u32[]{:S(2)}, u32[]{:S(2)}) collective-permute-start(bf16[32,1280]{1,0:T(8,128)(2,1)S(1)} %get-tuple-element.48), channel_id=1, source_target_pairs={{3,0},{0,1},{1,2},{2,3},{7,4},{4,5},{5,6},{6,7},{11,8},{8,9},{9,10... | collective-permute-start | bytes 245768 | tf_op jit(solution)/shard_map/ppermute | solution.py:21
  16.9 4.9 %collective-permute-start = (bf16[32,1280]{1,0:T(8,128)(2,1)S(1)}, bf16[32,1280]{1,0:T(8,128)(2,1)S(1)}, u32[]{:S(2)}, u32[]{:S(2)}) collective-permute-start(bf16[32,1280]{1,0:T(8,128)(2,1)S(1)} %get-tuple-element.48), channel_id=1, source_target_pairs={{1,0},{2,1},{3,2},{0,3},{5,4},{6,5},{7,6},{4,7},{9,8},{10,9},{11,1... | collective-permute-start | bytes 245768 | tf_op jit(solution)/shard_map/ppermute | solution.py:21
  21.9 14.8 %collective-permute-start.22 = (bf16[4,32,1280]{2,1,0:T(8,128)(2,1)S(1)}, bf16[4,32,1280]{2,1,0:T(8,128)(2,1)S(1)}, u32[]{:S(2)}, u32[]{:S(2)}) collective-permute-start(bf16[4,32,1280]{2,1,0:T(8,128)(2,1)S(1)} %pad_maximum_fusion.3.by_y), channel_id=1, source_target_pairs={{3,0},{0,1},{1,2},{2,3},{7,4},{4,5},{5,6},{6,7},{11,8},{8,9},{9,10... | collective-permute-start | bytes 983048 | tf_op jit(solution)/shard_map/ppermute | solution.py:21
  23.7 13.1 %collective-permute-start.8 = (bf16[2,64,1024]{2,1,0:T(8,128)(2,1)S(1)}, bf16[2,64,1024]{2,1,0:T(8,128)(2,1)S(1)}, u32[]{:S(2)}, u32[]{:S(2)}) collective-permute-start(bf16[2,64,1024]{2,1,0:T(8,128)(2,1)S(1)} %get-tuple-element.50), channel_id=1, source_target_pairs={{64,0},{96,32},{128,64},{160,96},{192,128},{224,160},{0,192},{32,2... | collective-permute-start | bytes 786440 | tf_op jit(solution)/shard_map/ppermute | solution.py:21
  25.7 12.6 %collective-permute-start.21 = (bf16[4,32,1280]{2,1,0:T(8,128)(2,1)S(1)}, bf16[4,32,1280]{2,1,0:T(8,128)(2,1)S(1)}, u32[]{:S(2)}, u32[]{:S(2)}) collective-permute-start(bf16[4,32,1280]{2,1,0:T(8,128)(2,1)S(1)} %pad_maximum_fusion.3.by_y), channel_id=1, source_target_pairs={{2,0},{3,1},{0,2},{1,3},{6,4},{7,5},{4,6},{5,7},{10,8},{11,9},{8,1... | collective-permute-start | bytes 983048 | tf_op jit(solution)/shard_map/ppermute | solution.py:21
  29.4 13.0 %collective-permute-start.20 = (bf16[4,32,1280]{2,1,0:T(8,128)(2,1)S(1)}, bf16[4,32,1280]{2,1,0:T(8,128)(2,1)S(1)}, u32[]{:S(2)}, u32[]{:S(2)}) collective-permute-start(bf16[4,32,1280]{2,1,0:T(8,128)(2,1)S(1)} %pad_maximum_fusion.3.by_y), channel_id=1, source_target_pairs={{1,0},{2,1},{3,2},{0,3},{5,4},{6,5},{7,6},{4,7},{9,8},{10,9},{11,1... | collective-permute-start | bytes 983048 | tf_op jit(solution)/shard_map/ppermute | solution.py:21
  29.5 15.2 %collective-permute-start.19 = (bf16[4,32,1280]{2,1,0:T(8,128)(2,1)S(1)}, bf16[4,32,1280]{2,1,0:T(8,128)(2,1)S(1)}, u32[]{:S(2)}, u32[]{:S(2)}) collective-permute-start(bf16[4,32,1280]{2,1,0:T(8,128)(2,1)S(1)} %pad_maximum_fusion.2.by_x), channel_id=1, source_target_pairs={{12,0},{0,4},{4,8},{8,12},{13,1},{1,5},{5,9},{9,13},{14,2},{2,6},{... | collective-permute-start | bytes 983048 | tf_op jit(solution)/shard_map/ppermute | solution.py:21
  36.7 9.3 %collective-permute-start.18 = (bf16[4,32,1280]{2,1,0:T(8,128)(2,1)S(1)}, bf16[4,32,1280]{2,1,0:T(8,128)(2,1)S(1)}, u32[]{:S(2)}, u32[]{:S(2)}) collective-permute-start(bf16[4,32,1280]{2,1,0:T(8,128)(2,1)S(1)} %pad_maximum_fusion.2.by_x), channel_id=1, source_target_pairs={{8,0},{12,4},{0,8},{4,12},{9,1},{13,5},{1,9},{5,13},{10,2},{14,6},... | collective-permute-start | bytes 983048 | tf_op jit(solution)/shard_map/ppermute | solution.py:21
  36.7 14.6 %collective-permute-start.17 = (bf16[4,32,1280]{2,1,0:T(8,128)(2,1)S(1)}, bf16[4,32,1280]{2,1,0:T(8,128)(2,1)S(1)}, u32[]{:S(2)}, u32[]{:S(2)}) collective-permute-start(bf16[4,32,1280]{2,1,0:T(8,128)(2,1)S(1)} %pad_maximum_fusion.2.by_x), channel_id=1, source_target_pairs={{4,0},{8,4},{12,8},{0,12},{5,1},{9,5},{13,9},{1,13},{6,2},{10,6},{... | collective-permute-start | bytes 983048 | tf_op jit(solution)/shard_map/ppermute | solution.py:21
  38.3 15.9 %collective-permute-start.10 = (bf16[2,64,1024]{2,1,0:T(8,128)(2,1)}, bf16[2,64,1024]{2,1,0:T(8,128)(2,1)S(1)}, u32[]{:S(2)}, u32[]{:S(2)}) collective-permute-start(bf16[2,64,1024]{2,1,0:T(8,128)(2,1)} %get-tuple-element.49), channel_id=1, source_target_pairs={{192,0},{224,32},{0,64},{32,96},{64,128},{96,160},{128,192},{160,2... | collective-permute-start | bytes 786440 | tf_op jit(solution)/shard_map/ppermute | solution.py:21
  42.4 13.9 %collective-permute-start.11 = (bf16[64,1024]{1,0:T(8,128)(2,1)}, bf16[64,1024]{1,0:T(8,128)(2,1)}, u32[]{:S(2)}, u32[]{:S(2)}) collective-permute-start(bf16[64,1024]{1,0:T(8,128)(2,1)} %p0.1), channel_id=1, source_target_pairs={{16,0},{0,16},{17,1},{1,17},{18,2},{2,18},{19,3},{3,19},{20,4},{4,... | collective-permute-start | bytes 393224 | tf_op jit(solution)/shard_map/ppermute | solution.py:21
  44.7 11.8 %collective-permute-start.9 = (bf16[64,1024]{1,0:T(8,128)(2,1)}, bf16[64,1024]{1,0:T(8,128)(2,1)}, u32[]{:S(2)}, u32[]{:S(2)}) collective-permute-start(bf16[64,1024]{1,0:T(8,128)(2,1)} %slice_bitcast_fusion), channel_id=1, source_target_pairs={{32,0},{64,32},{96,64},{128,96},{160,128},{192,160},{224,192},{0,2... | collective-permute-start | bytes 393224 | tf_op jit(solution)/shard_map/ppermute | solution.py:21
  52.1 0.6 copy-start.1
  52.7 2.5 %collective-permute-start.23 = (f32[16,256]{1,0:T(8,128)S(1)}, f32[16,256]{1,0:T(8,128)}, u32[]{:S(2)}, u32[]{:S(2)}) collective-permute-start(f32[16,256]{1,0:T(8,128)S(1)} %get-tuple-element.38), channel_id=1, source_target_pairs={{16,0},{0,16},{17,1},{1,17},{18,2},{2,18},{19,3},{3,19},{20,4},{4,... | collective-permute-start | bytes 49160 | tf_op jit(solution)/shard_map/ppermute | solution.py:21
  54.3 2.5 %collective-permute-start.12 = (bf16[64,1024]{1,0:T(8,128)(2,1)S(1)}, bf16[64,1024]{1,0:T(8,128)(2,1)S(1)}, u32[]{:S(2)}, u32[]{:S(2)}) collective-permute-start(bf16[64,1024]{1,0:T(8,128)(2,1)S(1)} %collective-permute-done.6.p1), channel_id=1, source_target_pairs={{16,0},{0,16},{17,1},{1,17},{18,2},{2,18},{19,3},{3,19},{20,4},{4,... | collective-permute-start | bytes 393224 | tf_op jit(solution)/shard_map/ppermute | solution.py:21
  54.3 3.8 %collective-permute-start.13 = (bf16[2,64,1024]{2,1,0:T(8,128)(2,1)S(1)}, bf16[2,64,1024]{2,1,0:T(8,128)(2,1)S(1)}, u32[]{:S(2)}, u32[]{:S(2)}) collective-permute-start(bf16[2,64,1024]{2,1,0:T(8,128)(2,1)S(1)} %collective-permute-done.8.p23), channel_id=1, source_target_pairs={{16,0},{0,16},{17,1},{1,17},{18,2},{2,18},{19,3},{3,19},{20,4},{4,... | collective-permute-start | bytes 786440 | tf_op jit(solution)/shard_map/ppermute | solution.py:21
  55.2 2.4 %collective-permute-start.15 = (bf16[2,64,1024]{2,1,0:T(8,128)(2,1)S(1)}, bf16[2,64,1024]{2,1,0:T(8,128)(2,1)S(1)}, u32[]{:S(2)}, u32[]{:S(2)}) collective-permute-start(bf16[2,64,1024]{2,1,0:T(8,128)(2,1)S(1)} %collective-permute-done.10.p65), channel_id=1, source_target_pairs={{16,0},{0,16},{17,1},{1,17},{18,2},{2,18},{19,3},{3,19},{20,4},{4,... | collective-permute-start | bytes 786440 | tf_op jit(solution)/shard_map/ppermute | solution.py:21
  56.3 1.3 collective-permute-start.16
  56.4 1.6 collective-permute-start.14
  58.0 0.7 copy-start.2
  97.2 25.1 %copy-start.3 = (f32[64,256]{1,0:T(8,128)S(1)}, f32[64,256]{1,0:T(8,128)}, u32[]{:S(2)}) copy-start(f32[64,256]{1,0:T(8,128)} %param.3) | copy-start | bytes 196612
  97.2 2.7 %collective-permute-start.24 = (f32[512,256]{1,0:T(8,128)S(1)}, f32[512,256]{1,0:T(8,128)S(1)}, u32[]{:S(2)}, u32[]{:S(2)}) collective-permute-start(f32[512,256]{1,0:T(8,128)S(1)} %get-tuple-element.44), channel_id=1, source_target_pairs={{16,0},{0,16},{17,1},{1,17},{18,2},{2,18},{19,3},{3,19},{20,4},{4,... | collective-permute-start | bytes 1572872 | tf_op jit(solution)/shard_map/ppermute | solution.py:21
  100.8 21.4 %all-to-all-start.2 = ((f32[8,64,256]{2,1,0:T(8,128)}), f32[8,64,256]{2,1,0:T(8,128)S(1)}, u32[]{:S(2)}, u32[]{:S(2)}) async-start(f32[8,64,256]{2,1,0:T(8,128)} %bitcast.12), calls=%async_computation.2 | async-start | bytes 1048576 | tf_op jit(solution)/shard_map/all_to_all | solution.py:260
  123.4 14.4 %all-to-all-start.3 = ((bf16[16,64,256]{2,1,0:T(8,128)(2,1)}), bf16[16,64,256]{2,1,0:T(8,128)(2,1)S(1)}, u32[]{:S(2)}, u32[]{:S(2)}) async-start(bf16[16,64,256]{2,1,0:T(8,128)(2,1)} %broadcast_in_dim.13), calls=%async_computation.3 | async-start | bytes 1048576 | tf_op jit(solution)/shard_map/all_to_all | solution.py:27
  138.6 3.3 %collective-permute-start.25 = (f32[528,256]{1,0:T(8,128)S(1)}, f32[528,256]{1,0:T(8,128)S(1)}, u32[]{:S(2)}, u32[]{:S(2)}) collective-permute-start(f32[528,256]{1,0:T(8,128)S(1)} %pad_maximum_fusion.1), channel_id=1, source_target_pairs={{16,0},{0,16},{17,1},{1,17},{18,2},{2,18},{19,3},{3,19},{20,4},{4,... | collective-permute-start | bytes 1622024 | tf_op jit(solution)/shard_map/ppermute | solution.py:21

commit v2 on v1

--- a/solution.py
+++ b/solution.py
@@ -84,7 +84,7 @@
 
 
 def rows_kernel(
-    p0, p1, p23, p4, p65, p7, o0, o1, o23, o4, o65, o7, cols, sq, kern, sums, held
+    p0, p1, p23, p4, p65, p7, o0, o1, o23, o4, o65, o7, cols, sq, part, more, kern, out, held, sums
 ):
     z, core = lax.axis_index(Z), lax.axis_index(CORE)
     nz, pts = lax.axis_size(Z), p0.shape[0]
@@ -119,6 +119,14 @@
         return 0
 
     lax.fori_loop(0, held.shape[0] // tall, block, 0)
+    lines = sums.shape[0]
+    deep = part.shape[0] // 2
+    at = pl.ds(pl.multiple_of(core * deep, deep), deep)
+    mine = part[at, :] + more[at, :]
+    for i in range(out.shape[0]):
+        out[i, :lines] = sums[...]
+        out[i, lines : lines + deep] = mine[:, :LANES]
+        out[i, lines + deep :] = mine[:, LANES:]
 
 
 def means_kernel(got, mean_ref, out):
@@ -181,33 +189,70 @@
             hh[0][i * deep : (i + 1) * deep, LANES:] = got[i, 8 + deep :, :]
 
 
+def start_kernel(unit, points, factor, first, second):
+    half, width = first.shape[0], points.shape[1]
+    hb = (factor[...] * unit).astype(BF16)
+    first[:, :width] = points[:half, :]
+    first[:, width:] = hb[:half]
+    second[:, :width] = points[half:, :]
+    second[:, width:] = hb[half:]
+
+
+def step_kernel(before, after, got, hh_ref, h_ref, out, *copies):
+    ah = got[0]
+    for i in range(1, got.shape[0]):
+        ah = ah + got[i]
+    hh = hh_ref[...]
+    h = h_ref[...] * before if before else h_ref[...]
+    square = jnp.sum(jnp.sum(hh * hh, axis=0, keepdims=True), axis=1, keepdims=True)
+    scale = 0.5 / jnp.sqrt(square + 1e-06)
+    product = jnp.dot(h, hh, precision=lax.Precision.HIGHEST, preferred_element_type=F32)
+    h = jnp.maximum(h - scale * (product - ah), 0.0)
+    out[...] = h / after if after else h
+    if copies:
+        hb = h.astype(BF16)
+        for i in range(copies[0].shape[0]):
+            copies[0][i] = hb
+
+
 def shards(points, factor):
     nz, ncore, ny, nx = (lax.axis_size(a) for a in ROW_COL)
     nrow, ncol = nz * ncore, ny * nx
     pts, rank = factor.shape
     total = pts * nrow * ncol
     unit = 2.0 / math.sqrt(total * rank)
-    h = factor * unit
-    hb = h.astype(BF16)
     width = points.shape[1]
     half = pts // 2
     shape = jax.ShapeDtypeStruct
 
-    both = jnp.concatenate([points, hb], axis=1)
-    first, second = both[:half], both[half:]
-    by_x = [from_ahead(first, X, s) for s in (1, 3, 2)]
-    by_y = [from_ahead(second, Y, s) for s in (1, 3, 2)]
+    first, second = call(
+        functools.partial(start_kernel, unit),
+        [shape((half, width + rank), BF16)] * 2,
+        [points, factor],
+        1,
+    )
+    tie = lax.optimization_barrier
     z1, z7 = from_ahead(points, Z, 1), from_ahead(points, Z, -1)
-    by_x, by_y, z1, z7 = lax.optimization_barrier((by_x, by_y, z1, z7))
-    by_x = jnp.stack([first, by_x[0], by_x[2], by_x[1]])
-    by_y = jnp.stack([second, by_y[0], by_y[2], by_y[1]])
+    x1, x3 = from_ahead(first, X, 1), from_ahead(first, X, -1)
+    y1, y3 = from_ahead(second, Y, 1), from_ahead(second, Y, -1)
+    z1, z7, first, second = tie((z1, z7, first, second))
     z23 = from_ahead(jnp.stack([points, z1]), Z, 2)
     z65 = from_ahead(jnp.stack([points, z7]), Z, -2)
+    x2, y2 = from_ahead(first, X, 2), from_ahead(second, Y, 2)
+    x1, x2, x3, y1, y2, y3 = tie((x1, x2, x3, y1, y2, y3))
+    by_x = jnp.stack([first, x1, x2, x3])
+    by_y = jnp.stack([second, y1, y2, y3])
+    from_y = [from_ahead(by_x, Y, s) for s in (1, 2, 3)]
+    from_x = [from_ahead(by_y, X, s) for s in (1, 2, 3)]
+    from_y[0], z23, z65, z1, z7 = tie((from_y[0], z23, z65, z1, z7))
     z4 = from_ahead(z23[1], Z, 1)
-    cols = [by_x] + [from_ahead(by_x, Y, s) for s in (1, 2, 3)]
-    cols += [by_y] + [from_ahead(by_y, X, s) for s in (1, 2, 3)]
+    other_0, other_1, other_7 = (from_ahead(v, CORE, 1) for v in (points, z1, z7))
     along_z = [points, z1, z23, z4, z65, z7]
-    other = [from_ahead(v, CORE, 1) for v in along_z]
+    cols = [by_x, *from_y, by_y, *from_x]
+    other_23, other_65 = from_ahead(z23, CORE, 1), from_ahead(z65, CORE, 1)
+    other = [other_0, other_1, other_23, other_65, other_7]
+    cols, other = tie((cols, other))
+    other.insert(3, from_ahead(z4, CORE, 1))
 
     part = rank // ncol
     group = nrow * pts
@@ -223,20 +268,19 @@
         2 * group * rank * rank,
         [pltpu.VMEM((rank, rank), F32)],
     )
-    own_part = own_part + from_ahead(own_part, CORE, 1)
-    kern, row_sum = call(
+    more_part = from_ahead(own_part, CORE, 1)
+    lines = group // LANES
+    kern, message = call(
         rows_kernel,
-        [shape((group, group), F32), shape((group // LANES, LANES), F32)],
-        [*along_z, *other, col_pts, col_sq],
+        [shape((group, group), F32), shape((nrow, lines + part, LANES), F32)],
+        [*along_z, *other, col_pts, col_sq, own_part, more_part],
         2 * group * group * width,
-        [pltpu.VMEM((group, width), BF16)],
-    )
-    core_part = lax.dynamic_slice_in_dim(own_part, lax.axis_index(CORE) * (part // 2), part // 2, 0)
-    message = jnp.concatenate([row_sum, core_part[:, :LANES], core_part[:, LANES:]])
+        [pltpu.VMEM((group, width), BF16), pltpu.VMEM((lines, LANES), F32)],
+    )
     mean_rows, message = call(
         means_kernel,
-        [shape(row_sum.shape, F32), shape((ncol, 8 + 2 * part, LANES), F32)],
-        [sent_to_all(message, ROW)],
+        [shape((lines, LANES), F32), shape((ncol, 8 + 2 * part, LANES), F32)],
+        [lax.all_to_all(message, ROW, 0, 0, tiled=True)],
         1,
     )
     gathered = lax.all_to_all(message, COL, 0, 0, tiled=True)
@@ -257,26 +301,29 @@
     aff_own, partial_own, hh = centred(True)
 
     def over_z(mine):
-        return jnp.sum(lax.all_to_all(mine, Z, 0, 0, tiled=True), axis=0)
-
-    def stepped(h, ah, hh):
-        scale = 0.5 / jnp.sqrt(jnp.sum(hh * hh) + 1e-06)
-        return jnp.maximum(h - scale * (jnp.dot(h, hh, precision=lax.Precision.HIGHEST) - ah), 0.0)
-
-    ah = over_z((partial_own + got).reshape(nz, pts, rank))
-    h = stepped(h, ah, hh)
-
-    hb_cols = sent_to_all(h.astype(BF16), COL).reshape(group, rank)
+        return lax.all_to_all(mine.reshape(nz, pts, rank), Z, 0, 0, tiled=True)
+
+    def stepped(before, after, ah, hh, h, copies):
+        outs = [shape((pts, rank), F32)] + [shape((ncol, pts, rank), BF16)] * copies
+        flops = 12 * pts * rank * rank
+        return call(functools.partial(step_kernel, before, after), outs, [ah, hh, h], flops)
+
+    ah = over_z(partial_own + got)
+    h, hb_cols = stepped(unit, None, ah, hh, factor, 1)
+
+    hb_cols = lax.all_to_all(hb_cols, COL, 0, 0, tiled=True).reshape(group, rank)
+    partial_other = jnp.dot(aff_other, hb_cols, preferred_element_type=F32)
+    got = from_ahead(partial_other, CORE, 1)
     gram = lax.dot_general(hb_cols, hb_cols, (((0,), (0,)), ((), ())), preferred_element_type=F32)
     own_part = lax.dynamic_slice_in_dim(gram, lax.axis_index(COL) * part, part, 0)
-    partial_other = jnp.dot(aff_other, hb_cols, preferred_element_type=F32)
-    got = from_ahead(jnp.concatenate([partial_other, own_part]), CORE, 1)
+    own_part = own_part + from_ahead(own_part, CORE, 1)
     partial_own = jnp.dot(aff_own, hb_cols, preferred_element_type=F32)
-    mine = (partial_own + got[: group // 2]).reshape(nz, pts, rank)
-    extra = jnp.broadcast_to(own_part + got[group // 2 :], (nz, part, rank))
-    own = over_z(jnp.concatenate([mine, extra], axis=1))
-    hh = sent_to_all(own[pts:], COL).reshape(rank, rank)
-    return stepped(h, own[:pts], hh) / unit
+    ah = over_z(partial_own + got)
+    for bit in (1, 2, 4):
+        own_part = own_part + lax.ppermute(own_part, Z, [(i, i ^ bit) for i in range(nz)])
+    ah, own_part = tie((ah, own_part))
+    hh = sent_to_all(own_part, COL).reshape(rank, rank)
+    return stepped(None, unit, ah, hh, h, 0)[0]
 
 
 def solution(mesh):

time: 179 us -> 172 us (0.961); the launches traced: 179 us -> 169 us
  waiting for transfers between devices: 47.6 us -> 28.4 us
  starting transfers between devices: 43.8 us -> 55.3 us
  blocking collectives: 66.4 us -> 73.5 us
  other arithmetic: 6.58 us -> 0.21 us
    all_to_all x1 -> x3, blocking collectives: 23.2 us -> 50.6 us  [the longest x1 20.4 us: over_z(): return lax.all_to_all(mine.reshape(nz, pts, rank), Z, 0, 0, tiled=True)]
    all_to_all x2 -> x1, waiting for transfers between devices: 27.4 us -> 0.01 us  [over_z(): return lax.all_to_all(mine.reshape(nz, pts, rank), Z, 0, 0, tiled=True)]
    all_to_all x2 -> x1, blocking collectives: 27.7 us -> 10.2 us  [sent_to_all(): return lax.all_to_all(copies, axes, split_axis=0, concat_axis=0, tiled=True)]
    ppermute x0 -> x3, waiting for transfers between devices: none -> 14.7 us  [shards(): lax.ppermute(own_part, Z, [(i, i ^ bit) for i in range(nz)])]
    ppermute x26 -> x27, starting transfers between devices: 36.7 us -> 44.8 us  [from_ahead(): lax.ppermute(value, axis, [((i + steps) % length, i) for i in range(lengt...]
    ppermute x0 -> x3, starting transfers between devices: none -> 7.05 us  [shards(): lax.ppermute(own_part, Z, [(i, i ^ bit) for i in range(nz)])]
    ppermute x26 -> x27, waiting for transfers between devices: 20.2 us -> 13.7 us  [from_ahead(): lax.ppermute(value, axis, [((i + steps) % length, i) for i in range(lengt...]
    all_to_all x2 -> x1, starting transfers between devices: 7.06 us -> 3.49 us  [over_z(): return lax.all_to_all(mine.reshape(nz, pts, rank), Z, 0, 0, tiled=True)]
  transfers between devices with their start and end apart: 28 -> 31, of which waited for: 12 -> 11; matrix products, arithmetic and copies ran while one was open for 2% -> 0% of each run, Pallas kernels for 1% -> 1%
where the time goes in v2:
time: 172 us; the launch traced here: 169 us
  blocking collectives  73.5 us (43%)
  starting transfers between devices  55.3 us (32%)
  waiting for transfers between devices  28.4 us (17%)
  Pallas kernels  7.71 us (4%)
  matrix products  2 us (1%)
  local copies, waits for them, and re-layouts  1.86 us (1%)
    ppermute x27, starting transfers between devices, from_ahead(): lax.ppermute(value, axis, [((i + steps) % length, i) for i in range(lengt...  44.8 us
    all_to_all x1, blocking collectives, over_z(): return lax.all_to_all(mine.reshape(nz, pts, rank), Z, 0, 0, tiled=True)  20.4 us
    all_to_all x1, blocking collectives, shards(): lax.all_to_all(message, ROW, 0, 0, tiled=True)  16.9 us
    ppermute x3, waiting for transfers between devices, shards(): lax.ppermute(own_part, Z, [(i, i ^ bit) for i in range(nz)])  14.7 us
    ppermute x27, waiting for transfers between devices, from_ahead(): lax.ppermute(value, axis, [((i + steps) % length, i) for i in range(lengt...  13.7 us
    all_to_all x1, blocking collectives, shards(): lax.all_to_all(hb_cols, COL, 0, 0, tiled=True).reshape(group, rank)  13.3 us
    all_to_all x1, blocking collectives, shards(): gathered = lax.all_to_all(message, COL, 0, 0, tiled=True)  12.7 us
    all_to_all x1, blocking collectives, sent_to_all(): return lax.all_to_all(copies, axes, split_axis=0, concat_axis=0, tiled=True)  10.2 us
  transfers between devices with their start and end apart: 31, of which 11 were waited for; matrix products, arithmetic and copies ran while one was open for 0% of the time, Pallas kernels for 1%

profile of v2, /device:TPU:1, one launch (start us, length us, event | category | flops | bytes accessed | tf_op | source)
XLA Modules:
  0.0 169.2 jit_solution(6097342159948447129)
XLA Ops:
  0.0 6.4 %collective-permute-start = (bf16[64,1024]{1,0:T(8,128)(2,1)}, bf16[64,1024]{1,0:T(8,128)(2,1)S(1)}, u32[]{:S(2)}, u32[]{:S(2)}) collective-permute-start(bf16[64,1024]{1,0:T(8,128)(2,1)} %p0.1), channel_id=1, source_target_pairs={{32,0},{64,32},{96,64},{128,96},{160,128},{192,160},{224,192},{0,2... | collective-permute-start | bytes 393224 | tf_op jit(solution)/shard_map/ppermute | solution.py:21
  8.2 2.6 %collective-permute-start.2 = (bf16[32,1280]{1,0:T(8,128)(2,1)S(1)}, bf16[32,1280]{1,0:T(8,128)(2,1)S(1)}, u32[]{:S(2)}, u32[]{:S(2)}) collective-permute-start(bf16[32,1280]{1,0:T(8,128)(2,1)S(1)} %get-tuple-element.54), channel_id=1, source_target_pairs={{1,0},{2,1},{3,2},{0,3},{5,4},{6,5},{7,6},{4,7},{9,8},{10,9},{11,1... | collective-permute-start | bytes 245768 | tf_op jit(solution)/shard_map/ppermute | solution.py:21
  10.8 2.7 %collective-permute-start.5 = (bf16[32,1280]{1,0:T(8,128)(2,1)S(1)}, bf16[32,1280]{1,0:T(8,128)(2,1)S(1)}, u32[]{:S(2)}, u32[]{:S(2)}) collective-permute-start(bf16[32,1280]{1,0:T(8,128)(2,1)S(1)} %get-tuple-element.55), channel_id=1, source_target_pairs={{4,0},{8,4},{12,8},{0,12},{5,1},{9,5},{13,9},{1,13},{6,2},{10,6},{... | collective-permute-start | bytes 245768 | tf_op jit(solution)/shard_map/ppermute | solution.py:21
  13.5 1.8 %collective-permute-start.3 = (bf16[32,1280]{1,0:T(8,128)(2,1)S(1)}, bf16[32,1280]{1,0:T(8,128)(2,1)S(1)}, u32[]{:S(2)}, u32[]{:S(2)}) collective-permute-start(bf16[32,1280]{1,0:T(8,128)(2,1)S(1)} %get-tuple-element.54), channel_id=1, source_target_pairs={{2,0},{3,1},{0,2},{1,3},{6,4},{7,5},{4,6},{5,7},{10,8},{11,9},{8,1... | collective-permute-start | bytes 245768 | tf_op jit(solution)/shard_map/ppermute | solution.py:21
  15.4 1.9 %collective-permute-start.6 = (bf16[32,1280]{1,0:T(8,128)(2,1)S(1)}, bf16[32,1280]{1,0:T(8,128)(2,1)S(1)}, u32[]{:S(2)}, u32[]{:S(2)}) collective-permute-start(bf16[32,1280]{1,0:T(8,128)(2,1)S(1)} %get-tuple-element.55), channel_id=1, source_target_pairs={{8,0},{12,4},{0,8},{4,12},{9,1},{13,5},{1,9},{5,13},{10,2},{14,6},... | collective-permute-start | bytes 245768 | tf_op jit(solution)/shard_map/ppermute | solution.py:21
  17.5 3.6 %collective-permute-start.9 = (bf16[2,64,1024]{2,1,0:T(8,128)(2,1)S(1)}, bf16[2,64,1024]{2,1,0:T(8,128)(2,1)S(1)}, u32[]{:S(2)}, u32[]{:S(2)}) collective-permute-start(bf16[2,64,1024]{2,1,0:T(8,128)(2,1)S(1)} %get-tuple-element.100), channel_id=1, source_target_pairs={{64,0},{96,32},{128,64},{160,96},{192,128},{224,160},{0,192},{32,2... | collective-permute-start | bytes 786440 | tf_op jit(solution)/shard_map/ppermute | solution.py:21
  21.1 2.1 %collective-permute-start.8 = (bf16[4,32,1280]{2,1,0:T(8,128)(2,1)S(1)}, bf16[4,32,1280]{2,1,0:T(8,128)(2,1)S(1)}, u32[]{:S(2)}, u32[]{:S(2)}) collective-permute-start(bf16[4,32,1280]{2,1,0:T(8,128)(2,1)S(1)} %pad_maximum_fusion.by_x), channel_id=1, source_target_pairs={{4,0},{8,4},{12,8},{0,12},{5,1},{9,5},{13,9},{1,13},{6,2},{10,6},{... | collective-permute-start | bytes 983048 | tf_op jit(solution)/shard_map/ppermute | solution.py:21
  24.0 2.3 %collective-permute-start.15 = (bf16[4,32,1280]{2,1,0:T(8,128)(2,1)S(1)}, bf16[4,32,1280]{2,1,0:T(8,128)(2,1)S(1)}, u32[]{:S(2)}, u32[]{:S(2)}) collective-permute-start(bf16[4,32,1280]{2,1,0:T(8,128)(2,1)S(1)} %pad_maximum_fusion.1.by_y), channel_id=1, source_target_pairs={{2,0},{3,1},{0,2},{1,3},{6,4},{7,5},{4,6},{5,7},{10,8},{11,9},{8,1... | collective-permute-start | bytes 983048 | tf_op jit(solution)/shard_map/ppermute | solution.py:21
  26.3 4.8 %collective-permute-start.17 = (bf16[64,1024]{1,0:T(8,128)(2,1)}, bf16[64,1024]{1,0:T(8,128)(2,1)S(1)}, u32[]{:S(2)}, u32[]{:S(2)}) collective-permute-start(bf16[64,1024]{1,0:T(8,128)(2,1)} %p0.1), channel_id=1, source_target_pairs={{16,0},{0,16},{17,1},{1,17},{18,2},{2,18},{19,3},{3,19},{20,4},{4,... | collective-permute-start | bytes 393224 | tf_op jit(solution)/shard_map/ppermute | solution.py:21
  31.3 1.6 collective-permute-start.16
  32.9 1.7 %collective-permute-start.12 = (bf16[4,32,1280]{2,1,0:T(8,128)(2,1)S(1)}, bf16[4,32,1280]{2,1,0:T(8,128)(2,1)S(1)}, u32[]{:S(2)}, u32[]{:S(2)}) collective-permute-start(bf16[4,32,1280]{2,1,0:T(8,128)(2,1)S(1)} %pad_maximum_fusion.by_x), channel_id=1, source_target_pairs={{8,0},{12,4},{0,8},{4,12},{9,1},{13,5},{1,9},{5,13},{10,2},{14,6},... | collective-permute-start | bytes 983048 | tf_op jit(solution)/shard_map/ppermute | solution.py:21
  34.7 2.3 %collective-permute-start.19 = (bf16[2,64,1024]{2,1,0:T(8,128)(2,1)S(1)}, bf16[2,64,1024]{2,1,0:T(8,128)(2,1)S(1)}, u32[]{:S(2)}, u32[]{:S(2)}) collective-permute-start(bf16[2,64,1024]{2,1,0:T(8,128)(2,1)S(1)} %collective-permute-done.9.p23), channel_id=1, source_target_pairs={{16,0},{0,16},{17,1},{1,17},{18,2},{2,18},{19,3},{3,19},{20,4},{4,... | collective-permute-start | bytes 786440 | tf_op jit(solution)/shard_map/ppermute | solution.py:21
  37.2 4.6 %collective-permute-done.16.x3 = bf16[4,32,1280]{2,1,0:T(8,128)(2,1)S(1)} collective-permute-done((bf16[4,32,1280]{2,1,0:T(8,128)(2,1)S(1)}, bf16[4,32,1280]{2,1,0:T(8,128)(2,1)S(1)}, u32[]{:S(2)}, u32[]{:S(2)}) %collective-permute-start.16) | collective-permute-done | bytes 327712 | tf_op jit(solution)/shard_map/ppermute | solution.py:21
  41.8 3.8 %collective-permute-start.11 = (bf16[64,1024]{1,0:T(8,128)(2,1)S(1)}, bf16[64,1024]{1,0:T(8,128)(2,1)S(1)}, u32[]{:S(2)}, u32[]{:S(2)}) collective-permute-start(bf16[64,1024]{1,0:T(8,128)(2,1)S(1)} %slice_bitcast_fusion), channel_id=1, source_target_pairs={{32,0},{64,32},{96,64},{128,96},{160,128},{192,160},{224,192},{0,2... | collective-permute-start | bytes 393224 | tf_op jit(solution)/shard_map/ppermute | solution.py:21
  45.5 1.5 collective-permute-start.18
  47.1 4.0 %collective-permute-done.13.y3 = bf16[4,32,1280]{2,1,0:T(8,128)(2,1)S(1)} collective-permute-done((bf16[4,32,1280]{2,1,0:T(8,128)(2,1)S(1)}, bf16[4,32,1280]{2,1,0:T(8,128)(2,1)S(1)}, u32[]{:S(2)}, u32[]{:S(2)}) %collective-permute-start.13) | collective-permute-done | bytes 327712 | tf_op jit(solution)/shard_map/ppermute | solution.py:21
  54.5 4.0 %shard_map.30 = (f32[1024,1024]{1,0:T(8,128)S(1)}, f32[16,24,128]{2,1,0:T(8,128)S(1)}) custom-call(bf16[64,1024]{1,0:T(8,128)(2,1)S(1)} %copy-done.1, bf16[64,1024]{1,0:T(8,128)(2,1)S(1)} %collective-permute-done.p1, bf16[2,64,1024]{2,1,0:T(8,128)(2,1)S(1)} %collective-permute-done.9.p23, bf16[64,1024]{1,0:T(8,128)(2,1)S(1)} %collective-permute-done.11.p4, ...), custom_call_target="tpu_custom_call" | custom-call | flops 2147483648 | bytes 8622080 | tf_op jit(solution)/shard_map/pallas_call | solution.py:37
  58.5 16.9 %all_to_all.30.got = f32[16,24,128]{2,1,0:T(8,128)S(1)} all-to-all(f32[16,24,128]{2,1,0:T(8,128)S(1)} %get-tuple-element.86), channel_id=1, replica_groups=mesh['row_0'=8,'row_1'=2,'col_0'=4,'col_1'=4] {'row_0','row_1'}, dimensions={0} | all-to-all | bytes 393216 | tf_op jit(solution)/shard_map/all_to_all | solution.py:283
  75.6 12.7 %all_to_all.31.got = f32[16,40,128]{2,1,0:T(8,128)S(1)} all-to-all(f32[16,40,128]{2,1,0:T(8,128)S(1)} %get-tuple-element.88), channel_id=1, replica_groups=mesh['row_0'=8,'row_1'=2,'col_0'=4,'col_1'=4] {'col_0','col_1'}, dimensions={0} | all-to-all | bytes 655360 | tf_op jit(solution)/shard_map/all_to_all | solution.py:286
  89.2 1.2 collective-permute-start.24
  91.9 20.4 %all_to_all.32.got = f32[8,64,256]{2,1,0:T(8,128)S(1)} all-to-all(f32[8,64,256]{2,1,0:T(8,128)S(1)} %bitcast.33), channel_id=1, replica_groups=mesh['row_0'=8,'row_1'=2,'col_0'=4,'col_1'=4] {'row_0'}, dimensions={0} | all-to-all | bytes 1048576 | tf_op jit(solution)/shard_map/all_to_all | solution.py:304
  112.6 13.3 %all_to_all.33 = bf16[16,64,256]{2,1,0:T(8,128)(2,1)S(1)} all-to-all(bf16[16,64,256]{2,1,0:T(8,128)(2,1)S(1)} %get-tuple-element.94), channel_id=1, replica_groups=mesh['row_0'=8,'row_1'=2,'col_0'=4,'col_1'=4] {'col_0','col_1'}, dimensions={0} | all-to-all | bytes 1048576 | tf_op jit(solution)/shard_map/all_to_all | solution.py:314
  126.3 2.0 %collective-permute-start.25 = (f32[512,256]{1,0:T(8,128)S(1)}, f32[512,256]{1,0:T(8,128)S(1)}, u32[]{:S(2)}, u32[]{:S(2)}) collective-permute-start(f32[512,256]{1,0:T(8,128)S(1)} %fusion), channel_id=1, source_target_pairs={{16,0},{0,16},{17,1},{1,17},{18,2},{2,18},{19,3},{3,19},{20,4},{4,... | collective-permute-start | bytes 1572872 | tf_op jit(solution)/shard_map/ppermute | solution.py:21
  128.3 1.5 collective-permute-done.25
  129.9 1.2 convolution_add_fusion
  131.1 3.5 %all-to-all-start.4 = ((f32[8,64,256]{2,1,0:T(8,128)}), f32[8,64,256]{2,1,0:T(8,128)S(1)}, u32[]{:S(2)}, u32[]{:S(2)}) async-start(f32[8,64,256]{2,1,0:T(8,128)} %bitcast.14), calls=%async_computation.4 | async-start | bytes 1048576 | tf_op jit(solution)/shard_map/all_to_all | solution.py:304
  136.3 1.6 collective-permute-start.27
  137.9 9.9 %collective-permute-done.27 = f32[16,256]{1,0:T(8,128)S(1)} collective-permute-done((f32[16,256]{1,0:T(8,128)S(1)}, f32[16,256]{1,0:T(8,128)S(1)}, u32[]{:S(2)}, u32[]{:S(2)}) %collective-permute-start.27) | collective-permute-done | bytes 16416 | tf_op jit(solution)/shard_map/ppermute | solution.py:323
  148.8 2.7 %collective-permute-done.28 = f32[16,256]{1,0:T(8,128)S(1)} collective-permute-done((f32[16,256]{1,0:T(8,128)S(1)}, f32[16,256]{1,0:T(8,128)S(1)}, u32[]{:S(2)}, u32[]{:S(2)}) %collective-permute-start.28) | collective-permute-done | bytes 16416 | tf_op jit(solution)/shard_map/ppermute | solution.py:323
  151.6 4.3 %collective-permute-start.29 = (f32[16,256]{1,0:T(8,128)S(1)}, f32[16,256]{1,0:T(8,128)S(1)}, u32[]{:S(2)}, u32[]{:S(2)}) collective-permute-start(f32[16,256]{1,0:T(8,128)S(1)} %add.30), channel_id=1, source_target_pairs={{0,128},{32,160},{64,192},{96,224},{128,0},{160,32},{192,64},{224,... | collective-permute-start | bytes 49160 | tf_op jit(solution)/shard_map/ppermute | solution.py:323
  155.9 2.2 %collective-permute-done.29 = f32[16,256]{1,0:T(8,128)S(1)} collective-permute-done((f32[16,256]{1,0:T(8,128)S(1)}, f32[16,256]{1,0:T(8,128)S(1)}, u32[]{:S(2)}, u32[]{:S(2)}) %collective-permute-start.29) | collective-permute-done | bytes 16416 | tf_op jit(solution)/shard_map/ppermute | solution.py:323
  158.1 10.2 %all_to_all.34 = f32[16,16,256]{2,1,0:T(8,128)S(1)} all-to-all(f32[16,16,256]{2,1,0:T(8,128)S(1)} %broadcast_in_dim.3), channel_id=1, replica_groups=mesh['row_0'=8,'row_1'=2,'col_0'=4,'col_1'=4] {'col_0','col_1'}, dimensions={0} | all-to-all | bytes 524288 | tf_op jit(solution)/shard_map/all_to_all | solution.py:27
  (65 shorter events, 13.9 us)
Async XLA Ops:
  0.0 13.5 %collective-permute-start = (bf16[64,1024]{1,0:T(8,128)(2,1)}, bf16[64,1024]{1,0:T(8,128)(2,1)S(1)}, u32[]{:S(2)}, u32[]{:S(2)}) collective-permute-start(bf16[64,1024]{1,0:T(8,128)(2,1)} %p0.1), channel_id=1, source_target_pairs={{32,0},{64,32},{96,64},{128,96},{160,128},{192,160},{224,192},{0,2... | collective-permute-start | bytes 393224 | tf_op jit(solution)/shard_map/ppermute | solution.py:21
  6.4 7.1 %collective-permute-start.1 = (bf16[64,1024]{1,0:T(8,128)(2,1)}, bf16[64,1024]{1,0:T(8,128)(2,1)S(1)}, u32[]{:S(2)}, u32[]{:S(2)}) collective-permute-start(bf16[64,1024]{1,0:T(8,128)(2,1)} %p0.1), channel_id=1, source_target_pairs={{224,0},{0,32},{32,64},{64,96},{96,128},{128,160},{160,192},{192,2... | collective-permute-start | bytes 393224 | tf_op jit(solution)/shard_map/ppermute | solution.py:21
  8.2 46.3 %copy-start.1 = (bf16[64,1024]{1,0:T(8,128)(2,1)S(1)}, bf16[64,1024]{1,0:T(8,128)(2,1)}, u32[]{:S(2)}) copy-start(bf16[64,1024]{1,0:T(8,128)(2,1)} %p0.1) | copy-start | bytes 393220
  8.2 7.1 %collective-permute-start.2 = (bf16[32,1280]{1,0:T(8,128)(2,1)S(1)}, bf16[32,1280]{1,0:T(8,128)(2,1)S(1)}, u32[]{:S(2)}, u32[]{:S(2)}) collective-permute-start(bf16[32,1280]{1,0:T(8,128)(2,1)S(1)} %get-tuple-element.54), channel_id=1, source_target_pairs={{1,0},{2,1},{3,2},{0,3},{5,4},{6,5},{7,6},{4,7},{9,8},{10,9},{11,1... | collective-permute-start | bytes 245768 | tf_op jit(solution)/shard_map/ppermute | solution.py:21
  10.8 6.6 %collective-permute-start.4 = (bf16[32,1280]{1,0:T(8,128)(2,1)S(1)}, bf16[32,1280]{1,0:T(8,128)(2,1)S(1)}, u32[]{:S(2)}, u32[]{:S(2)}) collective-permute-start(bf16[32,1280]{1,0:T(8,128)(2,1)S(1)} %get-tuple-element.54), channel_id=1, source_target_pairs={{3,0},{0,1},{1,2},{2,3},{7,4},{4,5},{5,6},{6,7},{11,8},{8,9},{9,10... | collective-permute-start | bytes 245768 | tf_op jit(solution)/shard_map/ppermute | solution.py:21
  10.8 6.7 %collective-permute-start.5 = (bf16[32,1280]{1,0:T(8,128)(2,1)S(1)}, bf16[32,1280]{1,0:T(8,128)(2,1)S(1)}, u32[]{:S(2)}, u32[]{:S(2)}) collective-permute-start(bf16[32,1280]{1,0:T(8,128)(2,1)S(1)} %get-tuple-element.55), channel_id=1, source_target_pairs={{4,0},{8,4},{12,8},{0,12},{5,1},{9,5},{13,9},{1,13},{6,2},{10,6},{... | collective-permute-start | bytes 245768 | tf_op jit(solution)/shard_map/ppermute | solution.py:21
  13.5 7.5 %collective-permute-start.7 = (bf16[32,1280]{1,0:T(8,128)(2,1)S(1)}, bf16[32,1280]{1,0:T(8,128)(2,1)S(1)}, u32[]{:S(2)}, u32[]{:S(2)}) collective-permute-start(bf16[32,1280]{1,0:T(8,128)(2,1)S(1)} %get-tuple-element.55), channel_id=1, source_target_pairs={{12,0},{0,4},{4,8},{8,12},{13,1},{1,5},{5,9},{9,13},{14,2},{2,6},{... | collective-permute-start | bytes 245768 | tf_op jit(solution)/shard_map/ppermute | solution.py:21
  13.5 7.5 %collective-permute-start.3 = (bf16[32,1280]{1,0:T(8,128)(2,1)S(1)}, bf16[32,1280]{1,0:T(8,128)(2,1)S(1)}, u32[]{:S(2)}, u32[]{:S(2)}) collective-permute-start(bf16[32,1280]{1,0:T(8,128)(2,1)S(1)} %get-tuple-element.54), channel_id=1, source_target_pairs={{2,0},{3,1},{0,2},{1,3},{6,4},{7,5},{4,6},{5,7},{10,8},{11,9},{8,1... | collective-permute-start | bytes 245768 | tf_op jit(solution)/shard_map/ppermute | solution.py:21
  15.4 5.7 %collective-permute-start.6 = (bf16[32,1280]{1,0:T(8,128)(2,1)S(1)}, bf16[32,1280]{1,0:T(8,128)(2,1)S(1)}, u32[]{:S(2)}, u32[]{:S(2)}) collective-permute-start(bf16[32,1280]{1,0:T(8,128)(2,1)S(1)} %get-tuple-element.55), channel_id=1, source_target_pairs={{8,0},{12,4},{0,8},{4,12},{9,1},{13,5},{1,9},{5,13},{10,2},{14,6},... | collective-permute-start | bytes 245768 | tf_op jit(solution)/shard_map/ppermute | solution.py:21
  17.4 8.9 %collective-permute-start.10 = (bf16[2,64,1024]{2,1,0:T(8,128)(2,1)S(1)}, bf16[2,64,1024]{2,1,0:T(8,128)(2,1)S(1)}, u32[]{:S(2)}, u32[]{:S(2)}) collective-permute-start(bf16[2,64,1024]{2,1,0:T(8,128)(2,1)S(1)} %get-tuple-element.99), channel_id=1, source_target_pairs={{192,0},{224,32},{0,64},{32,96},{64,128},{96,160},{128,192},{160,2... | collective-permute-start | bytes 786440 | tf_op jit(solution)/shard_map/ppermute | solution.py:21
  17.5 13.8 %collective-permute-start.9 = (bf16[2,64,1024]{2,1,0:T(8,128)(2,1)S(1)}, bf16[2,64,1024]{2,1,0:T(8,128)(2,1)S(1)}, u32[]{:S(2)}, u32[]{:S(2)}) collective-permute-start(bf16[2,64,1024]{2,1,0:T(8,128)(2,1)S(1)} %get-tuple-element.100), channel_id=1, source_target_pairs={{64,0},{96,32},{128,64},{160,96},{192,128},{224,160},{0,192},{32,2... | collective-permute-start | bytes 786440 | tf_op jit(solution)/shard_map/ppermute | solution.py:21
  21.1 11.8 %collective-permute-start.8 = (bf16[4,32,1280]{2,1,0:T(8,128)(2,1)S(1)}, bf16[4,32,1280]{2,1,0:T(8,128)(2,1)S(1)}, u32[]{:S(2)}, u32[]{:S(2)}) collective-permute-start(bf16[4,32,1280]{2,1,0:T(8,128)(2,1)S(1)} %pad_maximum_fusion.by_x), channel_id=1, source_target_pairs={{4,0},{8,4},{12,8},{0,12},{5,1},{9,5},{13,9},{1,13},{6,2},{10,6},{... | collective-permute-start | bytes 983048 | tf_op jit(solution)/shard_map/ppermute | solution.py:21
  23.2 11.5 %collective-permute-start.14 = (bf16[4,32,1280]{2,1,0:T(8,128)(2,1)S(1)}, bf16[4,32,1280]{2,1,0:T(8,128)(2,1)S(1)}, u32[]{:S(2)}, u32[]{:S(2)}) collective-permute-start(bf16[4,32,1280]{2,1,0:T(8,128)(2,1)S(1)} %pad_maximum_fusion.1.by_y), channel_id=1, source_target_pairs={{1,0},{2,1},{3,2},{0,3},{5,4},{6,5},{7,6},{4,7},{9,8},{10,9},{11,1... | collective-permute-start | bytes 983048 | tf_op jit(solution)/shard_map/ppermute | solution.py:21
  24.0 13.0 %collective-permute-start.15 = (bf16[4,32,1280]{2,1,0:T(8,128)(2,1)S(1)}, bf16[4,32,1280]{2,1,0:T(8,128)(2,1)S(1)}, u32[]{:S(2)}, u32[]{:S(2)}) collective-permute-start(bf16[4,32,1280]{2,1,0:T(8,128)(2,1)S(1)} %pad_maximum_fusion.1.by_y), channel_id=1, source_target_pairs={{2,0},{3,1},{0,2},{1,3},{6,4},{7,5},{4,6},{5,7},{10,8},{11,9},{8,1... | collective-permute-start | bytes 983048 | tf_op jit(solution)/shard_map/ppermute | solution.py:21
  26.3 8.2 %collective-permute-start.17 = (bf16[64,1024]{1,0:T(8,128)(2,1)}, bf16[64,1024]{1,0:T(8,128)(2,1)S(1)}, u32[]{:S(2)}, u32[]{:S(2)}) collective-permute-start(bf16[64,1024]{1,0:T(8,128)(2,1)} %p0.1), channel_id=1, source_target_pairs={{16,0},{0,16},{17,1},{1,17},{18,2},{2,18},{19,3},{3,19},{20,4},{4,... | collective-permute-start | bytes 393224 | tf_op jit(solution)/shard_map/ppermute | solution.py:21
  31.3 10.5 %collective-permute-start.16 = (bf16[4,32,1280]{2,1,0:T(8,128)(2,1)S(1)}, bf16[4,32,1280]{2,1,0:T(8,128)(2,1)S(1)}, u32[]{:S(2)}, u32[]{:S(2)}) collective-permute-start(bf16[4,32,1280]{2,1,0:T(8,128)(2,1)S(1)} %pad_maximum_fusion.1.by_y), channel_id=1, source_target_pairs={{3,0},{0,1},{1,2},{2,3},{7,4},{4,5},{5,6},{6,7},{11,8},{8,9},{9,10... | collective-permute-start | bytes 983048 | tf_op jit(solution)/shard_map/ppermute | solution.py:21
  32.9 12.7 %collective-permute-start.12 = (bf16[4,32,1280]{2,1,0:T(8,128)(2,1)S(1)}, bf16[4,32,1280]{2,1,0:T(8,128)(2,1)S(1)}, u32[]{:S(2)}, u32[]{:S(2)}) collective-permute-start(bf16[4,32,1280]{2,1,0:T(8,128)(2,1)S(1)} %pad_maximum_fusion.by_x), channel_id=1, source_target_pairs={{8,0},{12,4},{0,8},{4,12},{9,1},{13,5},{1,9},{5,13},{10,2},{14,6},... | collective-permute-start | bytes 983048 | tf_op jit(solution)/shard_map/ppermute | solution.py:21
  34.6 16.5 %collective-permute-start.13 = (bf16[4,32,1280]{2,1,0:T(8,128)(2,1)S(1)}, bf16[4,32,1280]{2,1,0:T(8,128)(2,1)S(1)}, u32[]{:S(2)}, u32[]{:S(2)}) collective-permute-start(bf16[4,32,1280]{2,1,0:T(8,128)(2,1)S(1)} %pad_maximum_fusion.by_x), channel_id=1, source_target_pairs={{12,0},{0,4},{4,8},{8,12},{13,1},{1,5},{5,9},{9,13},{14,2},{2,6},{... | collective-permute-start | bytes 983048 | tf_op jit(solution)/shard_map/ppermute | solution.py:21
  34.7 17.8 %collective-permute-start.19 = (bf16[2,64,1024]{2,1,0:T(8,128)(2,1)S(1)}, bf16[2,64,1024]{2,1,0:T(8,128)(2,1)S(1)}, u32[]{:S(2)}, u32[]{:S(2)}) collective-permute-start(bf16[2,64,1024]{2,1,0:T(8,128)(2,1)S(1)} %collective-permute-done.9.p23), channel_id=1, source_target_pairs={{16,0},{0,16},{17,1},{1,17},{18,2},{2,18},{19,3},{3,19},{20,4},{4,... | collective-permute-start | bytes 786440 | tf_op jit(solution)/shard_map/ppermute | solution.py:21
  37.0 15.5 %collective-permute-start.20 = (bf16[2,64,1024]{2,1,0:T(8,128)(2,1)S(1)}, bf16[2,64,1024]{2,1,0:T(8,128)(2,1)S(1)}, u32[]{:S(2)}, u32[]{:S(2)}) collective-permute-start(bf16[2,64,1024]{2,1,0:T(8,128)(2,1)S(1)} %collective-permute-done.10.p65), channel_id=1, source_target_pairs={{16,0},{0,16},{17,1},{1,17},{18,2},{2,18},{19,3},{3,19},{20,4},{4,... | collective-permute-start | bytes 786440 | tf_op jit(solution)/shard_map/ppermute | solution.py:21
  41.8 9.8 %collective-permute-start.11 = (bf16[64,1024]{1,0:T(8,128)(2,1)S(1)}, bf16[64,1024]{1,0:T(8,128)(2,1)S(1)}, u32[]{:S(2)}, u32[]{:S(2)}) collective-permute-start(bf16[64,1024]{1,0:T(8,128)(2,1)S(1)} %slice_bitcast_fusion), channel_id=1, source_target_pairs={{32,0},{64,32},{96,64},{128,96},{160,128},{192,160},{224,192},{0,2... | collective-permute-start | bytes 393224 | tf_op jit(solution)/shard_map/ppermute | solution.py:21
  45.5 6.0 %collective-permute-start.18 = (bf16[64,1024]{1,0:T(8,128)(2,1)S(1)}, bf16[64,1024]{1,0:T(8,128)(2,1)S(1)}, u32[]{:S(2)}, u32[]{:S(2)}) collective-permute-start(bf16[64,1024]{1,0:T(8,128)(2,1)S(1)} %collective-permute-done.p1), channel_id=1, source_target_pairs={{16,0},{0,16},{17,1},{1,17},{18,2},{2,18},{19,3},{3,19},{20,4},{4,... | collective-permute-start | bytes 393224 | tf_op jit(solution)/shard_map/ppermute | solution.py:21
  51.0 1.5 collective-permute-start.21
  51.5 2.1 %collective-permute-start.22 = (bf16[64,1024]{1,0:T(8,128)(2,1)S(1)}, bf16[64,1024]{1,0:T(8,128)(2,1)S(1)}, u32[]{:S(2)}, u32[]{:S(2)}) collective-permute-start(bf16[64,1024]{1,0:T(8,128)(2,1)S(1)} %collective-permute-done.11.p4), channel_id=1, source_target_pairs={{16,0},{0,16},{17,1},{1,17},{18,2},{2,18},{19,3},{3,19},{20,4},{4,... | collective-permute-start | bytes 393224 | tf_op jit(solution)/shard_map/ppermute | solution.py:21
  53.2 1.3 collective-permute-start.23
  89.2 2.7 %collective-permute-start.24 = (f32[512,256]{1,0:T(8,128)S(1)}, f32[512,256]{1,0:T(8,128)S(1)}, u32[]{:S(2)}, u32[]{:S(2)}) collective-permute-start(f32[512,256]{1,0:T(8,128)S(1)} %get-tuple-element.92), channel_id=1, source_target_pairs={{16,0},{0,16},{17,1},{1,17},{18,2},{2,18},{19,3},{3,19},{20,4},{4,... | collective-permute-start | bytes 1572872 | tf_op jit(solution)/shard_map/ppermute | solution.py:21
  126.3 3.5 %collective-permute-start.25 = (f32[512,256]{1,0:T(8,128)S(1)}, f32[512,256]{1,0:T(8,128)S(1)}, u32[]{:S(2)}, u32[]{:S(2)}) collective-permute-start(f32[512,256]{1,0:T(8,128)S(1)} %fusion), channel_id=1, source_target_pairs={{16,0},{0,16},{17,1},{1,17},{18,2},{2,18},{19,3},{3,19},{20,4},{4,... | collective-permute-start | bytes 1572872 | tf_op jit(solution)/shard_map/ppermute | solution.py:21
  131.1 27.0 %all-to-all-start.4 = ((f32[8,64,256]{2,1,0:T(8,128)}), f32[8,64,256]{2,1,0:T(8,128)S(1)}, u32[]{:S(2)}, u32[]{:S(2)}) async-start(f32[8,64,256]{2,1,0:T(8,128)} %bitcast.14), calls=%async_computation.4 | async-start | bytes 1048576 | tf_op jit(solution)/shard_map/all_to_all | solution.py:304
  134.9 1.3 collective-permute-start.26
  136.3 11.5 %collective-permute-start.27 = (f32[16,256]{1,0:T(8,128)S(1)}, f32[16,256]{1,0:T(8,128)S(1)}, u32[]{:S(2)}, u32[]{:S(2)}) collective-permute-start(f32[16,256]{1,0:T(8,128)S(1)} %fusion.7), channel_id=1, source_target_pairs={{0,32},{32,0},{64,96},{96,64},{128,160},{160,128},{192,224},{224,1... | collective-permute-start | bytes 49160 | tf_op jit(solution)/shard_map/ppermute | solution.py:323
  147.8 3.8 %collective-permute-start.28 = (f32[16,256]{1,0:T(8,128)S(1)}, f32[16,256]{1,0:T(8,128)S(1)}, u32[]{:S(2)}, u32[]{:S(2)}) collective-permute-start(f32[16,256]{1,0:T(8,128)S(1)} %add.29), channel_id=1, source_target_pairs={{0,64},{32,96},{64,0},{96,32},{128,192},{160,224},{192,128},{224,1... | collective-permute-start | bytes 49160 | tf_op jit(solution)/shard_map/ppermute | solution.py:323
  151.6 6.5 %collective-permute-start.29 = (f32[16,256]{1,0:T(8,128)S(1)}, f32[16,256]{1,0:T(8,128)S(1)}, u32[]{:S(2)}, u32[]{:S(2)}) collective-permute-start(f32[16,256]{1,0:T(8,128)S(1)} %add.30), channel_id=1, source_target_pairs={{0,128},{32,160},{64,192},{96,224},{128,0},{160,32},{192,64},{224,... | collective-permute-start | bytes 49160 | tf_op jit(solution)/shard_map/ppermute | solution.py:323
  (3 other events, 25.0 us)

commit v3 on v2

--- a/solution.py
+++ b/solution.py
@@ -152,7 +152,7 @@
         out[i] = whole
 
 
-def centred_kernel(own, kern, mean_ref, got, hb, aff, partial, *hh):
+def centred_kernel(own, kern, mean_ref, got, hb, aff, partial, *more):
     z, core = lax.axis_index(Z), lax.axis_index(CORE)
     n = got.shape[0]
     total = mean_ref.shape[0] * LANES * n
@@ -182,11 +182,27 @@
             values = values - mine - place + grand
             aff[i * LANES : (i + 1) * LANES, g * LANES : (g + 1) * LANES] = values.astype(BF16)
     partial[...] = jnp.dot(aff[...], hb[...], preferred_element_type=F32)
-    if hh:
+    if more:
+        hh_ref, scales = more
         deep = (got.shape[1] - 8) // 2
         for i in range(n):
-            hh[0][i * deep : (i + 1) * deep, :LANES] = got[i, 8 : 8 + deep, :]
-            hh[0][i * deep : (i + 1) * deep, LANES:] = got[i, 8 + deep :, :]
+            hh_ref[i * deep : (i + 1) * deep, :LANES] = got[i, 8 : 8 + deep, :]
+            hh_ref[i * deep : (i + 1) * deep, LANES:] = got[i, 8 + deep :, :]
+        hh = hh_ref[...]
+        line = lax.broadcasted_iota(jnp.int32, hh.shape, 0)
+        place = lax.broadcasted_iota(jnp.int32, hh.shape, 1)
+        norm = jnp.sum(jnp.where(line == place, hh, 0.0), axis=0, keepdims=True)
+        norm = jnp.sqrt(jnp.maximum(norm, 1e-30))
+        grown = norm * (1.05 + 1.05 * total * step_size(hh))
+        summed = grown * jnp.max(grown, axis=1, keepdims=True)
+        for i, (value, top) in enumerate(((norm, 512.0), (grown, 512.0), (summed, 32768.0))):
+            scales[2 * i : 2 * i + 1, :] = top / value
+            scales[2 * i + 1 : 2 * i + 2, :] = value / top
+
+
+def step_size(hh):
+    square = jnp.sum(jnp.sum(hh * hh, axis=0, keepdims=True), axis=1, keepdims=True)
+    return 0.5 / jnp.sqrt(square + 1e-06)
 
 
 def start_kernel(unit, points, factor, first, second):
@@ -198,16 +214,12 @@
     second[:, width:] = hb[half:]
 
 
-def step_kernel(before, after, got, hh_ref, h_ref, out, *copies):
-    ah = got[0]
-    for i in range(1, got.shape[0]):
-        ah = ah + got[i]
+def step_kernel(before, after, ah_ref, hh_ref, h_ref, out, *copies):
     hh = hh_ref[...]
     h = h_ref[...] * before if before else h_ref[...]
-    square = jnp.sum(jnp.sum(hh * hh, axis=0, keepdims=True), axis=1, keepdims=True)
-    scale = 0.5 / jnp.sqrt(square + 1e-06)
+    scale = step_size(hh)
     product = jnp.dot(h, hh, precision=lax.Precision.HIGHEST, preferred_element_type=F32)
-    h = jnp.maximum(h - scale * (product - ah), 0.0)
+    h = jnp.maximum(h - scale * (product - ah_ref[...]), 0.0)
     out[...] = h / after if after else h
     if copies:
         hb = h.astype(BF16)
@@ -288,7 +300,7 @@
     def centred(own):
         outs = [shape((group // 2, group), BF16), shape((group // 2, rank), F32)]
         if own:
-            outs.append(shape((rank, rank), F32))
+            outs += [shape((rank, rank), F32), shape((8, rank), F32)]
         return call(
             functools.partial(centred_kernel, own),
             outs,
@@ -298,31 +310,33 @@
 
     aff_other, partial_other = centred(False)
     got = from_ahead(partial_other, CORE, 1)
-    aff_own, partial_own, hh = centred(True)
+    aff_own, partial_own, hh, scales = centred(True)
 
     def over_z(mine):
-        return lax.all_to_all(mine.reshape(nz, pts, rank), Z, 0, 0, tiled=True)
+        mine = lax.all_to_all(mine.astype(jnp.float16), Z, 0, 0, tiled=True)
+        return jnp.sum(mine.astype(F32), axis=0)
 
     def stepped(before, after, ah, hh, h, copies):
         outs = [shape((pts, rank), F32)] + [shape((ncol, pts, rank), BF16)] * copies
         flops = 12 * pts * rank * rank
         return call(functools.partial(step_kernel, before, after), outs, [ah, hh, h], flops)
 
-    ah = over_z(partial_own + got)
+    mine = (partial_own + got) * scales[0]
+    ah = over_z(mine.reshape(nz, pts, rank)) * scales[1]
     h, hb_cols = stepped(unit, None, ah, hh, factor, 1)
 
     hb_cols = lax.all_to_all(hb_cols, COL, 0, 0, tiled=True).reshape(group, rank)
-    partial_other = jnp.dot(aff_other, hb_cols, preferred_element_type=F32)
-    got = from_ahead(partial_other, CORE, 1)
     gram = lax.dot_general(hb_cols, hb_cols, (((0,), (0,)), ((), ())), preferred_element_type=F32)
     own_part = lax.dynamic_slice_in_dim(gram, lax.axis_index(COL) * part, part, 0)
-    own_part = own_part + from_ahead(own_part, CORE, 1)
+    partial_other = jnp.dot(aff_other, hb_cols, preferred_element_type=F32)
+    got = from_ahead(jnp.concatenate([partial_other, own_part]), CORE, 1)
     partial_own = jnp.dot(aff_own, hb_cols, preferred_element_type=F32)
-    ah = over_z(partial_own + got)
-    for bit in (1, 2, 4):
-        own_part = own_part + lax.ppermute(own_part, Z, [(i, i ^ bit) for i in range(nz)])
-    ah, own_part = tie((ah, own_part))
-    hh = sent_to_all(own_part, COL).reshape(rank, rank)
+    mine = ((partial_own + got[: group // 2]) * scales[2]).reshape(nz, pts, rank)
+    extra = (own_part + got[group // 2 :]) * scales[4]
+    extra = jnp.broadcast_to(extra, (nz, part, rank))
+    own = over_z(jnp.concatenate([mine, extra], axis=1))
+    hh = sent_to_all(own[pts:] * scales[5], COL).reshape(rank, rank)
+    ah = own[:pts] * scales[3]
     return stepped(None, unit, ah, hh, h, 0)[0]
 
 

time: 172 us -> 157 us (0.913); the launches traced: 169 us -> 157 us
  blocking collectives: 73.5 us -> 60.6 us
  starting transfers between devices: 55.3 us -> 51.2 us
  waiting for transfers between devices: 28.4 us -> 31.9 us
    all_to_all x1 -> x2, waiting for transfers between devices: 0.01 us -> 19.1 us  [the longest x1 10.8 us: shards(): lax.all_to_all(hb_cols, COL, 0, 0, tiled=True).reshape(group, rank)]
    ppermute x3 -> x0, waiting for transfers between devices: 14.7 us -> none  [shards(): lax.ppermute(own_part, Z, [(i, i ^ bit) for i in range(nz)])]
    all_to_all x3 -> x2, blocking collectives: 43.9 us -> 30.9 us  [over_z(): mine = lax.all_to_all(mine.astype(jnp.float16), Z, 0, 0, tiled=True)]
    ppermute x3 -> x0, starting transfers between devices: 7.05 us -> none  [shards(): lax.ppermute(own_part, Z, [(i, i ^ bit) for i in range(nz)])]
    all_to_all x1 -> x2, starting transfers between devices: 3.49 us -> 7.1 us  [the longest x1 3.57 us: shards(): lax.all_to_all(hb_cols, COL, 0, 0, tiled=True).reshape(group, rank)]
    ppermute x27 -> x26, waiting for transfers between devices: 13.7 us -> 12.8 us  [from_ahead(): lax.ppermute(value, axis, [((i + steps) % length, i) for i in range(lengt...]
    ppermute x27 -> x26, starting transfers between devices: 44.8 us -> 44 us  [from_ahead(): lax.ppermute(value, axis, [((i + steps) % length, i) for i in range(lengt...]
  transfers between devices with their start and end apart: 31 -> 28, of which waited for: 11 -> 9; matrix products, arithmetic and copies ran while one was open for 0% -> 0% of each run, Pallas kernels for 1% -> 1%
where the time goes in v3:
time: 157 us
  blocking collectives  60.6 us (39%)
  starting transfers between devices  51.2 us (33%)
  waiting for transfers between devices  31.9 us (20%)
  Pallas kernels  8.59 us (5%)
  local copies, waits for them, and re-layouts  2.57 us (2%)
    ppermute x26, starting transfers between devices, from_ahead(): lax.ppermute(value, axis, [((i + steps) % length, i) for i in range(lengt...  44 us
    all_to_all x2, blocking collectives, over_z(): mine = lax.all_to_all(mine.astype(jnp.float16), Z, 0, 0, tiled=True)  30.9 us
    all_to_all x1, blocking collectives, shards(): lax.all_to_all(message, ROW, 0, 0, tiled=True)  17 us
    ppermute x26, waiting for transfers between devices, from_ahead(): lax.ppermute(value, axis, [((i + steps) % length, i) for i in range(lengt...  12.8 us
    all_to_all x1, blocking collectives, shards(): gathered = lax.all_to_all(message, COL, 0, 0, tiled=True)  12.7 us
    all_to_all x1, waiting for transfers between devices, shards(): lax.all_to_all(hb_cols, COL, 0, 0, tiled=True).reshape(group, rank)  10.8 us
    pallas_call x8, Pallas kernels, call(): pl.pallas_call(kernel, out_shape=outs, in_specs=[VMEM] * len(args), out_s...  8.59 us
    all_to_all x1, waiting for transfers between devices, sent_to_all(): return lax.all_to_all(copies, axes, split_axis=0, concat_axis=0, tiled=True)  8.26 us
  transfers between devices with their start and end apart: 28, of which 9 were waited for; matrix products, arithmetic and copies ran while one was open for 0% of the time, Pallas kernels for 1%

profile of v3, /device:TPU:1, one launch (start us, length us, event | category | flops | bytes accessed | tf_op | source)
XLA Modules:
  0.0 156.6 jit_solution(14338820519313397484)
XLA Ops:
  0.0 6.4 %collective-permute-start = (bf16[64,1024]{1,0:T(8,128)(2,1)}, bf16[64,1024]{1,0:T(8,128)(2,1)S(1)}, u32[]{:S(2)}, u32[]{:S(2)}) collective-permute-start(bf16[64,1024]{1,0:T(8,128)(2,1)} %p0.1), channel_id=1, source_target_pairs={{32,0},{64,32},{96,64},{128,96},{160,128},{192,160},{224,192},{0,2... | collective-permute-start | bytes 393224 | tf_op jit(solution)/shard_map/ppermute | solution.py:21
  6.4 1.0 copy-done
  8.2 2.6 %collective-permute-start.2 = (bf16[32,1280]{1,0:T(8,128)(2,1)S(1)}, bf16[32,1280]{1,0:T(8,128)(2,1)S(1)}, u32[]{:S(2)}, u32[]{:S(2)}) collective-permute-start(bf16[32,1280]{1,0:T(8,128)(2,1)S(1)} %get-tuple-element.53), channel_id=1, source_target_pairs={{1,0},{2,1},{3,2},{0,3},{5,4},{6,5},{7,6},{4,7},{9,8},{10,9},{11,1... | collective-permute-start | bytes 245768 | tf_op jit(solution)/shard_map/ppermute | solution.py:21
  10.8 2.7 %collective-permute-start.5 = (bf16[32,1280]{1,0:T(8,128)(2,1)S(1)}, bf16[32,1280]{1,0:T(8,128)(2,1)S(1)}, u32[]{:S(2)}, u32[]{:S(2)}) collective-permute-start(bf16[32,1280]{1,0:T(8,128)(2,1)S(1)} %get-tuple-element.54), channel_id=1, source_target_pairs={{4,0},{8,4},{12,8},{0,12},{5,1},{9,5},{13,9},{1,13},{6,2},{10,6},{... | collective-permute-start | bytes 245768 | tf_op jit(solution)/shard_map/ppermute | solution.py:21
  13.5 1.8 %collective-permute-start.3 = (bf16[32,1280]{1,0:T(8,128)(2,1)S(1)}, bf16[32,1280]{1,0:T(8,128)(2,1)S(1)}, u32[]{:S(2)}, u32[]{:S(2)}) collective-permute-start(bf16[32,1280]{1,0:T(8,128)(2,1)S(1)} %get-tuple-element.53), channel_id=1, source_target_pairs={{2,0},{3,1},{0,2},{1,3},{6,4},{7,5},{4,6},{5,7},{10,8},{11,9},{8,1... | collective-permute-start | bytes 245768 | tf_op jit(solution)/shard_map/ppermute | solution.py:21
  15.4 1.9 %collective-permute-start.6 = (bf16[32,1280]{1,0:T(8,128)(2,1)S(1)}, bf16[32,1280]{1,0:T(8,128)(2,1)S(1)}, u32[]{:S(2)}, u32[]{:S(2)}) collective-permute-start(bf16[32,1280]{1,0:T(8,128)(2,1)S(1)} %get-tuple-element.54), channel_id=1, source_target_pairs={{8,0},{12,4},{0,8},{4,12},{9,1},{13,5},{1,9},{5,13},{10,2},{14,6},... | collective-permute-start | bytes 245768 | tf_op jit(solution)/shard_map/ppermute | solution.py:21
  17.5 3.6 %collective-permute-start.9 = (bf16[2,64,1024]{2,1,0:T(8,128)(2,1)S(1)}, bf16[2,64,1024]{2,1,0:T(8,128)(2,1)S(1)}, u32[]{:S(2)}, u32[]{:S(2)}) collective-permute-start(bf16[2,64,1024]{2,1,0:T(8,128)(2,1)S(1)} %get-tuple-element.98), channel_id=1, source_target_pairs={{64,0},{96,32},{128,64},{160,96},{192,128},{224,160},{0,192},{32,2... | collective-permute-start | bytes 786440 | tf_op jit(solution)/shard_map/ppermute | solution.py:21
  21.1 2.1 %collective-permute-start.8 = (bf16[4,32,1280]{2,1,0:T(8,128)(2,1)S(1)}, bf16[4,32,1280]{2,1,0:T(8,128)(2,1)S(1)}, u32[]{:S(2)}, u32[]{:S(2)}) collective-permute-start(bf16[4,32,1280]{2,1,0:T(8,128)(2,1)S(1)} %pad_maximum_fusion.1.by_x), channel_id=1, source_target_pairs={{4,0},{8,4},{12,8},{0,12},{5,1},{9,5},{13,9},{1,13},{6,2},{10,6},{... | collective-permute-start | bytes 983048 | tf_op jit(solution)/shard_map/ppermute | solution.py:21
  24.0 2.3 %collective-permute-start.15 = (bf16[4,32,1280]{2,1,0:T(8,128)(2,1)S(1)}, bf16[4,32,1280]{2,1,0:T(8,128)(2,1)S(1)}, u32[]{:S(2)}, u32[]{:S(2)}) collective-permute-start(bf16[4,32,1280]{2,1,0:T(8,128)(2,1)S(1)} %pad_maximum_fusion.2.by_y), channel_id=1, source_target_pairs={{2,0},{3,1},{0,2},{1,3},{6,4},{7,5},{4,6},{5,7},{10,8},{11,9},{8,1... | collective-permute-start | bytes 983048 | tf_op jit(solution)/shard_map/ppermute | solution.py:21
  26.3 4.8 %collective-permute-start.17 = (bf16[64,1024]{1,0:T(8,128)(2,1)}, bf16[64,1024]{1,0:T(8,128)(2,1)S(1)}, u32[]{:S(2)}, u32[]{:S(2)}) collective-permute-start(bf16[64,1024]{1,0:T(8,128)(2,1)} %p0.1), channel_id=1, source_target_pairs={{16,0},{0,16},{17,1},{1,17},{18,2},{2,18},{19,3},{3,19},{20,4},{4,... | collective-permute-start | bytes 393224 | tf_op jit(solution)/shard_map/ppermute | solution.py:21
  31.3 1.6 %collective-permute-start.16 = (bf16[4,32,1280]{2,1,0:T(8,128)(2,1)S(1)}, bf16[4,32,1280]{2,1,0:T(8,128)(2,1)S(1)}, u32[]{:S(2)}, u32[]{:S(2)}) collective-permute-start(bf16[4,32,1280]{2,1,0:T(8,128)(2,1)S(1)} %pad_maximum_fusion.2.by_y), channel_id=1, source_target_pairs={{3,0},{0,1},{1,2},{2,3},{7,4},{4,5},{5,6},{6,7},{11,8},{8,9},{9,10... | collective-permute-start | bytes 983048 | tf_op jit(solution)/shard_map/ppermute | solution.py:21
  32.9 1.7 %collective-permute-start.12 = (bf16[4,32,1280]{2,1,0:T(8,128)(2,1)S(1)}, bf16[4,32,1280]{2,1,0:T(8,128)(2,1)S(1)}, u32[]{:S(2)}, u32[]{:S(2)}) collective-permute-start(bf16[4,32,1280]{2,1,0:T(8,128)(2,1)S(1)} %pad_maximum_fusion.1.by_x), channel_id=1, source_target_pairs={{8,0},{12,4},{0,8},{4,12},{9,1},{13,5},{1,9},{5,13},{10,2},{14,6},... | collective-permute-start | bytes 983048 | tf_op jit(solution)/shard_map/ppermute | solution.py:21
  34.7 2.3 %collective-permute-start.19 = (bf16[2,64,1024]{2,1,0:T(8,128)(2,1)S(1)}, bf16[2,64,1024]{2,1,0:T(8,128)(2,1)S(1)}, u32[]{:S(2)}, u32[]{:S(2)}) collective-permute-start(bf16[2,64,1024]{2,1,0:T(8,128)(2,1)S(1)} %collective-permute-done.9.p23), channel_id=1, source_target_pairs={{16,0},{0,16},{17,1},{1,17},{18,2},{2,18},{19,3},{3,19},{20,4},{4,... | collective-permute-start | bytes 786440 | tf_op jit(solution)/shard_map/ppermute | solution.py:21
  37.2 4.6 %collective-permute-done.16.x3 = bf16[4,32,1280]{2,1,0:T(8,128)(2,1)S(1)} collective-permute-done((bf16[4,32,1280]{2,1,0:T(8,128)(2,1)S(1)}, bf16[4,32,1280]{2,1,0:T(8,128)(2,1)S(1)}, u32[]{:S(2)}, u32[]{:S(2)}) %collective-permute-start.16) | collective-permute-done | bytes 327712 | tf_op jit(solution)/shard_map/ppermute | solution.py:21
  41.8 3.8 %collective-permute-start.11 = (bf16[64,1024]{1,0:T(8,128)(2,1)S(1)}, bf16[64,1024]{1,0:T(8,128)(2,1)S(1)}, u32[]{:S(2)}, u32[]{:S(2)}) collective-permute-start(bf16[64,1024]{1,0:T(8,128)(2,1)S(1)} %slice_bitcast_fusion), channel_id=1, source_target_pairs={{32,0},{64,32},{96,64},{128,96},{160,128},{192,160},{224,192},{0,2... | collective-permute-start | bytes 393224 | tf_op jit(solution)/shard_map/ppermute | solution.py:21
  45.5 1.5 collective-permute-start.18
  47.1 4.0 %collective-permute-done.13.y3 = bf16[4,32,1280]{2,1,0:T(8,128)(2,1)S(1)} collective-permute-done((bf16[4,32,1280]{2,1,0:T(8,128)(2,1)S(1)}, bf16[4,32,1280]{2,1,0:T(8,128)(2,1)S(1)}, u32[]{:S(2)}, u32[]{:S(2)}) %collective-permute-start.13) | collective-permute-done | bytes 327712 | tf_op jit(solution)/shard_map/ppermute | solution.py:21
  51.5 1.0 collective-permute-done.21.o7
  54.5 4.0 %shard_map.30 = (f32[1024,1024]{1,0:T(8,128)S(1)}, f32[16,24,128]{2,1,0:T(8,128)S(1)}) custom-call(bf16[64,1024]{1,0:T(8,128)(2,1)S(1)} %copy-done.1, bf16[64,1024]{1,0:T(8,128)(2,1)S(1)} %collective-permute-done.p1, bf16[2,64,1024]{2,1,0:T(8,128)(2,1)S(1)} %collective-permute-done.9.p23, bf16[64,1024]{1,0:T(8,128)(2,1)S(1)} %collective-permute-done.11.p4, ...), custom_call_target="tpu_custom_call" | custom-call | flops 2147483648 | bytes 8622080 | tf_op jit(solution)/shard_map/pallas_call | solution.py:37
  58.5 17.0 %all_to_all.30.got = f32[16,24,128]{2,1,0:T(8,128)S(1)} all-to-all(f32[16,24,128]{2,1,0:T(8,128)S(1)} %get-tuple-element.85), channel_id=1, replica_groups=mesh['row_0'=8,'row_1'=2,'col_0'=4,'col_1'=4] {'row_0','row_1'}, dimensions={0} | all-to-all | bytes 393216 | tf_op jit(solution)/shard_map/all_to_all | solution.py:295
  75.6 12.7 %all_to_all.31.got = f32[16,40,128]{2,1,0:T(8,128)S(1)} all-to-all(f32[16,40,128]{2,1,0:T(8,128)S(1)} %get-tuple-element.87), channel_id=1, replica_groups=mesh['row_0'=8,'row_1'=2,'col_0'=4,'col_1'=4] {'col_0','col_1'}, dimensions={0} | all-to-all | bytes 655360 | tf_op jit(solution)/shard_map/all_to_all | solution.py:298
  89.2 1.2 collective-permute-start.24
  92.0 14.8 %all_to_all.32 = f16[8,64,256]{2,1,0:T(8,128)(2,1)S(1)} all-to-all(f16[8,64,256]{2,1,0:T(8,128)(2,1)S(1)} %bitcast.40), channel_id=1, replica_groups=mesh['row_0'=8,'row_1'=2,'col_0'=4,'col_1'=4] {'row_0'}, dimensions={0} | all-to-all | bytes 524288 | tf_op jit(solution)/shard_map/all_to_all | solution.py:316
  106.8 1.1 shard_map.34
  107.9 3.6 %all-to-all-start.3 = ((bf16[16,64,256]{2,1,0:T(8,128)(2,1)}), bf16[16,64,256]{2,1,0:T(8,128)(2,1)S(1)}, u32[]{:S(2)}, u32[]{:S(2)}) async-start(bf16[16,64,256]{2,1,0:T(8,128)(2,1)} %get-tuple-element.94), calls=%async_computation.3 | async-start | bytes 1048576 | tf_op jit(solution)/shard_map/all_to_all | solution.py:328
  111.5 10.8 %all-to-all-done.3 = bf16[16,64,256]{2,1,0:T(8,128)(2,1)S(1)} async-done(((bf16[16,64,256]{2,1,0:T(8,128)(2,1)}), bf16[16,64,256]{2,1,0:T(8,128)(2,1)S(1)}, u32[]{:S(2)}, u32[]{:S(2)}) %all-to-all-start.3) | async-done | bytes 524320 | tf_op jit(solution)/shard_map/all_to_all | solution.py:328
  123.2 1.7 %collective-permute-start.25 = (f32[528,256]{1,0:T(8,128)S(1)}, f32[528,256]{1,0:T(8,128)S(1)}, u32[]{:S(2)}, u32[]{:S(2)}) collective-permute-start(f32[528,256]{1,0:T(8,128)S(1)} %pad_maximum_fusion), channel_id=1, source_target_pairs={{16,0},{0,16},{17,1},{1,17},{18,2},{2,18},{19,3},{3,19},{20,4},{4,... | collective-permute-start | bytes 1622024 | tf_op jit(solution)/shard_map/ppermute | solution.py:21
  124.9 1.6 collective-permute-done.25
  127.0 16.1 %all_to_all.33 = f16[8,80,256]{2,1,0:T(8,128)(2,1)S(1)} all-to-all(f16[8,80,256]{2,1,0:T(8,128)(2,1)S(1)} %pad_maximum_fusion.3), channel_id=1, replica_groups=mesh['row_0'=8,'row_1'=2,'col_0'=4,'col_1'=4] {'row_0'}, dimensions={0} | all-to-all | bytes 655360 | tf_op jit(solution)/shard_map/all_to_all | solution.py:316
  143.9 3.5 %all-to-all-start.5 = ((f32[16,16,256]{2,1,0:T(8,128)}), f32[16,16,256]{2,1,0:T(8,128)S(1)}, u32[]{:S(2)}, u32[]{:S(2)}) async-start(f32[16,16,256]{2,1,0:T(8,128)} %broadcast_in_dim.7), calls=%async_computation.5 | async-start | bytes 524288 | tf_op jit(solution)/shard_map/all_to_all | solution.py:27
  147.5 8.3 %all-to-all-done.5 = f32[16,16,256]{2,1,0:T(8,128)S(1)} async-done(((f32[16,16,256]{2,1,0:T(8,128)}), f32[16,16,256]{2,1,0:T(8,128)S(1)}, u32[]{:S(2)}, u32[]{:S(2)}) %all-to-all-start.5) | async-done | bytes 262176 | tf_op jit(solution)/shard_map/all_to_all | solution.py:27
  155.8 0.9 shard_map.35
  (64 shorter events, 9.7 us)
Async XLA Ops:
  0.0 13.5 %collective-permute-start = (bf16[64,1024]{1,0:T(8,128)(2,1)}, bf16[64,1024]{1,0:T(8,128)(2,1)S(1)}, u32[]{:S(2)}, u32[]{:S(2)}) collective-permute-start(bf16[64,1024]{1,0:T(8,128)(2,1)} %p0.1), channel_id=1, source_target_pairs={{32,0},{64,32},{96,64},{128,96},{160,128},{192,160},{224,192},{0,2... | collective-permute-start | bytes 393224 | tf_op jit(solution)/shard_map/ppermute | solution.py:21
  6.4 7.1 %collective-permute-start.1 = (bf16[64,1024]{1,0:T(8,128)(2,1)}, bf16[64,1024]{1,0:T(8,128)(2,1)S(1)}, u32[]{:S(2)}, u32[]{:S(2)}) collective-permute-start(bf16[64,1024]{1,0:T(8,128)(2,1)} %p0.1), channel_id=1, source_target_pairs={{224,0},{0,32},{32,64},{64,96},{96,128},{128,160},{160,192},{192,2... | collective-permute-start | bytes 393224 | tf_op jit(solution)/shard_map/ppermute | solution.py:21
  6.4 1.0 copy-start
  7.4 0.8 copy-start.2
  8.2 46.3 %copy-start.1 = (bf16[64,1024]{1,0:T(8,128)(2,1)S(1)}, bf16[64,1024]{1,0:T(8,128)(2,1)}, u32[]{:S(2)}) copy-start(bf16[64,1024]{1,0:T(8,128)(2,1)} %p0.1) | copy-start | bytes 393220
  8.2 7.1 %collective-permute-start.2 = (bf16[32,1280]{1,0:T(8,128)(2,1)S(1)}, bf16[32,1280]{1,0:T(8,128)(2,1)S(1)}, u32[]{:S(2)}, u32[]{:S(2)}) collective-permute-start(bf16[32,1280]{1,0:T(8,128)(2,1)S(1)} %get-tuple-element.53), channel_id=1, source_target_pairs={{1,0},{2,1},{3,2},{0,3},{5,4},{6,5},{7,6},{4,7},{9,8},{10,9},{11,1... | collective-permute-start | bytes 245768 | tf_op jit(solution)/shard_map/ppermute | solution.py:21
  10.8 6.6 %collective-permute-start.4 = (bf16[32,1280]{1,0:T(8,128)(2,1)S(1)}, bf16[32,1280]{1,0:T(8,128)(2,1)S(1)}, u32[]{:S(2)}, u32[]{:S(2)}) collective-permute-start(bf16[32,1280]{1,0:T(8,128)(2,1)S(1)} %get-tuple-element.53), channel_id=1, source_target_pairs={{3,0},{0,1},{1,2},{2,3},{7,4},{4,5},{5,6},{6,7},{11,8},{8,9},{9,10... | collective-permute-start | bytes 245768 | tf_op jit(solution)/shard_map/ppermute | solution.py:21
  10.8 6.7 %collective-permute-start.5 = (bf16[32,1280]{1,0:T(8,128)(2,1)S(1)}, bf16[32,1280]{1,0:T(8,128)(2,1)S(1)}, u32[]{:S(2)}, u32[]{:S(2)}) collective-permute-start(bf16[32,1280]{1,0:T(8,128)(2,1)S(1)} %get-tuple-element.54), channel_id=1, source_target_pairs={{4,0},{8,4},{12,8},{0,12},{5,1},{9,5},{13,9},{1,13},{6,2},{10,6},{... | collective-permute-start | bytes 245768 | tf_op jit(solution)/shard_map/ppermute | solution.py:21
  13.5 7.5 %collective-permute-start.7 = (bf16[32,1280]{1,0:T(8,128)(2,1)S(1)}, bf16[32,1280]{1,0:T(8,128)(2,1)S(1)}, u32[]{:S(2)}, u32[]{:S(2)}) collective-permute-start(bf16[32,1280]{1,0:T(8,128)(2,1)S(1)} %get-tuple-element.54), channel_id=1, source_target_pairs={{12,0},{0,4},{4,8},{8,12},{13,1},{1,5},{5,9},{9,13},{14,2},{2,6},{... | collective-permute-start | bytes 245768 | tf_op jit(solution)/shard_map/ppermute | solution.py:21
  13.5 7.5 %collective-permute-start.3 = (bf16[32,1280]{1,0:T(8,128)(2,1)S(1)}, bf16[32,1280]{1,0:T(8,128)(2,1)S(1)}, u32[]{:S(2)}, u32[]{:S(2)}) collective-permute-start(bf16[32,1280]{1,0:T(8,128)(2,1)S(1)} %get-tuple-element.53), channel_id=1, source_target_pairs={{2,0},{3,1},{0,2},{1,3},{6,4},{7,5},{4,6},{5,7},{10,8},{11,9},{8,1... | collective-permute-start | bytes 245768 | tf_op jit(solution)/shard_map/ppermute | solution.py:21
  15.4 5.7 %collective-permute-start.6 = (bf16[32,1280]{1,0:T(8,128)(2,1)S(1)}, bf16[32,1280]{1,0:T(8,128)(2,1)S(1)}, u32[]{:S(2)}, u32[]{:S(2)}) collective-permute-start(bf16[32,1280]{1,0:T(8,128)(2,1)S(1)} %get-tuple-element.54), channel_id=1, source_target_pairs={{8,0},{12,4},{0,8},{4,12},{9,1},{13,5},{1,9},{5,13},{10,2},{14,6},... | collective-permute-start | bytes 245768 | tf_op jit(solution)/shard_map/ppermute | solution.py:21
  17.4 8.9 %collective-permute-start.10 = (bf16[2,64,1024]{2,1,0:T(8,128)(2,1)S(1)}, bf16[2,64,1024]{2,1,0:T(8,128)(2,1)S(1)}, u32[]{:S(2)}, u32[]{:S(2)}) collective-permute-start(bf16[2,64,1024]{2,1,0:T(8,128)(2,1)S(1)} %get-tuple-element.97), channel_id=1, source_target_pairs={{192,0},{224,32},{0,64},{32,96},{64,128},{96,160},{128,192},{160,2... | collective-permute-start | bytes 786440 | tf_op jit(solution)/shard_map/ppermute | solution.py:21
  17.5 13.8 %collective-permute-start.9 = (bf16[2,64,1024]{2,1,0:T(8,128)(2,1)S(1)}, bf16[2,64,1024]{2,1,0:T(8,128)(2,1)S(1)}, u32[]{:S(2)}, u32[]{:S(2)}) collective-permute-start(bf16[2,64,1024]{2,1,0:T(8,128)(2,1)S(1)} %get-tuple-element.98), channel_id=1, source_target_pairs={{64,0},{96,32},{128,64},{160,96},{192,128},{224,160},{0,192},{32,2... | collective-permute-start | bytes 786440 | tf_op jit(solution)/shard_map/ppermute | solution.py:21
  21.1 11.8 %collective-permute-start.8 = (bf16[4,32,1280]{2,1,0:T(8,128)(2,1)S(1)}, bf16[4,32,1280]{2,1,0:T(8,128)(2,1)S(1)}, u32[]{:S(2)}, u32[]{:S(2)}) collective-permute-start(bf16[4,32,1280]{2,1,0:T(8,128)(2,1)S(1)} %pad_maximum_fusion.1.by_x), channel_id=1, source_target_pairs={{4,0},{8,4},{12,8},{0,12},{5,1},{9,5},{13,9},{1,13},{6,2},{10,6},{... | collective-permute-start | bytes 983048 | tf_op jit(solution)/shard_map/ppermute | solution.py:21
  23.2 11.5 %collective-permute-start.14 = (bf16[4,32,1280]{2,1,0:T(8,128)(2,1)S(1)}, bf16[4,32,1280]{2,1,0:T(8,128)(2,1)S(1)}, u32[]{:S(2)}, u32[]{:S(2)}) collective-permute-start(bf16[4,32,1280]{2,1,0:T(8,128)(2,1)S(1)} %pad_maximum_fusion.2.by_y), channel_id=1, source_target_pairs={{1,0},{2,1},{3,2},{0,3},{5,4},{6,5},{7,6},{4,7},{9,8},{10,9},{11,1... | collective-permute-start | bytes 983048 | tf_op jit(solution)/shard_map/ppermute | solution.py:21
  24.0 13.0 %collective-permute-start.15 = (bf16[4,32,1280]{2,1,0:T(8,128)(2,1)S(1)}, bf16[4,32,1280]{2,1,0:T(8,128)(2,1)S(1)}, u32[]{:S(2)}, u32[]{:S(2)}) collective-permute-start(bf16[4,32,1280]{2,1,0:T(8,128)(2,1)S(1)} %pad_maximum_fusion.2.by_y), channel_id=1, source_target_pairs={{2,0},{3,1},{0,2},{1,3},{6,4},{7,5},{4,6},{5,7},{10,8},{11,9},{8,1... | collective-permute-start | bytes 983048 | tf_op jit(solution)/shard_map/ppermute | solution.py:21
  26.3 8.2 %collective-permute-start.17 = (bf16[64,1024]{1,0:T(8,128)(2,1)}, bf16[64,1024]{1,0:T(8,128)(2,1)S(1)}, u32[]{:S(2)}, u32[]{:S(2)}) collective-permute-start(bf16[64,1024]{1,0:T(8,128)(2,1)} %p0.1), channel_id=1, source_target_pairs={{16,0},{0,16},{17,1},{1,17},{18,2},{2,18},{19,3},{3,19},{20,4},{4,... | collective-permute-start | bytes 393224 | tf_op jit(solution)/shard_map/ppermute | solution.py:21
  31.3 10.5 %collective-permute-start.16 = (bf16[4,32,1280]{2,1,0:T(8,128)(2,1)S(1)}, bf16[4,32,1280]{2,1,0:T(8,128)(2,1)S(1)}, u32[]{:S(2)}, u32[]{:S(2)}) collective-permute-start(bf16[4,32,1280]{2,1,0:T(8,128)(2,1)S(1)} %pad_maximum_fusion.2.by_y), channel_id=1, source_target_pairs={{3,0},{0,1},{1,2},{2,3},{7,4},{4,5},{5,6},{6,7},{11,8},{8,9},{9,10... | collective-permute-start | bytes 983048 | tf_op jit(solution)/shard_map/ppermute | solution.py:21
  32.9 12.7 %collective-permute-start.12 = (bf16[4,32,1280]{2,1,0:T(8,128)(2,1)S(1)}, bf16[4,32,1280]{2,1,0:T(8,128)(2,1)S(1)}, u32[]{:S(2)}, u32[]{:S(2)}) collective-permute-start(bf16[4,32,1280]{2,1,0:T(8,128)(2,1)S(1)} %pad_maximum_fusion.1.by_x), channel_id=1, source_target_pairs={{8,0},{12,4},{0,8},{4,12},{9,1},{13,5},{1,9},{5,13},{10,2},{14,6},... | collective-permute-start | bytes 983048 | tf_op jit(solution)/shard_map/ppermute | solution.py:21
  34.6 16.5 %collective-permute-start.13 = (bf16[4,32,1280]{2,1,0:T(8,128)(2,1)S(1)}, bf16[4,32,1280]{2,1,0:T(8,128)(2,1)S(1)}, u32[]{:S(2)}, u32[]{:S(2)}) collective-permute-start(bf16[4,32,1280]{2,1,0:T(8,128)(2,1)S(1)} %pad_maximum_fusion.1.by_x), channel_id=1, source_target_pairs={{12,0},{0,4},{4,8},{8,12},{13,1},{1,5},{5,9},{9,13},{14,2},{2,6},{... | collective-permute-start | bytes 983048 | tf_op jit(solution)/shard_map/ppermute | solution.py:21
  34.7 17.8 %collective-permute-start.19 = (bf16[2,64,1024]{2,1,0:T(8,128)(2,1)S(1)}, bf16[2,64,1024]{2,1,0:T(8,128)(2,1)S(1)}, u32[]{:S(2)}, u32[]{:S(2)}) collective-permute-start(bf16[2,64,1024]{2,1,0:T(8,128)(2,1)S(1)} %collective-permute-done.9.p23), channel_id=1, source_target_pairs={{16,0},{0,16},{17,1},{1,17},{18,2},{2,18},{19,3},{3,19},{20,4},{4,... | collective-permute-start | bytes 786440 | tf_op jit(solution)/shard_map/ppermute | solution.py:21
  37.0 15.5 %collective-permute-start.20 = (bf16[2,64,1024]{2,1,0:T(8,128)(2,1)S(1)}, bf16[2,64,1024]{2,1,0:T(8,128)(2,1)S(1)}, u32[]{:S(2)}, u32[]{:S(2)}) collective-permute-start(bf16[2,64,1024]{2,1,0:T(8,128)(2,1)S(1)} %collective-permute-done.10.p65), channel_id=1, source_target_pairs={{16,0},{0,16},{17,1},{1,17},{18,2},{2,18},{19,3},{3,19},{20,4},{4,... | collective-permute-start | bytes 786440 | tf_op jit(solution)/shard_map/ppermute | solution.py:21
  41.8 9.8 %collective-permute-start.11 = (bf16[64,1024]{1,0:T(8,128)(2,1)S(1)}, bf16[64,1024]{1,0:T(8,128)(2,1)S(1)}, u32[]{:S(2)}, u32[]{:S(2)}) collective-permute-start(bf16[64,1024]{1,0:T(8,128)(2,1)S(1)} %slice_bitcast_fusion), channel_id=1, source_target_pairs={{32,0},{64,32},{96,64},{128,96},{160,128},{192,160},{224,192},{0,2... | collective-permute-start | bytes 393224 | tf_op jit(solution)/shard_map/ppermute | solution.py:21
  45.5 6.0 %collective-permute-start.18 = (bf16[64,1024]{1,0:T(8,128)(2,1)S(1)}, bf16[64,1024]{1,0:T(8,128)(2,1)S(1)}, u32[]{:S(2)}, u32[]{:S(2)}) collective-permute-start(bf16[64,1024]{1,0:T(8,128)(2,1)S(1)} %collective-permute-done.p1), channel_id=1, source_target_pairs={{16,0},{0,16},{17,1},{1,17},{18,2},{2,18},{19,3},{3,19},{20,4},{4,... | collective-permute-start | bytes 393224 | tf_op jit(solution)/shard_map/ppermute | solution.py:21
  51.0 1.5 collective-permute-start.21
  51.5 2.2 %collective-permute-start.22 = (bf16[64,1024]{1,0:T(8,128)(2,1)S(1)}, bf16[64,1024]{1,0:T(8,128)(2,1)S(1)}, u32[]{:S(2)}, u32[]{:S(2)}) collective-permute-start(bf16[64,1024]{1,0:T(8,128)(2,1)S(1)} %collective-permute-done.11.p4), channel_id=1, source_target_pairs={{16,0},{0,16},{17,1},{1,17},{18,2},{2,18},{19,3},{3,19},{20,4},{4,... | collective-permute-start | bytes 393224 | tf_op jit(solution)/shard_map/ppermute | solution.py:21
  53.2 1.3 collective-permute-start.23
  89.2 17.6 %copy-start.3 = (f32[64,256]{1,0:T(8,128)S(1)}, f32[64,256]{1,0:T(8,128)}, u32[]{:S(2)}) copy-start(f32[64,256]{1,0:T(8,128)} %h_ref.1) | copy-start | bytes 196612
  89.2 2.7 %collective-permute-start.24 = (f32[512,256]{1,0:T(8,128)S(1)}, f32[512,256]{1,0:T(8,128)S(1)}, u32[]{:S(2)}, u32[]{:S(2)}) collective-permute-start(f32[512,256]{1,0:T(8,128)S(1)} %get-tuple-element.91), channel_id=1, source_target_pairs={{16,0},{0,16},{17,1},{1,17},{18,2},{2,18},{19,3},{3,19},{20,4},{4,... | collective-permute-start | bytes 1572872 | tf_op jit(solution)/shard_map/ppermute | solution.py:21
  107.9 14.4 %all-to-all-start.3 = ((bf16[16,64,256]{2,1,0:T(8,128)(2,1)}), bf16[16,64,256]{2,1,0:T(8,128)(2,1)S(1)}, u32[]{:S(2)}, u32[]{:S(2)}) async-start(bf16[16,64,256]{2,1,0:T(8,128)(2,1)} %get-tuple-element.94), calls=%async_computation.3 | async-start | bytes 1048576 | tf_op jit(solution)/shard_map/all_to_all | solution.py:328
  123.2 3.3 %collective-permute-start.25 = (f32[528,256]{1,0:T(8,128)S(1)}, f32[528,256]{1,0:T(8,128)S(1)}, u32[]{:S(2)}, u32[]{:S(2)}) collective-permute-start(f32[528,256]{1,0:T(8,128)S(1)} %pad_maximum_fusion), channel_id=1, source_target_pairs={{16,0},{0,16},{17,1},{1,17},{18,2},{2,18},{19,3},{3,19},{20,4},{4,... | collective-permute-start | bytes 1622024 | tf_op jit(solution)/shard_map/ppermute | solution.py:21
  143.9 11.8 %all-to-all-start.5 = ((f32[16,16,256]{2,1,0:T(8,128)}), f32[16,16,256]{2,1,0:T(8,128)S(1)}, u32[]{:S(2)}, u32[]{:S(2)}) async-start(f32[16,16,256]{2,1,0:T(8,128)} %broadcast_in_dim.7), calls=%async_computation.5 | async-start | bytes 524288 | tf_op jit(solution)/shard_map/all_to_all | solution.py:27

commit v4 on v3

--- a/solution.py
+++ b/solution.py
@@ -83,42 +83,30 @@
     part_ref[...] = gram_ref[pl.ds(at, part), :]
 
 
-def rows_kernel(
-    p0, p1, p23, p4, p65, p7, o0, o1, o23, o4, o65, o7, cols, sq, part, more, kern, out, held, sums
-):
-    z, core = lax.axis_index(Z), lax.axis_index(CORE)
-    nz, pts = lax.axis_size(Z), p0.shape[0]
-
-    def put(which, steps, value):
-        at = (which * nz + lax.rem(z + steps, nz)) * pts
-        held[pl.ds(pl.multiple_of(at, pts), pts), :] = value
-
-    for which, refs in ((core, (p0, p1, p23, p4, p65, p7)), (1 - core, (o0, o1, o23, o4, o65, o7))):
-        put(which, 0, refs[0][...])
-        put(which, 1, refs[1][...])
-        put(which, 2, refs[2][0])
-        put(which, 3, refs[2][1])
-        put(which, 4, refs[3][...])
-        put(which, 5, refs[4][1])
-        put(which, 6, refs[4][0])
-        put(which, 7, refs[5][...])
+def rows_kernel(own, other, cols, sq, part, more, kern, out, sums):
+    core = lax.axis_index(CORE)
     col_sq = jnp.concatenate([sq[g : g + 1, :] for g in range(sq.shape[0])], axis=1)
     tall = 2 * LANES
 
-    def block(i, _):
-        at = pl.ds(pl.multiple_of(i * tall, tall), tall)
-        rows = held[at, :]
+    def block(ref, first, i):
+        rows = ref[pl.ds(pl.multiple_of(i * tall, tall), tall), :]
+        at = first * ref.shape[0] // tall + i
         row_sq = jnp.sum(squares(rows), axis=1, keepdims=True)
         gram = rows_dot(rows, cols[...])
         values = jnp.exp((2.0 * gram - row_sq - col_sq) * (0.5 / EMBED_WIDTH))
-        kern[at, :] = values
+        kern[pl.ds(pl.multiple_of(at * tall, tall), tall), :] = values
         total = sum(values[:, g : g + LANES] for g in range(0, values.shape[1], LANES))
         for j in range(2):
             line = jnp.sum(total[j * LANES : (j + 1) * LANES].T, axis=0, keepdims=True)
-            sums[pl.ds(i * 2 + j, 1), :] = line
-        return 0
-
-    lax.fori_loop(0, held.shape[0] // tall, block, 0)
+            sums[pl.ds(at * 2 + j, 1), :] = line
+
+    for ref, first in ((own, core), (other, 1 - core)):
+
+        def body(i, _, ref=ref, first=first):
+            block(ref, first, i)
+            return 0
+
+        lax.fori_loop(0, ref.shape[0] // tall, body, 0)
     lines = sums.shape[0]
     deep = part.shape[0] // 2
     at = pl.ds(pl.multiple_of(core * deep, deep), deep)
@@ -205,13 +193,15 @@
     return 0.5 / jnp.sqrt(square + 1e-06)
 
 
-def start_kernel(unit, points, factor, first, second):
+def start_kernel(unit, points, factor, first, second, copies):
     half, width = first.shape[0], points.shape[1]
     hb = (factor[...] * unit).astype(BF16)
     first[:, :width] = points[:half, :]
     first[:, width:] = hb[:half]
     second[:, :width] = points[half:, :]
     second[:, width:] = hb[half:]
+    for i in range(copies.shape[0]):
+        copies[i] = points[...]
 
 
 def step_kernel(before, after, ah_ref, hh_ref, h_ref, out, *copies):
@@ -237,34 +227,25 @@
     half = pts // 2
     shape = jax.ShapeDtypeStruct
 
-    first, second = call(
+    first, second, copies = call(
         functools.partial(start_kernel, unit),
-        [shape((half, width + rank), BF16)] * 2,
+        [*[shape((half, width + rank), BF16)] * 2, shape((nz, pts, width), BF16)],
         [points, factor],
         1,
     )
     tie = lax.optimization_barrier
-    z1, z7 = from_ahead(points, Z, 1), from_ahead(points, Z, -1)
+    along_z = lax.all_to_all(copies, Z, 0, 0, tiled=True)
     x1, x3 = from_ahead(first, X, 1), from_ahead(first, X, -1)
     y1, y3 = from_ahead(second, Y, 1), from_ahead(second, Y, -1)
-    z1, z7, first, second = tie((z1, z7, first, second))
-    z23 = from_ahead(jnp.stack([points, z1]), Z, 2)
-    z65 = from_ahead(jnp.stack([points, z7]), Z, -2)
     x2, y2 = from_ahead(first, X, 2), from_ahead(second, Y, 2)
     x1, x2, x3, y1, y2, y3 = tie((x1, x2, x3, y1, y2, y3))
     by_x = jnp.stack([first, x1, x2, x3])
     by_y = jnp.stack([second, y1, y2, y3])
     from_y = [from_ahead(by_x, Y, s) for s in (1, 2, 3)]
     from_x = [from_ahead(by_y, X, s) for s in (1, 2, 3)]
-    from_y[0], z23, z65, z1, z7 = tie((from_y[0], z23, z65, z1, z7))
-    z4 = from_ahead(z23[1], Z, 1)
-    other_0, other_1, other_7 = (from_ahead(v, CORE, 1) for v in (points, z1, z7))
-    along_z = [points, z1, z23, z4, z65, z7]
+    from_y, from_x, along_z = tie((from_y, from_x, along_z.reshape(-1, width)))
     cols = [by_x, *from_y, by_y, *from_x]
-    other_23, other_65 = from_ahead(z23, CORE, 1), from_ahead(z65, CORE, 1)
-    other = [other_0, other_1, other_23, other_65, other_7]
-    cols, other = tie((cols, other))
-    other.insert(3, from_ahead(z4, CORE, 1))
+    other = from_ahead(along_z, CORE, 1)
 
     part = rank // ncol
     group = nrow * pts
@@ -285,9 +266,9 @@
     kern, message = call(
         rows_kernel,
         [shape((group, group), F32), shape((nrow, lines + part, LANES), F32)],
-        [*along_z, *other, col_pts, col_sq, own_part, more_part],
+        [along_z, other, col_pts, col_sq, own_part, more_part],
         2 * group * group * width,
-        [pltpu.VMEM((group, width), BF16), pltpu.VMEM((lines, LANES), F32)],
+        [pltpu.VMEM((lines, LANES), F32)],
     )
     mean_rows, message = call(
         means_kernel,

time: 157 us -> 154 us (0.981)
  starting transfers between devices: 51.2 us -> 36.7 us
  waiting for transfers between devices: 31.9 us -> 40.9 us
  local copies, waits for them, and re-layouts: 2.57 us -> 4.19 us
    ppermute x26 -> x16, starting transfers between devices: 44 us -> 20.6 us  [from_ahead(): lax.ppermute(value, axis, [((i + steps) % length, i) for i in range(lengt...]
    ppermute x26 -> x16, waiting for transfers between devices: 12.8 us -> 21.8 us  [from_ahead(): lax.ppermute(value, axis, [((i + steps) % length, i) for i in range(lengt...]
    all_to_all x0 -> x1, starting transfers between devices: none -> 9.01 us  [shards(): along_z = lax.all_to_all(copies, Z, 0, 0, tiled=True)]
    unnamed x8 -> x10, local copies, waits for them, and re-layouts: 1.82 us -> 3.44 us
  transfers between devices with their start and end apart: 28 -> 19, of which waited for: 9 -> 11; matrix products, arithmetic and copies ran while one was open for 0% -> 0% of each run, Pallas kernels for 1% -> 1%
where the time goes in v4:
time: 154 us
  blocking collectives  60.5 us (39%)
  waiting for transfers between devices  40.9 us (27%)
  starting transfers between devices  36.7 us (24%)
  Pallas kernels  9.54 us (6%)
  local copies, waits for them, and re-layouts  4.19 us (3%)
    all_to_all x2, blocking collectives, over_z(): mine = lax.all_to_all(mine.astype(jnp.float16), Z, 0, 0, tiled=True)  30.9 us
    ppermute x16, waiting for transfers between devices, from_ahead(): lax.ppermute(value, axis, [((i + steps) % length, i) for i in range(lengt...  21.8 us
    ppermute x16, starting transfers between devices, from_ahead(): lax.ppermute(value, axis, [((i + steps) % length, i) for i in range(lengt...  20.6 us
    all_to_all x1, blocking collectives, shards(): lax.all_to_all(message, ROW, 0, 0, tiled=True)  17.4 us
    all_to_all x1, blocking collectives, shards(): gathered = lax.all_to_all(message, COL, 0, 0, tiled=True)  12.2 us
    all_to_all x1, waiting for transfers between devices, shards(): lax.all_to_all(hb_cols, COL, 0, 0, tiled=True).reshape(group, rank)  10.8 us
    pallas_call x8, Pallas kernels, call(): pl.pallas_call(kernel, out_shape=outs, in_specs=[VMEM] * len(args), out_s...  9.54 us
    all_to_all x1, starting transfers between devices, shards(): along_z = lax.all_to_all(copies, Z, 0, 0, tiled=True)  9.01 us
  transfers between devices with their start and end apart: 19, of which 11 were waited for; matrix products, arithmetic and copies ran while one was open for 0% of the time, Pallas kernels for 1%

profile of v4, /device:TPU:1, one launch (start us, length us, event | category | flops | bytes accessed | tf_op | source)
XLA Modules:
  0.0 153.7 jit_solution(15376841025922966071)
XLA Ops:
  0.0 0.8 copy-done.2
  0.8 0.9 copy-done.4
  1.7 1.1 shard_map.28
  2.8 9.0 %all-to-all-start = ((bf16[8,64,1024]{2,1,0:T(8,128)(2,1)}), bf16[8,64,1024]{2,1,0:T(8,128)(2,1)S(1)}, u32[]{:S(2)}, u32[]{:S(2)}) async-start(bf16[8,64,1024]{2,1,0:T(8,128)(2,1)} %get-tuple-element.45), calls=%async_computation | async-start | bytes 2097152 | tf_op jit(solution)/shard_map/all_to_all | solution.py:237
  11.8 2.5 %collective-permute-start = (bf16[32,1280]{1,0:T(8,128)(2,1)S(1)}, bf16[32,1280]{1,0:T(8,128)(2,1)S(1)}, u32[]{:S(2)}, u32[]{:S(2)}) collective-permute-start(bf16[32,1280]{1,0:T(8,128)(2,1)S(1)} %get-tuple-element.37), channel_id=1, source_target_pairs={{1,0},{2,1},{3,2},{0,3},{5,4},{6,5},{7,6},{4,7},{9,8},{10,9},{11,1... | collective-permute-start | bytes 245768 | tf_op jit(solution)/shard_map/ppermute | solution.py:21
  15.4 2.7 %collective-permute-start.3 = (bf16[32,1280]{1,0:T(8,128)(2,1)S(1)}, bf16[32,1280]{1,0:T(8,128)(2,1)S(1)}, u32[]{:S(2)}, u32[]{:S(2)}) collective-permute-start(bf16[32,1280]{1,0:T(8,128)(2,1)S(1)} %get-tuple-element.38), channel_id=1, source_target_pairs={{4,0},{8,4},{12,8},{0,12},{5,1},{9,5},{13,9},{1,13},{6,2},{10,6},{... | collective-permute-start | bytes 245768 | tf_op jit(solution)/shard_map/ppermute | solution.py:21
  20.0 3.3 %collective-permute-done.4 = bf16[32,1280]{1,0:T(8,128)(2,1)S(1)} collective-permute-done((bf16[32,1280]{1,0:T(8,128)(2,1)S(1)}, bf16[32,1280]{1,0:T(8,128)(2,1)S(1)}, u32[]{:S(2)}, u32[]{:S(2)}) %collective-permute-start.4) | collective-permute-done | bytes 81952 | tf_op jit(solution)/shard_map/ppermute | solution.py:21
  23.3 0.9 collective-permute-done.5
  24.2 1.9 %collective-permute-start.10 = (bf16[4,32,1280]{2,1,0:T(8,128)(2,1)S(1)}, bf16[4,32,1280]{2,1,0:T(8,128)(2,1)S(1)}, u32[]{:S(2)}, u32[]{:S(2)}) collective-permute-start(bf16[4,32,1280]{2,1,0:T(8,128)(2,1)S(1)} %pad_maximum_fusion.2.by_y), channel_id=1, source_target_pairs={{2,0},{3,1},{0,2},{1,3},{6,4},{7,5},{4,6},{5,7},{10,8},{11,9},{8,1... | collective-permute-start | bytes 983048 | tf_op jit(solution)/shard_map/ppermute | solution.py:21
  26.9 1.9 %collective-permute-start.9 = (bf16[4,32,1280]{2,1,0:T(8,128)(2,1)S(1)}, bf16[4,32,1280]{2,1,0:T(8,128)(2,1)S(1)}, u32[]{:S(2)}, u32[]{:S(2)}) collective-permute-start(bf16[4,32,1280]{2,1,0:T(8,128)(2,1)S(1)} %pad_maximum_fusion.2.by_y), channel_id=1, source_target_pairs={{1,0},{2,1},{3,2},{0,3},{5,4},{6,5},{7,6},{4,7},{9,8},{10,9},{11,1... | collective-permute-start | bytes 983048 | tf_op jit(solution)/shard_map/ppermute | solution.py:21
  29.6 2.5 %collective-permute-done.10.x2 = bf16[4,32,1280]{2,1,0:T(8,128)(2,1)S(1)} collective-permute-done((bf16[4,32,1280]{2,1,0:T(8,128)(2,1)S(1)}, bf16[4,32,1280]{2,1,0:T(8,128)(2,1)S(1)}, u32[]{:S(2)}, u32[]{:S(2)}) %collective-permute-start.10) | collective-permute-done | bytes 327712 | tf_op jit(solution)/shard_map/ppermute | solution.py:21
  32.1 9.6 %collective-permute-done.11.x3 = bf16[4,32,1280]{2,1,0:T(8,128)(2,1)S(1)} collective-permute-done((bf16[4,32,1280]{2,1,0:T(8,128)(2,1)S(1)}, bf16[4,32,1280]{2,1,0:T(8,128)(2,1)S(1)}, u32[]{:S(2)}, u32[]{:S(2)}) %collective-permute-start.11) | collective-permute-done | bytes 327712 | tf_op jit(solution)/shard_map/ppermute | solution.py:21
  41.8 1.4 collective-permute-done.8.y3
  43.9 4.7 %collective-permute-start.12 = (bf16[512,1024]{1,0:T(8,128)(2,1)S(1)}, bf16[512,1024]{1,0:T(8,128)(2,1)S(1)}, u32[]{:S(2)}, u32[]{:S(2)}) collective-permute-start(bf16[512,1024]{1,0:T(8,128)(2,1)S(1)} %bitcast.28), channel_id=1, source_target_pairs={{16,0},{0,16},{17,1},{1,17},{18,2},{2,18},{19,3},{3,19},{20,4},{4,... | collective-permute-start | bytes 3145736 | tf_op jit(solution)/shard_map/ppermute | solution.py:21
  48.6 1.0 copy-done.1
  50.5 1.2 collective-permute-done.13.more
  51.7 3.9 %shard_map.30 = (f32[1024,1024]{1,0:T(8,128)S(1)}, f32[16,24,128]{2,1,0:T(8,128)S(1)}) custom-call(bf16[512,1024]{1,0:T(8,128)(2,1)S(1)} %bitcast.29, bf16[512,1024]{1,0:T(8,128)(2,1)S(1)} %collective-permute-done.12.other, bf16[1024,1024]{1,0:T(8,128)(2,1)S(1)} %get-tuple-element.53.cols, f32[8,128]{1,0:T(8,128)S(1)} %get-tuple-element.54.sq, ...), custom_call_target="tpu_custom_call" | custom-call | flops 2147483648 | bytes 8622080 | tf_op jit(solution)/shard_map/pallas_call | solution.py:37
  55.6 17.4 %all_to_all.35.got = f32[16,24,128]{2,1,0:T(8,128)S(1)} all-to-all(f32[16,24,128]{2,1,0:T(8,128)S(1)} %get-tuple-element.57), channel_id=1, replica_groups=mesh['row_0'=8,'row_1'=2,'col_0'=4,'col_1'=4] {'row_0','row_1'}, dimensions={0} | all-to-all | bytes 393216 | tf_op jit(solution)/shard_map/all_to_all | solution.py:276
  73.1 12.2 %all_to_all.36.got = f32[16,40,128]{2,1,0:T(8,128)S(1)} all-to-all(f32[16,40,128]{2,1,0:T(8,128)S(1)} %get-tuple-element.59), channel_id=1, replica_groups=mesh['row_0'=8,'row_1'=2,'col_0'=4,'col_1'=4] {'col_0','col_1'}, dimensions={0} | all-to-all | bytes 655360 | tf_op jit(solution)/shard_map/all_to_all | solution.py:279
  85.4 0.8 shard_map.33
  86.2 1.2 collective-permute-start.14
  87.4 0.9 shard_map.32
  89.0 14.8 %all_to_all.37 = f16[8,64,256]{2,1,0:T(8,128)(2,1)S(1)} all-to-all(f16[8,64,256]{2,1,0:T(8,128)(2,1)S(1)} %bitcast.35), channel_id=1, replica_groups=mesh['row_0'=8,'row_1'=2,'col_0'=4,'col_1'=4] {'row_0'}, dimensions={0} | all-to-all | bytes 524288 | tf_op jit(solution)/shard_map/all_to_all | solution.py:297
  103.8 1.1 shard_map.34
  105.0 3.6 %all-to-all-start.4 = ((bf16[16,64,256]{2,1,0:T(8,128)(2,1)}), bf16[16,64,256]{2,1,0:T(8,128)(2,1)S(1)}, u32[]{:S(2)}, u32[]{:S(2)}) async-start(bf16[16,64,256]{2,1,0:T(8,128)(2,1)} %get-tuple-element.66), calls=%async_computation.4 | async-start | bytes 1048576 | tf_op jit(solution)/shard_map/all_to_all | solution.py:309
  108.5 10.8 %all-to-all-done.4 = bf16[16,64,256]{2,1,0:T(8,128)(2,1)S(1)} async-done(((bf16[16,64,256]{2,1,0:T(8,128)(2,1)}), bf16[16,64,256]{2,1,0:T(8,128)(2,1)S(1)}, u32[]{:S(2)}, u32[]{:S(2)}) %all-to-all-start.4) | async-done | bytes 524320 | tf_op jit(solution)/shard_map/all_to_all | solution.py:309
  120.2 1.7 %collective-permute-start.15 = (f32[528,256]{1,0:T(8,128)S(1)}, f32[528,256]{1,0:T(8,128)S(1)}, u32[]{:S(2)}, u32[]{:S(2)}) collective-permute-start(f32[528,256]{1,0:T(8,128)S(1)} %pad_maximum_fusion), channel_id=1, source_target_pairs={{16,0},{0,16},{17,1},{1,17},{18,2},{2,18},{19,3},{3,19},{20,4},{4,... | collective-permute-start | bytes 1622024 | tf_op jit(solution)/shard_map/ppermute | solution.py:21
  121.9 1.6 %collective-permute-done.15 = f32[528,256]{1,0:T(8,128)S(1)} collective-permute-done((f32[528,256]{1,0:T(8,128)S(1)}, f32[528,256]{1,0:T(8,128)S(1)}, u32[]{:S(2)}, u32[]{:S(2)}) %collective-permute-start.15) | collective-permute-done | bytes 540704 | tf_op jit(solution)/shard_map/ppermute | solution.py:21
  124.0 16.1 %all_to_all.38 = f16[8,80,256]{2,1,0:T(8,128)(2,1)S(1)} all-to-all(f16[8,80,256]{2,1,0:T(8,128)(2,1)S(1)} %pad_maximum_fusion.3), channel_id=1, replica_groups=mesh['row_0'=8,'row_1'=2,'col_0'=4,'col_1'=4] {'row_0'}, dimensions={0} | all-to-all | bytes 655360 | tf_op jit(solution)/shard_map/all_to_all | solution.py:297
  141.0 3.5 %all-to-all-start.6 = ((f32[16,16,256]{2,1,0:T(8,128)}), f32[16,16,256]{2,1,0:T(8,128)S(1)}, u32[]{:S(2)}, u32[]{:S(2)}) async-start(f32[16,16,256]{2,1,0:T(8,128)} %broadcast_in_dim.7), calls=%async_computation.6 | async-start | bytes 524288 | tf_op jit(solution)/shard_map/all_to_all | solution.py:27
  144.5 8.3 %all-to-all-done.6 = f32[16,16,256]{2,1,0:T(8,128)S(1)} async-done(((f32[16,16,256]{2,1,0:T(8,128)}), f32[16,16,256]{2,1,0:T(8,128)S(1)}, u32[]{:S(2)}, u32[]{:S(2)}) %all-to-all-start.6) | async-done | bytes 262176 | tf_op jit(solution)/shard_map/all_to_all | solution.py:27
  152.8 0.9 shard_map.35
  (46 shorter events, 9.4 us)
Async XLA Ops:
  0.0 0.8 copy-start.2
  0.8 0.9 copy-start.4
  2.8 41.1 %all-to-all-start = ((bf16[8,64,1024]{2,1,0:T(8,128)(2,1)}), bf16[8,64,1024]{2,1,0:T(8,128)(2,1)S(1)}, u32[]{:S(2)}, u32[]{:S(2)}) async-start(bf16[8,64,1024]{2,1,0:T(8,128)(2,1)} %get-tuple-element.45), calls=%async_computation | async-start | bytes 2097152 | tf_op jit(solution)/shard_map/all_to_all | solution.py:237
  11.8 6.7 %collective-permute-start = (bf16[32,1280]{1,0:T(8,128)(2,1)S(1)}, bf16[32,1280]{1,0:T(8,128)(2,1)S(1)}, u32[]{:S(2)}, u32[]{:S(2)}) collective-permute-start(bf16[32,1280]{1,0:T(8,128)(2,1)S(1)} %get-tuple-element.37), channel_id=1, source_target_pairs={{1,0},{2,1},{3,2},{0,3},{5,4},{6,5},{7,6},{4,7},{9,8},{10,9},{11,1... | collective-permute-start | bytes 245768 | tf_op jit(solution)/shard_map/ppermute | solution.py:21
  14.3 4.9 %collective-permute-start.1 = (bf16[32,1280]{1,0:T(8,128)(2,1)S(1)}, bf16[32,1280]{1,0:T(8,128)(2,1)S(1)}, u32[]{:S(2)}, u32[]{:S(2)}) collective-permute-start(bf16[32,1280]{1,0:T(8,128)(2,1)S(1)} %get-tuple-element.37), channel_id=1, source_target_pairs={{2,0},{3,1},{0,2},{1,3},{6,4},{7,5},{4,6},{5,7},{10,8},{11,9},{8,1... | collective-permute-start | bytes 245768 | tf_op jit(solution)/shard_map/ppermute | solution.py:21
  14.8 5.2 %collective-permute-start.2 = (bf16[32,1280]{1,0:T(8,128)(2,1)S(1)}, bf16[32,1280]{1,0:T(8,128)(2,1)S(1)}, u32[]{:S(2)}, u32[]{:S(2)}) collective-permute-start(bf16[32,1280]{1,0:T(8,128)(2,1)S(1)} %get-tuple-element.37), channel_id=1, source_target_pairs={{3,0},{0,1},{1,2},{2,3},{7,4},{4,5},{5,6},{6,7},{11,8},{8,9},{9,10... | collective-permute-start | bytes 245768 | tf_op jit(solution)/shard_map/ppermute | solution.py:21
  15.4 4.5 %collective-permute-start.3 = (bf16[32,1280]{1,0:T(8,128)(2,1)S(1)}, bf16[32,1280]{1,0:T(8,128)(2,1)S(1)}, u32[]{:S(2)}, u32[]{:S(2)}) collective-permute-start(bf16[32,1280]{1,0:T(8,128)(2,1)S(1)} %get-tuple-element.38), channel_id=1, source_target_pairs={{4,0},{8,4},{12,8},{0,12},{5,1},{9,5},{13,9},{1,13},{6,2},{10,6},{... | collective-permute-start | bytes 245768 | tf_op jit(solution)/shard_map/ppermute | solution.py:21
  18.2 5.1 %collective-permute-start.4 = (bf16[32,1280]{1,0:T(8,128)(2,1)S(1)}, bf16[32,1280]{1,0:T(8,128)(2,1)S(1)}, u32[]{:S(2)}, u32[]{:S(2)}) collective-permute-start(bf16[32,1280]{1,0:T(8,128)(2,1)S(1)} %get-tuple-element.38), channel_id=1, source_target_pairs={{8,0},{12,4},{0,8},{4,12},{9,1},{13,5},{1,9},{5,13},{10,2},{14,6},... | collective-permute-start | bytes 245768 | tf_op jit(solution)/shard_map/ppermute | solution.py:21
  18.5 5.6 %collective-permute-start.5 = (bf16[32,1280]{1,0:T(8,128)(2,1)S(1)}, bf16[32,1280]{1,0:T(8,128)(2,1)S(1)}, u32[]{:S(2)}, u32[]{:S(2)}) collective-permute-start(bf16[32,1280]{1,0:T(8,128)(2,1)S(1)} %get-tuple-element.38), channel_id=1, source_target_pairs={{12,0},{0,4},{4,8},{8,12},{13,1},{1,5},{5,9},{9,13},{14,2},{2,6},{... | collective-permute-start | bytes 245768 | tf_op jit(solution)/shard_map/ppermute | solution.py:21
  24.2 7.9 %collective-permute-start.10 = (bf16[4,32,1280]{2,1,0:T(8,128)(2,1)S(1)}, bf16[4,32,1280]{2,1,0:T(8,128)(2,1)S(1)}, u32[]{:S(2)}, u32[]{:S(2)}) collective-permute-start(bf16[4,32,1280]{2,1,0:T(8,128)(2,1)S(1)} %pad_maximum_fusion.2.by_y), channel_id=1, source_target_pairs={{2,0},{3,1},{0,2},{1,3},{6,4},{7,5},{4,6},{5,7},{10,8},{11,9},{8,1... | collective-permute-start | bytes 983048 | tf_op jit(solution)/shard_map/ppermute | solution.py:21
  26.1 15.6 %collective-permute-start.11 = (bf16[4,32,1280]{2,1,0:T(8,128)(2,1)S(1)}, bf16[4,32,1280]{2,1,0:T(8,128)(2,1)S(1)}, u32[]{:S(2)}, u32[]{:S(2)}) collective-permute-start(bf16[4,32,1280]{2,1,0:T(8,128)(2,1)S(1)} %pad_maximum_fusion.2.by_y), channel_id=1, source_target_pairs={{3,0},{0,1},{1,2},{2,3},{7,4},{4,5},{5,6},{6,7},{11,8},{8,9},{9,10... | collective-permute-start | bytes 983048 | tf_op jit(solution)/shard_map/ppermute | solution.py:21
  26.9 14.8 %collective-permute-start.9 = (bf16[4,32,1280]{2,1,0:T(8,128)(2,1)S(1)}, bf16[4,32,1280]{2,1,0:T(8,128)(2,1)S(1)}, u32[]{:S(2)}, u32[]{:S(2)}) collective-permute-start(bf16[4,32,1280]{2,1,0:T(8,128)(2,1)S(1)} %pad_maximum_fusion.2.by_y), channel_id=1, source_target_pairs={{1,0},{2,1},{3,2},{0,3},{5,4},{6,5},{7,6},{4,7},{9,8},{10,9},{11,1... | collective-permute-start | bytes 983048 | tf_op jit(solution)/shard_map/ppermute | solution.py:21
  28.8 12.9 %collective-permute-start.6 = (bf16[4,32,1280]{2,1,0:T(8,128)(2,1)S(1)}, bf16[4,32,1280]{2,1,0:T(8,128)(2,1)S(1)}, u32[]{:S(2)}, u32[]{:S(2)}) collective-permute-start(bf16[4,32,1280]{2,1,0:T(8,128)(2,1)S(1)} %pad_maximum_fusion.1.by_x), channel_id=1, source_target_pairs={{4,0},{8,4},{12,8},{0,12},{5,1},{9,5},{13,9},{1,13},{6,2},{10,6},{... | collective-permute-start | bytes 983048 | tf_op jit(solution)/shard_map/ppermute | solution.py:21
  29.2 12.6 %collective-permute-start.7 = (bf16[4,32,1280]{2,1,0:T(8,128)(2,1)S(1)}, bf16[4,32,1280]{2,1,0:T(8,128)(2,1)S(1)}, u32[]{:S(2)}, u32[]{:S(2)}) collective-permute-start(bf16[4,32,1280]{2,1,0:T(8,128)(2,1)S(1)} %pad_maximum_fusion.1.by_x), channel_id=1, source_target_pairs={{8,0},{12,4},{0,8},{4,12},{9,1},{13,5},{1,9},{5,13},{10,2},{14,6},... | collective-permute-start | bytes 983048 | tf_op jit(solution)/shard_map/ppermute | solution.py:21
  32.1 11.0 %collective-permute-start.8 = (bf16[4,32,1280]{2,1,0:T(8,128)(2,1)S(1)}, bf16[4,32,1280]{2,1,0:T(8,128)(2,1)S(1)}, u32[]{:S(2)}, u32[]{:S(2)}) collective-permute-start(bf16[4,32,1280]{2,1,0:T(8,128)(2,1)S(1)} %pad_maximum_fusion.1.by_x), channel_id=1, source_target_pairs={{12,0},{0,4},{4,8},{8,12},{13,1},{1,5},{5,9},{9,13},{14,2},{2,6},{... | collective-permute-start | bytes 983048 | tf_op jit(solution)/shard_map/ppermute | solution.py:21
  43.2 0.7 copy-start
  43.9 7.8 %collective-permute-start.12 = (bf16[512,1024]{1,0:T(8,128)(2,1)S(1)}, bf16[512,1024]{1,0:T(8,128)(2,1)S(1)}, u32[]{:S(2)}, u32[]{:S(2)}) collective-permute-start(bf16[512,1024]{1,0:T(8,128)(2,1)S(1)} %bitcast.28), channel_id=1, source_target_pairs={{16,0},{0,16},{17,1},{1,17},{18,2},{2,18},{19,3},{3,19},{20,4},{4,... | collective-permute-start | bytes 3145736 | tf_op jit(solution)/shard_map/ppermute | solution.py:21
  48.6 1.0 copy-start.1
  50.3 1.4 collective-permute-start.13
  86.2 17.6 %copy-start.3 = (f32[64,256]{1,0:T(8,128)S(1)}, f32[64,256]{1,0:T(8,128)}, u32[]{:S(2)}) copy-start(f32[64,256]{1,0:T(8,128)} %h_ref.1) | copy-start | bytes 196612
  86.2 2.7 %collective-permute-start.14 = (f32[512,256]{1,0:T(8,128)S(1)}, f32[512,256]{1,0:T(8,128)S(1)}, u32[]{:S(2)}, u32[]{:S(2)}) collective-permute-start(f32[512,256]{1,0:T(8,128)S(1)} %get-tuple-element.63), channel_id=1, source_target_pairs={{16,0},{0,16},{17,1},{1,17},{18,2},{2,18},{19,3},{3,19},{20,4},{4,... | collective-permute-start | bytes 1572872 | tf_op jit(solution)/shard_map/ppermute | solution.py:21
  105.0 14.4 %all-to-all-start.4 = ((bf16[16,64,256]{2,1,0:T(8,128)(2,1)}), bf16[16,64,256]{2,1,0:T(8,128)(2,1)S(1)}, u32[]{:S(2)}, u32[]{:S(2)}) async-start(bf16[16,64,256]{2,1,0:T(8,128)(2,1)} %get-tuple-element.66), calls=%async_computation.4 | async-start | bytes 1048576 | tf_op jit(solution)/shard_map/all_to_all | solution.py:309
  120.2 3.3 %collective-permute-start.15 = (f32[528,256]{1,0:T(8,128)S(1)}, f32[528,256]{1,0:T(8,128)S(1)}, u32[]{:S(2)}, u32[]{:S(2)}) collective-permute-start(f32[528,256]{1,0:T(8,128)S(1)} %pad_maximum_fusion), channel_id=1, source_target_pairs={{16,0},{0,16},{17,1},{1,17},{18,2},{2,18},{19,3},{3,19},{20,4},{4,... | collective-permute-start | bytes 1622024 | tf_op jit(solution)/shard_map/ppermute | solution.py:21
  141.0 11.8 %all-to-all-start.6 = ((f32[16,16,256]{2,1,0:T(8,128)}), f32[16,16,256]{2,1,0:T(8,128)S(1)}, u32[]{:S(2)}, u32[]{:S(2)}) async-start(f32[16,16,256]{2,1,0:T(8,128)} %broadcast_in_dim.7), calls=%async_computation.6 | async-start | bytes 524288 | tf_op jit(solution)/shard_map/all_to_all | solution.py:27

commit v5 on v4

--- a/solution.py
+++ b/solution.py
@@ -32,12 +32,12 @@
 LANES = 128
 
 
-def call(kernel, outs, args, flops, scratch=(), vmem=24):
+def call(kernel, outs, args, flops, scratch=(), vmem=10, place=pltpu.VMEM):
     size = sum(math.prod(a.shape) * a.dtype.itemsize for a in (*outs, *args))
     return pl.pallas_call(
         kernel,
         out_shape=outs,
-        in_specs=[VMEM] * len(args),
+        in_specs=[pl.BlockSpec(memory_space=place)] * len(args),
         out_specs=[VMEM] * len(outs),
         scratch_shapes=list(scratch),
         compiler_params=pltpu.CompilerParams(vmem_limit_bytes=vmem << 20),
@@ -55,23 +55,30 @@
     return sum(g * g for g in groups)
 
 
-def columns_kernel(by_x, y1, y2, y3, by_y, x1, x2, x3, pts_ref, hb_ref, sq_ref, part_ref, gram_ref):
+def columns_kernel(
+    ax0, ax1, ax2, ax3, y1, y2, y3, by0, by1, by2, by3, x1, x2, x3, pts_ref, hb_ref, sq_ref, part_ref, gram_ref
+):
     ny, nx = lax.axis_size(Y), lax.axis_size(X)
     y, x = lax.axis_index(Y), lax.axis_index(X)
-    half = by_x.shape[1]
+    half = ax0.shape[0]
     width = pts_ref.shape[1]
-    for far, ref in enumerate((by_x, y1, y2, y3)):
+
+    def put(far, near, lower, value):
+        at = (lax.rem(y + far, ny) * nx + lax.rem(x + near, nx)) * 2 * half + lower
+        at = pl.ds(pl.multiple_of(at, half), half)
+        pts_ref[at, :] = value[:, :width]
+        hb_ref[at, :] = value[:, width:]
+
+    for near, ref in enumerate((ax0, ax1, ax2, ax3)):
+        put(0, near, 0, ref[...])
+    for far, ref in enumerate((by0, by1, by2, by3)):
+        put(far, 0, half, ref[...])
+    for far, ref in enumerate((y1, y2, y3)):
         for near in range(nx):
-            at = lax.rem(y + far, ny) * nx + lax.rem(x + near, nx)
-            at = pl.multiple_of(at * 2 * half, half)
-            pts_ref[pl.ds(at, half), :] = ref[near, :, :width]
-            hb_ref[pl.ds(at, half), :] = ref[near, :, width:]
-    for far, ref in enumerate((by_y, x1, x2, x3)):
-        for near in range(ny):
-            at = lax.rem(y + near, ny) * nx + lax.rem(x + far, nx)
-            at = pl.multiple_of(at * 2 * half + half, half)
-            pts_ref[pl.ds(at, half), :] = ref[near, :, :width]
-            hb_ref[pl.ds(at, half), :] = ref[near, :, width:]
+            put(far + 1, near, 0, ref[near])
+    for near, ref in enumerate((x1, x2, x3)):
+        for far in range(ny):
+            put(far, near + 1, half, ref[far])
     for block in range(pts_ref.shape[0] // LANES):
         sums = squares(pts_ref[block * LANES : (block + 1) * LANES, :])
         sq_ref[block : block + 1, :] = jnp.sum(sums.T, axis=0, keepdims=True)
@@ -83,38 +90,43 @@
     part_ref[...] = gram_ref[pl.ds(at, part), :]
 
 
-def rows_kernel(own, other, cols, sq, part, more, kern, out, sums):
-    core = lax.axis_index(CORE)
+def rows_kernel(rows_ref, cols, sq, kern, sums):
     col_sq = jnp.concatenate([sq[g : g + 1, :] for g in range(sq.shape[0])], axis=1)
     tall = 2 * LANES
 
-    def block(ref, first, i):
-        rows = ref[pl.ds(pl.multiple_of(i * tall, tall), tall), :]
-        at = first * ref.shape[0] // tall + i
+    def block(i, _):
+        at = pl.ds(pl.multiple_of(i * tall, tall), tall)
+        rows = rows_ref[at, :]
         row_sq = jnp.sum(squares(rows), axis=1, keepdims=True)
         gram = rows_dot(rows, cols[...])
         values = jnp.exp((2.0 * gram - row_sq - col_sq) * (0.5 / EMBED_WIDTH))
-        kern[pl.ds(pl.multiple_of(at * tall, tall), tall), :] = values
+        kern[at, :] = values
         total = sum(values[:, g : g + LANES] for g in range(0, values.shape[1], LANES))
         for j in range(2):
             line = jnp.sum(total[j * LANES : (j + 1) * LANES].T, axis=0, keepdims=True)
-            sums[pl.ds(at * 2 + j, 1), :] = line
-
-    for ref, first in ((own, core), (other, 1 - core)):
-
-        def body(i, _, ref=ref, first=first):
-            block(ref, first, i)
-            return 0
-
-        lax.fori_loop(0, ref.shape[0] // tall, body, 0)
-    lines = sums.shape[0]
+            sums[pl.ds(i * 2 + j, 1), :] = line
+        return 0
+
+    lax.fori_loop(0, rows_ref.shape[0] // tall, block, 0)
+
+
+def last_rows_kernel(rows_ref, cols, sq, own_sums, part, more, kern, out, sums):
+    rows_kernel(rows_ref, cols, sq, kern, sums)
+    core = lax.axis_index(CORE)
+    mine = own_sums[...]
+    theirs = sums[...]
+    lines = 2 * mine.shape[0]
     deep = part.shape[0] // 2
     at = pl.ds(pl.multiple_of(core * deep, deep), deep)
-    mine = part[at, :] + more[at, :]
+    gram = part[at, :] + more[at, :]
+    swap = core == 1
+    both = jnp.concatenate(
+        [jnp.where(swap, theirs, mine), jnp.where(swap, mine, theirs)], axis=0
+    )
     for i in range(out.shape[0]):
-        out[i, :lines] = sums[...]
-        out[i, lines : lines + deep] = mine[:, :LANES]
-        out[i, lines + deep :] = mine[:, LANES:]
+        out[i, :lines] = both
+        out[i, lines : lines + deep] = gram[:, :LANES]
+        out[i, lines + deep :] = gram[:, LANES:]
 
 
 def means_kernel(got, mean_ref, out):
@@ -160,15 +172,14 @@
             pair.append(jnp.where(odd if j == 0 else jnp.logical_not(odd), swapped, line))
         places.append(jnp.where(lane < LANES // 2, pair[0], pair[1]))
     lines = mean_ref.shape[0] // 2
-    rows = aff.shape[0]
     for i in range(lines):
         line = mean_ref[pl.ds(which * lines + i, 1), :]
         mine = jnp.broadcast_to(line, (LANES, LANES)).T
-        at = pl.ds(pl.multiple_of(which * rows + i * LANES, LANES), LANES)
+        at = slice(i * LANES, (i + 1) * LANES)
         for g, place in enumerate(places):
             values = kern[at, g * LANES : (g + 1) * LANES]
             values = values - mine - place + grand
-            aff[i * LANES : (i + 1) * LANES, g * LANES : (g + 1) * LANES] = values.astype(BF16)
+            aff[at, g * LANES : (g + 1) * LANES] = values.astype(BF16)
     partial[...] = jnp.dot(aff[...], hb[...], preferred_element_type=F32)
     if more:
         hh_ref, scales = more
@@ -193,15 +204,24 @@
     return 0.5 / jnp.sqrt(square + 1e-06)
 
 
-def start_kernel(unit, points, factor, first, second, copies):
+def start_kernel(unit, points, factor, first, second, copies, wide, done):
     half, width = first.shape[0], points.shape[1]
-    hb = (factor[...] * unit).astype(BF16)
-    first[:, :width] = points[:half, :]
+    fetches = [
+        pltpu.make_async_copy(points, copies.at[0], done.at[0]),
+        pltpu.make_async_copy(factor, wide, done.at[1]),
+    ]
+    for fetch in fetches:
+        fetch.start()
+    for fetch in fetches:
+        fetch.wait()
+    value = copies[0]
+    hb = (wide[...] * unit).astype(BF16)
+    first[:, :width] = value[:half]
     first[:, width:] = hb[:half]
-    second[:, :width] = points[half:, :]
+    second[:, :width] = value[half:]
     second[:, width:] = hb[half:]
-    for i in range(copies.shape[0]):
-        copies[i] = points[...]
+    for i in range(1, copies.shape[0]):
+        copies[i] = value
 
 
 def step_kernel(before, after, ah_ref, hh_ref, h_ref, out, *copies):
@@ -232,6 +252,9 @@
         [*[shape((half, width + rank), BF16)] * 2, shape((nz, pts, width), BF16)],
         [points, factor],
         1,
+        [pltpu.VMEM((pts, rank), F32), pltpu.SemaphoreType.DMA((2,))],
+        vmem=60,
+        place=pl.ANY,
     )
     tie = lax.optimization_barrier
     along_z = lax.all_to_all(copies, Z, 0, 0, tiled=True)
@@ -243,9 +266,7 @@
     by_y = jnp.stack([second, y1, y2, y3])
     from_y = [from_ahead(by_x, Y, s) for s in (1, 2, 3)]
     from_x = [from_ahead(by_y, X, s) for s in (1, 2, 3)]
-    from_y, from_x, along_z = tie((from_y, from_x, along_z.reshape(-1, width)))
-    cols = [by_x, *from_y, by_y, *from_x]
-    other = from_ahead(along_z, CORE, 1)
+    cols = [first, x1, x2, x3, *from_y, second, y1, y2, y3, *from_x]
 
     part = rank // ncol
     group = nrow * pts
@@ -261,14 +282,22 @@
         2 * group * rank * rank,
         [pltpu.VMEM((rank, rank), F32)],
     )
+    own_part, along_z = tie((own_part, along_z.reshape(-1, width)))
+    other = from_ahead(along_z, CORE, 1)
     more_part = from_ahead(own_part, CORE, 1)
     lines = group // LANES
-    kern, message = call(
+    own_kern, own_sums = call(
         rows_kernel,
-        [shape((group, group), F32), shape((nrow, lines + part, LANES), F32)],
-        [along_z, other, col_pts, col_sq, own_part, more_part],
-        2 * group * group * width,
-        [pltpu.VMEM((lines, LANES), F32)],
+        [shape((group // 2, group), F32), shape((lines // 2, LANES), F32)],
+        [along_z, col_pts, col_sq],
+        group * group * width,
+    )
+    other_kern, message = call(
+        last_rows_kernel,
+        [shape((group // 2, group), F32), shape((nrow, lines + part, LANES), F32)],
+        [other, col_pts, col_sq, own_sums, own_part, more_part],
+        group * group * width,
+        [pltpu.VMEM((lines // 2, LANES), F32)],
     )
     mean_rows, message = call(
         means_kernel,
@@ -285,7 +314,7 @@
         return call(
             functools.partial(centred_kernel, own),
             outs,
-            [kern, mean_rows, gathered, hb_cols],
+            [own_kern if own else other_kern, mean_rows, gathered, hb_cols],
             group * group * rank,
         )
 

time: 154 us -> 155 us (level)
  waiting for transfers between devices: 40.9 us -> 38 us
  blocking collectives: 60.5 us -> 63.3 us
    ppermute x16, waiting for transfers between devices: 21.8 us -> 19 us  [from_ahead(): lax.ppermute(value, axis, [((i + steps) % length, i) for i in range(lengt...]
    all_to_all x1, blocking collectives: 12.2 us -> 15 us  [shards(): gathered = lax.all_to_all(message, COL, 0, 0, tiled=True)]
    pallas_call x8 -> x9, Pallas kernels: 9.54 us -> 10.5 us  [call(): pl.pallas_call(kernel, out_shape=outs, in_specs=[pl.BlockSpec(memory_spac...]
  transfers between devices with their start and end apart: 19 -> 19, of which waited for: 11 -> 10; matrix products, arithmetic and copies ran while one was open for 0% -> 0% of each run, Pallas kernels for 1% -> 2%
where the time goes in v5:
time: 155 us
  blocking collectives  63.3 us (41%)
  waiting for transfers between devices  38 us (25%)
  starting transfers between devices  37.1 us (24%)
  Pallas kernels  10.5 us (7%)
  local copies, waits for them, and re-layouts  3.71 us (2%)
    all_to_all x2, blocking collectives, over_z(): mine = lax.all_to_all(mine.astype(jnp.float16), Z, 0, 0, tiled=True)  30.9 us
    ppermute x16, starting transfers between devices, from_ahead(): lax.ppermute(value, axis, [((i + steps) % length, i) for i in range(lengt...  20.8 us
    ppermute x16, waiting for transfers between devices, from_ahead(): lax.ppermute(value, axis, [((i + steps) % length, i) for i in range(lengt...  19 us
    all_to_all x1, blocking collectives, shards(): lax.all_to_all(message, ROW, 0, 0, tiled=True)  17.5 us
    all_to_all x1, blocking collectives, shards(): gathered = lax.all_to_all(message, COL, 0, 0, tiled=True)  15 us
    all_to_all x1, waiting for transfers between devices, shards(): lax.all_to_all(hb_cols, COL, 0, 0, tiled=True).reshape(group, rank)  10.8 us
    pallas_call x9, Pallas kernels, call(): pl.pallas_call(kernel, out_shape=outs, in_specs=[pl.BlockSpec(memory_spac...  10.5 us
    all_to_all x1, starting transfers between devices, shards(): along_z = lax.all_to_all(copies, Z, 0, 0, tiled=True)  9.16 us
  transfers between devices with their start and end apart: 19, of which 10 were waited for; matrix products, arithmetic and copies ran while one was open for 0% of the time, Pallas kernels for 2%

profile of v5, /device:TPU:1, one launch (start us, length us, event | category | flops | bytes accessed | tf_op | source)
XLA Modules:
  0.0 154.6 jit_solution(8218753547583019424)
XLA Ops:
  0.0 2.0 %shard_map.28 = (bf16[32,1280]{1,0:T(8,128)(2,1)}, bf16[32,1280]{1,0:T(8,128)(2,1)}, bf16[8,64,1024]{2,1,0:T(8,128)(2,1)}) custom-call(bf16[64,1024]{1,0:T(8,128)(2,1)} %points.1, f32[64,256]{1,0:T(8,128)} %h_ref.1), custom_call_target="tpu_custom_call" | custom-call | flops 1 | bytes 1409024 | tf_op jit(solution)/shard_map/pallas_call | solution.py:37
  2.0 9.2 %all-to-all-start = ((bf16[8,64,1024]{2,1,0:T(8,128)(2,1)}), bf16[8,64,1024]{2,1,0:T(8,128)(2,1)S(1)}, u32[]{:S(2)}, u32[]{:S(2)}) async-start(bf16[8,64,1024]{2,1,0:T(8,128)(2,1)} %get-tuple-element.43), calls=%async_computation | async-start | bytes 2097152 | tf_op jit(solution)/shard_map/all_to_all | solution.py:260
  11.2 2.6 %collective-permute-start = (bf16[32,1280]{1,0:T(8,128)(2,1)S(1)}, bf16[32,1280]{1,0:T(8,128)(2,1)S(1)}, u32[]{:S(2)}, u32[]{:S(2)}) collective-permute-start(bf16[32,1280]{1,0:T(8,128)(2,1)S(1)} %copy-done), channel_id=1, source_target_pairs={{1,0},{2,1},{3,2},{0,3},{5,4},{6,5},{7,6},{4,7},{9,8},{10,9},{11,1... | collective-permute-start | bytes 245768 | tf_op jit(solution)/shard_map/ppermute | solution.py:21
  14.9 2.7 %collective-permute-start.3 = (bf16[32,1280]{1,0:T(8,128)(2,1)S(1)}, bf16[32,1280]{1,0:T(8,128)(2,1)S(1)}, u32[]{:S(2)}, u32[]{:S(2)}) collective-permute-start(bf16[32,1280]{1,0:T(8,128)(2,1)S(1)} %copy-done.1), channel_id=1, source_target_pairs={{4,0},{8,4},{12,8},{0,12},{5,1},{9,5},{13,9},{1,13},{6,2},{10,6},{... | collective-permute-start | bytes 245768 | tf_op jit(solution)/shard_map/ppermute | solution.py:21
  19.4 3.3 %collective-permute-done.4.by2 = bf16[32,1280]{1,0:T(8,128)(2,1)S(1)} collective-permute-done((bf16[32,1280]{1,0:T(8,128)(2,1)S(1)}, bf16[32,1280]{1,0:T(8,128)(2,1)S(1)}, u32[]{:S(2)}, u32[]{:S(2)}) %collective-permute-start.4) | collective-permute-done | bytes 81952 | tf_op jit(solution)/shard_map/ppermute | solution.py:21
  22.7 0.9 collective-permute-done.5.by3
  24.4 0.8 collective-permute-start.8
  25.2 2.1 %collective-permute-start.9 = (bf16[4,32,1280]{2,1,0:T(8,128)(2,1)S(1)}, bf16[4,32,1280]{2,1,0:T(8,128)(2,1)S(1)}, u32[]{:S(2)}, u32[]{:S(2)}) collective-permute-start(bf16[4,32,1280]{2,1,0:T(8,128)(2,1)S(1)} %pad_maximum_fusion.2), channel_id=1, source_target_pairs={{1,0},{2,1},{3,2},{0,3},{5,4},{6,5},{7,6},{4,7},{9,8},{10,9},{11,1... | collective-permute-start | bytes 983048 | tf_op jit(solution)/shard_map/ppermute | solution.py:21
  27.4 1.2 collective-permute-start.10
  28.6 1.4 collective-permute-done.6.y1
  30.0 1.5 collective-permute-start.11
  31.8 10.2 %collective-permute-done.8.y3 = bf16[4,32,1280]{2,1,0:T(8,128)(2,1)S(1)} collective-permute-done((bf16[4,32,1280]{2,1,0:T(8,128)(2,1)S(1)}, bf16[4,32,1280]{2,1,0:T(8,128)(2,1)S(1)}, u32[]{:S(2)}, u32[]{:S(2)}) %collective-permute-start.8) | collective-permute-done | bytes 327712 | tf_op jit(solution)/shard_map/ppermute | solution.py:21
  42.7 1.3 copy-done.3
  44.1 4.0 %collective-permute-start.12 = (bf16[512,1024]{1,0:T(8,128)(2,1)S(1)}, bf16[512,1024]{1,0:T(8,128)(2,1)S(1)}, u32[]{:S(2)}, u32[]{:S(2)}) collective-permute-start(bf16[512,1024]{1,0:T(8,128)(2,1)S(1)} %bitcast.28), channel_id=1, source_target_pairs={{16,0},{0,16},{17,1},{1,17},{18,2},{2,18},{19,3},{3,19},{20,4},{4,... | collective-permute-start | bytes 3145736 | tf_op jit(solution)/shard_map/ppermute | solution.py:21
  48.1 1.6 %copy-done.4 = bf16[1024,1024]{1,0:T(8,128)(2,1)S(1)} copy-done((bf16[1024,1024]{1,0:T(8,128)(2,1)S(1)}, bf16[1024,1024]{1,0:T(8,128)(2,1)}, u32[]{:S(2)}) %copy-start.4) | copy-done | bytes 2097176
  49.7 1.9 %shard_map.30 = (f32[512,1024]{1,0:T(8,128)S(1)}, f32[4,128]{1,0:T(4,128)S(1)}) custom-call(bf16[512,1024]{1,0:T(8,128)(2,1)S(1)} %bitcast.29, bf16[1024,1024]{1,0:T(8,128)(2,1)S(1)} %copy-done.4, f32[8,128]{1,0:T(8,128)S(1)} %get-tuple-element.46.sq), custom_call_target="tpu_custom_call" | custom-call | flops 1073741824 | bytes 5249024 | tf_op jit(solution)/shard_map/pallas_call | solution.py:37
  51.7 2.0 %shard_map.31 = (f32[512,1024]{1,0:T(8,128)S(1)}, f32[16,24,128]{2,1,0:T(8,128)S(1)}) custom-call(bf16[512,1024]{1,0:T(8,128)(2,1)S(1)} %collective-permute-done.12.rows_ref, bf16[1024,1024]{1,0:T(8,128)(2,1)S(1)} %copy-done.4, f32[8,128]{1,0:T(8,128)S(1)} %get-tuple-element.46.sq, f32[4,128]{1,0:T(4,128)S(1)} %get-tuple-element.48.own_sums, ...), custom_call_target="tpu_custom_call" | custom-call | flops 1073741824 | bytes 5478400 | tf_op jit(solution)/shard_map/pallas_call | solution.py:37
  53.7 17.5 %all_to_all.35.got = f32[16,24,128]{2,1,0:T(8,128)S(1)} all-to-all(f32[16,24,128]{2,1,0:T(8,128)S(1)} %get-tuple-element.50), channel_id=1, replica_groups=mesh['row_0'=8,'row_1'=2,'col_0'=4,'col_1'=4] {'row_0','row_1'}, dimensions={0} | all-to-all | bytes 393216 | tf_op jit(solution)/shard_map/all_to_all | solution.py:305
  71.3 15.0 %all_to_all.36.got = f32[16,40,128]{2,1,0:T(8,128)S(1)} all-to-all(f32[16,40,128]{2,1,0:T(8,128)S(1)} %get-tuple-element.52), channel_id=1, replica_groups=mesh['row_0'=8,'row_1'=2,'col_0'=4,'col_1'=4] {'col_0','col_1'}, dimensions={0} | all-to-all | bytes 655360 | tf_op jit(solution)/shard_map/all_to_all | solution.py:308
  86.2 0.9 shard_map.34
  87.1 1.2 collective-permute-start.14
  88.3 0.9 shard_map.33
  89.9 14.8 %all_to_all.37 = f16[8,64,256]{2,1,0:T(8,128)(2,1)S(1)} all-to-all(f16[8,64,256]{2,1,0:T(8,128)(2,1)S(1)} %bitcast.41), channel_id=1, replica_groups=mesh['row_0'=8,'row_1'=2,'col_0'=4,'col_1'=4] {'row_0'}, dimensions={0} | all-to-all | bytes 524288 | tf_op jit(solution)/shard_map/all_to_all | solution.py:326
  104.7 1.1 shard_map.35
  105.9 3.6 %all-to-all-start.4 = ((bf16[16,64,256]{2,1,0:T(8,128)(2,1)}), bf16[16,64,256]{2,1,0:T(8,128)(2,1)S(1)}, u32[]{:S(2)}, u32[]{:S(2)}) async-start(bf16[16,64,256]{2,1,0:T(8,128)(2,1)} %get-tuple-element.60), calls=%async_computation.4 | async-start | bytes 1048576 | tf_op jit(solution)/shard_map/all_to_all | solution.py:338
  109.4 10.8 %all-to-all-done.4 = bf16[16,64,256]{2,1,0:T(8,128)(2,1)S(1)} async-done(((bf16[16,64,256]{2,1,0:T(8,128)(2,1)}), bf16[16,64,256]{2,1,0:T(8,128)(2,1)S(1)}, u32[]{:S(2)}, u32[]{:S(2)}) %all-to-all-start.4) | async-done | bytes 524320 | tf_op jit(solution)/shard_map/all_to_all | solution.py:338
  121.1 1.7 %collective-permute-start.15 = (f32[528,256]{1,0:T(8,128)S(1)}, f32[528,256]{1,0:T(8,128)S(1)}, u32[]{:S(2)}, u32[]{:S(2)}) collective-permute-start(f32[528,256]{1,0:T(8,128)S(1)} %pad_maximum_fusion), channel_id=1, source_target_pairs={{16,0},{0,16},{17,1},{1,17},{18,2},{2,18},{19,3},{3,19},{20,4},{4,... | collective-permute-start | bytes 1622024 | tf_op jit(solution)/shard_map/ppermute | solution.py:21
  122.8 1.6 %collective-permute-done.15 = f32[528,256]{1,0:T(8,128)S(1)} collective-permute-done((f32[528,256]{1,0:T(8,128)S(1)}, f32[528,256]{1,0:T(8,128)S(1)}, u32[]{:S(2)}, u32[]{:S(2)}) %collective-permute-start.15) | collective-permute-done | bytes 540704 | tf_op jit(solution)/shard_map/ppermute | solution.py:21
  125.0 16.1 %all_to_all.38 = f16[8,80,256]{2,1,0:T(8,128)(2,1)S(1)} all-to-all(f16[8,80,256]{2,1,0:T(8,128)(2,1)S(1)} %pad_maximum_fusion.3), channel_id=1, replica_groups=mesh['row_0'=8,'row_1'=2,'col_0'=4,'col_1'=4] {'row_0'}, dimensions={0} | all-to-all | bytes 655360 | tf_op jit(solution)/shard_map/all_to_all | solution.py:326
  141.9 3.5 %all-to-all-start.6 = ((f32[16,16,256]{2,1,0:T(8,128)}), f32[16,16,256]{2,1,0:T(8,128)S(1)}, u32[]{:S(2)}, u32[]{:S(2)}) async-start(f32[16,16,256]{2,1,0:T(8,128)} %broadcast_in_dim.7), calls=%async_computation.6 | async-start | bytes 524288 | tf_op jit(solution)/shard_map/all_to_all | solution.py:27
  145.4 8.3 %all-to-all-done.6 = f32[16,16,256]{2,1,0:T(8,128)S(1)} async-done(((f32[16,16,256]{2,1,0:T(8,128)}), f32[16,16,256]{2,1,0:T(8,128)S(1)}, u32[]{:S(2)}, u32[]{:S(2)}) %all-to-all-start.6) | async-done | bytes 262176 | tf_op jit(solution)/shard_map/all_to_all | solution.py:27
  153.7 0.9 shard_map.36
  (47 shorter events, 7.9 us)
Async XLA Ops:
  2.0 9.2 %copy-start = (bf16[32,1280]{1,0:T(8,128)(2,1)S(1)}, bf16[32,1280]{1,0:T(8,128)(2,1)}, u32[]{:S(2)}) copy-start(bf16[32,1280]{1,0:T(8,128)(2,1)} %get-tuple-element.34.ax0) | copy-start | bytes 245764
  2.0 12.9 %copy-start.1 = (bf16[32,1280]{1,0:T(8,128)(2,1)S(1)}, bf16[32,1280]{1,0:T(8,128)(2,1)}, u32[]{:S(2)}) copy-start(bf16[32,1280]{1,0:T(8,128)(2,1)} %get-tuple-element.35.by0) | copy-start | bytes 245764
  2.0 42.0 %all-to-all-start = ((bf16[8,64,1024]{2,1,0:T(8,128)(2,1)}), bf16[8,64,1024]{2,1,0:T(8,128)(2,1)S(1)}, u32[]{:S(2)}, u32[]{:S(2)}) async-start(bf16[8,64,1024]{2,1,0:T(8,128)(2,1)} %get-tuple-element.43), calls=%async_computation | async-start | bytes 2097152 | tf_op jit(solution)/shard_map/all_to_all | solution.py:260
  11.2 6.8 %collective-permute-start = (bf16[32,1280]{1,0:T(8,128)(2,1)S(1)}, bf16[32,1280]{1,0:T(8,128)(2,1)S(1)}, u32[]{:S(2)}, u32[]{:S(2)}) collective-permute-start(bf16[32,1280]{1,0:T(8,128)(2,1)S(1)} %copy-done), channel_id=1, source_target_pairs={{1,0},{2,1},{3,2},{0,3},{5,4},{6,5},{7,6},{4,7},{9,8},{10,9},{11,1... | collective-permute-start | bytes 245768 | tf_op jit(solution)/shard_map/ppermute | solution.py:21
  13.8 4.9 %collective-permute-start.1 = (bf16[32,1280]{1,0:T(8,128)(2,1)S(1)}, bf16[32,1280]{1,0:T(8,128)(2,1)S(1)}, u32[]{:S(2)}, u32[]{:S(2)}) collective-permute-start(bf16[32,1280]{1,0:T(8,128)(2,1)S(1)} %copy-done), channel_id=1, source_target_pairs={{2,0},{3,1},{0,2},{1,3},{6,4},{7,5},{4,6},{5,7},{10,8},{11,9},{8,1... | collective-permute-start | bytes 245768 | tf_op jit(solution)/shard_map/ppermute | solution.py:21
  14.3 5.2 %collective-permute-start.2 = (bf16[32,1280]{1,0:T(8,128)(2,1)S(1)}, bf16[32,1280]{1,0:T(8,128)(2,1)S(1)}, u32[]{:S(2)}, u32[]{:S(2)}) collective-permute-start(bf16[32,1280]{1,0:T(8,128)(2,1)S(1)} %copy-done), channel_id=1, source_target_pairs={{3,0},{0,1},{1,2},{2,3},{7,4},{4,5},{5,6},{6,7},{11,8},{8,9},{9,10... | collective-permute-start | bytes 245768 | tf_op jit(solution)/shard_map/ppermute | solution.py:21
  14.9 4.5 %collective-permute-start.3 = (bf16[32,1280]{1,0:T(8,128)(2,1)S(1)}, bf16[32,1280]{1,0:T(8,128)(2,1)S(1)}, u32[]{:S(2)}, u32[]{:S(2)}) collective-permute-start(bf16[32,1280]{1,0:T(8,128)(2,1)S(1)} %copy-done.1), channel_id=1, source_target_pairs={{4,0},{8,4},{12,8},{0,12},{5,1},{9,5},{13,9},{1,13},{6,2},{10,6},{... | collective-permute-start | bytes 245768 | tf_op jit(solution)/shard_map/ppermute | solution.py:21
  17.6 5.1 %collective-permute-start.4 = (bf16[32,1280]{1,0:T(8,128)(2,1)S(1)}, bf16[32,1280]{1,0:T(8,128)(2,1)S(1)}, u32[]{:S(2)}, u32[]{:S(2)}) collective-permute-start(bf16[32,1280]{1,0:T(8,128)(2,1)S(1)} %copy-done.1), channel_id=1, source_target_pairs={{8,0},{12,4},{0,8},{4,12},{9,1},{13,5},{1,9},{5,13},{10,2},{14,6},... | collective-permute-start | bytes 245768 | tf_op jit(solution)/shard_map/ppermute | solution.py:21
  18.0 5.6 %collective-permute-start.5 = (bf16[32,1280]{1,0:T(8,128)(2,1)S(1)}, bf16[32,1280]{1,0:T(8,128)(2,1)S(1)}, u32[]{:S(2)}, u32[]{:S(2)}) collective-permute-start(bf16[32,1280]{1,0:T(8,128)(2,1)S(1)} %copy-done.1), channel_id=1, source_target_pairs={{12,0},{0,4},{4,8},{8,12},{13,1},{1,5},{5,9},{9,13},{14,2},{2,6},{... | collective-permute-start | bytes 245768 | tf_op jit(solution)/shard_map/ppermute | solution.py:21
  23.6 6.4 %collective-permute-start.6 = (bf16[4,32,1280]{2,1,0:T(8,128)(2,1)S(1)}, bf16[4,32,1280]{2,1,0:T(8,128)(2,1)S(1)}, u32[]{:S(2)}, u32[]{:S(2)}) collective-permute-start(bf16[4,32,1280]{2,1,0:T(8,128)(2,1)S(1)} %pad_maximum_fusion.1), channel_id=1, source_target_pairs={{4,0},{8,4},{12,8},{0,12},{5,1},{9,5},{13,9},{1,13},{6,2},{10,6},{... | collective-permute-start | bytes 983048 | tf_op jit(solution)/shard_map/ppermute | solution.py:21
  24.1 7.6 %collective-permute-start.7 = (bf16[4,32,1280]{2,1,0:T(8,128)(2,1)S(1)}, bf16[4,32,1280]{2,1,0:T(8,128)(2,1)S(1)}, u32[]{:S(2)}, u32[]{:S(2)}) collective-permute-start(bf16[4,32,1280]{2,1,0:T(8,128)(2,1)S(1)} %pad_maximum_fusion.1), channel_id=1, source_target_pairs={{8,0},{12,4},{0,8},{4,12},{9,1},{13,5},{1,9},{5,13},{10,2},{14,6},... | collective-permute-start | bytes 983048 | tf_op jit(solution)/shard_map/ppermute | solution.py:21
  24.4 17.5 %collective-permute-start.8 = (bf16[4,32,1280]{2,1,0:T(8,128)(2,1)S(1)}, bf16[4,32,1280]{2,1,0:T(8,128)(2,1)S(1)}, u32[]{:S(2)}, u32[]{:S(2)}) collective-permute-start(bf16[4,32,1280]{2,1,0:T(8,128)(2,1)S(1)} %pad_maximum_fusion.1), channel_id=1, source_target_pairs={{12,0},{0,4},{4,8},{8,12},{13,1},{1,5},{5,9},{9,13},{14,2},{2,6},{... | collective-permute-start | bytes 983048 | tf_op jit(solution)/shard_map/ppermute | solution.py:21
  25.2 16.7 %collective-permute-start.9 = (bf16[4,32,1280]{2,1,0:T(8,128)(2,1)S(1)}, bf16[4,32,1280]{2,1,0:T(8,128)(2,1)S(1)}, u32[]{:S(2)}, u32[]{:S(2)}) collective-permute-start(bf16[4,32,1280]{2,1,0:T(8,128)(2,1)S(1)} %pad_maximum_fusion.2), channel_id=1, source_target_pairs={{1,0},{2,1},{3,2},{0,3},{5,4},{6,5},{7,6},{4,7},{9,8},{10,9},{11,1... | collective-permute-start | bytes 983048 | tf_op jit(solution)/shard_map/ppermute | solution.py:21
  27.4 14.6 %collective-permute-start.10 = (bf16[4,32,1280]{2,1,0:T(8,128)(2,1)S(1)}, bf16[4,32,1280]{2,1,0:T(8,128)(2,1)S(1)}, u32[]{:S(2)}, u32[]{:S(2)}) collective-permute-start(bf16[4,32,1280]{2,1,0:T(8,128)(2,1)S(1)} %pad_maximum_fusion.2), channel_id=1, source_target_pairs={{2,0},{3,1},{0,2},{1,3},{6,4},{7,5},{4,6},{5,7},{10,8},{11,9},{8,1... | collective-permute-start | bytes 983048 | tf_op jit(solution)/shard_map/ppermute | solution.py:21
  30.0 12.0 %collective-permute-start.11 = (bf16[4,32,1280]{2,1,0:T(8,128)(2,1)S(1)}, bf16[4,32,1280]{2,1,0:T(8,128)(2,1)S(1)}, u32[]{:S(2)}, u32[]{:S(2)}) collective-permute-start(bf16[4,32,1280]{2,1,0:T(8,128)(2,1)S(1)} %pad_maximum_fusion.2), channel_id=1, source_target_pairs={{3,0},{0,1},{1,2},{2,3},{7,4},{4,5},{5,6},{6,7},{11,8},{8,9},{9,10... | collective-permute-start | bytes 983048 | tf_op jit(solution)/shard_map/ppermute | solution.py:21
  42.7 1.4 copy-start.3
  44.1 7.6 %collective-permute-start.12 = (bf16[512,1024]{1,0:T(8,128)(2,1)S(1)}, bf16[512,1024]{1,0:T(8,128)(2,1)S(1)}, u32[]{:S(2)}, u32[]{:S(2)}) collective-permute-start(bf16[512,1024]{1,0:T(8,128)(2,1)S(1)} %bitcast.28), channel_id=1, source_target_pairs={{16,0},{0,16},{17,1},{1,17},{18,2},{2,18},{19,3},{3,19},{20,4},{4,... | collective-permute-start | bytes 3145736 | tf_op jit(solution)/shard_map/ppermute | solution.py:21
  48.1 3.5 %collective-permute-start.13 = (f32[16,256]{1,0:T(8,128)S(1)}, f32[16,256]{1,0:T(8,128)S(1)}, u32[]{:S(2)}, u32[]{:S(2)}) collective-permute-start(f32[16,256]{1,0:T(8,128)S(1)} %get-tuple-element.49.part), channel_id=1, source_target_pairs={{16,0},{0,16},{17,1},{1,17},{18,2},{2,18},{19,3},{3,19},{20,4},{4,... | collective-permute-start | bytes 49160 | tf_op jit(solution)/shard_map/ppermute | solution.py:21
  48.1 1.6 %copy-start.4 = (bf16[1024,1024]{1,0:T(8,128)(2,1)S(1)}, bf16[1024,1024]{1,0:T(8,128)(2,1)}, u32[]{:S(2)}) copy-start(bf16[1024,1024]{1,0:T(8,128)(2,1)} %copy-done.3) | copy-start | bytes 6291460
  87.1 2.7 %collective-permute-start.14 = (f32[512,256]{1,0:T(8,128)S(1)}, f32[512,256]{1,0:T(8,128)S(1)}, u32[]{:S(2)}, u32[]{:S(2)}) collective-permute-start(f32[512,256]{1,0:T(8,128)S(1)} %get-tuple-element.57), channel_id=1, source_target_pairs={{16,0},{0,16},{17,1},{1,17},{18,2},{2,18},{19,3},{3,19},{20,4},{4,... | collective-permute-start | bytes 1572872 | tf_op jit(solution)/shard_map/ppermute | solution.py:21
  88.3 16.4 %copy-start.2 = (f32[64,256]{1,0:T(8,128)S(1)}, f32[64,256]{1,0:T(8,128)}, u32[]{:S(2)}) copy-start(f32[64,256]{1,0:T(8,128)} %h_ref.1) | copy-start | bytes 196612
  105.9 14.4 %all-to-all-start.4 = ((bf16[16,64,256]{2,1,0:T(8,128)(2,1)}), bf16[16,64,256]{2,1,0:T(8,128)(2,1)S(1)}, u32[]{:S(2)}, u32[]{:S(2)}) async-start(bf16[16,64,256]{2,1,0:T(8,128)(2,1)} %get-tuple-element.60), calls=%async_computation.4 | async-start | bytes 1048576 | tf_op jit(solution)/shard_map/all_to_all | solution.py:338
  121.1 3.3 %collective-permute-start.15 = (f32[528,256]{1,0:T(8,128)S(1)}, f32[528,256]{1,0:T(8,128)S(1)}, u32[]{:S(2)}, u32[]{:S(2)}) collective-permute-start(f32[528,256]{1,0:T(8,128)S(1)} %pad_maximum_fusion), channel_id=1, source_target_pairs={{16,0},{0,16},{17,1},{1,17},{18,2},{2,18},{19,3},{3,19},{20,4},{4,... | collective-permute-start | bytes 1622024 | tf_op jit(solution)/shard_map/ppermute | solution.py:21
  141.9 11.8 %all-to-all-start.6 = ((f32[16,16,256]{2,1,0:T(8,128)}), f32[16,16,256]{2,1,0:T(8,128)S(1)}, u32[]{:S(2)}, u32[]{:S(2)}) async-start(f32[16,16,256]{2,1,0:T(8,128)} %broadcast_in_dim.7), calls=%async_computation.6 | async-start | bytes 524288 | tf_op jit(solution)/shard_map/all_to_all | solution.py:27

commit v6 on v5

--- a/solution.py
+++ b/solution.py
@@ -56,7 +56,7 @@
 
 
 def columns_kernel(
-    ax0, ax1, ax2, ax3, y1, y2, y3, by0, by1, by2, by3, x1, x2, x3, pts_ref, hb_ref, sq_ref, part_ref, gram_ref
+    y2, x2, y1, x1, y3, x3, ax0, ax1, ax2, ax3, by0, by1, by2, by3, pts_ref, hb_ref, sq_ref, part_ref, gram_ref
 ):
     ny, nx = lax.axis_size(Y), lax.axis_size(X)
     y, x = lax.axis_index(Y), lax.axis_index(X)
@@ -264,9 +264,13 @@
     x1, x2, x3, y1, y2, y3 = tie((x1, x2, x3, y1, y2, y3))
     by_x = jnp.stack([first, x1, x2, x3])
     by_y = jnp.stack([second, y1, y2, y3])
-    from_y = [from_ahead(by_x, Y, s) for s in (1, 2, 3)]
-    from_x = [from_ahead(by_y, X, s) for s in (1, 2, 3)]
-    cols = [first, x1, x2, x3, *from_y, second, y1, y2, y3, *from_x]
+    y_two, x_two = from_ahead(by_x, Y, 2), from_ahead(by_y, X, 2)
+    y_one, x_one = from_ahead(by_x, Y, 1), from_ahead(by_y, X, 1)
+    y_three, x_three = from_ahead(by_x, Y, 3), from_ahead(by_y, X, 3)
+    far = [y_two, x_two, y_one, x_one, y_three, x_three]
+    far, along_z = tie((far, along_z.reshape(-1, width)))
+    other = from_ahead(along_z, CORE, 1)
+    cols = [*far, first, x1, x2, x3, second, y1, y2, y3]
 
     part = rank // ncol
     group = nrow * pts
@@ -282,8 +286,6 @@
         2 * group * rank * rank,
         [pltpu.VMEM((rank, rank), F32)],
     )
-    own_part, along_z = tie((own_part, along_z.reshape(-1, width)))
-    other = from_ahead(along_z, CORE, 1)
     more_part = from_ahead(own_part, CORE, 1)
     lines = group // LANES
     own_kern, own_sums = call(
@@ -336,14 +338,14 @@
     h, hb_cols = stepped(unit, None, ah, hh, factor, 1)
 
     hb_cols = lax.all_to_all(hb_cols, COL, 0, 0, tiled=True).reshape(group, rank)
+    partial_other = jnp.dot(aff_other, hb_cols, preferred_element_type=F32)
+    got = from_ahead(partial_other, CORE, 1)
     gram = lax.dot_general(hb_cols, hb_cols, (((0,), (0,)), ((), ())), preferred_element_type=F32)
     own_part = lax.dynamic_slice_in_dim(gram, lax.axis_index(COL) * part, part, 0)
-    partial_other = jnp.dot(aff_other, hb_cols, preferred_element_type=F32)
-    got = from_ahead(jnp.concatenate([partial_other, own_part]), CORE, 1)
+    more_part = from_ahead(own_part, CORE, 1)
     partial_own = jnp.dot(aff_own, hb_cols, preferred_element_type=F32)
-    mine = ((partial_own + got[: group // 2]) * scales[2]).reshape(nz, pts, rank)
-    extra = (own_part + got[group // 2 :]) * scales[4]
-    extra = jnp.broadcast_to(extra, (nz, part, rank))
+    mine = ((partial_own + got) * scales[2]).reshape(nz, pts, rank)
+    extra = jnp.broadcast_to((own_part + more_part) * scales[4], (nz, part, rank))
     own = over_z(jnp.concatenate([mine, extra], axis=1))
     hh = sent_to_all(own[pts:] * scales[5], COL).reshape(rank, rank)
     ah = own[:pts] * scales[3]

time: 155 us -> 152 us (0.981)
  starting transfers between devices: 37.1 us -> 40.4 us
  waiting for transfers between devices: 38 us -> 35 us
  blocking collectives: 63.3 us -> 61.1 us
    ppermute x16 -> x17, starting transfers between devices: 20.8 us -> 24.1 us  [from_ahead(): lax.ppermute(value, axis, [((i + steps) % length, i) for i in range(lengt...]
    ppermute x16 -> x17, waiting for transfers between devices: 19 us -> 15.9 us  [from_ahead(): lax.ppermute(value, axis, [((i + steps) % length, i) for i in range(lengt...]
    all_to_all x1, blocking collectives: 15 us -> 12.6 us  [shards(): gathered = lax.all_to_all(message, COL, 0, 0, tiled=True)]
  transfers between devices with their start and end apart: 19 -> 20, of which waited for: 10 -> 10; matrix products, arithmetic and copies ran while one was open for 0% -> 0% of each run, Pallas kernels for 2% -> 2%
where the time goes in v6:
time: 152 us; the launch traced here: 151 us
  blocking collectives  61.1 us (40%)
  starting transfers between devices  40.4 us (27%)
  waiting for transfers between devices  35 us (23%)
  Pallas kernels  10.4 us (7%)
  local copies, waits for them, and re-layouts  2.47 us (2%)
    all_to_all x2, blocking collectives, over_z(): mine = lax.all_to_all(mine.astype(jnp.float16), Z, 0, 0, tiled=True)  30.9 us
    ppermute x17, starting transfers between devices, from_ahead(): lax.ppermute(value, axis, [((i + steps) % length, i) for i in range(lengt...  24.1 us
    all_to_all x1, blocking collectives, shards(): lax.all_to_all(message, ROW, 0, 0, tiled=True)  17.6 us
    ppermute x17, waiting for transfers between devices, from_ahead(): lax.ppermute(value, axis, [((i + steps) % length, i) for i in range(lengt...  15.9 us
    all_to_all x1, blocking collectives, shards(): gathered = lax.all_to_all(message, COL, 0, 0, tiled=True)  12.6 us
    all_to_all x1, waiting for transfers between devices, shards(): lax.all_to_all(hb_cols, COL, 0, 0, tiled=True).reshape(group, rank)  10.8 us
    pallas_call x9, Pallas kernels, call(): pl.pallas_call(kernel, out_shape=outs, in_specs=[pl.BlockSpec(memory_spac...  10.4 us
    all_to_all x1, starting transfers between devices, shards(): along_z = lax.all_to_all(copies, Z, 0, 0, tiled=True)  9.16 us
  transfers between devices with their start and end apart: 20, of which 10 were waited for; matrix products, arithmetic and copies ran while one was open for 0% of the time, Pallas kernels for 2%

profile of v6, /device:TPU:1, one launch (start us, length us, event | category | flops | bytes accessed | tf_op | source)
XLA Modules:
  0.0 151.1 jit_solution(11671117701363200013)
XLA Ops:
  0.0 2.0 %shard_map.28 = (bf16[32,1280]{1,0:T(8,128)(2,1)}, bf16[32,1280]{1,0:T(8,128)(2,1)}, bf16[8,64,1024]{2,1,0:T(8,128)(2,1)}) custom-call(bf16[64,1024]{1,0:T(8,128)(2,1)} %points.1, f32[64,256]{1,0:T(8,128)} %h_ref.1), custom_call_target="tpu_custom_call" | custom-call | flops 1 | bytes 1409024 | tf_op jit(solution)/shard_map/pallas_call | solution.py:37
  2.0 9.2 %all-to-all-start = ((bf16[8,64,1024]{2,1,0:T(8,128)(2,1)}), bf16[8,64,1024]{2,1,0:T(8,128)(2,1)S(1)}, u32[]{:S(2)}, u32[]{:S(2)}) async-start(bf16[8,64,1024]{2,1,0:T(8,128)(2,1)} %get-tuple-element.47), calls=%async_computation | async-start | bytes 2097152 | tf_op jit(solution)/shard_map/all_to_all | solution.py:260
  11.2 2.6 %collective-permute-start = (bf16[32,1280]{1,0:T(8,128)(2,1)S(1)}, bf16[32,1280]{1,0:T(8,128)(2,1)S(1)}, u32[]{:S(2)}, u32[]{:S(2)}) collective-permute-start(bf16[32,1280]{1,0:T(8,128)(2,1)S(1)} %copy-done), channel_id=1, source_target_pairs={{1,0},{2,1},{3,2},{0,3},{5,4},{6,5},{7,6},{4,7},{9,8},{10,9},{11,1... | collective-permute-start | bytes 245768 | tf_op jit(solution)/shard_map/ppermute | solution.py:21
  14.9 2.7 %collective-permute-start.3 = (bf16[32,1280]{1,0:T(8,128)(2,1)S(1)}, bf16[32,1280]{1,0:T(8,128)(2,1)S(1)}, u32[]{:S(2)}, u32[]{:S(2)}) collective-permute-start(bf16[32,1280]{1,0:T(8,128)(2,1)S(1)} %copy-done.1), channel_id=1, source_target_pairs={{4,0},{8,4},{12,8},{0,12},{5,1},{9,5},{13,9},{1,13},{6,2},{10,6},{... | collective-permute-start | bytes 245768 | tf_op jit(solution)/shard_map/ppermute | solution.py:21
  19.4 3.3 %collective-permute-done.4.by2 = bf16[32,1280]{1,0:T(8,128)(2,1)S(1)} collective-permute-done((bf16[32,1280]{1,0:T(8,128)(2,1)S(1)}, bf16[32,1280]{1,0:T(8,128)(2,1)S(1)}, u32[]{:S(2)}, u32[]{:S(2)}) %collective-permute-start.4) | collective-permute-done | bytes 81952 | tf_op jit(solution)/shard_map/ppermute | solution.py:21
  22.7 0.9 collective-permute-done.5.by3
  25.0 1.9 %collective-permute-start.7 = (bf16[4,32,1280]{2,1,0:T(8,128)(2,1)S(1)}, bf16[4,32,1280]{2,1,0:T(8,128)(2,1)S(1)}, u32[]{:S(2)}, u32[]{:S(2)}) collective-permute-start(bf16[4,32,1280]{2,1,0:T(8,128)(2,1)S(1)} %pad_maximum_fusion.1), channel_id=1, source_target_pairs={{2,0},{3,1},{0,2},{1,3},{6,4},{7,5},{4,6},{5,7},{10,8},{11,9},{8,1... | collective-permute-start | bytes 983048 | tf_op jit(solution)/shard_map/ppermute | solution.py:21
  27.0 2.1 %collective-permute-start.9 = (bf16[4,32,1280]{2,1,0:T(8,128)(2,1)S(1)}, bf16[4,32,1280]{2,1,0:T(8,128)(2,1)S(1)}, u32[]{:S(2)}, u32[]{:S(2)}) collective-permute-start(bf16[4,32,1280]{2,1,0:T(8,128)(2,1)S(1)} %pad_maximum_fusion.1), channel_id=1, source_target_pairs={{1,0},{2,1},{3,2},{0,3},{5,4},{6,5},{7,6},{4,7},{9,8},{10,9},{11,1... | collective-permute-start | bytes 983048 | tf_op jit(solution)/shard_map/ppermute | solution.py:21
  29.0 0.8 collective-permute-start.10
  29.8 1.7 %collective-permute-done.6.y2 = bf16[4,32,1280]{2,1,0:T(8,128)(2,1)S(1)} collective-permute-done((bf16[4,32,1280]{2,1,0:T(8,128)(2,1)S(1)}, bf16[4,32,1280]{2,1,0:T(8,128)(2,1)S(1)}, u32[]{:S(2)}, u32[]{:S(2)}) %collective-permute-start.6) | collective-permute-done | bytes 327712 | tf_op jit(solution)/shard_map/ppermute | solution.py:21
  31.5 1.5 %collective-permute-start.11 = (bf16[4,32,1280]{2,1,0:T(8,128)(2,1)S(1)}, bf16[4,32,1280]{2,1,0:T(8,128)(2,1)S(1)}, u32[]{:S(2)}, u32[]{:S(2)}) collective-permute-start(bf16[4,32,1280]{2,1,0:T(8,128)(2,1)S(1)} %pad_maximum_fusion.1), channel_id=1, source_target_pairs={{3,0},{0,1},{1,2},{2,3},{7,4},{4,5},{5,6},{6,7},{11,8},{8,9},{9,10... | collective-permute-start | bytes 983048 | tf_op jit(solution)/shard_map/ppermute | solution.py:21
  33.0 5.7 %collective-permute-done.8.y1 = bf16[4,32,1280]{2,1,0:T(8,128)(2,1)S(1)} collective-permute-done((bf16[4,32,1280]{2,1,0:T(8,128)(2,1)S(1)}, bf16[4,32,1280]{2,1,0:T(8,128)(2,1)S(1)}, u32[]{:S(2)}, u32[]{:S(2)}) %collective-permute-start.8) | collective-permute-done | bytes 327712 | tf_op jit(solution)/shard_map/ppermute | solution.py:21
  38.7 1.8 %collective-permute-done.9.x1 = bf16[4,32,1280]{2,1,0:T(8,128)(2,1)S(1)} collective-permute-done((bf16[4,32,1280]{2,1,0:T(8,128)(2,1)S(1)}, bf16[4,32,1280]{2,1,0:T(8,128)(2,1)S(1)}, u32[]{:S(2)}, u32[]{:S(2)}) %collective-permute-start.9) | collective-permute-done | bytes 327712 | tf_op jit(solution)/shard_map/ppermute | solution.py:21
  41.2 5.7 %collective-permute-start.12 = (bf16[512,1024]{1,0:T(8,128)(2,1)S(1)}, bf16[512,1024]{1,0:T(8,128)(2,1)S(1)}, u32[]{:S(2)}, u32[]{:S(2)}) collective-permute-start(bf16[512,1024]{1,0:T(8,128)(2,1)S(1)} %bitcast.28), channel_id=1, source_target_pairs={{16,0},{0,16},{17,1},{1,17},{18,2},{2,18},{19,3},{3,19},{20,4},{4,... | collective-permute-start | bytes 3145736 | tf_op jit(solution)/shard_map/ppermute | solution.py:21
  46.9 1.0 copy-done.3
  48.9 1.9 %shard_map.30 = (f32[512,1024]{1,0:T(8,128)S(1)}, f32[4,128]{1,0:T(4,128)S(1)}) custom-call(bf16[512,1024]{1,0:T(8,128)(2,1)S(1)} %bitcast.29, bf16[1024,1024]{1,0:T(8,128)(2,1)S(1)} %get-tuple-element.55.cols, f32[8,128]{1,0:T(8,128)S(1)} %get-tuple-element.56.sq), custom_call_target="tpu_custom_call" | custom-call | flops 1073741824 | bytes 5249024 | tf_op jit(solution)/shard_map/pallas_call | solution.py:37
  50.8 1.9 %shard_map.31 = (f32[512,1024]{1,0:T(8,128)S(1)}, f32[16,24,128]{2,1,0:T(8,128)S(1)}) custom-call(bf16[512,1024]{1,0:T(8,128)(2,1)S(1)} %collective-permute-done.12.rows_ref, bf16[1024,1024]{1,0:T(8,128)(2,1)S(1)} %get-tuple-element.55.cols, f32[8,128]{1,0:T(8,128)S(1)} %get-tuple-element.56.sq, f32[4,128]{1,0:T(4,128)S(1)} %get-tuple-element.58.own_sums, ...), custom_call_target="tpu_custom_call" | custom-call | flops 1073741824 | bytes 5478400 | tf_op jit(solution)/shard_map/pallas_call | solution.py:37
  52.8 17.6 %all_to_all.35.got = f32[16,24,128]{2,1,0:T(8,128)S(1)} all-to-all(f32[16,24,128]{2,1,0:T(8,128)S(1)} %get-tuple-element.60), channel_id=1, replica_groups=mesh['row_0'=8,'row_1'=2,'col_0'=4,'col_1'=4] {'row_0','row_1'}, dimensions={0} | all-to-all | bytes 393216 | tf_op jit(solution)/shard_map/all_to_all | solution.py:307
  70.5 12.6 %all_to_all.36.got = f32[16,40,128]{2,1,0:T(8,128)S(1)} all-to-all(f32[16,40,128]{2,1,0:T(8,128)S(1)} %get-tuple-element.62), channel_id=1, replica_groups=mesh['row_0'=8,'row_1'=2,'col_0'=4,'col_1'=4] {'col_0','col_1'}, dimensions={0} | all-to-all | bytes 655360 | tf_op jit(solution)/shard_map/all_to_all | solution.py:310
  83.1 0.8 shard_map.34
  83.9 1.2 collective-permute-start.14
  85.1 0.9 shard_map.33
  86.8 14.8 %all_to_all.37 = f16[8,64,256]{2,1,0:T(8,128)(2,1)S(1)} all-to-all(f16[8,64,256]{2,1,0:T(8,128)(2,1)S(1)} %bitcast.41), channel_id=1, replica_groups=mesh['row_0'=8,'row_1'=2,'col_0'=4,'col_1'=4] {'row_0'}, dimensions={0} | all-to-all | bytes 524288 | tf_op jit(solution)/shard_map/all_to_all | solution.py:328
  101.6 1.1 shard_map.35
  102.7 3.6 %all-to-all-start.4 = ((bf16[16,64,256]{2,1,0:T(8,128)(2,1)}), bf16[16,64,256]{2,1,0:T(8,128)(2,1)S(1)}, u32[]{:S(2)}, u32[]{:S(2)}) async-start(bf16[16,64,256]{2,1,0:T(8,128)(2,1)} %get-tuple-element.70), calls=%async_computation.4 | async-start | bytes 1048576 | tf_op jit(solution)/shard_map/all_to_all | solution.py:340
  106.3 10.8 %all-to-all-done.4 = bf16[16,64,256]{2,1,0:T(8,128)(2,1)S(1)} async-done(((bf16[16,64,256]{2,1,0:T(8,128)(2,1)}), bf16[16,64,256]{2,1,0:T(8,128)(2,1)S(1)}, u32[]{:S(2)}, u32[]{:S(2)}) %all-to-all-start.4) | async-done | bytes 524320 | tf_op jit(solution)/shard_map/all_to_all | solution.py:340
  117.6 1.7 %collective-permute-start.15 = (f32[512,256]{1,0:T(8,128)S(1)}, f32[512,256]{1,0:T(8,128)S(1)}, u32[]{:S(2)}, u32[]{:S(2)}) collective-permute-start(f32[512,256]{1,0:T(8,128)S(1)} %fusion.3), channel_id=1, source_target_pairs={{16,0},{0,16},{17,1},{1,17},{18,2},{2,18},{19,3},{3,19},{20,4},{4,... | collective-permute-start | bytes 1572872 | tf_op jit(solution)/shard_map/ppermute | solution.py:21
  119.7 1.2 collective-permute-done.16
  121.5 16.1 %all_to_all.38 = f16[8,80,256]{2,1,0:T(8,128)(2,1)S(1)} all-to-all(f16[8,80,256]{2,1,0:T(8,128)(2,1)S(1)} %pad_maximum_fusion.2), channel_id=1, replica_groups=mesh['row_0'=8,'row_1'=2,'col_0'=4,'col_1'=4] {'row_0'}, dimensions={0} | all-to-all | bytes 655360 | tf_op jit(solution)/shard_map/all_to_all | solution.py:328
  138.4 3.5 %all-to-all-start.6 = ((f32[16,16,256]{2,1,0:T(8,128)}), f32[16,16,256]{2,1,0:T(8,128)S(1)}, u32[]{:S(2)}, u32[]{:S(2)}) async-start(f32[16,16,256]{2,1,0:T(8,128)} %broadcast_in_dim.7), calls=%async_computation.6 | async-start | bytes 524288 | tf_op jit(solution)/shard_map/all_to_all | solution.py:27
  142.0 8.3 %all-to-all-done.6 = f32[16,16,256]{2,1,0:T(8,128)S(1)} async-done(((f32[16,16,256]{2,1,0:T(8,128)}), f32[16,16,256]{2,1,0:T(8,128)S(1)}, u32[]{:S(2)}, u32[]{:S(2)}) %all-to-all-start.6) | async-done | bytes 262176 | tf_op jit(solution)/shard_map/all_to_all | solution.py:27
  150.2 0.9 shard_map.36
  (48 shorter events, 9.3 us)
Async XLA Ops:
  2.0 9.2 %copy-start = (bf16[32,1280]{1,0:T(8,128)(2,1)S(1)}, bf16[32,1280]{1,0:T(8,128)(2,1)}, u32[]{:S(2)}) copy-start(bf16[32,1280]{1,0:T(8,128)(2,1)} %get-tuple-element.39.ax0) | copy-start | bytes 245764
  2.0 12.9 %copy-start.1 = (bf16[32,1280]{1,0:T(8,128)(2,1)S(1)}, bf16[32,1280]{1,0:T(8,128)(2,1)}, u32[]{:S(2)}) copy-start(bf16[32,1280]{1,0:T(8,128)(2,1)} %get-tuple-element.40.by0) | copy-start | bytes 245764
  2.0 39.2 %all-to-all-start = ((bf16[8,64,1024]{2,1,0:T(8,128)(2,1)}), bf16[8,64,1024]{2,1,0:T(8,128)(2,1)S(1)}, u32[]{:S(2)}, u32[]{:S(2)}) async-start(bf16[8,64,1024]{2,1,0:T(8,128)(2,1)} %get-tuple-element.47), calls=%async_computation | async-start | bytes 2097152 | tf_op jit(solution)/shard_map/all_to_all | solution.py:260
  11.2 6.8 %collective-permute-start = (bf16[32,1280]{1,0:T(8,128)(2,1)S(1)}, bf16[32,1280]{1,0:T(8,128)(2,1)S(1)}, u32[]{:S(2)}, u32[]{:S(2)}) collective-permute-start(bf16[32,1280]{1,0:T(8,128)(2,1)S(1)} %copy-done), channel_id=1, source_target_pairs={{1,0},{2,1},{3,2},{0,3},{5,4},{6,5},{7,6},{4,7},{9,8},{10,9},{11,1... | collective-permute-start | bytes 245768 | tf_op jit(solution)/shard_map/ppermute | solution.py:21
  13.8 4.9 %collective-permute-start.1 = (bf16[32,1280]{1,0:T(8,128)(2,1)S(1)}, bf16[32,1280]{1,0:T(8,128)(2,1)S(1)}, u32[]{:S(2)}, u32[]{:S(2)}) collective-permute-start(bf16[32,1280]{1,0:T(8,128)(2,1)S(1)} %copy-done), channel_id=1, source_target_pairs={{2,0},{3,1},{0,2},{1,3},{6,4},{7,5},{4,6},{5,7},{10,8},{11,9},{8,1... | collective-permute-start | bytes 245768 | tf_op jit(solution)/shard_map/ppermute | solution.py:21
  14.3 5.2 %collective-permute-start.2 = (bf16[32,1280]{1,0:T(8,128)(2,1)S(1)}, bf16[32,1280]{1,0:T(8,128)(2,1)S(1)}, u32[]{:S(2)}, u32[]{:S(2)}) collective-permute-start(bf16[32,1280]{1,0:T(8,128)(2,1)S(1)} %copy-done), channel_id=1, source_target_pairs={{3,0},{0,1},{1,2},{2,3},{7,4},{4,5},{5,6},{6,7},{11,8},{8,9},{9,10... | collective-permute-start | bytes 245768 | tf_op jit(solution)/shard_map/ppermute | solution.py:21
  14.9 4.5 %collective-permute-start.3 = (bf16[32,1280]{1,0:T(8,128)(2,1)S(1)}, bf16[32,1280]{1,0:T(8,128)(2,1)S(1)}, u32[]{:S(2)}, u32[]{:S(2)}) collective-permute-start(bf16[32,1280]{1,0:T(8,128)(2,1)S(1)} %copy-done.1), channel_id=1, source_target_pairs={{4,0},{8,4},{12,8},{0,12},{5,1},{9,5},{13,9},{1,13},{6,2},{10,6},{... | collective-permute-start | bytes 245768 | tf_op jit(solution)/shard_map/ppermute | solution.py:21
  17.6 5.1 %collective-permute-start.4 = (bf16[32,1280]{1,0:T(8,128)(2,1)S(1)}, bf16[32,1280]{1,0:T(8,128)(2,1)S(1)}, u32[]{:S(2)}, u32[]{:S(2)}) collective-permute-start(bf16[32,1280]{1,0:T(8,128)(2,1)S(1)} %copy-done.1), channel_id=1, source_target_pairs={{8,0},{12,4},{0,8},{4,12},{9,1},{13,5},{1,9},{5,13},{10,2},{14,6},... | collective-permute-start | bytes 245768 | tf_op jit(solution)/shard_map/ppermute | solution.py:21
  18.0 5.6 %collective-permute-start.5 = (bf16[32,1280]{1,0:T(8,128)(2,1)S(1)}, bf16[32,1280]{1,0:T(8,128)(2,1)S(1)}, u32[]{:S(2)}, u32[]{:S(2)}) collective-permute-start(bf16[32,1280]{1,0:T(8,128)(2,1)S(1)} %copy-done.1), channel_id=1, source_target_pairs={{12,0},{0,4},{4,8},{8,12},{13,1},{1,5},{5,9},{9,13},{14,2},{2,6},{... | collective-permute-start | bytes 245768 | tf_op jit(solution)/shard_map/ppermute | solution.py:21
  23.6 7.9 %collective-permute-start.6 = (bf16[4,32,1280]{2,1,0:T(8,128)(2,1)S(1)}, bf16[4,32,1280]{2,1,0:T(8,128)(2,1)S(1)}, u32[]{:S(2)}, u32[]{:S(2)}) collective-permute-start(bf16[4,32,1280]{2,1,0:T(8,128)(2,1)S(1)} %pad_maximum_fusion), channel_id=1, source_target_pairs={{8,0},{12,4},{0,8},{4,12},{9,1},{13,5},{1,9},{5,13},{10,2},{14,6},... | collective-permute-start | bytes 983048 | tf_op jit(solution)/shard_map/ppermute | solution.py:21
  24.3 14.4 %collective-permute-start.8 = (bf16[4,32,1280]{2,1,0:T(8,128)(2,1)S(1)}, bf16[4,32,1280]{2,1,0:T(8,128)(2,1)S(1)}, u32[]{:S(2)}, u32[]{:S(2)}) collective-permute-start(bf16[4,32,1280]{2,1,0:T(8,128)(2,1)S(1)} %pad_maximum_fusion), channel_id=1, source_target_pairs={{4,0},{8,4},{12,8},{0,12},{5,1},{9,5},{13,9},{1,13},{6,2},{10,6},{... | collective-permute-start | bytes 983048 | tf_op jit(solution)/shard_map/ppermute | solution.py:21
  25.0 8.0 %collective-permute-start.7 = (bf16[4,32,1280]{2,1,0:T(8,128)(2,1)S(1)}, bf16[4,32,1280]{2,1,0:T(8,128)(2,1)S(1)}, u32[]{:S(2)}, u32[]{:S(2)}) collective-permute-start(bf16[4,32,1280]{2,1,0:T(8,128)(2,1)S(1)} %pad_maximum_fusion.1), channel_id=1, source_target_pairs={{2,0},{3,1},{0,2},{1,3},{6,4},{7,5},{4,6},{5,7},{10,8},{11,9},{8,1... | collective-permute-start | bytes 983048 | tf_op jit(solution)/shard_map/ppermute | solution.py:21
  27.0 13.5 %collective-permute-start.9 = (bf16[4,32,1280]{2,1,0:T(8,128)(2,1)S(1)}, bf16[4,32,1280]{2,1,0:T(8,128)(2,1)S(1)}, u32[]{:S(2)}, u32[]{:S(2)}) collective-permute-start(bf16[4,32,1280]{2,1,0:T(8,128)(2,1)S(1)} %pad_maximum_fusion.1), channel_id=1, source_target_pairs={{1,0},{2,1},{3,2},{0,3},{5,4},{6,5},{7,6},{4,7},{9,8},{10,9},{11,1... | collective-permute-start | bytes 983048 | tf_op jit(solution)/shard_map/ppermute | solution.py:21
  29.0 11.5 %collective-permute-start.10 = (bf16[4,32,1280]{2,1,0:T(8,128)(2,1)S(1)}, bf16[4,32,1280]{2,1,0:T(8,128)(2,1)S(1)}, u32[]{:S(2)}, u32[]{:S(2)}) collective-permute-start(bf16[4,32,1280]{2,1,0:T(8,128)(2,1)S(1)} %pad_maximum_fusion), channel_id=1, source_target_pairs={{12,0},{0,4},{4,8},{8,12},{13,1},{1,5},{5,9},{9,13},{14,2},{2,6},{... | collective-permute-start | bytes 983048 | tf_op jit(solution)/shard_map/ppermute | solution.py:21
  31.5 9.0 %collective-permute-start.11 = (bf16[4,32,1280]{2,1,0:T(8,128)(2,1)S(1)}, bf16[4,32,1280]{2,1,0:T(8,128)(2,1)S(1)}, u32[]{:S(2)}, u32[]{:S(2)}) collective-permute-start(bf16[4,32,1280]{2,1,0:T(8,128)(2,1)S(1)} %pad_maximum_fusion.1), channel_id=1, source_target_pairs={{3,0},{0,1},{1,2},{2,3},{7,4},{4,5},{5,6},{6,7},{11,8},{8,9},{9,10... | collective-permute-start | bytes 983048 | tf_op jit(solution)/shard_map/ppermute | solution.py:21
  40.5 0.7 copy-start.2
  41.2 9.6 %collective-permute-start.12 = (bf16[512,1024]{1,0:T(8,128)(2,1)S(1)}, bf16[512,1024]{1,0:T(8,128)(2,1)S(1)}, u32[]{:S(2)}, u32[]{:S(2)}) collective-permute-start(bf16[512,1024]{1,0:T(8,128)(2,1)S(1)} %bitcast.28), channel_id=1, source_target_pairs={{16,0},{0,16},{17,1},{1,17},{18,2},{2,18},{19,3},{3,19},{20,4},{4,... | collective-permute-start | bytes 3145736 | tf_op jit(solution)/shard_map/ppermute | solution.py:21
  46.9 1.0 copy-start.3
  48.6 2.2 %collective-permute-start.13 = (f32[16,256]{1,0:T(8,128)S(1)}, f32[16,256]{1,0:T(8,128)S(1)}, u32[]{:S(2)}, u32[]{:S(2)}) collective-permute-start(f32[16,256]{1,0:T(8,128)S(1)} %get-tuple-element.59.part), channel_id=1, source_target_pairs={{16,0},{0,16},{17,1},{1,17},{18,2},{2,18},{19,3},{3,19},{20,4},{4,... | collective-permute-start | bytes 49160 | tf_op jit(solution)/shard_map/ppermute | solution.py:21
  83.9 2.7 %collective-permute-start.14 = (f32[512,256]{1,0:T(8,128)S(1)}, f32[512,256]{1,0:T(8,128)S(1)}, u32[]{:S(2)}, u32[]{:S(2)}) collective-permute-start(f32[512,256]{1,0:T(8,128)S(1)} %get-tuple-element.67), channel_id=1, source_target_pairs={{16,0},{0,16},{17,1},{1,17},{18,2},{2,18},{19,3},{3,19},{20,4},{4,... | collective-permute-start | bytes 1572872 | tf_op jit(solution)/shard_map/ppermute | solution.py:21
  85.1 16.5 %copy-start.4 = (f32[64,256]{1,0:T(8,128)S(1)}, f32[64,256]{1,0:T(8,128)}, u32[]{:S(2)}) copy-start(f32[64,256]{1,0:T(8,128)} %h_ref.1) | copy-start | bytes 196612
  102.7 14.4 %all-to-all-start.4 = ((bf16[16,64,256]{2,1,0:T(8,128)(2,1)}), bf16[16,64,256]{2,1,0:T(8,128)(2,1)S(1)}, u32[]{:S(2)}, u32[]{:S(2)}) async-start(bf16[16,64,256]{2,1,0:T(8,128)(2,1)} %get-tuple-element.70), calls=%async_computation.4 | async-start | bytes 1048576 | tf_op jit(solution)/shard_map/all_to_all | solution.py:340
  117.6 3.3 %collective-permute-start.15 = (f32[512,256]{1,0:T(8,128)S(1)}, f32[512,256]{1,0:T(8,128)S(1)}, u32[]{:S(2)}, u32[]{:S(2)}) collective-permute-start(f32[512,256]{1,0:T(8,128)S(1)} %fusion.3), channel_id=1, source_target_pairs={{16,0},{0,16},{17,1},{1,17},{18,2},{2,18},{19,3},{3,19},{20,4},{4,... | collective-permute-start | bytes 1572872 | tf_op jit(solution)/shard_map/ppermute | solution.py:21
  119.6 1.3 collective-permute-start.16
  138.4 11.8 %all-to-all-start.6 = ((f32[16,16,256]{2,1,0:T(8,128)}), f32[16,16,256]{2,1,0:T(8,128)S(1)}, u32[]{:S(2)}, u32[]{:S(2)}) async-start(f32[16,16,256]{2,1,0:T(8,128)} %broadcast_in_dim.7), calls=%async_computation.6 | async-start | bytes 524288 | tf_op jit(solution)/shard_map/all_to_all | solution.py:27

commit v7 on v6

--- a/solution.py
+++ b/solution.py
@@ -32,13 +32,13 @@
 LANES = 128
 
 
-def call(kernel, outs, args, flops, scratch=(), vmem=10, place=pltpu.VMEM):
+def call(kernel, outs, args, flops, scratch=(), vmem=10, place=pltpu.VMEM, last=pltpu.VMEM):
     size = sum(math.prod(a.shape) * a.dtype.itemsize for a in (*outs, *args))
     return pl.pallas_call(
         kernel,
         out_shape=outs,
         in_specs=[pl.BlockSpec(memory_space=place)] * len(args),
-        out_specs=[VMEM] * len(outs),
+        out_specs=[VMEM] * (len(outs) - 1) + [pl.BlockSpec(memory_space=last)],
         scratch_shapes=list(scratch),
         compiler_params=pltpu.CompilerParams(vmem_limit_bytes=vmem << 20),
         cost_estimate=pl.CostEstimate(flops=flops, bytes_accessed=size, transcendentals=0),
@@ -204,24 +204,26 @@
     return 0.5 / jnp.sqrt(square + 1e-06)
 
 
-def start_kernel(unit, points, factor, first, second, copies, wide, done):
+def start_kernel(unit, points, factor, first, second, copies, value, wide, done):
     half, width = first.shape[0], points.shape[1]
     fetches = [
-        pltpu.make_async_copy(points, copies.at[0], done.at[0]),
+        pltpu.make_async_copy(points, value, done.at[0]),
         pltpu.make_async_copy(factor, wide, done.at[1]),
+    ]
+    fetches += [
+        pltpu.make_async_copy(points, copies.at[i], done.at[2 + i]) for i in range(copies.shape[0])
     ]
     for fetch in fetches:
         fetch.start()
-    for fetch in fetches:
+    fetches[0].wait()
+    first[:, :width] = value[:half, :]
+    second[:, :width] = value[half:, :]
+    fetches[1].wait()
+    hb = (wide[...] * unit).astype(BF16)
+    first[:, width:] = hb[:half]
+    second[:, width:] = hb[half:]
+    for fetch in fetches[2:]:
         fetch.wait()
-    value = copies[0]
-    hb = (wide[...] * unit).astype(BF16)
-    first[:, :width] = value[:half]
-    first[:, width:] = hb[:half]
-    second[:, :width] = value[half:]
-    second[:, width:] = hb[half:]
-    for i in range(1, copies.shape[0]):
-        copies[i] = value
 
 
 def step_kernel(before, after, ah_ref, hh_ref, h_ref, out, *copies):
@@ -252,9 +254,14 @@
         [*[shape((half, width + rank), BF16)] * 2, shape((nz, pts, width), BF16)],
         [points, factor],
         1,
-        [pltpu.VMEM((pts, rank), F32), pltpu.SemaphoreType.DMA((2,))],
+        [
+            pltpu.VMEM((pts, width), BF16),
+            pltpu.VMEM((pts, rank), F32),
+            pltpu.SemaphoreType.DMA((2 + nz,)),
+        ],
         vmem=60,
         place=pl.ANY,
+        last=pl.ANY,
     )
     tie = lax.optimization_barrier
     along_z = lax.all_to_all(copies, Z, 0, 0, tiled=True)

time: 152 us -> 183 us (1.20)
  Pallas kernels: 10.4 us -> 42 us
    pallas_call x9, Pallas kernels: 10.4 us -> 42 us  [call(): pl.pallas_call(kernel, out_shape=outs, in_specs=[pl.BlockSpec(memory_spac...]
where the time goes in v7:
time: 183 us
  blocking collectives  61 us (33%)
  Pallas kernels  42 us (23%)
  starting transfers between devices  40.4 us (22%)
  waiting for transfers between devices  35 us (19%)
  local copies, waits for them, and re-layouts  2.47 us (1%)
    pallas_call x9, Pallas kernels, call(): pl.pallas_call(kernel, out_shape=outs, in_specs=[pl.BlockSpec(memory_spac...  42 us
    all_to_all x2, blocking collectives, over_z(): mine = lax.all_to_all(mine.astype(jnp.float16), Z, 0, 0, tiled=True)  30.9 us
    ppermute x17, starting transfers between devices, from_ahead(): lax.ppermute(value, axis, [((i + steps) % length, i) for i in range(lengt...  24.1 us
    all_to_all x1, blocking collectives, shards(): lax.all_to_all(message, ROW, 0, 0, tiled=True)  17.6 us
    ppermute x17, waiting for transfers between devices, from_ahead(): lax.ppermute(value, axis, [((i + steps) % length, i) for i in range(lengt...  15.9 us
    all_to_all x1, blocking collectives, shards(): gathered = lax.all_to_all(message, COL, 0, 0, tiled=True)  12.6 us
    all_to_all x1, waiting for transfers between devices, shards(): lax.all_to_all(hb_cols, COL, 0, 0, tiled=True).reshape(group, rank)  10.8 us
    all_to_all x1, starting transfers between devices, shards(): along_z = lax.all_to_all(copies, Z, 0, 0, tiled=True)  9.16 us
  transfers between devices with their start and end apart: 20, of which 10 were waited for; matrix products, arithmetic and copies ran while one was open for 0% of the time, Pallas kernels for 2%

profile of v7, /device:TPU:1, one launch (start us, length us, event | category | flops | bytes accessed | tf_op | source)
XLA Modules:
  0.0 182.7 jit_solution(542584023842190186)
XLA Ops:
  0.0 33.6 %shard_map.28 = (bf16[32,1280]{1,0:T(8,128)(2,1)}, bf16[32,1280]{1,0:T(8,128)(2,1)}, bf16[8,64,1024]{2,1,0:T(8,128)(2,1)}) custom-call(bf16[64,1024]{1,0:T(8,128)(2,1)} %points.1, f32[64,256]{1,0:T(8,128)} %h_ref.1), custom_call_target="tpu_custom_call" | custom-call | flops 1 | bytes 1409024 | tf_op jit(solution)/shard_map/pallas_call | solution.py:37
  33.6 9.2 %all-to-all-start = ((bf16[8,64,1024]{2,1,0:T(8,128)(2,1)}), bf16[8,64,1024]{2,1,0:T(8,128)(2,1)S(1)}, u32[]{:S(2)}, u32[]{:S(2)}) async-start(bf16[8,64,1024]{2,1,0:T(8,128)(2,1)} %get-tuple-element.47), calls=%async_computation | async-start | bytes 2097152 | tf_op jit(solution)/shard_map/all_to_all | solution.py:267
  42.8 2.6 %collective-permute-start = (bf16[32,1280]{1,0:T(8,128)(2,1)S(1)}, bf16[32,1280]{1,0:T(8,128)(2,1)S(1)}, u32[]{:S(2)}, u32[]{:S(2)}) collective-permute-start(bf16[32,1280]{1,0:T(8,128)(2,1)S(1)} %copy-done), channel_id=1, source_target_pairs={{1,0},{2,1},{3,2},{0,3},{5,4},{6,5},{7,6},{4,7},{9,8},{10,9},{11,1... | collective-permute-start | bytes 245768 | tf_op jit(solution)/shard_map/ppermute | solution.py:21
  46.5 2.7 %collective-permute-start.3 = (bf16[32,1280]{1,0:T(8,128)(2,1)S(1)}, bf16[32,1280]{1,0:T(8,128)(2,1)S(1)}, u32[]{:S(2)}, u32[]{:S(2)}) collective-permute-start(bf16[32,1280]{1,0:T(8,128)(2,1)S(1)} %copy-done.1), channel_id=1, source_target_pairs={{4,0},{8,4},{12,8},{0,12},{5,1},{9,5},{13,9},{1,13},{6,2},{10,6},{... | collective-permute-start | bytes 245768 | tf_op jit(solution)/shard_map/ppermute | solution.py:21
  51.0 3.3 %collective-permute-done.4.by2 = bf16[32,1280]{1,0:T(8,128)(2,1)S(1)} collective-permute-done((bf16[32,1280]{1,0:T(8,128)(2,1)S(1)}, bf16[32,1280]{1,0:T(8,128)(2,1)S(1)}, u32[]{:S(2)}, u32[]{:S(2)}) %collective-permute-start.4) | collective-permute-done | bytes 81952 | tf_op jit(solution)/shard_map/ppermute | solution.py:21
  54.3 0.9 collective-permute-done.5.by3
  56.6 1.9 %collective-permute-start.7 = (bf16[4,32,1280]{2,1,0:T(8,128)(2,1)S(1)}, bf16[4,32,1280]{2,1,0:T(8,128)(2,1)S(1)}, u32[]{:S(2)}, u32[]{:S(2)}) collective-permute-start(bf16[4,32,1280]{2,1,0:T(8,128)(2,1)S(1)} %pad_maximum_fusion.1), channel_id=1, source_target_pairs={{2,0},{3,1},{0,2},{1,3},{6,4},{7,5},{4,6},{5,7},{10,8},{11,9},{8,1... | collective-permute-start | bytes 983048 | tf_op jit(solution)/shard_map/ppermute | solution.py:21
  58.6 2.1 %collective-permute-start.9 = (bf16[4,32,1280]{2,1,0:T(8,128)(2,1)S(1)}, bf16[4,32,1280]{2,1,0:T(8,128)(2,1)S(1)}, u32[]{:S(2)}, u32[]{:S(2)}) collective-permute-start(bf16[4,32,1280]{2,1,0:T(8,128)(2,1)S(1)} %pad_maximum_fusion.1), channel_id=1, source_target_pairs={{1,0},{2,1},{3,2},{0,3},{5,4},{6,5},{7,6},{4,7},{9,8},{10,9},{11,1... | collective-permute-start | bytes 983048 | tf_op jit(solution)/shard_map/ppermute | solution.py:21
  60.6 0.8 collective-permute-start.10
  61.4 1.7 collective-permute-done.6.y2
  63.1 1.5 collective-permute-start.11
  64.6 5.7 %collective-permute-done.8.y1 = bf16[4,32,1280]{2,1,0:T(8,128)(2,1)S(1)} collective-permute-done((bf16[4,32,1280]{2,1,0:T(8,128)(2,1)S(1)}, bf16[4,32,1280]{2,1,0:T(8,128)(2,1)S(1)}, u32[]{:S(2)}, u32[]{:S(2)}) %collective-permute-start.8) | collective-permute-done | bytes 327712 | tf_op jit(solution)/shard_map/ppermute | solution.py:21
  70.3 1.8 collective-permute-done.9.x1
  72.8 5.7 %collective-permute-start.12 = (bf16[512,1024]{1,0:T(8,128)(2,1)S(1)}, bf16[512,1024]{1,0:T(8,128)(2,1)S(1)}, u32[]{:S(2)}, u32[]{:S(2)}) collective-permute-start(bf16[512,1024]{1,0:T(8,128)(2,1)S(1)} %bitcast.28), channel_id=1, source_target_pairs={{16,0},{0,16},{17,1},{1,17},{18,2},{2,18},{19,3},{3,19},{20,4},{4,... | collective-permute-start | bytes 3145736 | tf_op jit(solution)/shard_map/ppermute | solution.py:21
  78.5 1.0 copy-done.3
  80.5 1.9 %shard_map.30 = (f32[512,1024]{1,0:T(8,128)S(1)}, f32[4,128]{1,0:T(4,128)S(1)}) custom-call(bf16[512,1024]{1,0:T(8,128)(2,1)S(1)} %bitcast.29, bf16[1024,1024]{1,0:T(8,128)(2,1)S(1)} %get-tuple-element.55.cols, f32[8,128]{1,0:T(8,128)S(1)} %get-tuple-element.56.sq), custom_call_target="tpu_custom_call" | custom-call | flops 1073741824 | bytes 5249024 | tf_op jit(solution)/shard_map/pallas_call | solution.py:37
  82.5 1.9 %shard_map.31 = (f32[512,1024]{1,0:T(8,128)S(1)}, f32[16,24,128]{2,1,0:T(8,128)S(1)}) custom-call(bf16[512,1024]{1,0:T(8,128)(2,1)S(1)} %collective-permute-done.12.rows_ref, bf16[1024,1024]{1,0:T(8,128)(2,1)S(1)} %get-tuple-element.55.cols, f32[8,128]{1,0:T(8,128)S(1)} %get-tuple-element.56.sq, f32[4,128]{1,0:T(4,128)S(1)} %get-tuple-element.58.own_sums, ...), custom_call_target="tpu_custom_call" | custom-call | flops 1073741824 | bytes 5478400 | tf_op jit(solution)/shard_map/pallas_call | solution.py:37
  84.4 17.6 %all_to_all.35.got = f32[16,24,128]{2,1,0:T(8,128)S(1)} all-to-all(f32[16,24,128]{2,1,0:T(8,128)S(1)} %get-tuple-element.60), channel_id=1, replica_groups=mesh['row_0'=8,'row_1'=2,'col_0'=4,'col_1'=4] {'row_0','row_1'}, dimensions={0} | all-to-all | bytes 393216 | tf_op jit(solution)/shard_map/all_to_all | solution.py:314
  102.1 12.6 %all_to_all.36.got = f32[16,40,128]{2,1,0:T(8,128)S(1)} all-to-all(f32[16,40,128]{2,1,0:T(8,128)S(1)} %get-tuple-element.62), channel_id=1, replica_groups=mesh['row_0'=8,'row_1'=2,'col_0'=4,'col_1'=4] {'col_0','col_1'}, dimensions={0} | all-to-all | bytes 655360 | tf_op jit(solution)/shard_map/all_to_all | solution.py:317
  114.6 0.8 shard_map.34
  115.5 1.2 collective-permute-start.14
  116.7 0.9 shard_map.33
  118.3 14.8 %all_to_all.37 = f16[8,64,256]{2,1,0:T(8,128)(2,1)S(1)} all-to-all(f16[8,64,256]{2,1,0:T(8,128)(2,1)S(1)} %bitcast.41), channel_id=1, replica_groups=mesh['row_0'=8,'row_1'=2,'col_0'=4,'col_1'=4] {'row_0'}, dimensions={0} | all-to-all | bytes 524288 | tf_op jit(solution)/shard_map/all_to_all | solution.py:335
  133.2 1.1 shard_map.35
  134.3 3.6 %all-to-all-start.4 = ((bf16[16,64,256]{2,1,0:T(8,128)(2,1)}), bf16[16,64,256]{2,1,0:T(8,128)(2,1)S(1)}, u32[]{:S(2)}, u32[]{:S(2)}) async-start(bf16[16,64,256]{2,1,0:T(8,128)(2,1)} %get-tuple-element.70), calls=%async_computation.4 | async-start | bytes 1048576 | tf_op jit(solution)/shard_map/all_to_all | solution.py:347
  137.9 10.8 %all-to-all-done.4 = bf16[16,64,256]{2,1,0:T(8,128)(2,1)S(1)} async-done(((bf16[16,64,256]{2,1,0:T(8,128)(2,1)}), bf16[16,64,256]{2,1,0:T(8,128)(2,1)S(1)}, u32[]{:S(2)}, u32[]{:S(2)}) %all-to-all-start.4) | async-done | bytes 524320 | tf_op jit(solution)/shard_map/all_to_all | solution.py:347
  149.1 1.7 collective-permute-start.15
  151.3 1.2 collective-permute-done.16
  153.1 16.1 %all_to_all.38 = f16[8,80,256]{2,1,0:T(8,128)(2,1)S(1)} all-to-all(f16[8,80,256]{2,1,0:T(8,128)(2,1)S(1)} %pad_maximum_fusion.2), channel_id=1, replica_groups=mesh['row_0'=8,'row_1'=2,'col_0'=4,'col_1'=4] {'row_0'}, dimensions={0} | all-to-all | bytes 655360 | tf_op jit(solution)/shard_map/all_to_all | solution.py:335
  170.0 3.5 %all-to-all-start.6 = ((f32[16,16,256]{2,1,0:T(8,128)}), f32[16,16,256]{2,1,0:T(8,128)S(1)}, u32[]{:S(2)}, u32[]{:S(2)}) async-start(f32[16,16,256]{2,1,0:T(8,128)} %broadcast_in_dim.7), calls=%async_computation.6 | async-start | bytes 524288 | tf_op jit(solution)/shard_map/all_to_all | solution.py:27
  173.5 8.3 %all-to-all-done.6 = f32[16,16,256]{2,1,0:T(8,128)S(1)} async-done(((f32[16,16,256]{2,1,0:T(8,128)}), f32[16,16,256]{2,1,0:T(8,128)S(1)}, u32[]{:S(2)}, u32[]{:S(2)}) %all-to-all-start.6) | async-done | bytes 262176 | tf_op jit(solution)/shard_map/all_to_all | solution.py:27
  181.8 0.9 shard_map.36
  (48 shorter events, 9.3 us)
Async XLA Ops:
  33.6 9.2 %copy-start = (bf16[32,1280]{1,0:T(8,128)(2,1)S(1)}, bf16[32,1280]{1,0:T(8,128)(2,1)}, u32[]{:S(2)}) copy-start(bf16[32,1280]{1,0:T(8,128)(2,1)} %get-tuple-element.39.ax0) | copy-start | bytes 245764
  33.6 12.9 %copy-start.1 = (bf16[32,1280]{1,0:T(8,128)(2,1)S(1)}, bf16[32,1280]{1,0:T(8,128)(2,1)}, u32[]{:S(2)}) copy-start(bf16[32,1280]{1,0:T(8,128)(2,1)} %get-tuple-element.40.by0) | copy-start | bytes 245764
  33.6 39.2 %all-to-all-start = ((bf16[8,64,1024]{2,1,0:T(8,128)(2,1)}), bf16[8,64,1024]{2,1,0:T(8,128)(2,1)S(1)}, u32[]{:S(2)}, u32[]{:S(2)}) async-start(bf16[8,64,1024]{2,1,0:T(8,128)(2,1)} %get-tuple-element.47), calls=%async_computation | async-start | bytes 2097152 | tf_op jit(solution)/shard_map/all_to_all | solution.py:267
  42.8 6.8 %collective-permute-start = (bf16[32,1280]{1,0:T(8,128)(2,1)S(1)}, bf16[32,1280]{1,0:T(8,128)(2,1)S(1)}, u32[]{:S(2)}, u32[]{:S(2)}) collective-permute-start(bf16[32,1280]{1,0:T(8,128)(2,1)S(1)} %copy-done), channel_id=1, source_target_pairs={{1,0},{2,1},{3,2},{0,3},{5,4},{6,5},{7,6},{4,7},{9,8},{10,9},{11,1... | collective-permute-start | bytes 245768 | tf_op jit(solution)/shard_map/ppermute | solution.py:21
  45.4 4.9 %collective-permute-start.1 = (bf16[32,1280]{1,0:T(8,128)(2,1)S(1)}, bf16[32,1280]{1,0:T(8,128)(2,1)S(1)}, u32[]{:S(2)}, u32[]{:S(2)}) collective-permute-start(bf16[32,1280]{1,0:T(8,128)(2,1)S(1)} %copy-done), channel_id=1, source_target_pairs={{2,0},{3,1},{0,2},{1,3},{6,4},{7,5},{4,6},{5,7},{10,8},{11,9},{8,1... | collective-permute-start | bytes 245768 | tf_op jit(solution)/shard_map/ppermute | solution.py:21
  45.9 5.2 %collective-permute-start.2 = (bf16[32,1280]{1,0:T(8,128)(2,1)S(1)}, bf16[32,1280]{1,0:T(8,128)(2,1)S(1)}, u32[]{:S(2)}, u32[]{:S(2)}) collective-permute-start(bf16[32,1280]{1,0:T(8,128)(2,1)S(1)} %copy-done), channel_id=1, source_target_pairs={{3,0},{0,1},{1,2},{2,3},{7,4},{4,5},{5,6},{6,7},{11,8},{8,9},{9,10... | collective-permute-start | bytes 245768 | tf_op jit(solution)/shard_map/ppermute | solution.py:21
  46.5 4.5 %collective-permute-start.3 = (bf16[32,1280]{1,0:T(8,128)(2,1)S(1)}, bf16[32,1280]{1,0:T(8,128)(2,1)S(1)}, u32[]{:S(2)}, u32[]{:S(2)}) collective-permute-start(bf16[32,1280]{1,0:T(8,128)(2,1)S(1)} %copy-done.1), channel_id=1, source_target_pairs={{4,0},{8,4},{12,8},{0,12},{5,1},{9,5},{13,9},{1,13},{6,2},{10,6},{... | collective-permute-start | bytes 245768 | tf_op jit(solution)/shard_map/ppermute | solution.py:21
  49.2 5.1 %collective-permute-start.4 = (bf16[32,1280]{1,0:T(8,128)(2,1)S(1)}, bf16[32,1280]{1,0:T(8,128)(2,1)S(1)}, u32[]{:S(2)}, u32[]{:S(2)}) collective-permute-start(bf16[32,1280]{1,0:T(8,128)(2,1)S(1)} %copy-done.1), channel_id=1, source_target_pairs={{8,0},{12,4},{0,8},{4,12},{9,1},{13,5},{1,9},{5,13},{10,2},{14,6},... | collective-permute-start | bytes 245768 | tf_op jit(solution)/shard_map/ppermute | solution.py:21
  49.6 5.6 %collective-permute-start.5 = (bf16[32,1280]{1,0:T(8,128)(2,1)S(1)}, bf16[32,1280]{1,0:T(8,128)(2,1)S(1)}, u32[]{:S(2)}, u32[]{:S(2)}) collective-permute-start(bf16[32,1280]{1,0:T(8,128)(2,1)S(1)} %copy-done.1), channel_id=1, source_target_pairs={{12,0},{0,4},{4,8},{8,12},{13,1},{1,5},{5,9},{9,13},{14,2},{2,6},{... | collective-permute-start | bytes 245768 | tf_op jit(solution)/shard_map/ppermute | solution.py:21
  55.2 7.9 %collective-permute-start.6 = (bf16[4,32,1280]{2,1,0:T(8,128)(2,1)S(1)}, bf16[4,32,1280]{2,1,0:T(8,128)(2,1)S(1)}, u32[]{:S(2)}, u32[]{:S(2)}) collective-permute-start(bf16[4,32,1280]{2,1,0:T(8,128)(2,1)S(1)} %pad_maximum_fusion), channel_id=1, source_target_pairs={{8,0},{12,4},{0,8},{4,12},{9,1},{13,5},{1,9},{5,13},{10,2},{14,6},... | collective-permute-start | bytes 983048 | tf_op jit(solution)/shard_map/ppermute | solution.py:21
  55.9 14.4 %collective-permute-start.8 = (bf16[4,32,1280]{2,1,0:T(8,128)(2,1)S(1)}, bf16[4,32,1280]{2,1,0:T(8,128)(2,1)S(1)}, u32[]{:S(2)}, u32[]{:S(2)}) collective-permute-start(bf16[4,32,1280]{2,1,0:T(8,128)(2,1)S(1)} %pad_maximum_fusion), channel_id=1, source_target_pairs={{4,0},{8,4},{12,8},{0,12},{5,1},{9,5},{13,9},{1,13},{6,2},{10,6},{... | collective-permute-start | bytes 983048 | tf_op jit(solution)/shard_map/ppermute | solution.py:21
  56.6 8.0 %collective-permute-start.7 = (bf16[4,32,1280]{2,1,0:T(8,128)(2,1)S(1)}, bf16[4,32,1280]{2,1,0:T(8,128)(2,1)S(1)}, u32[]{:S(2)}, u32[]{:S(2)}) collective-permute-start(bf16[4,32,1280]{2,1,0:T(8,128)(2,1)S(1)} %pad_maximum_fusion.1), channel_id=1, source_target_pairs={{2,0},{3,1},{0,2},{1,3},{6,4},{7,5},{4,6},{5,7},{10,8},{11,9},{8,1... | collective-permute-start | bytes 983048 | tf_op jit(solution)/shard_map/ppermute | solution.py:21
  58.6 13.5 %collective-permute-start.9 = (bf16[4,32,1280]{2,1,0:T(8,128)(2,1)S(1)}, bf16[4,32,1280]{2,1,0:T(8,128)(2,1)S(1)}, u32[]{:S(2)}, u32[]{:S(2)}) collective-permute-start(bf16[4,32,1280]{2,1,0:T(8,128)(2,1)S(1)} %pad_maximum_fusion.1), channel_id=1, source_target_pairs={{1,0},{2,1},{3,2},{0,3},{5,4},{6,5},{7,6},{4,7},{9,8},{10,9},{11,1... | collective-permute-start | bytes 983048 | tf_op jit(solution)/shard_map/ppermute | solution.py:21
  60.6 11.5 %collective-permute-start.10 = (bf16[4,32,1280]{2,1,0:T(8,128)(2,1)S(1)}, bf16[4,32,1280]{2,1,0:T(8,128)(2,1)S(1)}, u32[]{:S(2)}, u32[]{:S(2)}) collective-permute-start(bf16[4,32,1280]{2,1,0:T(8,128)(2,1)S(1)} %pad_maximum_fusion), channel_id=1, source_target_pairs={{12,0},{0,4},{4,8},{8,12},{13,1},{1,5},{5,9},{9,13},{14,2},{2,6},{... | collective-permute-start | bytes 983048 | tf_op jit(solution)/shard_map/ppermute | solution.py:21
  63.1 9.0 %collective-permute-start.11 = (bf16[4,32,1280]{2,1,0:T(8,128)(2,1)S(1)}, bf16[4,32,1280]{2,1,0:T(8,128)(2,1)S(1)}, u32[]{:S(2)}, u32[]{:S(2)}) collective-permute-start(bf16[4,32,1280]{2,1,0:T(8,128)(2,1)S(1)} %pad_maximum_fusion.1), channel_id=1, source_target_pairs={{3,0},{0,1},{1,2},{2,3},{7,4},{4,5},{5,6},{6,7},{11,8},{8,9},{9,10... | collective-permute-start | bytes 983048 | tf_op jit(solution)/shard_map/ppermute | solution.py:21
  72.1 0.7 copy-start.2
  72.8 9.6 %collective-permute-start.12 = (bf16[512,1024]{1,0:T(8,128)(2,1)S(1)}, bf16[512,1024]{1,0:T(8,128)(2,1)S(1)}, u32[]{:S(2)}, u32[]{:S(2)}) collective-permute-start(bf16[512,1024]{1,0:T(8,128)(2,1)S(1)} %bitcast.28), channel_id=1, source_target_pairs={{16,0},{0,16},{17,1},{1,17},{18,2},{2,18},{19,3},{3,19},{20,4},{4,... | collective-permute-start | bytes 3145736 | tf_op jit(solution)/shard_map/ppermute | solution.py:21
  78.5 1.0 copy-start.3
  80.2 2.2 %collective-permute-start.13 = (f32[16,256]{1,0:T(8,128)S(1)}, f32[16,256]{1,0:T(8,128)S(1)}, u32[]{:S(2)}, u32[]{:S(2)}) collective-permute-start(f32[16,256]{1,0:T(8,128)S(1)} %get-tuple-element.59.part), channel_id=1, source_target_pairs={{16,0},{0,16},{17,1},{1,17},{18,2},{2,18},{19,3},{3,19},{20,4},{4,... | collective-permute-start | bytes 49160 | tf_op jit(solution)/shard_map/ppermute | solution.py:21
  115.5 2.7 %collective-permute-start.14 = (f32[512,256]{1,0:T(8,128)S(1)}, f32[512,256]{1,0:T(8,128)S(1)}, u32[]{:S(2)}, u32[]{:S(2)}) collective-permute-start(f32[512,256]{1,0:T(8,128)S(1)} %get-tuple-element.67), channel_id=1, source_target_pairs={{16,0},{0,16},{17,1},{1,17},{18,2},{2,18},{19,3},{3,19},{20,4},{4,... | collective-permute-start | bytes 1572872 | tf_op jit(solution)/shard_map/ppermute | solution.py:21
  116.7 16.5 %copy-start.4 = (f32[64,256]{1,0:T(8,128)S(1)}, f32[64,256]{1,0:T(8,128)}, u32[]{:S(2)}) copy-start(f32[64,256]{1,0:T(8,128)} %h_ref.1) | copy-start | bytes 196612
  134.3 14.4 %all-to-all-start.4 = ((bf16[16,64,256]{2,1,0:T(8,128)(2,1)}), bf16[16,64,256]{2,1,0:T(8,128)(2,1)S(1)}, u32[]{:S(2)}, u32[]{:S(2)}) async-start(bf16[16,64,256]{2,1,0:T(8,128)(2,1)} %get-tuple-element.70), calls=%async_computation.4 | async-start | bytes 1048576 | tf_op jit(solution)/shard_map/all_to_all | solution.py:347
  149.1 3.4 %collective-permute-start.15 = (f32[512,256]{1,0:T(8,128)S(1)}, f32[512,256]{1,0:T(8,128)S(1)}, u32[]{:S(2)}, u32[]{:S(2)}) collective-permute-start(f32[512,256]{1,0:T(8,128)S(1)} %fusion.3), channel_id=1, source_target_pairs={{16,0},{0,16},{17,1},{1,17},{18,2},{2,18},{19,3},{3,19},{20,4},{4,... | collective-permute-start | bytes 1572872 | tf_op jit(solution)/shard_map/ppermute | solution.py:21
  151.2 1.3 collective-permute-start.16
  170.0 11.8 %all-to-all-start.6 = ((f32[16,16,256]{2,1,0:T(8,128)}), f32[16,16,256]{2,1,0:T(8,128)S(1)}, u32[]{:S(2)}, u32[]{:S(2)}) async-start(f32[16,16,256]{2,1,0:T(8,128)} %broadcast_in_dim.7), calls=%async_computation.6 | async-start | bytes 524288 | tf_op jit(solution)/shard_map/all_to_all | solution.py:27

commit v8 on v7

--- a/solution.py
+++ b/solution.py
@@ -210,20 +210,22 @@
         pltpu.make_async_copy(points, value, done.at[0]),
         pltpu.make_async_copy(factor, wide, done.at[1]),
     ]
-    fetches += [
-        pltpu.make_async_copy(points, copies.at[i], done.at[2 + i]) for i in range(copies.shape[0])
-    ]
     for fetch in fetches:
         fetch.start()
     fetches[0].wait()
+    stores = [
+        pltpu.make_async_copy(value, copies.at[i], done.at[2 + i]) for i in range(copies.shape[0])
+    ]
+    for store in stores:
+        store.start()
     first[:, :width] = value[:half, :]
     second[:, :width] = value[half:, :]
     fetches[1].wait()
     hb = (wide[...] * unit).astype(BF16)
     first[:, width:] = hb[:half]
     second[:, width:] = hb[half:]
-    for fetch in fetches[2:]:
-        fetch.wait()
+    for store in stores:
+        store.wait()
 
 
 def step_kernel(before, after, ah_ref, hh_ref, h_ref, out, *copies):

time: 183 us -> 152 us (0.83)
  Pallas kernels: 42 us -> 11.1 us
    pallas_call x9, Pallas kernels: 42 us -> 11.1 us  [call(): pl.pallas_call(kernel, out_shape=outs, in_specs=[pl.BlockSpec(memory_spac...]
where the time goes in v8:
time: 152 us
  blocking collectives  61 us (40%)
  starting transfers between devices  40.4 us (27%)
  waiting for transfers between devices  35 us (23%)
  Pallas kernels  11.1 us (7%)
  local copies, waits for them, and re-layouts  2.47 us (2%)
    all_to_all x2, blocking collectives, over_z(): mine = lax.all_to_all(mine.astype(jnp.float16), Z, 0, 0, tiled=True)  30.9 us
    ppermute x17, starting transfers between devices, from_ahead(): lax.ppermute(value, axis, [((i + steps) % length, i) for i in range(lengt...  24.1 us
    all_to_all x1, blocking collectives, shards(): lax.all_to_all(message, ROW, 0, 0, tiled=True)  17.5 us
    ppermute x17, waiting for transfers between devices, from_ahead(): lax.ppermute(value, axis, [((i + steps) % length, i) for i in range(lengt...  15.9 us
    all_to_all x1, blocking collectives, shards(): gathered = lax.all_to_all(message, COL, 0, 0, tiled=True)  12.6 us
    pallas_call x9, Pallas kernels, call(): pl.pallas_call(kernel, out_shape=outs, in_specs=[pl.BlockSpec(memory_spac...  11.1 us
    all_to_all x1, waiting for transfers between devices, shards(): lax.all_to_all(hb_cols, COL, 0, 0, tiled=True).reshape(group, rank)  10.8 us
    all_to_all x1, starting transfers between devices, shards(): along_z = lax.all_to_all(copies, Z, 0, 0, tiled=True)  9.16 us
  transfers between devices with their start and end apart: 20, of which 10 were waited for; matrix products, arithmetic and copies ran while one was open for 0% of the time, Pallas kernels for 2%

profile of v8, /device:TPU:1, one launch (start us, length us, event | category | flops | bytes accessed | tf_op | source)
XLA Modules:
  0.0 151.7 jit_solution(3641657474937627496)
XLA Ops:
  0.0 2.6 %shard_map.28 = (bf16[32,1280]{1,0:T(8,128)(2,1)}, bf16[32,1280]{1,0:T(8,128)(2,1)}, bf16[8,64,1024]{2,1,0:T(8,128)(2,1)}) custom-call(bf16[64,1024]{1,0:T(8,128)(2,1)} %points.1, f32[64,256]{1,0:T(8,128)} %h_ref.1), custom_call_target="tpu_custom_call" | custom-call | flops 1 | bytes 1409024 | tf_op jit(solution)/shard_map/pallas_call | solution.py:37
  2.7 9.2 %all-to-all-start = ((bf16[8,64,1024]{2,1,0:T(8,128)(2,1)}), bf16[8,64,1024]{2,1,0:T(8,128)(2,1)S(1)}, u32[]{:S(2)}, u32[]{:S(2)}) async-start(bf16[8,64,1024]{2,1,0:T(8,128)(2,1)} %get-tuple-element.47), calls=%async_computation | async-start | bytes 2097152 | tf_op jit(solution)/shard_map/all_to_all | solution.py:269
  11.8 2.6 %collective-permute-start = (bf16[32,1280]{1,0:T(8,128)(2,1)S(1)}, bf16[32,1280]{1,0:T(8,128)(2,1)S(1)}, u32[]{:S(2)}, u32[]{:S(2)}) collective-permute-start(bf16[32,1280]{1,0:T(8,128)(2,1)S(1)} %copy-done), channel_id=1, source_target_pairs={{1,0},{2,1},{3,2},{0,3},{5,4},{6,5},{7,6},{4,7},{9,8},{10,9},{11,1... | collective-permute-start | bytes 245768 | tf_op jit(solution)/shard_map/ppermute | solution.py:21
  15.5 2.7 %collective-permute-start.3 = (bf16[32,1280]{1,0:T(8,128)(2,1)S(1)}, bf16[32,1280]{1,0:T(8,128)(2,1)S(1)}, u32[]{:S(2)}, u32[]{:S(2)}) collective-permute-start(bf16[32,1280]{1,0:T(8,128)(2,1)S(1)} %copy-done.1), channel_id=1, source_target_pairs={{4,0},{8,4},{12,8},{0,12},{5,1},{9,5},{13,9},{1,13},{6,2},{10,6},{... | collective-permute-start | bytes 245768 | tf_op jit(solution)/shard_map/ppermute | solution.py:21
  20.1 3.3 %collective-permute-done.4.by2 = bf16[32,1280]{1,0:T(8,128)(2,1)S(1)} collective-permute-done((bf16[32,1280]{1,0:T(8,128)(2,1)S(1)}, bf16[32,1280]{1,0:T(8,128)(2,1)S(1)}, u32[]{:S(2)}, u32[]{:S(2)}) %collective-permute-start.4) | collective-permute-done | bytes 81952 | tf_op jit(solution)/shard_map/ppermute | solution.py:21
  23.3 0.9 collective-permute-done.5.by3
  25.6 1.9 %collective-permute-start.7 = (bf16[4,32,1280]{2,1,0:T(8,128)(2,1)S(1)}, bf16[4,32,1280]{2,1,0:T(8,128)(2,1)S(1)}, u32[]{:S(2)}, u32[]{:S(2)}) collective-permute-start(bf16[4,32,1280]{2,1,0:T(8,128)(2,1)S(1)} %pad_maximum_fusion.1), channel_id=1, source_target_pairs={{2,0},{3,1},{0,2},{1,3},{6,4},{7,5},{4,6},{5,7},{10,8},{11,9},{8,1... | collective-permute-start | bytes 983048 | tf_op jit(solution)/shard_map/ppermute | solution.py:21
  27.6 2.1 %collective-permute-start.9 = (bf16[4,32,1280]{2,1,0:T(8,128)(2,1)S(1)}, bf16[4,32,1280]{2,1,0:T(8,128)(2,1)S(1)}, u32[]{:S(2)}, u32[]{:S(2)}) collective-permute-start(bf16[4,32,1280]{2,1,0:T(8,128)(2,1)S(1)} %pad_maximum_fusion.1), channel_id=1, source_target_pairs={{1,0},{2,1},{3,2},{0,3},{5,4},{6,5},{7,6},{4,7},{9,8},{10,9},{11,1... | collective-permute-start | bytes 983048 | tf_op jit(solution)/shard_map/ppermute | solution.py:21
  29.6 0.8 collective-permute-start.10
  30.5 1.7 %collective-permute-done.6.y2 = bf16[4,32,1280]{2,1,0:T(8,128)(2,1)S(1)} collective-permute-done((bf16[4,32,1280]{2,1,0:T(8,128)(2,1)S(1)}, bf16[4,32,1280]{2,1,0:T(8,128)(2,1)S(1)}, u32[]{:S(2)}, u32[]{:S(2)}) %collective-permute-start.6) | collective-permute-done | bytes 327712 | tf_op jit(solution)/shard_map/ppermute | solution.py:21
  32.1 1.5 %collective-permute-start.11 = (bf16[4,32,1280]{2,1,0:T(8,128)(2,1)S(1)}, bf16[4,32,1280]{2,1,0:T(8,128)(2,1)S(1)}, u32[]{:S(2)}, u32[]{:S(2)}) collective-permute-start(bf16[4,32,1280]{2,1,0:T(8,128)(2,1)S(1)} %pad_maximum_fusion.1), channel_id=1, source_target_pairs={{3,0},{0,1},{1,2},{2,3},{7,4},{4,5},{5,6},{6,7},{11,8},{8,9},{9,10... | collective-permute-start | bytes 983048 | tf_op jit(solution)/shard_map/ppermute | solution.py:21
  33.7 5.7 %collective-permute-done.8.y1 = bf16[4,32,1280]{2,1,0:T(8,128)(2,1)S(1)} collective-permute-done((bf16[4,32,1280]{2,1,0:T(8,128)(2,1)S(1)}, bf16[4,32,1280]{2,1,0:T(8,128)(2,1)S(1)}, u32[]{:S(2)}, u32[]{:S(2)}) %collective-permute-start.8) | collective-permute-done | bytes 327712 | tf_op jit(solution)/shard_map/ppermute | solution.py:21
  39.3 1.8 %collective-permute-done.9.x1 = bf16[4,32,1280]{2,1,0:T(8,128)(2,1)S(1)} collective-permute-done((bf16[4,32,1280]{2,1,0:T(8,128)(2,1)S(1)}, bf16[4,32,1280]{2,1,0:T(8,128)(2,1)S(1)}, u32[]{:S(2)}, u32[]{:S(2)}) %collective-permute-start.9) | collective-permute-done | bytes 327712 | tf_op jit(solution)/shard_map/ppermute | solution.py:21
  41.8 5.7 %collective-permute-start.12 = (bf16[512,1024]{1,0:T(8,128)(2,1)S(1)}, bf16[512,1024]{1,0:T(8,128)(2,1)S(1)}, u32[]{:S(2)}, u32[]{:S(2)}) collective-permute-start(bf16[512,1024]{1,0:T(8,128)(2,1)S(1)} %bitcast.28), channel_id=1, source_target_pairs={{16,0},{0,16},{17,1},{1,17},{18,2},{2,18},{19,3},{3,19},{20,4},{4,... | collective-permute-start | bytes 3145736 | tf_op jit(solution)/shard_map/ppermute | solution.py:21
  47.6 1.0 copy-done.3
  49.5 1.9 %shard_map.30 = (f32[512,1024]{1,0:T(8,128)S(1)}, f32[4,128]{1,0:T(4,128)S(1)}) custom-call(bf16[512,1024]{1,0:T(8,128)(2,1)S(1)} %bitcast.29, bf16[1024,1024]{1,0:T(8,128)(2,1)S(1)} %get-tuple-element.55.cols, f32[8,128]{1,0:T(8,128)S(1)} %get-tuple-element.56.sq), custom_call_target="tpu_custom_call" | custom-call | flops 1073741824 | bytes 5249024 | tf_op jit(solution)/shard_map/pallas_call | solution.py:37
  51.5 1.9 %shard_map.31 = (f32[512,1024]{1,0:T(8,128)S(1)}, f32[16,24,128]{2,1,0:T(8,128)S(1)}) custom-call(bf16[512,1024]{1,0:T(8,128)(2,1)S(1)} %collective-permute-done.12.rows_ref, bf16[1024,1024]{1,0:T(8,128)(2,1)S(1)} %get-tuple-element.55.cols, f32[8,128]{1,0:T(8,128)S(1)} %get-tuple-element.56.sq, f32[4,128]{1,0:T(4,128)S(1)} %get-tuple-element.58.own_sums, ...), custom_call_target="tpu_custom_call" | custom-call | flops 1073741824 | bytes 5478400 | tf_op jit(solution)/shard_map/pallas_call | solution.py:37
  53.4 17.5 %all_to_all.35.got = f32[16,24,128]{2,1,0:T(8,128)S(1)} all-to-all(f32[16,24,128]{2,1,0:T(8,128)S(1)} %get-tuple-element.60), channel_id=1, replica_groups=mesh['row_0'=8,'row_1'=2,'col_0'=4,'col_1'=4] {'row_0','row_1'}, dimensions={0} | all-to-all | bytes 393216 | tf_op jit(solution)/shard_map/all_to_all | solution.py:316
  71.1 12.6 %all_to_all.36.got = f32[16,40,128]{2,1,0:T(8,128)S(1)} all-to-all(f32[16,40,128]{2,1,0:T(8,128)S(1)} %get-tuple-element.62), channel_id=1, replica_groups=mesh['row_0'=8,'row_1'=2,'col_0'=4,'col_1'=4] {'col_0','col_1'}, dimensions={0} | all-to-all | bytes 655360 | tf_op jit(solution)/shard_map/all_to_all | solution.py:319
  83.7 0.8 shard_map.34
  84.5 1.2 collective-permute-start.14
  85.7 0.9 shard_map.33
  87.4 14.8 %all_to_all.37 = f16[8,64,256]{2,1,0:T(8,128)(2,1)S(1)} all-to-all(f16[8,64,256]{2,1,0:T(8,128)(2,1)S(1)} %bitcast.41), channel_id=1, replica_groups=mesh['row_0'=8,'row_1'=2,'col_0'=4,'col_1'=4] {'row_0'}, dimensions={0} | all-to-all | bytes 524288 | tf_op jit(solution)/shard_map/all_to_all | solution.py:337
  102.2 1.1 shard_map.35
  103.3 3.6 %all-to-all-start.4 = ((bf16[16,64,256]{2,1,0:T(8,128)(2,1)}), bf16[16,64,256]{2,1,0:T(8,128)(2,1)S(1)}, u32[]{:S(2)}, u32[]{:S(2)}) async-start(bf16[16,64,256]{2,1,0:T(8,128)(2,1)} %get-tuple-element.70), calls=%async_computation.4 | async-start | bytes 1048576 | tf_op jit(solution)/shard_map/all_to_all | solution.py:349
  106.9 10.8 %all-to-all-done.4 = bf16[16,64,256]{2,1,0:T(8,128)(2,1)S(1)} async-done(((bf16[16,64,256]{2,1,0:T(8,128)(2,1)}), bf16[16,64,256]{2,1,0:T(8,128)(2,1)S(1)}, u32[]{:S(2)}, u32[]{:S(2)}) %all-to-all-start.4) | async-done | bytes 524320 | tf_op jit(solution)/shard_map/all_to_all | solution.py:349
  118.2 1.7 %collective-permute-start.15 = (f32[512,256]{1,0:T(8,128)S(1)}, f32[512,256]{1,0:T(8,128)S(1)}, u32[]{:S(2)}, u32[]{:S(2)}) collective-permute-start(f32[512,256]{1,0:T(8,128)S(1)} %fusion.3), channel_id=1, source_target_pairs={{16,0},{0,16},{17,1},{1,17},{18,2},{2,18},{19,3},{3,19},{20,4},{4,... | collective-permute-start | bytes 1572872 | tf_op jit(solution)/shard_map/ppermute | solution.py:21
  120.3 1.2 collective-permute-done.16
  122.1 16.1 %all_to_all.38 = f16[8,80,256]{2,1,0:T(8,128)(2,1)S(1)} all-to-all(f16[8,80,256]{2,1,0:T(8,128)(2,1)S(1)} %pad_maximum_fusion.2), channel_id=1, replica_groups=mesh['row_0'=8,'row_1'=2,'col_0'=4,'col_1'=4] {'row_0'}, dimensions={0} | all-to-all | bytes 655360 | tf_op jit(solution)/shard_map/all_to_all | solution.py:337
  139.0 3.5 %all-to-all-start.6 = ((f32[16,16,256]{2,1,0:T(8,128)}), f32[16,16,256]{2,1,0:T(8,128)S(1)}, u32[]{:S(2)}, u32[]{:S(2)}) async-start(f32[16,16,256]{2,1,0:T(8,128)} %broadcast_in_dim.7), calls=%async_computation.6 | async-start | bytes 524288 | tf_op jit(solution)/shard_map/all_to_all | solution.py:27
  142.6 8.3 %all-to-all-done.6 = f32[16,16,256]{2,1,0:T(8,128)S(1)} async-done(((f32[16,16,256]{2,1,0:T(8,128)}), f32[16,16,256]{2,1,0:T(8,128)S(1)}, u32[]{:S(2)}, u32[]{:S(2)}) %all-to-all-start.6) | async-done | bytes 262176 | tf_op jit(solution)/shard_map/all_to_all | solution.py:27
  150.8 0.9 shard_map.36
  (48 shorter events, 9.3 us)
Async XLA Ops:
  2.6 9.2 %copy-start = (bf16[32,1280]{1,0:T(8,128)(2,1)S(1)}, bf16[32,1280]{1,0:T(8,128)(2,1)}, u32[]{:S(2)}) copy-start(bf16[32,1280]{1,0:T(8,128)(2,1)} %get-tuple-element.39.ax0) | copy-start | bytes 245764
  2.7 12.9 %copy-start.1 = (bf16[32,1280]{1,0:T(8,128)(2,1)S(1)}, bf16[32,1280]{1,0:T(8,128)(2,1)}, u32[]{:S(2)}) copy-start(bf16[32,1280]{1,0:T(8,128)(2,1)} %get-tuple-element.40.by0) | copy-start | bytes 245764
  2.7 39.2 %all-to-all-start = ((bf16[8,64,1024]{2,1,0:T(8,128)(2,1)}), bf16[8,64,1024]{2,1,0:T(8,128)(2,1)S(1)}, u32[]{:S(2)}, u32[]{:S(2)}) async-start(bf16[8,64,1024]{2,1,0:T(8,128)(2,1)} %get-tuple-element.47), calls=%async_computation | async-start | bytes 2097152 | tf_op jit(solution)/shard_map/all_to_all | solution.py:269
  11.8 6.8 %collective-permute-start = (bf16[32,1280]{1,0:T(8,128)(2,1)S(1)}, bf16[32,1280]{1,0:T(8,128)(2,1)S(1)}, u32[]{:S(2)}, u32[]{:S(2)}) collective-permute-start(bf16[32,1280]{1,0:T(8,128)(2,1)S(1)} %copy-done), channel_id=1, source_target_pairs={{1,0},{2,1},{3,2},{0,3},{5,4},{6,5},{7,6},{4,7},{9,8},{10,9},{11,1... | collective-permute-start | bytes 245768 | tf_op jit(solution)/shard_map/ppermute | solution.py:21
  14.4 4.9 %collective-permute-start.1 = (bf16[32,1280]{1,0:T(8,128)(2,1)S(1)}, bf16[32,1280]{1,0:T(8,128)(2,1)S(1)}, u32[]{:S(2)}, u32[]{:S(2)}) collective-permute-start(bf16[32,1280]{1,0:T(8,128)(2,1)S(1)} %copy-done), channel_id=1, source_target_pairs={{2,0},{3,1},{0,2},{1,3},{6,4},{7,5},{4,6},{5,7},{10,8},{11,9},{8,1... | collective-permute-start | bytes 245768 | tf_op jit(solution)/shard_map/ppermute | solution.py:21
  14.9 5.2 %collective-permute-start.2 = (bf16[32,1280]{1,0:T(8,128)(2,1)S(1)}, bf16[32,1280]{1,0:T(8,128)(2,1)S(1)}, u32[]{:S(2)}, u32[]{:S(2)}) collective-permute-start(bf16[32,1280]{1,0:T(8,128)(2,1)S(1)} %copy-done), channel_id=1, source_target_pairs={{3,0},{0,1},{1,2},{2,3},{7,4},{4,5},{5,6},{6,7},{11,8},{8,9},{9,10... | collective-permute-start | bytes 245768 | tf_op jit(solution)/shard_map/ppermute | solution.py:21
  15.5 4.5 %collective-permute-start.3 = (bf16[32,1280]{1,0:T(8,128)(2,1)S(1)}, bf16[32,1280]{1,0:T(8,128)(2,1)S(1)}, u32[]{:S(2)}, u32[]{:S(2)}) collective-permute-start(bf16[32,1280]{1,0:T(8,128)(2,1)S(1)} %copy-done.1), channel_id=1, source_target_pairs={{4,0},{8,4},{12,8},{0,12},{5,1},{9,5},{13,9},{1,13},{6,2},{10,6},{... | collective-permute-start | bytes 245768 | tf_op jit(solution)/shard_map/ppermute | solution.py:21
  18.2 5.1 %collective-permute-start.4 = (bf16[32,1280]{1,0:T(8,128)(2,1)S(1)}, bf16[32,1280]{1,0:T(8,128)(2,1)S(1)}, u32[]{:S(2)}, u32[]{:S(2)}) collective-permute-start(bf16[32,1280]{1,0:T(8,128)(2,1)S(1)} %copy-done.1), channel_id=1, source_target_pairs={{8,0},{12,4},{0,8},{4,12},{9,1},{13,5},{1,9},{5,13},{10,2},{14,6},... | collective-permute-start | bytes 245768 | tf_op jit(solution)/shard_map/ppermute | solution.py:21
  18.6 5.6 %collective-permute-start.5 = (bf16[32,1280]{1,0:T(8,128)(2,1)S(1)}, bf16[32,1280]{1,0:T(8,128)(2,1)S(1)}, u32[]{:S(2)}, u32[]{:S(2)}) collective-permute-start(bf16[32,1280]{1,0:T(8,128)(2,1)S(1)} %copy-done.1), channel_id=1, source_target_pairs={{12,0},{0,4},{4,8},{8,12},{13,1},{1,5},{5,9},{9,13},{14,2},{2,6},{... | collective-permute-start | bytes 245768 | tf_op jit(solution)/shard_map/ppermute | solution.py:21
  24.3 7.9 %collective-permute-start.6 = (bf16[4,32,1280]{2,1,0:T(8,128)(2,1)S(1)}, bf16[4,32,1280]{2,1,0:T(8,128)(2,1)S(1)}, u32[]{:S(2)}, u32[]{:S(2)}) collective-permute-start(bf16[4,32,1280]{2,1,0:T(8,128)(2,1)S(1)} %pad_maximum_fusion), channel_id=1, source_target_pairs={{8,0},{12,4},{0,8},{4,12},{9,1},{13,5},{1,9},{5,13},{10,2},{14,6},... | collective-permute-start | bytes 983048 | tf_op jit(solution)/shard_map/ppermute | solution.py:21
  24.9 14.4 %collective-permute-start.8 = (bf16[4,32,1280]{2,1,0:T(8,128)(2,1)S(1)}, bf16[4,32,1280]{2,1,0:T(8,128)(2,1)S(1)}, u32[]{:S(2)}, u32[]{:S(2)}) collective-permute-start(bf16[4,32,1280]{2,1,0:T(8,128)(2,1)S(1)} %pad_maximum_fusion), channel_id=1, source_target_pairs={{4,0},{8,4},{12,8},{0,12},{5,1},{9,5},{13,9},{1,13},{6,2},{10,6},{... | collective-permute-start | bytes 983048 | tf_op jit(solution)/shard_map/ppermute | solution.py:21
  25.6 8.0 %collective-permute-start.7 = (bf16[4,32,1280]{2,1,0:T(8,128)(2,1)S(1)}, bf16[4,32,1280]{2,1,0:T(8,128)(2,1)S(1)}, u32[]{:S(2)}, u32[]{:S(2)}) collective-permute-start(bf16[4,32,1280]{2,1,0:T(8,128)(2,1)S(1)} %pad_maximum_fusion.1), channel_id=1, source_target_pairs={{2,0},{3,1},{0,2},{1,3},{6,4},{7,5},{4,6},{5,7},{10,8},{11,9},{8,1... | collective-permute-start | bytes 983048 | tf_op jit(solution)/shard_map/ppermute | solution.py:21
  27.6 13.5 %collective-permute-start.9 = (bf16[4,32,1280]{2,1,0:T(8,128)(2,1)S(1)}, bf16[4,32,1280]{2,1,0:T(8,128)(2,1)S(1)}, u32[]{:S(2)}, u32[]{:S(2)}) collective-permute-start(bf16[4,32,1280]{2,1,0:T(8,128)(2,1)S(1)} %pad_maximum_fusion.1), channel_id=1, source_target_pairs={{1,0},{2,1},{3,2},{0,3},{5,4},{6,5},{7,6},{4,7},{9,8},{10,9},{11,1... | collective-permute-start | bytes 983048 | tf_op jit(solution)/shard_map/ppermute | solution.py:21
  29.6 11.5 %collective-permute-start.10 = (bf16[4,32,1280]{2,1,0:T(8,128)(2,1)S(1)}, bf16[4,32,1280]{2,1,0:T(8,128)(2,1)S(1)}, u32[]{:S(2)}, u32[]{:S(2)}) collective-permute-start(bf16[4,32,1280]{2,1,0:T(8,128)(2,1)S(1)} %pad_maximum_fusion), channel_id=1, source_target_pairs={{12,0},{0,4},{4,8},{8,12},{13,1},{1,5},{5,9},{9,13},{14,2},{2,6},{... | collective-permute-start | bytes 983048 | tf_op jit(solution)/shard_map/ppermute | solution.py:21
  32.1 9.0 %collective-permute-start.11 = (bf16[4,32,1280]{2,1,0:T(8,128)(2,1)S(1)}, bf16[4,32,1280]{2,1,0:T(8,128)(2,1)S(1)}, u32[]{:S(2)}, u32[]{:S(2)}) collective-permute-start(bf16[4,32,1280]{2,1,0:T(8,128)(2,1)S(1)} %pad_maximum_fusion.1), channel_id=1, source_target_pairs={{3,0},{0,1},{1,2},{2,3},{7,4},{4,5},{5,6},{6,7},{11,8},{8,9},{9,10... | collective-permute-start | bytes 983048 | tf_op jit(solution)/shard_map/ppermute | solution.py:21
  41.1 0.7 copy-start.2
  41.8 9.6 %collective-permute-start.12 = (bf16[512,1024]{1,0:T(8,128)(2,1)S(1)}, bf16[512,1024]{1,0:T(8,128)(2,1)S(1)}, u32[]{:S(2)}, u32[]{:S(2)}) collective-permute-start(bf16[512,1024]{1,0:T(8,128)(2,1)S(1)} %bitcast.28), channel_id=1, source_target_pairs={{16,0},{0,16},{17,1},{1,17},{18,2},{2,18},{19,3},{3,19},{20,4},{4,... | collective-permute-start | bytes 3145736 | tf_op jit(solution)/shard_map/ppermute | solution.py:21
  47.6 1.0 copy-start.3
  49.3 2.2 %collective-permute-start.13 = (f32[16,256]{1,0:T(8,128)S(1)}, f32[16,256]{1,0:T(8,128)S(1)}, u32[]{:S(2)}, u32[]{:S(2)}) collective-permute-start(f32[16,256]{1,0:T(8,128)S(1)} %get-tuple-element.59.part), channel_id=1, source_target_pairs={{16,0},{0,16},{17,1},{1,17},{18,2},{2,18},{19,3},{3,19},{20,4},{4,... | collective-permute-start | bytes 49160 | tf_op jit(solution)/shard_map/ppermute | solution.py:21
  84.5 2.7 %collective-permute-start.14 = (f32[512,256]{1,0:T(8,128)S(1)}, f32[512,256]{1,0:T(8,128)S(1)}, u32[]{:S(2)}, u32[]{:S(2)}) collective-permute-start(f32[512,256]{1,0:T(8,128)S(1)} %get-tuple-element.67), channel_id=1, source_target_pairs={{16,0},{0,16},{17,1},{1,17},{18,2},{2,18},{19,3},{3,19},{20,4},{4,... | collective-permute-start | bytes 1572872 | tf_op jit(solution)/shard_map/ppermute | solution.py:21
  85.7 16.5 %copy-start.4 = (f32[64,256]{1,0:T(8,128)S(1)}, f32[64,256]{1,0:T(8,128)}, u32[]{:S(2)}) copy-start(f32[64,256]{1,0:T(8,128)} %h_ref.1) | copy-start | bytes 196612
  103.3 14.4 %all-to-all-start.4 = ((bf16[16,64,256]{2,1,0:T(8,128)(2,1)}), bf16[16,64,256]{2,1,0:T(8,128)(2,1)S(1)}, u32[]{:S(2)}, u32[]{:S(2)}) async-start(bf16[16,64,256]{2,1,0:T(8,128)(2,1)} %get-tuple-element.70), calls=%async_computation.4 | async-start | bytes 1048576 | tf_op jit(solution)/shard_map/all_to_all | solution.py:349
  118.2 3.3 %collective-permute-start.15 = (f32[512,256]{1,0:T(8,128)S(1)}, f32[512,256]{1,0:T(8,128)S(1)}, u32[]{:S(2)}, u32[]{:S(2)}) collective-permute-start(f32[512,256]{1,0:T(8,128)S(1)} %fusion.3), channel_id=1, source_target_pairs={{16,0},{0,16},{17,1},{1,17},{18,2},{2,18},{19,3},{3,19},{20,4},{4,... | collective-permute-start | bytes 1572872 | tf_op jit(solution)/shard_map/ppermute | solution.py:21
  120.2 1.3 collective-permute-start.16
  139.0 11.8 %all-to-all-start.6 = ((f32[16,16,256]{2,1,0:T(8,128)}), f32[16,16,256]{2,1,0:T(8,128)S(1)}, u32[]{:S(2)}, u32[]{:S(2)}) async-start(f32[16,16,256]{2,1,0:T(8,128)} %broadcast_in_dim.7), calls=%async_computation.6 | async-start | bytes 524288 | tf_op jit(solution)/shard_map/all_to_all | solution.py:27

commit v9 on v6

--- a/solution.py
+++ b/solution.py
@@ -107,7 +107,7 @@
             sums[pl.ds(i * 2 + j, 1), :] = line
         return 0
 
-    lax.fori_loop(0, rows_ref.shape[0] // tall, block, 0)
+    lax.fori_loop(0, rows_ref.shape[0] // tall, block, 0, unroll=True)
 
 
 def last_rows_kernel(rows_ref, cols, sq, own_sums, part, more, kern, out, sums):

time: 152 us -> 151 us (level)
  no operation moved by 1% of the time
where the time goes in v9:
time: 151 us
  blocking collectives  61 us (40%)
  starting transfers between devices  40.4 us (27%)
  waiting for transfers between devices  35 us (23%)
  Pallas kernels  9.94 us (7%)
  local copies, waits for them, and re-layouts  2.47 us (2%)
    all_to_all x2, blocking collectives, over_z(): mine = lax.all_to_all(mine.astype(jnp.float16), Z, 0, 0, tiled=True)  30.9 us
    ppermute x17, starting transfers between devices, from_ahead(): lax.ppermute(value, axis, [((i + steps) % length, i) for i in range(lengt...  24.1 us
    all_to_all x1, blocking collectives, shards(): lax.all_to_all(message, ROW, 0, 0, tiled=True)  17.6 us
    ppermute x17, waiting for transfers between devices, from_ahead(): lax.ppermute(value, axis, [((i + steps) % length, i) for i in range(lengt...  15.9 us
    all_to_all x1, blocking collectives, shards(): gathered = lax.all_to_all(message, COL, 0, 0, tiled=True)  12.6 us
    all_to_all x1, waiting for transfers between devices, shards(): lax.all_to_all(hb_cols, COL, 0, 0, tiled=True).reshape(group, rank)  10.8 us
    pallas_call x9, Pallas kernels, call(): pl.pallas_call(kernel, out_shape=outs, in_specs=[pl.BlockSpec(memory_spac...  9.94 us
    all_to_all x1, starting transfers between devices, shards(): along_z = lax.all_to_all(copies, Z, 0, 0, tiled=True)  9.16 us
  transfers between devices with their start and end apart: 20, of which 10 were waited for; matrix products, arithmetic and copies ran while one was open for 0% of the time, Pallas kernels for 2%

profile of v9, /device:TPU:1, one launch (start us, length us, event | category | flops | bytes accessed | tf_op | source)
XLA Modules:
  0.0 150.6 jit_solution(10264668458014846541)
XLA Ops:
  0.0 2.0 %shard_map.28 = (bf16[32,1280]{1,0:T(8,128)(2,1)}, bf16[32,1280]{1,0:T(8,128)(2,1)}, bf16[8,64,1024]{2,1,0:T(8,128)(2,1)}) custom-call(bf16[64,1024]{1,0:T(8,128)(2,1)} %points.1, f32[64,256]{1,0:T(8,128)} %h_ref.1), custom_call_target="tpu_custom_call" | custom-call | flops 1 | bytes 1409024 | tf_op jit(solution)/shard_map/pallas_call | solution.py:37
  2.0 9.2 %all-to-all-start = ((bf16[8,64,1024]{2,1,0:T(8,128)(2,1)}), bf16[8,64,1024]{2,1,0:T(8,128)(2,1)S(1)}, u32[]{:S(2)}, u32[]{:S(2)}) async-start(bf16[8,64,1024]{2,1,0:T(8,128)(2,1)} %get-tuple-element.47), calls=%async_computation | async-start | bytes 2097152 | tf_op jit(solution)/shard_map/all_to_all | solution.py:260
  11.2 2.6 %collective-permute-start = (bf16[32,1280]{1,0:T(8,128)(2,1)S(1)}, bf16[32,1280]{1,0:T(8,128)(2,1)S(1)}, u32[]{:S(2)}, u32[]{:S(2)}) collective-permute-start(bf16[32,1280]{1,0:T(8,128)(2,1)S(1)} %copy-done), channel_id=1, source_target_pairs={{1,0},{2,1},{3,2},{0,3},{5,4},{6,5},{7,6},{4,7},{9,8},{10,9},{11,1... | collective-permute-start | bytes 245768 | tf_op jit(solution)/shard_map/ppermute | solution.py:21
  14.9 2.7 %collective-permute-start.3 = (bf16[32,1280]{1,0:T(8,128)(2,1)S(1)}, bf16[32,1280]{1,0:T(8,128)(2,1)S(1)}, u32[]{:S(2)}, u32[]{:S(2)}) collective-permute-start(bf16[32,1280]{1,0:T(8,128)(2,1)S(1)} %copy-done.1), channel_id=1, source_target_pairs={{4,0},{8,4},{12,8},{0,12},{5,1},{9,5},{13,9},{1,13},{6,2},{10,6},{... | collective-permute-start | bytes 245768 | tf_op jit(solution)/shard_map/ppermute | solution.py:21
  19.4 3.3 %collective-permute-done.4.by2 = bf16[32,1280]{1,0:T(8,128)(2,1)S(1)} collective-permute-done((bf16[32,1280]{1,0:T(8,128)(2,1)S(1)}, bf16[32,1280]{1,0:T(8,128)(2,1)S(1)}, u32[]{:S(2)}, u32[]{:S(2)}) %collective-permute-start.4) | collective-permute-done | bytes 81952 | tf_op jit(solution)/shard_map/ppermute | solution.py:21
  22.7 0.9 collective-permute-done.5.by3
  25.0 1.9 %collective-permute-start.7 = (bf16[4,32,1280]{2,1,0:T(8,128)(2,1)S(1)}, bf16[4,32,1280]{2,1,0:T(8,128)(2,1)S(1)}, u32[]{:S(2)}, u32[]{:S(2)}) collective-permute-start(bf16[4,32,1280]{2,1,0:T(8,128)(2,1)S(1)} %pad_maximum_fusion.1), channel_id=1, source_target_pairs={{2,0},{3,1},{0,2},{1,3},{6,4},{7,5},{4,6},{5,7},{10,8},{11,9},{8,1... | collective-permute-start | bytes 983048 | tf_op jit(solution)/shard_map/ppermute | solution.py:21
  27.0 2.1 %collective-permute-start.9 = (bf16[4,32,1280]{2,1,0:T(8,128)(2,1)S(1)}, bf16[4,32,1280]{2,1,0:T(8,128)(2,1)S(1)}, u32[]{:S(2)}, u32[]{:S(2)}) collective-permute-start(bf16[4,32,1280]{2,1,0:T(8,128)(2,1)S(1)} %pad_maximum_fusion.1), channel_id=1, source_target_pairs={{1,0},{2,1},{3,2},{0,3},{5,4},{6,5},{7,6},{4,7},{9,8},{10,9},{11,1... | collective-permute-start | bytes 983048 | tf_op jit(solution)/shard_map/ppermute | solution.py:21
  29.0 0.8 collective-permute-start.10
  29.8 1.7 %collective-permute-done.6.y2 = bf16[4,32,1280]{2,1,0:T(8,128)(2,1)S(1)} collective-permute-done((bf16[4,32,1280]{2,1,0:T(8,128)(2,1)S(1)}, bf16[4,32,1280]{2,1,0:T(8,128)(2,1)S(1)}, u32[]{:S(2)}, u32[]{:S(2)}) %collective-permute-start.6) | collective-permute-done | bytes 327712 | tf_op jit(solution)/shard_map/ppermute | solution.py:21
  31.5 1.5 %collective-permute-start.11 = (bf16[4,32,1280]{2,1,0:T(8,128)(2,1)S(1)}, bf16[4,32,1280]{2,1,0:T(8,128)(2,1)S(1)}, u32[]{:S(2)}, u32[]{:S(2)}) collective-permute-start(bf16[4,32,1280]{2,1,0:T(8,128)(2,1)S(1)} %pad_maximum_fusion.1), channel_id=1, source_target_pairs={{3,0},{0,1},{1,2},{2,3},{7,4},{4,5},{5,6},{6,7},{11,8},{8,9},{9,10... | collective-permute-start | bytes 983048 | tf_op jit(solution)/shard_map/ppermute | solution.py:21
  33.0 5.7 %collective-permute-done.8.y1 = bf16[4,32,1280]{2,1,0:T(8,128)(2,1)S(1)} collective-permute-done((bf16[4,32,1280]{2,1,0:T(8,128)(2,1)S(1)}, bf16[4,32,1280]{2,1,0:T(8,128)(2,1)S(1)}, u32[]{:S(2)}, u32[]{:S(2)}) %collective-permute-start.8) | collective-permute-done | bytes 327712 | tf_op jit(solution)/shard_map/ppermute | solution.py:21
  38.7 1.8 %collective-permute-done.9.x1 = bf16[4,32,1280]{2,1,0:T(8,128)(2,1)S(1)} collective-permute-done((bf16[4,32,1280]{2,1,0:T(8,128)(2,1)S(1)}, bf16[4,32,1280]{2,1,0:T(8,128)(2,1)S(1)}, u32[]{:S(2)}, u32[]{:S(2)}) %collective-permute-start.9) | collective-permute-done | bytes 327712 | tf_op jit(solution)/shard_map/ppermute | solution.py:21
  41.2 5.7 %collective-permute-start.12 = (bf16[512,1024]{1,0:T(8,128)(2,1)S(1)}, bf16[512,1024]{1,0:T(8,128)(2,1)S(1)}, u32[]{:S(2)}, u32[]{:S(2)}) collective-permute-start(bf16[512,1024]{1,0:T(8,128)(2,1)S(1)} %bitcast.28), channel_id=1, source_target_pairs={{16,0},{0,16},{17,1},{1,17},{18,2},{2,18},{19,3},{3,19},{20,4},{4,... | collective-permute-start | bytes 3145736 | tf_op jit(solution)/shard_map/ppermute | solution.py:21
  46.9 1.0 copy-done.3
  48.9 1.7 %shard_map.30 = (f32[512,1024]{1,0:T(8,128)S(1)}, f32[4,128]{1,0:T(4,128)S(1)}) custom-call(bf16[512,1024]{1,0:T(8,128)(2,1)S(1)} %bitcast.29, bf16[1024,1024]{1,0:T(8,128)(2,1)S(1)} %get-tuple-element.55.cols, f32[8,128]{1,0:T(8,128)S(1)} %get-tuple-element.56.sq), custom_call_target="tpu_custom_call" | custom-call | flops 1073741824 | bytes 5249024 | tf_op jit(solution)/shard_map/pallas_call | solution.py:37
  50.6 1.7 %shard_map.31 = (f32[512,1024]{1,0:T(8,128)S(1)}, f32[16,24,128]{2,1,0:T(8,128)S(1)}) custom-call(bf16[512,1024]{1,0:T(8,128)(2,1)S(1)} %collective-permute-done.12.rows_ref, bf16[1024,1024]{1,0:T(8,128)(2,1)S(1)} %get-tuple-element.55.cols, f32[8,128]{1,0:T(8,128)S(1)} %get-tuple-element.56.sq, f32[4,128]{1,0:T(4,128)S(1)} %get-tuple-element.58.own_sums, ...), custom_call_target="tpu_custom_call" | custom-call | flops 1073741824 | bytes 5478400 | tf_op jit(solution)/shard_map/pallas_call | solution.py:37
  52.3 17.6 %all_to_all.35.got = f32[16,24,128]{2,1,0:T(8,128)S(1)} all-to-all(f32[16,24,128]{2,1,0:T(8,128)S(1)} %get-tuple-element.60), channel_id=1, replica_groups=mesh['row_0'=8,'row_1'=2,'col_0'=4,'col_1'=4] {'row_0','row_1'}, dimensions={0} | all-to-all | bytes 393216 | tf_op jit(solution)/shard_map/all_to_all | solution.py:307
  70.0 12.6 %all_to_all.36.got = f32[16,40,128]{2,1,0:T(8,128)S(1)} all-to-all(f32[16,40,128]{2,1,0:T(8,128)S(1)} %get-tuple-element.62), channel_id=1, replica_groups=mesh['row_0'=8,'row_1'=2,'col_0'=4,'col_1'=4] {'col_0','col_1'}, dimensions={0} | all-to-all | bytes 655360 | tf_op jit(solution)/shard_map/all_to_all | solution.py:310
  82.6 0.8 shard_map.34
  83.4 1.2 collective-permute-start.14
  84.6 0.9 shard_map.33
  86.2 14.8 %all_to_all.37 = f16[8,64,256]{2,1,0:T(8,128)(2,1)S(1)} all-to-all(f16[8,64,256]{2,1,0:T(8,128)(2,1)S(1)} %bitcast.41), channel_id=1, replica_groups=mesh['row_0'=8,'row_1'=2,'col_0'=4,'col_1'=4] {'row_0'}, dimensions={0} | all-to-all | bytes 524288 | tf_op jit(solution)/shard_map/all_to_all | solution.py:328
  101.1 1.1 shard_map.35
  102.2 3.6 %all-to-all-start.4 = ((bf16[16,64,256]{2,1,0:T(8,128)(2,1)}), bf16[16,64,256]{2,1,0:T(8,128)(2,1)S(1)}, u32[]{:S(2)}, u32[]{:S(2)}) async-start(bf16[16,64,256]{2,1,0:T(8,128)(2,1)} %get-tuple-element.70), calls=%async_computation.4 | async-start | bytes 1048576 | tf_op jit(solution)/shard_map/all_to_all | solution.py:340
  105.8 10.8 %all-to-all-done.4 = bf16[16,64,256]{2,1,0:T(8,128)(2,1)S(1)} async-done(((bf16[16,64,256]{2,1,0:T(8,128)(2,1)}), bf16[16,64,256]{2,1,0:T(8,128)(2,1)S(1)}, u32[]{:S(2)}, u32[]{:S(2)}) %all-to-all-start.4) | async-done | bytes 524320 | tf_op jit(solution)/shard_map/all_to_all | solution.py:340
  117.0 1.7 %collective-permute-start.15 = (f32[512,256]{1,0:T(8,128)S(1)}, f32[512,256]{1,0:T(8,128)S(1)}, u32[]{:S(2)}, u32[]{:S(2)}) collective-permute-start(f32[512,256]{1,0:T(8,128)S(1)} %fusion.3), channel_id=1, source_target_pairs={{16,0},{0,16},{17,1},{1,17},{18,2},{2,18},{19,3},{3,19},{20,4},{4,... | collective-permute-start | bytes 1572872 | tf_op jit(solution)/shard_map/ppermute | solution.py:21
  119.2 1.2 collective-permute-done.16
  121.0 16.1 %all_to_all.38 = f16[8,80,256]{2,1,0:T(8,128)(2,1)S(1)} all-to-all(f16[8,80,256]{2,1,0:T(8,128)(2,1)S(1)} %pad_maximum_fusion.2), channel_id=1, replica_groups=mesh['row_0'=8,'row_1'=2,'col_0'=4,'col_1'=4] {'row_0'}, dimensions={0} | all-to-all | bytes 655360 | tf_op jit(solution)/shard_map/all_to_all | solution.py:328
  137.9 3.5 %all-to-all-start.6 = ((f32[16,16,256]{2,1,0:T(8,128)}), f32[16,16,256]{2,1,0:T(8,128)S(1)}, u32[]{:S(2)}, u32[]{:S(2)}) async-start(f32[16,16,256]{2,1,0:T(8,128)} %broadcast_in_dim.7), calls=%async_computation.6 | async-start | bytes 524288 | tf_op jit(solution)/shard_map/all_to_all | solution.py:27
  141.4 8.3 %all-to-all-done.6 = f32[16,16,256]{2,1,0:T(8,128)S(1)} async-done(((f32[16,16,256]{2,1,0:T(8,128)}), f32[16,16,256]{2,1,0:T(8,128)S(1)}, u32[]{:S(2)}, u32[]{:S(2)}) %all-to-all-start.6) | async-done | bytes 262176 | tf_op jit(solution)/shard_map/all_to_all | solution.py:27
  149.7 0.9 shard_map.36
  (48 shorter events, 9.3 us)
Async XLA Ops:
  2.0 9.2 %copy-start = (bf16[32,1280]{1,0:T(8,128)(2,1)S(1)}, bf16[32,1280]{1,0:T(8,128)(2,1)}, u32[]{:S(2)}) copy-start(bf16[32,1280]{1,0:T(8,128)(2,1)} %get-tuple-element.39.ax0) | copy-start | bytes 245764
  2.0 12.9 %copy-start.1 = (bf16[32,1280]{1,0:T(8,128)(2,1)S(1)}, bf16[32,1280]{1,0:T(8,128)(2,1)}, u32[]{:S(2)}) copy-start(bf16[32,1280]{1,0:T(8,128)(2,1)} %get-tuple-element.40.by0) | copy-start | bytes 245764
  2.0 39.2 %all-to-all-start = ((bf16[8,64,1024]{2,1,0:T(8,128)(2,1)}), bf16[8,64,1024]{2,1,0:T(8,128)(2,1)S(1)}, u32[]{:S(2)}, u32[]{:S(2)}) async-start(bf16[8,64,1024]{2,1,0:T(8,128)(2,1)} %get-tuple-element.47), calls=%async_computation | async-start | bytes 2097152 | tf_op jit(solution)/shard_map/all_to_all | solution.py:260
  11.2 6.8 %collective-permute-start = (bf16[32,1280]{1,0:T(8,128)(2,1)S(1)}, bf16[32,1280]{1,0:T(8,128)(2,1)S(1)}, u32[]{:S(2)}, u32[]{:S(2)}) collective-permute-start(bf16[32,1280]{1,0:T(8,128)(2,1)S(1)} %copy-done), channel_id=1, source_target_pairs={{1,0},{2,1},{3,2},{0,3},{5,4},{6,5},{7,6},{4,7},{9,8},{10,9},{11,1... | collective-permute-start | bytes 245768 | tf_op jit(solution)/shard_map/ppermute | solution.py:21
  13.8 4.9 %collective-permute-start.1 = (bf16[32,1280]{1,0:T(8,128)(2,1)S(1)}, bf16[32,1280]{1,0:T(8,128)(2,1)S(1)}, u32[]{:S(2)}, u32[]{:S(2)}) collective-permute-start(bf16[32,1280]{1,0:T(8,128)(2,1)S(1)} %copy-done), channel_id=1, source_target_pairs={{2,0},{3,1},{0,2},{1,3},{6,4},{7,5},{4,6},{5,7},{10,8},{11,9},{8,1... | collective-permute-start | bytes 245768 | tf_op jit(solution)/shard_map/ppermute | solution.py:21
  14.3 5.2 %collective-permute-start.2 = (bf16[32,1280]{1,0:T(8,128)(2,1)S(1)}, bf16[32,1280]{1,0:T(8,128)(2,1)S(1)}, u32[]{:S(2)}, u32[]{:S(2)}) collective-permute-start(bf16[32,1280]{1,0:T(8,128)(2,1)S(1)} %copy-done), channel_id=1, source_target_pairs={{3,0},{0,1},{1,2},{2,3},{7,4},{4,5},{5,6},{6,7},{11,8},{8,9},{9,10... | collective-permute-start | bytes 245768 | tf_op jit(solution)/shard_map/ppermute | solution.py:21
  14.9 4.5 %collective-permute-start.3 = (bf16[32,1280]{1,0:T(8,128)(2,1)S(1)}, bf16[32,1280]{1,0:T(8,128)(2,1)S(1)}, u32[]{:S(2)}, u32[]{:S(2)}) collective-permute-start(bf16[32,1280]{1,0:T(8,128)(2,1)S(1)} %copy-done.1), channel_id=1, source_target_pairs={{4,0},{8,4},{12,8},{0,12},{5,1},{9,5},{13,9},{1,13},{6,2},{10,6},{... | collective-permute-start | bytes 245768 | tf_op jit(solution)/shard_map/ppermute | solution.py:21
  17.6 5.1 %collective-permute-start.4 = (bf16[32,1280]{1,0:T(8,128)(2,1)S(1)}, bf16[32,1280]{1,0:T(8,128)(2,1)S(1)}, u32[]{:S(2)}, u32[]{:S(2)}) collective-permute-start(bf16[32,1280]{1,0:T(8,128)(2,1)S(1)} %copy-done.1), channel_id=1, source_target_pairs={{8,0},{12,4},{0,8},{4,12},{9,1},{13,5},{1,9},{5,13},{10,2},{14,6},... | collective-permute-start | bytes 245768 | tf_op jit(solution)/shard_map/ppermute | solution.py:21
  18.0 5.6 %collective-permute-start.5 = (bf16[32,1280]{1,0:T(8,128)(2,1)S(1)}, bf16[32,1280]{1,0:T(8,128)(2,1)S(1)}, u32[]{:S(2)}, u32[]{:S(2)}) collective-permute-start(bf16[32,1280]{1,0:T(8,128)(2,1)S(1)} %copy-done.1), channel_id=1, source_target_pairs={{12,0},{0,4},{4,8},{8,12},{13,1},{1,5},{5,9},{9,13},{14,2},{2,6},{... | collective-permute-start | bytes 245768 | tf_op jit(solution)/shard_map/ppermute | solution.py:21
  23.6 7.9 %collective-permute-start.6 = (bf16[4,32,1280]{2,1,0:T(8,128)(2,1)S(1)}, bf16[4,32,1280]{2,1,0:T(8,128)(2,1)S(1)}, u32[]{:S(2)}, u32[]{:S(2)}) collective-permute-start(bf16[4,32,1280]{2,1,0:T(8,128)(2,1)S(1)} %pad_maximum_fusion), channel_id=1, source_target_pairs={{8,0},{12,4},{0,8},{4,12},{9,1},{13,5},{1,9},{5,13},{10,2},{14,6},... | collective-permute-start | bytes 983048 | tf_op jit(solution)/shard_map/ppermute | solution.py:21
  24.3 14.4 %collective-permute-start.8 = (bf16[4,32,1280]{2,1,0:T(8,128)(2,1)S(1)}, bf16[4,32,1280]{2,1,0:T(8,128)(2,1)S(1)}, u32[]{:S(2)}, u32[]{:S(2)}) collective-permute-start(bf16[4,32,1280]{2,1,0:T(8,128)(2,1)S(1)} %pad_maximum_fusion), channel_id=1, source_target_pairs={{4,0},{8,4},{12,8},{0,12},{5,1},{9,5},{13,9},{1,13},{6,2},{10,6},{... | collective-permute-start | bytes 983048 | tf_op jit(solution)/shard_map/ppermute | solution.py:21
  25.0 8.0 %collective-permute-start.7 = (bf16[4,32,1280]{2,1,0:T(8,128)(2,1)S(1)}, bf16[4,32,1280]{2,1,0:T(8,128)(2,1)S(1)}, u32[]{:S(2)}, u32[]{:S(2)}) collective-permute-start(bf16[4,32,1280]{2,1,0:T(8,128)(2,1)S(1)} %pad_maximum_fusion.1), channel_id=1, source_target_pairs={{2,0},{3,1},{0,2},{1,3},{6,4},{7,5},{4,6},{5,7},{10,8},{11,9},{8,1... | collective-permute-start | bytes 983048 | tf_op jit(solution)/shard_map/ppermute | solution.py:21
  27.0 13.5 %collective-permute-start.9 = (bf16[4,32,1280]{2,1,0:T(8,128)(2,1)S(1)}, bf16[4,32,1280]{2,1,0:T(8,128)(2,1)S(1)}, u32[]{:S(2)}, u32[]{:S(2)}) collective-permute-start(bf16[4,32,1280]{2,1,0:T(8,128)(2,1)S(1)} %pad_maximum_fusion.1), channel_id=1, source_target_pairs={{1,0},{2,1},{3,2},{0,3},{5,4},{6,5},{7,6},{4,7},{9,8},{10,9},{11,1... | collective-permute-start | bytes 983048 | tf_op jit(solution)/shard_map/ppermute | solution.py:21
  29.0 11.5 %collective-permute-start.10 = (bf16[4,32,1280]{2,1,0:T(8,128)(2,1)S(1)}, bf16[4,32,1280]{2,1,0:T(8,128)(2,1)S(1)}, u32[]{:S(2)}, u32[]{:S(2)}) collective-permute-start(bf16[4,32,1280]{2,1,0:T(8,128)(2,1)S(1)} %pad_maximum_fusion), channel_id=1, source_target_pairs={{12,0},{0,4},{4,8},{8,12},{13,1},{1,5},{5,9},{9,13},{14,2},{2,6},{... | collective-permute-start | bytes 983048 | tf_op jit(solution)/shard_map/ppermute | solution.py:21
  31.5 9.0 %collective-permute-start.11 = (bf16[4,32,1280]{2,1,0:T(8,128)(2,1)S(1)}, bf16[4,32,1280]{2,1,0:T(8,128)(2,1)S(1)}, u32[]{:S(2)}, u32[]{:S(2)}) collective-permute-start(bf16[4,32,1280]{2,1,0:T(8,128)(2,1)S(1)} %pad_maximum_fusion.1), channel_id=1, source_target_pairs={{3,0},{0,1},{1,2},{2,3},{7,4},{4,5},{5,6},{6,7},{11,8},{8,9},{9,10... | collective-permute-start | bytes 983048 | tf_op jit(solution)/shard_map/ppermute | solution.py:21
  40.5 0.7 copy-start.2
  41.2 9.4 %collective-permute-start.12 = (bf16[512,1024]{1,0:T(8,128)(2,1)S(1)}, bf16[512,1024]{1,0:T(8,128)(2,1)S(1)}, u32[]{:S(2)}, u32[]{:S(2)}) collective-permute-start(bf16[512,1024]{1,0:T(8,128)(2,1)S(1)} %bitcast.28), channel_id=1, source_target_pairs={{16,0},{0,16},{17,1},{1,17},{18,2},{2,18},{19,3},{3,19},{20,4},{4,... | collective-permute-start | bytes 3145736 | tf_op jit(solution)/shard_map/ppermute | solution.py:21
  46.9 1.0 copy-start.3
  48.6 2.0 %collective-permute-start.13 = (f32[16,256]{1,0:T(8,128)S(1)}, f32[16,256]{1,0:T(8,128)S(1)}, u32[]{:S(2)}, u32[]{:S(2)}) collective-permute-start(f32[16,256]{1,0:T(8,128)S(1)} %get-tuple-element.59.part), channel_id=1, source_target_pairs={{16,0},{0,16},{17,1},{1,17},{18,2},{2,18},{19,3},{3,19},{20,4},{4,... | collective-permute-start | bytes 49160 | tf_op jit(solution)/shard_map/ppermute | solution.py:21
  83.4 2.7 %collective-permute-start.14 = (f32[512,256]{1,0:T(8,128)S(1)}, f32[512,256]{1,0:T(8,128)S(1)}, u32[]{:S(2)}, u32[]{:S(2)}) collective-permute-start(f32[512,256]{1,0:T(8,128)S(1)} %get-tuple-element.67), channel_id=1, source_target_pairs={{16,0},{0,16},{17,1},{1,17},{18,2},{2,18},{19,3},{3,19},{20,4},{4,... | collective-permute-start | bytes 1572872 | tf_op jit(solution)/shard_map/ppermute | solution.py:21
  84.6 16.5 %copy-start.4 = (f32[64,256]{1,0:T(8,128)S(1)}, f32[64,256]{1,0:T(8,128)}, u32[]{:S(2)}) copy-start(f32[64,256]{1,0:T(8,128)} %h_ref.1) | copy-start | bytes 196612
  102.2 14.4 %all-to-all-start.4 = ((bf16[16,64,256]{2,1,0:T(8,128)(2,1)}), bf16[16,64,256]{2,1,0:T(8,128)(2,1)S(1)}, u32[]{:S(2)}, u32[]{:S(2)}) async-start(bf16[16,64,256]{2,1,0:T(8,128)(2,1)} %get-tuple-element.70), calls=%async_computation.4 | async-start | bytes 1048576 | tf_op jit(solution)/shard_map/all_to_all | solution.py:340
  117.0 3.3 %collective-permute-start.15 = (f32[512,256]{1,0:T(8,128)S(1)}, f32[512,256]{1,0:T(8,128)S(1)}, u32[]{:S(2)}, u32[]{:S(2)}) collective-permute-start(f32[512,256]{1,0:T(8,128)S(1)} %fusion.3), channel_id=1, source_target_pairs={{16,0},{0,16},{17,1},{1,17},{18,2},{2,18},{19,3},{3,19},{20,4},{4,... | collective-permute-start | bytes 1572872 | tf_op jit(solution)/shard_map/ppermute | solution.py:21
  119.1 1.3 collective-permute-start.16
  137.9 11.8 %all-to-all-start.6 = ((f32[16,16,256]{2,1,0:T(8,128)}), f32[16,16,256]{2,1,0:T(8,128)S(1)}, u32[]{:S(2)}, u32[]{:S(2)}) async-start(f32[16,16,256]{2,1,0:T(8,128)} %broadcast_in_dim.7), calls=%async_computation.6 | async-start | bytes 524288 | tf_op jit(solution)/shard_map/all_to_all | solution.py:27

commit v10 on v9

--- a/solution.py
+++ b/solution.py
@@ -56,7 +56,7 @@
 
 
 def columns_kernel(
-    y2, x2, y1, x1, y3, x3, ax0, ax1, ax2, ax3, by0, by1, by2, by3, pts_ref, hb_ref, sq_ref, part_ref, gram_ref
+    x3, y3, x1, y1, x2, y2, ax0, ax1, ax2, ax3, by0, by1, by2, by3, pts_ref, hb_ref, sq_ref, part_ref, gram_ref
 ):
     ny, nx = lax.axis_size(Y), lax.axis_size(X)
     y, x = lax.axis_index(Y), lax.axis_index(X)
@@ -204,6 +204,15 @@
     return 0.5 / jnp.sqrt(square + 1e-06)
 
 
+def gram_kernel(hb, part_ref, gram_ref):
+    gram_ref[...] = lax.dot_general(
+        hb[...], hb[...], (((0,), (0,)), ((), ())), preferred_element_type=F32
+    )
+    part = part_ref.shape[0]
+    at = pl.multiple_of(lax.axis_index(COL) * part, part)
+    part_ref[...] = gram_ref[pl.ds(at, part), :]
+
+
 def start_kernel(unit, points, factor, first, second, copies, wide, done):
     half, width = first.shape[0], points.shape[1]
     fetches = [
@@ -264,10 +273,11 @@
     x1, x2, x3, y1, y2, y3 = tie((x1, x2, x3, y1, y2, y3))
     by_x = jnp.stack([first, x1, x2, x3])
     by_y = jnp.stack([second, y1, y2, y3])
+    by_x, by_y = tie((by_x, by_y))
+    y_three, x_three = from_ahead(by_x, Y, 3), from_ahead(by_y, X, 3)
+    y_one, x_one = from_ahead(by_x, Y, 1), from_ahead(by_y, X, 1)
     y_two, x_two = from_ahead(by_x, Y, 2), from_ahead(by_y, X, 2)
-    y_one, x_one = from_ahead(by_x, Y, 1), from_ahead(by_y, X, 1)
-    y_three, x_three = from_ahead(by_x, Y, 3), from_ahead(by_y, X, 3)
-    far = [y_two, x_two, y_one, x_one, y_three, x_three]
+    far = [x_three, y_three, x_one, y_one, x_two, y_two]
     far, along_z = tie((far, along_z.reshape(-1, width)))
     other = from_ahead(along_z, CORE, 1)
     cols = [*far, first, x1, x2, x3, second, y1, y2, y3]
@@ -340,8 +350,13 @@
     hb_cols = lax.all_to_all(hb_cols, COL, 0, 0, tiled=True).reshape(group, rank)
     partial_other = jnp.dot(aff_other, hb_cols, preferred_element_type=F32)
     got = from_ahead(partial_other, CORE, 1)
-    gram = lax.dot_general(hb_cols, hb_cols, (((0,), (0,)), ((), ())), preferred_element_type=F32)
-    own_part = lax.dynamic_slice_in_dim(gram, lax.axis_index(COL) * part, part, 0)
+    (own_part,) = call(
+        gram_kernel,
+        [shape((part, rank), F32)],
+        [hb_cols],
+        2 * group * rank * rank,
+        [pltpu.VMEM((rank, rank), F32)],
+    )
     more_part = from_ahead(own_part, CORE, 1)
     partial_own = jnp.dot(aff_own, hb_cols, preferred_element_type=F32)
     mine = ((partial_own + got) * scales[2]).reshape(nz, pts, rank)

time: 151 us -> 151 us (level)
  blocking collectives: 61 us -> 74.5 us
  waiting for transfers between devices: 35 us -> 26.9 us
  starting transfers between devices: 40.4 us -> 35.5 us
    all_to_all x0 -> x1, blocking collectives: none -> 13.3 us  [shards(): lax.all_to_all(hb_cols, COL, 0, 0, tiled=True).reshape(group, rank)]
    all_to_all x1 -> x0, waiting for transfers between devices: 10.8 us -> none  [shards(): lax.all_to_all(hb_cols, COL, 0, 0, tiled=True).reshape(group, rank)]
    all_to_all x1 -> x0, starting transfers between devices: 3.57 us -> none  [shards(): lax.all_to_all(hb_cols, COL, 0, 0, tiled=True).reshape(group, rank)]
    ppermute x17, waiting for transfers between devices: 15.9 us -> 18.6 us  [from_ahead(): lax.ppermute(value, axis, [((i + steps) % length, i) for i in range(lengt...]
    pallas_call x9 -> x10, Pallas kernels: 9.94 us -> 9.56 us  [call(): pl.pallas_call(kernel, out_shape=outs, in_specs=[pl.BlockSpec(memory_spac...]
  transfers between devices with their start and end apart: 20 -> 19, of which waited for: 10 -> 9; matrix products, arithmetic and copies ran while one was open for 0% -> 0% of each run, Pallas kernels for 2% -> 2%
where the time goes in v10:
time: 151 us; the launch traced here: 150 us
  blocking collectives  74.5 us (49%)
  starting transfers between devices  35.5 us (24%)
  waiting for transfers between devices  26.9 us (18%)
  Pallas kernels  9.56 us (6%)
  local copies, waits for them, and re-layouts  2.45 us (2%)
    all_to_all x2, blocking collectives, over_z(): mine = lax.all_to_all(mine.astype(jnp.float16), Z, 0, 0, tiled=True)  30.9 us
    ppermute x17, starting transfers between devices, from_ahead(): lax.ppermute(value, axis, [((i + steps) % length, i) for i in range(lengt...  22.8 us
    ppermute x17, waiting for transfers between devices, from_ahead(): lax.ppermute(value, axis, [((i + steps) % length, i) for i in range(lengt...  18.6 us
    all_to_all x1, blocking collectives, shards(): lax.all_to_all(message, ROW, 0, 0, tiled=True)  17.5 us
    all_to_all x1, blocking collectives, shards(): lax.all_to_all(hb_cols, COL, 0, 0, tiled=True).reshape(group, rank)  13.3 us
    all_to_all x1, blocking collectives, shards(): gathered = lax.all_to_all(message, COL, 0, 0, tiled=True)  12.8 us
    pallas_call x10, Pallas kernels, call(): pl.pallas_call(kernel, out_shape=outs, in_specs=[pl.BlockSpec(memory_spac...  9.56 us
    all_to_all x1, starting transfers between devices, shards(): along_z = lax.all_to_all(copies, Z, 0, 0, tiled=True)  9.16 us
  transfers between devices with their start and end apart: 19, of which 9 were waited for; matrix products, arithmetic and copies ran while one was open for 0% of the time, Pallas kernels for 2%

profile of v10, /device:TPU:1, one launch (start us, length us, event | category | flops | bytes accessed | tf_op | source)
XLA Modules:
  0.0 150.3 jit_solution(16702642839166033984)
XLA Ops:
  0.0 2.0 %shard_map.28 = (bf16[32,1280]{1,0:T(8,128)(2,1)}, bf16[32,1280]{1,0:T(8,128)(2,1)}, bf16[8,64,1024]{2,1,0:T(8,128)(2,1)}) custom-call(bf16[64,1024]{1,0:T(8,128)(2,1)} %points.1, f32[64,256]{1,0:T(8,128)} %h_ref.1), custom_call_target="tpu_custom_call" | custom-call | flops 1 | bytes 1409024 | tf_op jit(solution)/shard_map/pallas_call | solution.py:37
  2.1 9.2 %all-to-all-start = ((bf16[8,64,1024]{2,1,0:T(8,128)(2,1)}), bf16[8,64,1024]{2,1,0:T(8,128)(2,1)S(1)}, u32[]{:S(2)}, u32[]{:S(2)}) async-start(bf16[8,64,1024]{2,1,0:T(8,128)(2,1)} %get-tuple-element.51), calls=%async_computation | async-start | bytes 2097152 | tf_op jit(solution)/shard_map/all_to_all | solution.py:269
  11.2 1.3 collective-permute-start.2
  12.5 2.5 %collective-permute-start.1 = (bf16[32,1280]{1,0:T(8,128)(2,1)S(1)}, bf16[32,1280]{1,0:T(8,128)(2,1)S(1)}, u32[]{:S(2)}, u32[]{:S(2)}) collective-permute-start(bf16[32,1280]{1,0:T(8,128)(2,1)S(1)} %copy-done), channel_id=1, source_target_pairs={{2,0},{3,1},{0,2},{1,3},{6,4},{7,5},{4,6},{5,7},{10,8},{11,9},{8,1... | collective-permute-start | bytes 245768 | tf_op jit(solution)/shard_map/ppermute | solution.py:21
  15.0 1.2 collective-permute-start
  16.1 1.3 collective-permute-start.5
  17.4 2.6 %collective-permute-start.4 = (bf16[32,1280]{1,0:T(8,128)(2,1)S(1)}, bf16[32,1280]{1,0:T(8,128)(2,1)S(1)}, u32[]{:S(2)}, u32[]{:S(2)}) collective-permute-start(bf16[32,1280]{1,0:T(8,128)(2,1)S(1)} %copy-done.1), channel_id=1, source_target_pairs={{8,0},{12,4},{0,8},{4,12},{9,1},{13,5},{1,9},{5,13},{10,2},{14,6},... | collective-permute-start | bytes 245768 | tf_op jit(solution)/shard_map/ppermute | solution.py:21
  20.0 1.1 collective-permute-start.3
  21.1 1.9 %collective-permute-done.4.by2 = bf16[32,1280]{1,0:T(8,128)(2,1)S(1)} collective-permute-done((bf16[32,1280]{1,0:T(8,128)(2,1)S(1)}, bf16[32,1280]{1,0:T(8,128)(2,1)S(1)}, u32[]{:S(2)}, u32[]{:S(2)}) %collective-permute-start.4) | collective-permute-done | bytes 81952 | tf_op jit(solution)/shard_map/ppermute | solution.py:21
  23.0 1.2 collective-permute-done.3.by1
  24.6 2.5 %collective-permute-start.8 = (bf16[4,32,1280]{2,1,0:T(8,128)(2,1)S(1)}, bf16[4,32,1280]{2,1,0:T(8,128)(2,1)S(1)}, u32[]{:S(2)}, u32[]{:S(2)}) collective-permute-start(bf16[4,32,1280]{2,1,0:T(8,128)(2,1)S(1)} %get-tuple-element.49), channel_id=1, source_target_pairs={{1,0},{2,1},{3,2},{0,3},{5,4},{6,5},{7,6},{4,7},{9,8},{10,9},{11,1... | collective-permute-start | bytes 983048 | tf_op jit(solution)/shard_map/ppermute | solution.py:21
  27.1 1.5 collective-permute-start.11
  29.2 3.2 %collective-permute-done.10.x2 = bf16[4,32,1280]{2,1,0:T(8,128)(2,1)S(1)} collective-permute-done((bf16[4,32,1280]{2,1,0:T(8,128)(2,1)S(1)}, bf16[4,32,1280]{2,1,0:T(8,128)(2,1)S(1)}, u32[]{:S(2)}, u32[]{:S(2)}) %collective-permute-start.10) | collective-permute-done | bytes 327712 | tf_op jit(solution)/shard_map/ppermute | solution.py:21
  32.4 6.2 %collective-permute-done.8.x1 = bf16[4,32,1280]{2,1,0:T(8,128)(2,1)S(1)} collective-permute-done((bf16[4,32,1280]{2,1,0:T(8,128)(2,1)S(1)}, bf16[4,32,1280]{2,1,0:T(8,128)(2,1)S(1)}, u32[]{:S(2)}, u32[]{:S(2)}) %collective-permute-start.8) | collective-permute-done | bytes 327712 | tf_op jit(solution)/shard_map/ppermute | solution.py:21
  38.7 2.8 %collective-permute-done.6.x3 = bf16[4,32,1280]{2,1,0:T(8,128)(2,1)S(1)} collective-permute-done((bf16[4,32,1280]{2,1,0:T(8,128)(2,1)S(1)}, bf16[4,32,1280]{2,1,0:T(8,128)(2,1)S(1)}, u32[]{:S(2)}, u32[]{:S(2)}) %collective-permute-start.6) | collective-permute-done | bytes 327712 | tf_op jit(solution)/shard_map/ppermute | solution.py:21
  41.4 1.5 %collective-permute-done.9.y1 = bf16[4,32,1280]{2,1,0:T(8,128)(2,1)S(1)} collective-permute-done((bf16[4,32,1280]{2,1,0:T(8,128)(2,1)S(1)}, bf16[4,32,1280]{2,1,0:T(8,128)(2,1)S(1)}, u32[]{:S(2)}, u32[]{:S(2)}) %collective-permute-start.9) | collective-permute-done | bytes 327712 | tf_op jit(solution)/shard_map/ppermute | solution.py:21
  43.7 4.5 %collective-permute-start.12 = (bf16[512,1024]{1,0:T(8,128)(2,1)S(1)}, bf16[512,1024]{1,0:T(8,128)(2,1)S(1)}, u32[]{:S(2)}, u32[]{:S(2)}) collective-permute-start(bf16[512,1024]{1,0:T(8,128)(2,1)S(1)} %bitcast.27), channel_id=1, source_target_pairs={{16,0},{0,16},{17,1},{1,17},{18,2},{2,18},{19,3},{3,19},{20,4},{4,... | collective-permute-start | bytes 3145736 | tf_op jit(solution)/shard_map/ppermute | solution.py:21
  48.2 1.0 copy-done.3
  50.2 1.7 %shard_map.30 = (f32[512,1024]{1,0:T(8,128)S(1)}, f32[4,128]{1,0:T(4,128)S(1)}) custom-call(bf16[512,1024]{1,0:T(8,128)(2,1)S(1)} %bitcast.28, bf16[1024,1024]{1,0:T(8,128)(2,1)S(1)} %get-tuple-element.59.cols, f32[8,128]{1,0:T(8,128)S(1)} %get-tuple-element.60.sq), custom_call_target="tpu_custom_call" | custom-call | flops 1073741824 | bytes 5249024 | tf_op jit(solution)/shard_map/pallas_call | solution.py:37
  51.9 1.7 %shard_map.31 = (f32[512,1024]{1,0:T(8,128)S(1)}, f32[16,24,128]{2,1,0:T(8,128)S(1)}) custom-call(bf16[512,1024]{1,0:T(8,128)(2,1)S(1)} %collective-permute-done.12.rows_ref, bf16[1024,1024]{1,0:T(8,128)(2,1)S(1)} %get-tuple-element.59.cols, f32[8,128]{1,0:T(8,128)S(1)} %get-tuple-element.60.sq, f32[4,128]{1,0:T(4,128)S(1)} %get-tuple-element.62.own_sums, ...), custom_call_target="tpu_custom_call" | custom-call | flops 1073741824 | bytes 5478400 | tf_op jit(solution)/shard_map/pallas_call | solution.py:37
  53.6 17.5 %all_to_all.35.got = f32[16,24,128]{2,1,0:T(8,128)S(1)} all-to-all(f32[16,24,128]{2,1,0:T(8,128)S(1)} %get-tuple-element.64), channel_id=1, replica_groups=mesh['row_0'=8,'row_1'=2,'col_0'=4,'col_1'=4] {'row_0','row_1'}, dimensions={0} | all-to-all | bytes 393216 | tf_op jit(solution)/shard_map/all_to_all | solution.py:317
  71.3 12.8 %all_to_all.36.got = f32[16,40,128]{2,1,0:T(8,128)S(1)} all-to-all(f32[16,40,128]{2,1,0:T(8,128)S(1)} %get-tuple-element.66), channel_id=1, replica_groups=mesh['row_0'=8,'row_1'=2,'col_0'=4,'col_1'=4] {'col_0','col_1'}, dimensions={0} | all-to-all | bytes 655360 | tf_op jit(solution)/shard_map/all_to_all | solution.py:320
  84.9 1.2 collective-permute-start.14
  86.1 0.9 shard_map.33
  87.7 14.8 %all_to_all.37 = f16[8,64,256]{2,1,0:T(8,128)(2,1)S(1)} all-to-all(f16[8,64,256]{2,1,0:T(8,128)(2,1)S(1)} %bitcast.38), channel_id=1, replica_groups=mesh['row_0'=8,'row_1'=2,'col_0'=4,'col_1'=4] {'row_0'}, dimensions={0} | all-to-all | bytes 524288 | tf_op jit(solution)/shard_map/all_to_all | solution.py:338
  102.8 13.3 %all_to_all.38 = bf16[16,64,256]{2,1,0:T(8,128)(2,1)S(1)} all-to-all(bf16[16,64,256]{2,1,0:T(8,128)(2,1)S(1)} %get-tuple-element.74), channel_id=1, replica_groups=mesh['row_0'=8,'row_1'=2,'col_0'=4,'col_1'=4] {'col_0','col_1'}, dimensions={0} | all-to-all | bytes 1048576 | tf_op jit(solution)/shard_map/all_to_all | solution.py:350
  116.5 2.0 %collective-permute-start.15 = (f32[512,256]{1,0:T(8,128)S(1)}, f32[512,256]{1,0:T(8,128)S(1)}, u32[]{:S(2)}, u32[]{:S(2)}) collective-permute-start(f32[512,256]{1,0:T(8,128)S(1)} %fusion.3), channel_id=1, source_target_pairs={{16,0},{0,16},{17,1},{1,17},{18,2},{2,18},{19,3},{3,19},{20,4},{4,... | collective-permute-start | bytes 1572872 | tf_op jit(solution)/shard_map/ppermute | solution.py:21
  119.0 1.2 collective-permute-done.16
  120.7 16.1 %all_to_all.39 = f16[8,80,256]{2,1,0:T(8,128)(2,1)S(1)} all-to-all(f16[8,80,256]{2,1,0:T(8,128)(2,1)S(1)} %pad_maximum_fusion.2), channel_id=1, replica_groups=mesh['row_0'=8,'row_1'=2,'col_0'=4,'col_1'=4] {'row_0'}, dimensions={0} | all-to-all | bytes 655360 | tf_op jit(solution)/shard_map/all_to_all | solution.py:338
  137.6 3.5 %all-to-all-start.6 = ((f32[16,16,256]{2,1,0:T(8,128)}), f32[16,16,256]{2,1,0:T(8,128)S(1)}, u32[]{:S(2)}, u32[]{:S(2)}) async-start(f32[16,16,256]{2,1,0:T(8,128)} %broadcast_in_dim.7), calls=%async_computation.6 | async-start | bytes 524288 | tf_op jit(solution)/shard_map/all_to_all | solution.py:27
  141.2 8.3 %all-to-all-done.6 = f32[16,16,256]{2,1,0:T(8,128)S(1)} async-done(((f32[16,16,256]{2,1,0:T(8,128)}), f32[16,16,256]{2,1,0:T(8,128)S(1)}, u32[]{:S(2)}, u32[]{:S(2)}) %all-to-all-start.6) | async-done | bytes 262176 | tf_op jit(solution)/shard_map/all_to_all | solution.py:27
  149.5 0.9 shard_map.37
  (45 shorter events, 7.1 us)
Async XLA Ops:
  2.0 9.2 %copy-start = (bf16[32,1280]{1,0:T(8,128)(2,1)S(1)}, bf16[32,1280]{1,0:T(8,128)(2,1)}, u32[]{:S(2)}) copy-start(bf16[32,1280]{1,0:T(8,128)(2,1)} %get-tuple-element.41.ax0) | copy-start | bytes 245764
  2.1 14.1 %copy-start.1 = (bf16[32,1280]{1,0:T(8,128)(2,1)S(1)}, bf16[32,1280]{1,0:T(8,128)(2,1)}, u32[]{:S(2)}) copy-start(bf16[32,1280]{1,0:T(8,128)(2,1)} %get-tuple-element.42.by0) | copy-start | bytes 245764
  2.1 41.6 %all-to-all-start = ((bf16[8,64,1024]{2,1,0:T(8,128)(2,1)}), bf16[8,64,1024]{2,1,0:T(8,128)(2,1)S(1)}, u32[]{:S(2)}, u32[]{:S(2)}) async-start(bf16[8,64,1024]{2,1,0:T(8,128)(2,1)} %get-tuple-element.51), calls=%async_computation | async-start | bytes 2097152 | tf_op jit(solution)/shard_map/all_to_all | solution.py:269
  11.2 8.8 %collective-permute-start.2 = (bf16[32,1280]{1,0:T(8,128)(2,1)S(1)}, bf16[32,1280]{1,0:T(8,128)(2,1)S(1)}, u32[]{:S(2)}, u32[]{:S(2)}) collective-permute-start(bf16[32,1280]{1,0:T(8,128)(2,1)S(1)} %copy-done), channel_id=1, source_target_pairs={{3,0},{0,1},{1,2},{2,3},{7,4},{4,5},{5,6},{6,7},{11,8},{8,9},{9,10... | collective-permute-start | bytes 245768 | tf_op jit(solution)/shard_map/ppermute | solution.py:21
  12.5 8.6 %collective-permute-start.1 = (bf16[32,1280]{1,0:T(8,128)(2,1)S(1)}, bf16[32,1280]{1,0:T(8,128)(2,1)S(1)}, u32[]{:S(2)}, u32[]{:S(2)}) collective-permute-start(bf16[32,1280]{1,0:T(8,128)(2,1)S(1)} %copy-done), channel_id=1, source_target_pairs={{2,0},{3,1},{0,2},{1,3},{6,4},{7,5},{4,6},{5,7},{10,8},{11,9},{8,1... | collective-permute-start | bytes 245768 | tf_op jit(solution)/shard_map/ppermute | solution.py:21
  15.0 6.2 %collective-permute-start = (bf16[32,1280]{1,0:T(8,128)(2,1)S(1)}, bf16[32,1280]{1,0:T(8,128)(2,1)S(1)}, u32[]{:S(2)}, u32[]{:S(2)}) collective-permute-start(bf16[32,1280]{1,0:T(8,128)(2,1)S(1)} %copy-done), channel_id=1, source_target_pairs={{1,0},{2,1},{3,2},{0,3},{5,4},{6,5},{7,6},{4,7},{9,8},{10,9},{11,1... | collective-permute-start | bytes 245768 | tf_op jit(solution)/shard_map/ppermute | solution.py:21
  16.1 5.0 %collective-permute-start.5 = (bf16[32,1280]{1,0:T(8,128)(2,1)S(1)}, bf16[32,1280]{1,0:T(8,128)(2,1)S(1)}, u32[]{:S(2)}, u32[]{:S(2)}) collective-permute-start(bf16[32,1280]{1,0:T(8,128)(2,1)S(1)} %copy-done.1), channel_id=1, source_target_pairs={{12,0},{0,4},{4,8},{8,12},{13,1},{1,5},{5,9},{9,13},{14,2},{2,6},{... | collective-permute-start | bytes 245768 | tf_op jit(solution)/shard_map/ppermute | solution.py:21
  17.4 5.6 %collective-permute-start.4 = (bf16[32,1280]{1,0:T(8,128)(2,1)S(1)}, bf16[32,1280]{1,0:T(8,128)(2,1)S(1)}, u32[]{:S(2)}, u32[]{:S(2)}) collective-permute-start(bf16[32,1280]{1,0:T(8,128)(2,1)S(1)} %copy-done.1), channel_id=1, source_target_pairs={{8,0},{12,4},{0,8},{4,12},{9,1},{13,5},{1,9},{5,13},{10,2},{14,6},... | collective-permute-start | bytes 245768 | tf_op jit(solution)/shard_map/ppermute | solution.py:21
  20.0 4.1 %collective-permute-start.3 = (bf16[32,1280]{1,0:T(8,128)(2,1)S(1)}, bf16[32,1280]{1,0:T(8,128)(2,1)S(1)}, u32[]{:S(2)}, u32[]{:S(2)}) collective-permute-start(bf16[32,1280]{1,0:T(8,128)(2,1)S(1)} %copy-done.1), channel_id=1, source_target_pairs={{4,0},{8,4},{12,8},{0,12},{5,1},{9,5},{13,9},{1,13},{6,2},{10,6},{... | collective-permute-start | bytes 245768 | tf_op jit(solution)/shard_map/ppermute | solution.py:21
  24.3 8.1 %collective-permute-start.10 = (bf16[4,32,1280]{2,1,0:T(8,128)(2,1)S(1)}, bf16[4,32,1280]{2,1,0:T(8,128)(2,1)S(1)}, u32[]{:S(2)}, u32[]{:S(2)}) collective-permute-start(bf16[4,32,1280]{2,1,0:T(8,128)(2,1)S(1)} %get-tuple-element.49), channel_id=1, source_target_pairs={{2,0},{3,1},{0,2},{1,3},{6,4},{7,5},{4,6},{5,7},{10,8},{11,9},{8,1... | collective-permute-start | bytes 983048 | tf_op jit(solution)/shard_map/ppermute | solution.py:21
  24.6 14.1 %collective-permute-start.8 = (bf16[4,32,1280]{2,1,0:T(8,128)(2,1)S(1)}, bf16[4,32,1280]{2,1,0:T(8,128)(2,1)S(1)}, u32[]{:S(2)}, u32[]{:S(2)}) collective-permute-start(bf16[4,32,1280]{2,1,0:T(8,128)(2,1)S(1)} %get-tuple-element.49), channel_id=1, source_target_pairs={{1,0},{2,1},{3,2},{0,3},{5,4},{6,5},{7,6},{4,7},{9,8},{10,9},{11,1... | collective-permute-start | bytes 983048 | tf_op jit(solution)/shard_map/ppermute | solution.py:21
  27.1 14.4 %collective-permute-start.6 = (bf16[4,32,1280]{2,1,0:T(8,128)(2,1)S(1)}, bf16[4,32,1280]{2,1,0:T(8,128)(2,1)S(1)}, u32[]{:S(2)}, u32[]{:S(2)}) collective-permute-start(bf16[4,32,1280]{2,1,0:T(8,128)(2,1)S(1)} %get-tuple-element.49), channel_id=1, source_target_pairs={{3,0},{0,1},{1,2},{2,3},{7,4},{4,5},{5,6},{6,7},{11,8},{8,9},{9,10... | collective-permute-start | bytes 983048 | tf_op jit(solution)/shard_map/ppermute | solution.py:21
  27.1 14.4 %collective-permute-start.11 = (bf16[4,32,1280]{2,1,0:T(8,128)(2,1)S(1)}, bf16[4,32,1280]{2,1,0:T(8,128)(2,1)S(1)}, u32[]{:S(2)}, u32[]{:S(2)}) collective-permute-start(bf16[4,32,1280]{2,1,0:T(8,128)(2,1)S(1)} %get-tuple-element.50), channel_id=1, source_target_pairs={{8,0},{12,4},{0,8},{4,12},{9,1},{13,5},{1,9},{5,13},{10,2},{14,6},... | collective-permute-start | bytes 983048 | tf_op jit(solution)/shard_map/ppermute | solution.py:21
  28.5 14.4 %collective-permute-start.9 = (bf16[4,32,1280]{2,1,0:T(8,128)(2,1)S(1)}, bf16[4,32,1280]{2,1,0:T(8,128)(2,1)S(1)}, u32[]{:S(2)}, u32[]{:S(2)}) collective-permute-start(bf16[4,32,1280]{2,1,0:T(8,128)(2,1)S(1)} %get-tuple-element.50), channel_id=1, source_target_pairs={{4,0},{8,4},{12,8},{0,12},{5,1},{9,5},{13,9},{1,13},{6,2},{10,6},{... | collective-permute-start | bytes 983048 | tf_op jit(solution)/shard_map/ppermute | solution.py:21
  32.4 10.6 %collective-permute-start.7 = (bf16[4,32,1280]{2,1,0:T(8,128)(2,1)S(1)}, bf16[4,32,1280]{2,1,0:T(8,128)(2,1)S(1)}, u32[]{:S(2)}, u32[]{:S(2)}) collective-permute-start(bf16[4,32,1280]{2,1,0:T(8,128)(2,1)S(1)} %get-tuple-element.50), channel_id=1, source_target_pairs={{12,0},{0,4},{4,8},{8,12},{13,1},{1,5},{5,9},{9,13},{14,2},{2,6},{... | collective-permute-start | bytes 983048 | tf_op jit(solution)/shard_map/ppermute | solution.py:21
  43.0 0.7 copy-start.2
  43.7 8.2 %collective-permute-start.12 = (bf16[512,1024]{1,0:T(8,128)(2,1)S(1)}, bf16[512,1024]{1,0:T(8,128)(2,1)S(1)}, u32[]{:S(2)}, u32[]{:S(2)}) collective-permute-start(bf16[512,1024]{1,0:T(8,128)(2,1)S(1)} %bitcast.27), channel_id=1, source_target_pairs={{16,0},{0,16},{17,1},{1,17},{18,2},{2,18},{19,3},{3,19},{20,4},{4,... | collective-permute-start | bytes 3145736 | tf_op jit(solution)/shard_map/ppermute | solution.py:21
  48.2 1.0 copy-start.3
  49.9 2.0 %collective-permute-start.13 = (f32[16,256]{1,0:T(8,128)S(1)}, f32[16,256]{1,0:T(8,128)S(1)}, u32[]{:S(2)}, u32[]{:S(2)}) collective-permute-start(f32[16,256]{1,0:T(8,128)S(1)} %get-tuple-element.63.part), channel_id=1, source_target_pairs={{16,0},{0,16},{17,1},{1,17},{18,2},{2,18},{19,3},{3,19},{20,4},{4,... | collective-permute-start | bytes 49160 | tf_op jit(solution)/shard_map/ppermute | solution.py:21
  84.9 2.7 %collective-permute-start.14 = (f32[512,256]{1,0:T(8,128)S(1)}, f32[512,256]{1,0:T(8,128)S(1)}, u32[]{:S(2)}, u32[]{:S(2)}) collective-permute-start(f32[512,256]{1,0:T(8,128)S(1)} %get-tuple-element.71), channel_id=1, source_target_pairs={{16,0},{0,16},{17,1},{1,17},{18,2},{2,18},{19,3},{3,19},{20,4},{4,... | collective-permute-start | bytes 1572872 | tf_op jit(solution)/shard_map/ppermute | solution.py:21
  86.1 16.4 %copy-start.4 = (f32[64,256]{1,0:T(8,128)S(1)}, f32[64,256]{1,0:T(8,128)}, u32[]{:S(2)}) copy-start(f32[64,256]{1,0:T(8,128)} %h_ref.1) | copy-start | bytes 196612
  116.5 3.6 %collective-permute-start.15 = (f32[512,256]{1,0:T(8,128)S(1)}, f32[512,256]{1,0:T(8,128)S(1)}, u32[]{:S(2)}, u32[]{:S(2)}) collective-permute-start(f32[512,256]{1,0:T(8,128)S(1)} %fusion.3), channel_id=1, source_target_pairs={{16,0},{0,16},{17,1},{1,17},{18,2},{2,18},{19,3},{3,19},{20,4},{4,... | collective-permute-start | bytes 1572872 | tf_op jit(solution)/shard_map/ppermute | solution.py:21
  118.9 1.3 collective-permute-start.16
  137.6 11.8 %all-to-all-start.6 = ((f32[16,16,256]{2,1,0:T(8,128)}), f32[16,16,256]{2,1,0:T(8,128)S(1)}, u32[]{:S(2)}, u32[]{:S(2)}) async-start(f32[16,16,256]{2,1,0:T(8,128)} %broadcast_in_dim.7), calls=%async_computation.6 | async-start | bytes 524288 | tf_op jit(solution)/shard_map/all_to_all | solution.py:27

commit v11 on v10

--- a/solution.py
+++ b/solution.py
@@ -362,8 +362,8 @@
     mine = ((partial_own + got) * scales[2]).reshape(nz, pts, rank)
     extra = jnp.broadcast_to((own_part + more_part) * scales[4], (nz, part, rank))
     own = over_z(jnp.concatenate([mine, extra], axis=1))
-    hh = sent_to_all(own[pts:] * scales[5], COL).reshape(rank, rank)
-    ah = own[:pts] * scales[3]
+    ah, own_part = tie((own[:pts] * scales[3], own[pts:] * scales[5]))
+    hh = sent_to_all(own_part, COL).reshape(rank, rank)
     return stepped(None, unit, ah, hh, h, 0)[0]
 
 

time: 151 us -> 149 us (0.987)
  blocking collectives: 74.5 us -> 85.1 us
  waiting for transfers between devices: 26.9 us -> 18.6 us
  starting transfers between devices: 35.5 us -> 32 us
    all_to_all x0 -> x1, blocking collectives: none -> 10.7 us  [sent_to_all(): return lax.all_to_all(copies, axes, split_axis=0, concat_axis=0, tiled=True)]
    all_to_all x1 -> x0, waiting for transfers between devices: 8.27 us -> none  [sent_to_all(): return lax.all_to_all(copies, axes, split_axis=0, concat_axis=0, tiled=True)]
    all_to_all x1 -> x0, starting transfers between devices: 3.53 us -> none  [sent_to_all(): return lax.all_to_all(copies, axes, split_axis=0, concat_axis=0, tiled=True)]
  transfers between devices with their start and end apart: 19 -> 18, of which waited for: 9 -> 8; matrix products, arithmetic and copies ran while one was open for 0% -> 0% of each run, Pallas kernels for 2% -> 2%
where the time goes in v11:
time: 149 us
  blocking collectives  85.1 us (57%)
  starting transfers between devices  32 us (21%)
  waiting for transfers between devices  18.6 us (12%)
  Pallas kernels  9.58 us (6%)
  local copies, waits for them, and re-layouts  1.75 us (1%)
    all_to_all x2, blocking collectives, over_z(): mine = lax.all_to_all(mine.astype(jnp.float16), Z, 0, 0, tiled=True)  30.9 us
    ppermute x17, starting transfers between devices, from_ahead(): lax.ppermute(value, axis, [((i + steps) % length, i) for i in range(lengt...  22.8 us
    ppermute x17, waiting for transfers between devices, from_ahead(): lax.ppermute(value, axis, [((i + steps) % length, i) for i in range(lengt...  18.6 us
    all_to_all x1, blocking collectives, shards(): lax.all_to_all(message, ROW, 0, 0, tiled=True)  17.5 us
    all_to_all x1, blocking collectives, shards(): lax.all_to_all(hb_cols, COL, 0, 0, tiled=True).reshape(group, rank)  13.3 us
    all_to_all x1, blocking collectives, shards(): gathered = lax.all_to_all(message, COL, 0, 0, tiled=True)  12.8 us
    all_to_all x1, blocking collectives, sent_to_all(): return lax.all_to_all(copies, axes, split_axis=0, concat_axis=0, tiled=True)  10.7 us
    pallas_call x10, Pallas kernels, call(): pl.pallas_call(kernel, out_shape=outs, in_specs=[pl.BlockSpec(memory_spac...  9.58 us
  transfers between devices with their start and end apart: 18, of which 8 were waited for; matrix products, arithmetic and copies ran while one was open for 0% of the time, Pallas kernels for 2%

profile of v11, /device:TPU:1, one launch (start us, length us, event | category | flops | bytes accessed | tf_op | source)
XLA Modules:
  0.0 148.6 jit_solution(3440945481644196650)
XLA Ops:
  0.0 2.0 %shard_map.28 = (bf16[32,1280]{1,0:T(8,128)(2,1)}, bf16[32,1280]{1,0:T(8,128)(2,1)}, bf16[8,64,1024]{2,1,0:T(8,128)(2,1)}) custom-call(bf16[64,1024]{1,0:T(8,128)(2,1)} %points.1, f32[64,256]{1,0:T(8,128)} %h_ref.1), custom_call_target="tpu_custom_call" | custom-call | flops 1 | bytes 1409024 | tf_op jit(solution)/shard_map/pallas_call | solution.py:37
  2.1 9.2 %all-to-all-start = ((bf16[8,64,1024]{2,1,0:T(8,128)(2,1)}), bf16[8,64,1024]{2,1,0:T(8,128)(2,1)S(1)}, u32[]{:S(2)}, u32[]{:S(2)}) async-start(bf16[8,64,1024]{2,1,0:T(8,128)(2,1)} %get-tuple-element.53), calls=%async_computation | async-start | bytes 2097152 | tf_op jit(solution)/shard_map/all_to_all | solution.py:269
  11.2 1.3 collective-permute-start.2
  12.5 2.5 %collective-permute-start.1 = (bf16[32,1280]{1,0:T(8,128)(2,1)S(1)}, bf16[32,1280]{1,0:T(8,128)(2,1)S(1)}, u32[]{:S(2)}, u32[]{:S(2)}) collective-permute-start(bf16[32,1280]{1,0:T(8,128)(2,1)S(1)} %copy-done), channel_id=1, source_target_pairs={{2,0},{3,1},{0,2},{1,3},{6,4},{7,5},{4,6},{5,7},{10,8},{11,9},{8,1... | collective-permute-start | bytes 245768 | tf_op jit(solution)/shard_map/ppermute | solution.py:21
  15.0 1.2 collective-permute-start
  16.1 1.3 collective-permute-start.5
  17.4 2.6 %collective-permute-start.4 = (bf16[32,1280]{1,0:T(8,128)(2,1)S(1)}, bf16[32,1280]{1,0:T(8,128)(2,1)S(1)}, u32[]{:S(2)}, u32[]{:S(2)}) collective-permute-start(bf16[32,1280]{1,0:T(8,128)(2,1)S(1)} %copy-done.1), channel_id=1, source_target_pairs={{8,0},{12,4},{0,8},{4,12},{9,1},{13,5},{1,9},{5,13},{10,2},{14,6},... | collective-permute-start | bytes 245768 | tf_op jit(solution)/shard_map/ppermute | solution.py:21
  20.0 1.1 collective-permute-start.3
  21.1 1.9 %collective-permute-done.4.by2 = bf16[32,1280]{1,0:T(8,128)(2,1)S(1)} collective-permute-done((bf16[32,1280]{1,0:T(8,128)(2,1)S(1)}, bf16[32,1280]{1,0:T(8,128)(2,1)S(1)}, u32[]{:S(2)}, u32[]{:S(2)}) %collective-permute-start.4) | collective-permute-done | bytes 81952 | tf_op jit(solution)/shard_map/ppermute | solution.py:21
  23.0 1.2 collective-permute-done.3.by1
  24.6 2.5 %collective-permute-start.8 = (bf16[4,32,1280]{2,1,0:T(8,128)(2,1)S(1)}, bf16[4,32,1280]{2,1,0:T(8,128)(2,1)S(1)}, u32[]{:S(2)}, u32[]{:S(2)}) collective-permute-start(bf16[4,32,1280]{2,1,0:T(8,128)(2,1)S(1)} %get-tuple-element.51), channel_id=1, source_target_pairs={{1,0},{2,1},{3,2},{0,3},{5,4},{6,5},{7,6},{4,7},{9,8},{10,9},{11,1... | collective-permute-start | bytes 983048 | tf_op jit(solution)/shard_map/ppermute | solution.py:21
  27.1 1.5 collective-permute-start.11
  29.2 3.2 %collective-permute-done.10.x2 = bf16[4,32,1280]{2,1,0:T(8,128)(2,1)S(1)} collective-permute-done((bf16[4,32,1280]{2,1,0:T(8,128)(2,1)S(1)}, bf16[4,32,1280]{2,1,0:T(8,128)(2,1)S(1)}, u32[]{:S(2)}, u32[]{:S(2)}) %collective-permute-start.10) | collective-permute-done | bytes 327712 | tf_op jit(solution)/shard_map/ppermute | solution.py:21
  32.4 6.2 %collective-permute-done.8.x1 = bf16[4,32,1280]{2,1,0:T(8,128)(2,1)S(1)} collective-permute-done((bf16[4,32,1280]{2,1,0:T(8,128)(2,1)S(1)}, bf16[4,32,1280]{2,1,0:T(8,128)(2,1)S(1)}, u32[]{:S(2)}, u32[]{:S(2)}) %collective-permute-start.8) | collective-permute-done | bytes 327712 | tf_op jit(solution)/shard_map/ppermute | solution.py:21
  38.7 2.8 %collective-permute-done.6.x3 = bf16[4,32,1280]{2,1,0:T(8,128)(2,1)S(1)} collective-permute-done((bf16[4,32,1280]{2,1,0:T(8,128)(2,1)S(1)}, bf16[4,32,1280]{2,1,0:T(8,128)(2,1)S(1)}, u32[]{:S(2)}, u32[]{:S(2)}) %collective-permute-start.6) | collective-permute-done | bytes 327712 | tf_op jit(solution)/shard_map/ppermute | solution.py:21
  41.4 1.5 %collective-permute-done.9.y1 = bf16[4,32,1280]{2,1,0:T(8,128)(2,1)S(1)} collective-permute-done((bf16[4,32,1280]{2,1,0:T(8,128)(2,1)S(1)}, bf16[4,32,1280]{2,1,0:T(8,128)(2,1)S(1)}, u32[]{:S(2)}, u32[]{:S(2)}) %collective-permute-start.9) | collective-permute-done | bytes 327712 | tf_op jit(solution)/shard_map/ppermute | solution.py:21
  43.7 4.5 %collective-permute-start.12 = (bf16[512,1024]{1,0:T(8,128)(2,1)S(1)}, bf16[512,1024]{1,0:T(8,128)(2,1)S(1)}, u32[]{:S(2)}, u32[]{:S(2)}) collective-permute-start(bf16[512,1024]{1,0:T(8,128)(2,1)S(1)} %bitcast.27), channel_id=1, source_target_pairs={{16,0},{0,16},{17,1},{1,17},{18,2},{2,18},{19,3},{3,19},{20,4},{4,... | collective-permute-start | bytes 3145736 | tf_op jit(solution)/shard_map/ppermute | solution.py:21
  48.2 1.0 copy-done.3
  50.2 1.7 %shard_map.30 = (f32[512,1024]{1,0:T(8,128)S(1)}, f32[4,128]{1,0:T(4,128)S(1)}) custom-call(bf16[512,1024]{1,0:T(8,128)(2,1)S(1)} %bitcast.28, bf16[1024,1024]{1,0:T(8,128)(2,1)S(1)} %get-tuple-element.61.cols, f32[8,128]{1,0:T(8,128)S(1)} %get-tuple-element.62.sq), custom_call_target="tpu_custom_call" | custom-call | flops 1073741824 | bytes 5249024 | tf_op jit(solution)/shard_map/pallas_call | solution.py:37
  51.9 1.7 %shard_map.31 = (f32[512,1024]{1,0:T(8,128)S(1)}, f32[16,24,128]{2,1,0:T(8,128)S(1)}) custom-call(bf16[512,1024]{1,0:T(8,128)(2,1)S(1)} %collective-permute-done.12.rows_ref, bf16[1024,1024]{1,0:T(8,128)(2,1)S(1)} %get-tuple-element.61.cols, f32[8,128]{1,0:T(8,128)S(1)} %get-tuple-element.62.sq, f32[4,128]{1,0:T(4,128)S(1)} %get-tuple-element.64.own_sums, ...), custom_call_target="tpu_custom_call" | custom-call | flops 1073741824 | bytes 5478400 | tf_op jit(solution)/shard_map/pallas_call | solution.py:37
  53.6 17.5 %all_to_all.35.got = f32[16,24,128]{2,1,0:T(8,128)S(1)} all-to-all(f32[16,24,128]{2,1,0:T(8,128)S(1)} %get-tuple-element.66), channel_id=1, replica_groups=mesh['row_0'=8,'row_1'=2,'col_0'=4,'col_1'=4] {'row_0','row_1'}, dimensions={0} | all-to-all | bytes 393216 | tf_op jit(solution)/shard_map/all_to_all | solution.py:317
  71.3 12.8 %all_to_all.36.got = f32[16,40,128]{2,1,0:T(8,128)S(1)} all-to-all(f32[16,40,128]{2,1,0:T(8,128)S(1)} %get-tuple-element.68), channel_id=1, replica_groups=mesh['row_0'=8,'row_1'=2,'col_0'=4,'col_1'=4] {'col_0','col_1'}, dimensions={0} | all-to-all | bytes 655360 | tf_op jit(solution)/shard_map/all_to_all | solution.py:320
  84.1 0.8 shard_map.34
  84.9 1.2 collective-permute-start.14
  86.1 0.9 shard_map.33
  87.7 14.8 %all_to_all.37 = f16[8,64,256]{2,1,0:T(8,128)(2,1)S(1)} all-to-all(f16[8,64,256]{2,1,0:T(8,128)(2,1)S(1)} %bitcast.38), channel_id=1, replica_groups=mesh['row_0'=8,'row_1'=2,'col_0'=4,'col_1'=4] {'row_0'}, dimensions={0} | all-to-all | bytes 524288 | tf_op jit(solution)/shard_map/all_to_all | solution.py:338
  102.9 13.3 %all_to_all.38 = bf16[16,64,256]{2,1,0:T(8,128)(2,1)S(1)} all-to-all(bf16[16,64,256]{2,1,0:T(8,128)(2,1)S(1)} %get-tuple-element.76), channel_id=1, replica_groups=mesh['row_0'=8,'row_1'=2,'col_0'=4,'col_1'=4] {'col_0','col_1'}, dimensions={0} | all-to-all | bytes 1048576 | tf_op jit(solution)/shard_map/all_to_all | solution.py:350
  116.6 2.0 %collective-permute-start.15 = (f32[512,256]{1,0:T(8,128)S(1)}, f32[512,256]{1,0:T(8,128)S(1)}, u32[]{:S(2)}, u32[]{:S(2)}) collective-permute-start(f32[512,256]{1,0:T(8,128)S(1)} %fusion.3), channel_id=1, source_target_pairs={{16,0},{0,16},{17,1},{1,17},{18,2},{2,18},{19,3},{3,19},{20,4},{4,... | collective-permute-start | bytes 1572872 | tf_op jit(solution)/shard_map/ppermute | solution.py:21
  119.0 1.2 collective-permute-done.16
  120.8 16.1 %all_to_all.39 = f16[8,80,256]{2,1,0:T(8,128)(2,1)S(1)} all-to-all(f16[8,80,256]{2,1,0:T(8,128)(2,1)S(1)} %pad_maximum_fusion.2), channel_id=1, replica_groups=mesh['row_0'=8,'row_1'=2,'col_0'=4,'col_1'=4] {'row_0'}, dimensions={0} | all-to-all | bytes 655360 | tf_op jit(solution)/shard_map/all_to_all | solution.py:338
  137.0 10.7 %all_to_all.40 = f32[16,16,256]{2,1,0:T(8,128)S(1)} all-to-all(f32[16,16,256]{2,1,0:T(8,128)S(1)} %broadcast_in_dim.7), channel_id=1, replica_groups=mesh['row_0'=8,'row_1'=2,'col_0'=4,'col_1'=4] {'col_0','col_1'}, dimensions={0} | all-to-all | bytes 524288 | tf_op jit(solution)/shard_map/all_to_all | solution.py:27
  147.7 0.9 shard_map.37
  (44 shorter events, 5.6 us)
Async XLA Ops:
  2.0 9.2 %copy-start = (bf16[32,1280]{1,0:T(8,128)(2,1)S(1)}, bf16[32,1280]{1,0:T(8,128)(2,1)}, u32[]{:S(2)}) copy-start(bf16[32,1280]{1,0:T(8,128)(2,1)} %get-tuple-element.43.ax0) | copy-start | bytes 245764
  2.0 14.1 %copy-start.1 = (bf16[32,1280]{1,0:T(8,128)(2,1)S(1)}, bf16[32,1280]{1,0:T(8,128)(2,1)}, u32[]{:S(2)}) copy-start(bf16[32,1280]{1,0:T(8,128)(2,1)} %get-tuple-element.44.by0) | copy-start | bytes 245764
  2.1 41.6 %all-to-all-start = ((bf16[8,64,1024]{2,1,0:T(8,128)(2,1)}), bf16[8,64,1024]{2,1,0:T(8,128)(2,1)S(1)}, u32[]{:S(2)}, u32[]{:S(2)}) async-start(bf16[8,64,1024]{2,1,0:T(8,128)(2,1)} %get-tuple-element.53), calls=%async_computation | async-start | bytes 2097152 | tf_op jit(solution)/shard_map/all_to_all | solution.py:269
  11.2 8.8 %collective-permute-start.2 = (bf16[32,1280]{1,0:T(8,128)(2,1)S(1)}, bf16[32,1280]{1,0:T(8,128)(2,1)S(1)}, u32[]{:S(2)}, u32[]{:S(2)}) collective-permute-start(bf16[32,1280]{1,0:T(8,128)(2,1)S(1)} %copy-done), channel_id=1, source_target_pairs={{3,0},{0,1},{1,2},{2,3},{7,4},{4,5},{5,6},{6,7},{11,8},{8,9},{9,10... | collective-permute-start | bytes 245768 | tf_op jit(solution)/shard_map/ppermute | solution.py:21
  12.5 8.6 %collective-permute-start.1 = (bf16[32,1280]{1,0:T(8,128)(2,1)S(1)}, bf16[32,1280]{1,0:T(8,128)(2,1)S(1)}, u32[]{:S(2)}, u32[]{:S(2)}) collective-permute-start(bf16[32,1280]{1,0:T(8,128)(2,1)S(1)} %copy-done), channel_id=1, source_target_pairs={{2,0},{3,1},{0,2},{1,3},{6,4},{7,5},{4,6},{5,7},{10,8},{11,9},{8,1... | collective-permute-start | bytes 245768 | tf_op jit(solution)/shard_map/ppermute | solution.py:21
  15.0 6.2 %collective-permute-start = (bf16[32,1280]{1,0:T(8,128)(2,1)S(1)}, bf16[32,1280]{1,0:T(8,128)(2,1)S(1)}, u32[]{:S(2)}, u32[]{:S(2)}) collective-permute-start(bf16[32,1280]{1,0:T(8,128)(2,1)S(1)} %copy-done), channel_id=1, source_target_pairs={{1,0},{2,1},{3,2},{0,3},{5,4},{6,5},{7,6},{4,7},{9,8},{10,9},{11,1... | collective-permute-start | bytes 245768 | tf_op jit(solution)/shard_map/ppermute | solution.py:21
  16.1 5.0 %collective-permute-start.5 = (bf16[32,1280]{1,0:T(8,128)(2,1)S(1)}, bf16[32,1280]{1,0:T(8,128)(2,1)S(1)}, u32[]{:S(2)}, u32[]{:S(2)}) collective-permute-start(bf16[32,1280]{1,0:T(8,128)(2,1)S(1)} %copy-done.1), channel_id=1, source_target_pairs={{12,0},{0,4},{4,8},{8,12},{13,1},{1,5},{5,9},{9,13},{14,2},{2,6},{... | collective-permute-start | bytes 245768 | tf_op jit(solution)/shard_map/ppermute | solution.py:21
  17.4 5.6 %collective-permute-start.4 = (bf16[32,1280]{1,0:T(8,128)(2,1)S(1)}, bf16[32,1280]{1,0:T(8,128)(2,1)S(1)}, u32[]{:S(2)}, u32[]{:S(2)}) collective-permute-start(bf16[32,1280]{1,0:T(8,128)(2,1)S(1)} %copy-done.1), channel_id=1, source_target_pairs={{8,0},{12,4},{0,8},{4,12},{9,1},{13,5},{1,9},{5,13},{10,2},{14,6},... | collective-permute-start | bytes 245768 | tf_op jit(solution)/shard_map/ppermute | solution.py:21
  20.0 4.1 %collective-permute-start.3 = (bf16[32,1280]{1,0:T(8,128)(2,1)S(1)}, bf16[32,1280]{1,0:T(8,128)(2,1)S(1)}, u32[]{:S(2)}, u32[]{:S(2)}) collective-permute-start(bf16[32,1280]{1,0:T(8,128)(2,1)S(1)} %copy-done.1), channel_id=1, source_target_pairs={{4,0},{8,4},{12,8},{0,12},{5,1},{9,5},{13,9},{1,13},{6,2},{10,6},{... | collective-permute-start | bytes 245768 | tf_op jit(solution)/shard_map/ppermute | solution.py:21
  24.3 8.1 %collective-permute-start.10 = (bf16[4,32,1280]{2,1,0:T(8,128)(2,1)S(1)}, bf16[4,32,1280]{2,1,0:T(8,128)(2,1)S(1)}, u32[]{:S(2)}, u32[]{:S(2)}) collective-permute-start(bf16[4,32,1280]{2,1,0:T(8,128)(2,1)S(1)} %get-tuple-element.51), channel_id=1, source_target_pairs={{2,0},{3,1},{0,2},{1,3},{6,4},{7,5},{4,6},{5,7},{10,8},{11,9},{8,1... | collective-permute-start | bytes 983048 | tf_op jit(solution)/shard_map/ppermute | solution.py:21
  24.6 14.1 %collective-permute-start.8 = (bf16[4,32,1280]{2,1,0:T(8,128)(2,1)S(1)}, bf16[4,32,1280]{2,1,0:T(8,128)(2,1)S(1)}, u32[]{:S(2)}, u32[]{:S(2)}) collective-permute-start(bf16[4,32,1280]{2,1,0:T(8,128)(2,1)S(1)} %get-tuple-element.51), channel_id=1, source_target_pairs={{1,0},{2,1},{3,2},{0,3},{5,4},{6,5},{7,6},{4,7},{9,8},{10,9},{11,1... | collective-permute-start | bytes 983048 | tf_op jit(solution)/shard_map/ppermute | solution.py:21
  27.1 14.4 %collective-permute-start.6 = (bf16[4,32,1280]{2,1,0:T(8,128)(2,1)S(1)}, bf16[4,32,1280]{2,1,0:T(8,128)(2,1)S(1)}, u32[]{:S(2)}, u32[]{:S(2)}) collective-permute-start(bf16[4,32,1280]{2,1,0:T(8,128)(2,1)S(1)} %get-tuple-element.51), channel_id=1, source_target_pairs={{3,0},{0,1},{1,2},{2,3},{7,4},{4,5},{5,6},{6,7},{11,8},{8,9},{9,10... | collective-permute-start | bytes 983048 | tf_op jit(solution)/shard_map/ppermute | solution.py:21
  27.1 14.4 %collective-permute-start.11 = (bf16[4,32,1280]{2,1,0:T(8,128)(2,1)S(1)}, bf16[4,32,1280]{2,1,0:T(8,128)(2,1)S(1)}, u32[]{:S(2)}, u32[]{:S(2)}) collective-permute-start(bf16[4,32,1280]{2,1,0:T(8,128)(2,1)S(1)} %get-tuple-element.52), channel_id=1, source_target_pairs={{8,0},{12,4},{0,8},{4,12},{9,1},{13,5},{1,9},{5,13},{10,2},{14,6},... | collective-permute-start | bytes 983048 | tf_op jit(solution)/shard_map/ppermute | solution.py:21
  28.5 14.4 %collective-permute-start.9 = (bf16[4,32,1280]{2,1,0:T(8,128)(2,1)S(1)}, bf16[4,32,1280]{2,1,0:T(8,128)(2,1)S(1)}, u32[]{:S(2)}, u32[]{:S(2)}) collective-permute-start(bf16[4,32,1280]{2,1,0:T(8,128)(2,1)S(1)} %get-tuple-element.52), channel_id=1, source_target_pairs={{4,0},{8,4},{12,8},{0,12},{5,1},{9,5},{13,9},{1,13},{6,2},{10,6},{... | collective-permute-start | bytes 983048 | tf_op jit(solution)/shard_map/ppermute | solution.py:21
  32.4 10.6 %collective-permute-start.7 = (bf16[4,32,1280]{2,1,0:T(8,128)(2,1)S(1)}, bf16[4,32,1280]{2,1,0:T(8,128)(2,1)S(1)}, u32[]{:S(2)}, u32[]{:S(2)}) collective-permute-start(bf16[4,32,1280]{2,1,0:T(8,128)(2,1)S(1)} %get-tuple-element.52), channel_id=1, source_target_pairs={{12,0},{0,4},{4,8},{8,12},{13,1},{1,5},{5,9},{9,13},{14,2},{2,6},{... | collective-permute-start | bytes 983048 | tf_op jit(solution)/shard_map/ppermute | solution.py:21
  43.0 0.7 copy-start.2
  43.7 8.2 %collective-permute-start.12 = (bf16[512,1024]{1,0:T(8,128)(2,1)S(1)}, bf16[512,1024]{1,0:T(8,128)(2,1)S(1)}, u32[]{:S(2)}, u32[]{:S(2)}) collective-permute-start(bf16[512,1024]{1,0:T(8,128)(2,1)S(1)} %bitcast.27), channel_id=1, source_target_pairs={{16,0},{0,16},{17,1},{1,17},{18,2},{2,18},{19,3},{3,19},{20,4},{4,... | collective-permute-start | bytes 3145736 | tf_op jit(solution)/shard_map/ppermute | solution.py:21
  48.2 1.0 copy-start.3
  49.9 2.0 %collective-permute-start.13 = (f32[16,256]{1,0:T(8,128)S(1)}, f32[16,256]{1,0:T(8,128)S(1)}, u32[]{:S(2)}, u32[]{:S(2)}) collective-permute-start(f32[16,256]{1,0:T(8,128)S(1)} %get-tuple-element.65.part), channel_id=1, source_target_pairs={{16,0},{0,16},{17,1},{1,17},{18,2},{2,18},{19,3},{3,19},{20,4},{4,... | collective-permute-start | bytes 49160 | tf_op jit(solution)/shard_map/ppermute | solution.py:21
  84.9 2.7 %collective-permute-start.14 = (f32[512,256]{1,0:T(8,128)S(1)}, f32[512,256]{1,0:T(8,128)S(1)}, u32[]{:S(2)}, u32[]{:S(2)}) collective-permute-start(f32[512,256]{1,0:T(8,128)S(1)} %get-tuple-element.73), channel_id=1, source_target_pairs={{16,0},{0,16},{17,1},{1,17},{18,2},{2,18},{19,3},{3,19},{20,4},{4,... | collective-permute-start | bytes 1572872 | tf_op jit(solution)/shard_map/ppermute | solution.py:21
  86.1 16.5 %copy-start.4 = (f32[64,256]{1,0:T(8,128)S(1)}, f32[64,256]{1,0:T(8,128)}, u32[]{:S(2)}) copy-start(f32[64,256]{1,0:T(8,128)} %h_ref.1) | copy-start | bytes 196612
  116.6 3.6 %collective-permute-start.15 = (f32[512,256]{1,0:T(8,128)S(1)}, f32[512,256]{1,0:T(8,128)S(1)}, u32[]{:S(2)}, u32[]{:S(2)}) collective-permute-start(f32[512,256]{1,0:T(8,128)S(1)} %fusion.3), channel_id=1, source_target_pairs={{16,0},{0,16},{17,1},{1,17},{18,2},{2,18},{19,3},{3,19},{20,4},{4,... | collective-permute-start | bytes 1572872 | tf_op jit(solution)/shard_map/ppermute | solution.py:21
  118.9 1.3 collective-permute-start.16

commit v12 on v11

--- a/solution.py
+++ b/solution.py
@@ -274,9 +274,10 @@
     by_x = jnp.stack([first, x1, x2, x3])
     by_y = jnp.stack([second, y1, y2, y3])
     by_x, by_y = tie((by_x, by_y))
-    y_three, x_three = from_ahead(by_x, Y, 3), from_ahead(by_y, X, 3)
     y_one, x_one = from_ahead(by_x, Y, 1), from_ahead(by_y, X, 1)
     y_two, x_two = from_ahead(by_x, Y, 2), from_ahead(by_y, X, 2)
+    by_x, by_y, x_two = tie((by_x, by_y, x_two))
+    y_three, x_three = from_ahead(by_x, Y, 3), from_ahead(by_y, X, 3)
     far = [x_three, y_three, x_one, y_one, x_two, y_two]
     far, along_z = tie((far, along_z.reshape(-1, width)))
     other = from_ahead(along_z, CORE, 1)

time: 149 us -> 149 us (level)
  starting transfers between devices: 32 us -> 35.2 us
  waiting for transfers between devices: 18.6 us -> 16.1 us
    ppermute x17, starting transfers between devices: 22.8 us -> 26 us  [from_ahead(): lax.ppermute(value, axis, [((i + steps) % length, i) for i in range(lengt...]
    ppermute x17, waiting for transfers between devices: 18.6 us -> 16.1 us  [from_ahead(): lax.ppermute(value, axis, [((i + steps) % length, i) for i in range(lengt...]
  transfers between devices with their start and end apart: 18 -> 18, of which waited for: 8 -> 6; matrix products, arithmetic and copies ran while one was open for 0% -> 0% of each run, Pallas kernels for 2% -> 2%
where the time goes in v12:
time: 149 us; the launch traced here: 148 us
  blocking collectives  84.4 us (57%)
  starting transfers between devices  35.2 us (24%)
  waiting for transfers between devices  16.1 us (11%)
  Pallas kernels  9.58 us (6%)
  local copies, waits for them, and re-layouts  1.74 us (1%)
    all_to_all x2, blocking collectives, over_z(): mine = lax.all_to_all(mine.astype(jnp.float16), Z, 0, 0, tiled=True)  30.9 us
    ppermute x17, starting transfers between devices, from_ahead(): lax.ppermute(value, axis, [((i + steps) % length, i) for i in range(lengt...  26 us
    all_to_all x1, blocking collectives, shards(): lax.all_to_all(message, ROW, 0, 0, tiled=True)  17.5 us
    ppermute x17, waiting for transfers between devices, from_ahead(): lax.ppermute(value, axis, [((i + steps) % length, i) for i in range(lengt...  16.1 us
    all_to_all x1, blocking collectives, shards(): lax.all_to_all(hb_cols, COL, 0, 0, tiled=True).reshape(group, rank)  13.3 us
    all_to_all x1, blocking collectives, shards(): gathered = lax.all_to_all(message, COL, 0, 0, tiled=True)  12 us
    all_to_all x1, blocking collectives, sent_to_all(): return lax.all_to_all(copies, axes, split_axis=0, concat_axis=0, tiled=True)  10.7 us
    pallas_call x10, Pallas kernels, call(): pl.pallas_call(kernel, out_shape=outs, in_specs=[pl.BlockSpec(memory_spac...  9.58 us
  transfers between devices with their start and end apart: 18, of which 6 were waited for; matrix products, arithmetic and copies ran while one was open for 0% of the time, Pallas kernels for 2%

profile of v12, /device:TPU:1, one launch (start us, length us, event | category | flops | bytes accessed | tf_op | source)
XLA Modules:
  0.0 148.4 jit_solution(9560878623863085339)
XLA Ops:
  0.0 2.0 %shard_map.28 = (bf16[32,1280]{1,0:T(8,128)(2,1)}, bf16[32,1280]{1,0:T(8,128)(2,1)}, bf16[8,64,1024]{2,1,0:T(8,128)(2,1)}) custom-call(bf16[64,1024]{1,0:T(8,128)(2,1)} %points.1, f32[64,256]{1,0:T(8,128)} %h_ref.1), custom_call_target="tpu_custom_call" | custom-call | flops 1 | bytes 1409024 | tf_op jit(solution)/shard_map/pallas_call | solution.py:37
  2.1 9.2 %all-to-all-start = ((bf16[8,64,1024]{2,1,0:T(8,128)(2,1)}), bf16[8,64,1024]{2,1,0:T(8,128)(2,1)S(1)}, u32[]{:S(2)}, u32[]{:S(2)}) async-start(bf16[8,64,1024]{2,1,0:T(8,128)(2,1)} %get-tuple-element.59), calls=%async_computation | async-start | bytes 2097152 | tf_op jit(solution)/shard_map/all_to_all | solution.py:269
  11.2 1.3 collective-permute-start.2
  12.5 2.5 %collective-permute-start.1 = (bf16[32,1280]{1,0:T(8,128)(2,1)S(1)}, bf16[32,1280]{1,0:T(8,128)(2,1)S(1)}, u32[]{:S(2)}, u32[]{:S(2)}) collective-permute-start(bf16[32,1280]{1,0:T(8,128)(2,1)S(1)} %copy-done), channel_id=1, source_target_pairs={{2,0},{3,1},{0,2},{1,3},{6,4},{7,5},{4,6},{5,7},{10,8},{11,9},{8,1... | collective-permute-start | bytes 245768 | tf_op jit(solution)/shard_map/ppermute | solution.py:21
  15.0 1.2 collective-permute-start
  16.1 1.3 collective-permute-start.5
  17.4 2.6 %collective-permute-start.4 = (bf16[32,1280]{1,0:T(8,128)(2,1)S(1)}, bf16[32,1280]{1,0:T(8,128)(2,1)S(1)}, u32[]{:S(2)}, u32[]{:S(2)}) collective-permute-start(bf16[32,1280]{1,0:T(8,128)(2,1)S(1)} %copy-done.1), channel_id=1, source_target_pairs={{8,0},{12,4},{0,8},{4,12},{9,1},{13,5},{1,9},{5,13},{10,2},{14,6},... | collective-permute-start | bytes 245768 | tf_op jit(solution)/shard_map/ppermute | solution.py:21
  20.0 1.1 collective-permute-start.3
  21.1 1.9 %collective-permute-done.4.by2 = bf16[32,1280]{1,0:T(8,128)(2,1)S(1)} collective-permute-done((bf16[32,1280]{1,0:T(8,128)(2,1)S(1)}, bf16[32,1280]{1,0:T(8,128)(2,1)S(1)}, u32[]{:S(2)}, u32[]{:S(2)}) %collective-permute-start.4) | collective-permute-done | bytes 81952 | tf_op jit(solution)/shard_map/ppermute | solution.py:21
  23.0 1.2 collective-permute-done.3.by1
  24.6 1.5 collective-permute-start.11
  26.8 2.5 %collective-permute-start.9 = (bf16[4,32,1280]{2,1,0:T(8,128)(2,1)S(1)}, bf16[4,32,1280]{2,1,0:T(8,128)(2,1)S(1)}, u32[]{:S(2)}, u32[]{:S(2)}) collective-permute-start(bf16[4,32,1280]{2,1,0:T(8,128)(2,1)S(1)} %get-tuple-element.56), channel_id=1, source_target_pairs={{1,0},{2,1},{3,2},{0,3},{5,4},{6,5},{7,6},{4,7},{9,8},{10,9},{11,1... | collective-permute-start | bytes 983048 | tf_op jit(solution)/shard_map/ppermute | solution.py:21
  29.2 3.2 %collective-permute-done.6.x2 = bf16[4,32,1280]{2,1,0:T(8,128)(2,1)S(1)} collective-permute-done((bf16[4,32,1280]{2,1,0:T(8,128)(2,1)S(1)}, bf16[4,32,1280]{2,1,0:T(8,128)(2,1)S(1)}, u32[]{:S(2)}, u32[]{:S(2)}) %collective-permute-start.6) | collective-permute-done | bytes 327712 | tf_op jit(solution)/shard_map/ppermute | solution.py:21
  32.8 8.0 %collective-permute-done.10.y1 = bf16[4,32,1280]{2,1,0:T(8,128)(2,1)S(1)} collective-permute-done((bf16[4,32,1280]{2,1,0:T(8,128)(2,1)S(1)}, bf16[4,32,1280]{2,1,0:T(8,128)(2,1)S(1)}, u32[]{:S(2)}, u32[]{:S(2)}) %collective-permute-start.10) | collective-permute-done | bytes 327712 | tf_op jit(solution)/shard_map/ppermute | solution.py:21
  40.8 0.7 copy-done.2
  41.5 7.3 %collective-permute-start.12 = (bf16[512,1024]{1,0:T(8,128)(2,1)S(1)}, bf16[512,1024]{1,0:T(8,128)(2,1)S(1)}, u32[]{:S(2)}, u32[]{:S(2)}) collective-permute-start(bf16[512,1024]{1,0:T(8,128)(2,1)S(1)} %bitcast.27), channel_id=1, source_target_pairs={{16,0},{0,16},{17,1},{1,17},{18,2},{2,18},{19,3},{3,19},{20,4},{4,... | collective-permute-start | bytes 3145736 | tf_op jit(solution)/shard_map/ppermute | solution.py:21
  48.8 1.0 copy-done.3
  49.8 0.7 shard_map.29
  50.8 1.7 %shard_map.30 = (f32[512,1024]{1,0:T(8,128)S(1)}, f32[4,128]{1,0:T(4,128)S(1)}) custom-call(bf16[512,1024]{1,0:T(8,128)(2,1)S(1)} %bitcast.28, bf16[1024,1024]{1,0:T(8,128)(2,1)S(1)} %get-tuple-element.67.cols, f32[8,128]{1,0:T(8,128)S(1)} %get-tuple-element.68.sq), custom_call_target="tpu_custom_call" | custom-call | flops 1073741824 | bytes 5249024 | tf_op jit(solution)/shard_map/pallas_call | solution.py:37
  52.5 1.7 %shard_map.31 = (f32[512,1024]{1,0:T(8,128)S(1)}, f32[16,24,128]{2,1,0:T(8,128)S(1)}) custom-call(bf16[512,1024]{1,0:T(8,128)(2,1)S(1)} %collective-permute-done.12.rows_ref, bf16[1024,1024]{1,0:T(8,128)(2,1)S(1)} %get-tuple-element.67.cols, f32[8,128]{1,0:T(8,128)S(1)} %get-tuple-element.68.sq, f32[4,128]{1,0:T(4,128)S(1)} %get-tuple-element.70.own_sums, ...), custom_call_target="tpu_custom_call" | custom-call | flops 1073741824 | bytes 5478400 | tf_op jit(solution)/shard_map/pallas_call | solution.py:37
  54.2 17.5 %all_to_all.35.got = f32[16,24,128]{2,1,0:T(8,128)S(1)} all-to-all(f32[16,24,128]{2,1,0:T(8,128)S(1)} %get-tuple-element.72), channel_id=1, replica_groups=mesh['row_0'=8,'row_1'=2,'col_0'=4,'col_1'=4] {'row_0','row_1'}, dimensions={0} | all-to-all | bytes 393216 | tf_op jit(solution)/shard_map/all_to_all | solution.py:318
  71.9 12.0 %all_to_all.36.got = f32[16,40,128]{2,1,0:T(8,128)S(1)} all-to-all(f32[16,40,128]{2,1,0:T(8,128)S(1)} %get-tuple-element.74), channel_id=1, replica_groups=mesh['row_0'=8,'row_1'=2,'col_0'=4,'col_1'=4] {'col_0','col_1'}, dimensions={0} | all-to-all | bytes 655360 | tf_op jit(solution)/shard_map/all_to_all | solution.py:321
  83.9 0.8 shard_map.34
  84.8 1.2 collective-permute-start.14
  85.9 0.9 shard_map.33
  87.6 14.8 %all_to_all.37 = f16[8,64,256]{2,1,0:T(8,128)(2,1)S(1)} all-to-all(f16[8,64,256]{2,1,0:T(8,128)(2,1)S(1)} %bitcast.38), channel_id=1, replica_groups=mesh['row_0'=8,'row_1'=2,'col_0'=4,'col_1'=4] {'row_0'}, dimensions={0} | all-to-all | bytes 524288 | tf_op jit(solution)/shard_map/all_to_all | solution.py:339
  102.7 13.3 %all_to_all.38 = bf16[16,64,256]{2,1,0:T(8,128)(2,1)S(1)} all-to-all(bf16[16,64,256]{2,1,0:T(8,128)(2,1)S(1)} %get-tuple-element.82), channel_id=1, replica_groups=mesh['row_0'=8,'row_1'=2,'col_0'=4,'col_1'=4] {'col_0','col_1'}, dimensions={0} | all-to-all | bytes 1048576 | tf_op jit(solution)/shard_map/all_to_all | solution.py:351
  116.4 2.0 %collective-permute-start.15 = (f32[512,256]{1,0:T(8,128)S(1)}, f32[512,256]{1,0:T(8,128)S(1)}, u32[]{:S(2)}, u32[]{:S(2)}) collective-permute-start(f32[512,256]{1,0:T(8,128)S(1)} %fusion.3), channel_id=1, source_target_pairs={{16,0},{0,16},{17,1},{1,17},{18,2},{2,18},{19,3},{3,19},{20,4},{4,... | collective-permute-start | bytes 1572872 | tf_op jit(solution)/shard_map/ppermute | solution.py:21
  118.9 1.2 collective-permute-done.16
  120.6 16.1 %all_to_all.39 = f16[8,80,256]{2,1,0:T(8,128)(2,1)S(1)} all-to-all(f16[8,80,256]{2,1,0:T(8,128)(2,1)S(1)} %pad_maximum_fusion.2), channel_id=1, replica_groups=mesh['row_0'=8,'row_1'=2,'col_0'=4,'col_1'=4] {'row_0'}, dimensions={0} | all-to-all | bytes 655360 | tf_op jit(solution)/shard_map/all_to_all | solution.py:339
  136.9 10.7 %all_to_all.40 = f32[16,16,256]{2,1,0:T(8,128)S(1)} all-to-all(f32[16,16,256]{2,1,0:T(8,128)S(1)} %broadcast_in_dim.7), channel_id=1, replica_groups=mesh['row_0'=8,'row_1'=2,'col_0'=4,'col_1'=4] {'col_0','col_1'}, dimensions={0} | all-to-all | bytes 524288 | tf_op jit(solution)/shard_map/all_to_all | solution.py:27
  147.5 0.9 shard_map.37
  (44 shorter events, 4.5 us)
Async XLA Ops:
  2.0 9.2 %copy-start = (bf16[32,1280]{1,0:T(8,128)(2,1)S(1)}, bf16[32,1280]{1,0:T(8,128)(2,1)}, u32[]{:S(2)}) copy-start(bf16[32,1280]{1,0:T(8,128)(2,1)} %get-tuple-element.46.ax0) | copy-start | bytes 245764
  2.0 14.1 %copy-start.1 = (bf16[32,1280]{1,0:T(8,128)(2,1)S(1)}, bf16[32,1280]{1,0:T(8,128)(2,1)}, u32[]{:S(2)}) copy-start(bf16[32,1280]{1,0:T(8,128)(2,1)} %get-tuple-element.47.by0) | copy-start | bytes 245764
  2.1 39.4 %all-to-all-start = ((bf16[8,64,1024]{2,1,0:T(8,128)(2,1)}), bf16[8,64,1024]{2,1,0:T(8,128)(2,1)S(1)}, u32[]{:S(2)}, u32[]{:S(2)}) async-start(bf16[8,64,1024]{2,1,0:T(8,128)(2,1)} %get-tuple-element.59), calls=%async_computation | async-start | bytes 2097152 | tf_op jit(solution)/shard_map/all_to_all | solution.py:269
  11.2 8.8 %collective-permute-start.2 = (bf16[32,1280]{1,0:T(8,128)(2,1)S(1)}, bf16[32,1280]{1,0:T(8,128)(2,1)S(1)}, u32[]{:S(2)}, u32[]{:S(2)}) collective-permute-start(bf16[32,1280]{1,0:T(8,128)(2,1)S(1)} %copy-done), channel_id=1, source_target_pairs={{3,0},{0,1},{1,2},{2,3},{7,4},{4,5},{5,6},{6,7},{11,8},{8,9},{9,10... | collective-permute-start | bytes 245768 | tf_op jit(solution)/shard_map/ppermute | solution.py:21
  12.5 8.6 %collective-permute-start.1 = (bf16[32,1280]{1,0:T(8,128)(2,1)S(1)}, bf16[32,1280]{1,0:T(8,128)(2,1)S(1)}, u32[]{:S(2)}, u32[]{:S(2)}) collective-permute-start(bf16[32,1280]{1,0:T(8,128)(2,1)S(1)} %copy-done), channel_id=1, source_target_pairs={{2,0},{3,1},{0,2},{1,3},{6,4},{7,5},{4,6},{5,7},{10,8},{11,9},{8,1... | collective-permute-start | bytes 245768 | tf_op jit(solution)/shard_map/ppermute | solution.py:21
  15.0 6.2 %collective-permute-start = (bf16[32,1280]{1,0:T(8,128)(2,1)S(1)}, bf16[32,1280]{1,0:T(8,128)(2,1)S(1)}, u32[]{:S(2)}, u32[]{:S(2)}) collective-permute-start(bf16[32,1280]{1,0:T(8,128)(2,1)S(1)} %copy-done), channel_id=1, source_target_pairs={{1,0},{2,1},{3,2},{0,3},{5,4},{6,5},{7,6},{4,7},{9,8},{10,9},{11,1... | collective-permute-start | bytes 245768 | tf_op jit(solution)/shard_map/ppermute | solution.py:21
  16.1 5.0 %collective-permute-start.5 = (bf16[32,1280]{1,0:T(8,128)(2,1)S(1)}, bf16[32,1280]{1,0:T(8,128)(2,1)S(1)}, u32[]{:S(2)}, u32[]{:S(2)}) collective-permute-start(bf16[32,1280]{1,0:T(8,128)(2,1)S(1)} %copy-done.1), channel_id=1, source_target_pairs={{12,0},{0,4},{4,8},{8,12},{13,1},{1,5},{5,9},{9,13},{14,2},{2,6},{... | collective-permute-start | bytes 245768 | tf_op jit(solution)/shard_map/ppermute | solution.py:21
  17.4 5.6 %collective-permute-start.4 = (bf16[32,1280]{1,0:T(8,128)(2,1)S(1)}, bf16[32,1280]{1,0:T(8,128)(2,1)S(1)}, u32[]{:S(2)}, u32[]{:S(2)}) collective-permute-start(bf16[32,1280]{1,0:T(8,128)(2,1)S(1)} %copy-done.1), channel_id=1, source_target_pairs={{8,0},{12,4},{0,8},{4,12},{9,1},{13,5},{1,9},{5,13},{10,2},{14,6},... | collective-permute-start | bytes 245768 | tf_op jit(solution)/shard_map/ppermute | solution.py:21
  20.0 4.1 %collective-permute-start.3 = (bf16[32,1280]{1,0:T(8,128)(2,1)S(1)}, bf16[32,1280]{1,0:T(8,128)(2,1)S(1)}, u32[]{:S(2)}, u32[]{:S(2)}) collective-permute-start(bf16[32,1280]{1,0:T(8,128)(2,1)S(1)} %copy-done.1), channel_id=1, source_target_pairs={{4,0},{8,4},{12,8},{0,12},{5,1},{9,5},{13,9},{1,13},{6,2},{10,6},{... | collective-permute-start | bytes 245768 | tf_op jit(solution)/shard_map/ppermute | solution.py:21
  24.3 8.1 %collective-permute-start.6 = (bf16[4,32,1280]{2,1,0:T(8,128)(2,1)S(1)}, bf16[4,32,1280]{2,1,0:T(8,128)(2,1)S(1)}, u32[]{:S(2)}, u32[]{:S(2)}) collective-permute-start(bf16[4,32,1280]{2,1,0:T(8,128)(2,1)S(1)} %get-tuple-element.56), channel_id=1, source_target_pairs={{2,0},{3,1},{0,2},{1,3},{6,4},{7,5},{4,6},{5,7},{10,8},{11,9},{8,1... | collective-permute-start | bytes 983048 | tf_op jit(solution)/shard_map/ppermute | solution.py:21
  24.6 8.2 %collective-permute-start.11 = (bf16[4,32,1280]{2,1,0:T(8,128)(2,1)S(1)}, bf16[4,32,1280]{2,1,0:T(8,128)(2,1)S(1)}, u32[]{:S(2)}, u32[]{:S(2)}) collective-permute-start(bf16[4,32,1280]{2,1,0:T(8,128)(2,1)S(1)} %get-tuple-element.57), channel_id=1, source_target_pairs={{8,0},{12,4},{0,8},{4,12},{9,1},{13,5},{1,9},{5,13},{10,2},{14,6},... | collective-permute-start | bytes 983048 | tf_op jit(solution)/shard_map/ppermute | solution.py:21
  26.0 14.7 %collective-permute-start.10 = (bf16[4,32,1280]{2,1,0:T(8,128)(2,1)S(1)}, bf16[4,32,1280]{2,1,0:T(8,128)(2,1)S(1)}, u32[]{:S(2)}, u32[]{:S(2)}) collective-permute-start(bf16[4,32,1280]{2,1,0:T(8,128)(2,1)S(1)} %get-tuple-element.57), channel_id=1, source_target_pairs={{4,0},{8,4},{12,8},{0,12},{5,1},{9,5},{13,9},{1,13},{6,2},{10,6},{... | collective-permute-start | bytes 983048 | tf_op jit(solution)/shard_map/ppermute | solution.py:21
  26.8 14.0 %collective-permute-start.9 = (bf16[4,32,1280]{2,1,0:T(8,128)(2,1)S(1)}, bf16[4,32,1280]{2,1,0:T(8,128)(2,1)S(1)}, u32[]{:S(2)}, u32[]{:S(2)}) collective-permute-start(bf16[4,32,1280]{2,1,0:T(8,128)(2,1)S(1)} %get-tuple-element.56), channel_id=1, source_target_pairs={{1,0},{2,1},{3,2},{0,3},{5,4},{6,5},{7,6},{4,7},{9,8},{10,9},{11,1... | collective-permute-start | bytes 983048 | tf_op jit(solution)/shard_map/ppermute | solution.py:21
  32.4 8.4 %collective-permute-start.7 = (bf16[4,32,1280]{2,1,0:T(8,128)(2,1)S(1)}, bf16[4,32,1280]{2,1,0:T(8,128)(2,1)S(1)}, u32[]{:S(2)}, u32[]{:S(2)}) collective-permute-start(bf16[4,32,1280]{2,1,0:T(8,128)(2,1)S(1)} %get-tuple-element.56), channel_id=1, source_target_pairs={{3,0},{0,1},{1,2},{2,3},{7,4},{4,5},{5,6},{6,7},{11,8},{8,9},{9,10... | collective-permute-start | bytes 983048 | tf_op jit(solution)/shard_map/ppermute | solution.py:21
  32.8 8.0 %collective-permute-start.8 = (bf16[4,32,1280]{2,1,0:T(8,128)(2,1)S(1)}, bf16[4,32,1280]{2,1,0:T(8,128)(2,1)S(1)}, u32[]{:S(2)}, u32[]{:S(2)}) collective-permute-start(bf16[4,32,1280]{2,1,0:T(8,128)(2,1)S(1)} %get-tuple-element.57), channel_id=1, source_target_pairs={{12,0},{0,4},{4,8},{8,12},{13,1},{1,5},{5,9},{9,13},{14,2},{2,6},{... | collective-permute-start | bytes 983048 | tf_op jit(solution)/shard_map/ppermute | solution.py:21
  40.8 0.7 copy-start.2
  41.5 11.0 %collective-permute-start.12 = (bf16[512,1024]{1,0:T(8,128)(2,1)S(1)}, bf16[512,1024]{1,0:T(8,128)(2,1)S(1)}, u32[]{:S(2)}, u32[]{:S(2)}) collective-permute-start(bf16[512,1024]{1,0:T(8,128)(2,1)S(1)} %bitcast.27), channel_id=1, source_target_pairs={{16,0},{0,16},{17,1},{1,17},{18,2},{2,18},{19,3},{3,19},{20,4},{4,... | collective-permute-start | bytes 3145736 | tf_op jit(solution)/shard_map/ppermute | solution.py:21
  48.8 1.0 copy-start.3
  50.5 2.0 %collective-permute-start.13 = (f32[16,256]{1,0:T(8,128)S(1)}, f32[16,256]{1,0:T(8,128)S(1)}, u32[]{:S(2)}, u32[]{:S(2)}) collective-permute-start(f32[16,256]{1,0:T(8,128)S(1)} %get-tuple-element.71.part), channel_id=1, source_target_pairs={{16,0},{0,16},{17,1},{1,17},{18,2},{2,18},{19,3},{3,19},{20,4},{4,... | collective-permute-start | bytes 49160 | tf_op jit(solution)/shard_map/ppermute | solution.py:21
  84.8 2.7 %collective-permute-start.14 = (f32[512,256]{1,0:T(8,128)S(1)}, f32[512,256]{1,0:T(8,128)S(1)}, u32[]{:S(2)}, u32[]{:S(2)}) collective-permute-start(f32[512,256]{1,0:T(8,128)S(1)} %get-tuple-element.79), channel_id=1, source_target_pairs={{16,0},{0,16},{17,1},{1,17},{18,2},{2,18},{19,3},{3,19},{20,4},{4,... | collective-permute-start | bytes 1572872 | tf_op jit(solution)/shard_map/ppermute | solution.py:21
  85.9 16.5 %copy-start.4 = (f32[64,256]{1,0:T(8,128)S(1)}, f32[64,256]{1,0:T(8,128)}, u32[]{:S(2)}) copy-start(f32[64,256]{1,0:T(8,128)} %h_ref.1) | copy-start | bytes 196612
  116.4 3.6 %collective-permute-start.15 = (f32[512,256]{1,0:T(8,128)S(1)}, f32[512,256]{1,0:T(8,128)S(1)}, u32[]{:S(2)}, u32[]{:S(2)}) collective-permute-start(f32[512,256]{1,0:T(8,128)S(1)} %fusion.3), channel_id=1, source_target_pairs={{16,0},{0,16},{17,1},{1,17},{18,2},{2,18},{19,3},{3,19},{20,4},{4,... | collective-permute-start | bytes 1572872 | tf_op jit(solution)/shard_map/ppermute | solution.py:21
  118.8 1.3 collective-permute-start.16

commit v13 on v12

--- a/solution.py
+++ b/solution.py
@@ -267,9 +267,10 @@
     )
     tie = lax.optimization_barrier
     along_z = lax.all_to_all(copies, Z, 0, 0, tiled=True)
-    x1, x3 = from_ahead(first, X, 1), from_ahead(first, X, -1)
-    y1, y3 = from_ahead(second, Y, 1), from_ahead(second, Y, -1)
-    x2, y2 = from_ahead(first, X, 2), from_ahead(second, Y, 2)
+    y1, x1 = from_ahead(second, Y, 1), from_ahead(first, X, 1)
+    y2, x2 = from_ahead(second, Y, 2), from_ahead(first, X, 2)
+    ahead, behind, x2 = tie((first, second, x2))
+    y3, x3 = from_ahead(behind, Y, -1), from_ahead(ahead, X, -1)
     x1, x2, x3, y1, y2, y3 = tie((x1, x2, x3, y1, y2, y3))
     by_x = jnp.stack([first, x1, x2, x3])
     by_y = jnp.stack([second, y1, y2, y3])

time: 149 us -> 150 us (level)
  transfers between devices with their start and end apart: 18 -> 18, of which waited for: 6 -> 9; matrix products, arithmetic and copies ran while one was open for 0% -> 0% of each run, Pallas kernels for 2% -> 2%
where the time goes in v13:
time: 150 us
  blocking collectives  85.7 us (57%)
  starting transfers between devices  35.3 us (24%)
  waiting for transfers between devices  16.1 us (11%)
  Pallas kernels  9.58 us (6%)
  local copies, waits for them, and re-layouts  1.75 us (1%)
    all_to_all x2, blocking collectives, over_z(): mine = lax.all_to_all(mine.astype(jnp.float16), Z, 0, 0, tiled=True)  30.9 us
    ppermute x17, starting transfers between devices, from_ahead(): lax.ppermute(value, axis, [((i + steps) % length, i) for i in range(lengt...  26.1 us
    all_to_all x1, blocking collectives, shards(): lax.all_to_all(message, ROW, 0, 0, tiled=True)  17.5 us
    ppermute x17, waiting for transfers between devices, from_ahead(): lax.ppermute(value, axis, [((i + steps) % length, i) for i in range(lengt...  16.1 us
    all_to_all x1, blocking collectives, shards(): gathered = lax.all_to_all(message, COL, 0, 0, tiled=True)  13.4 us
    all_to_all x1, blocking collectives, shards(): lax.all_to_all(hb_cols, COL, 0, 0, tiled=True).reshape(group, rank)  13.3 us
    all_to_all x1, blocking collectives, sent_to_all(): return lax.all_to_all(copies, axes, split_axis=0, concat_axis=0, tiled=True)  10.7 us
    pallas_call x10, Pallas kernels, call(): pl.pallas_call(kernel, out_shape=outs, in_specs=[pl.BlockSpec(memory_spac...  9.58 us
  transfers between devices with their start and end apart: 18, of which 9 were waited for; matrix products, arithmetic and copies ran while one was open for 0% of the time, Pallas kernels for 2%

profile of v13, /device:TPU:1, one launch (start us, length us, event | category | flops | bytes accessed | tf_op | source)
XLA Modules:
  0.0 149.9 jit_solution(15665272287790379490)
XLA Ops:
  0.0 2.0 %shard_map.28 = (bf16[32,1280]{1,0:T(8,128)(2,1)}, bf16[32,1280]{1,0:T(8,128)(2,1)}, bf16[8,64,1024]{2,1,0:T(8,128)(2,1)}) custom-call(bf16[64,1024]{1,0:T(8,128)(2,1)} %points.1, f32[64,256]{1,0:T(8,128)} %h_ref.1), custom_call_target="tpu_custom_call" | custom-call | flops 1 | bytes 1409024 | tf_op jit(solution)/shard_map/pallas_call | solution.py:37
  2.1 9.2 %all-to-all-start = ((bf16[8,64,1024]{2,1,0:T(8,128)(2,1)}), bf16[8,64,1024]{2,1,0:T(8,128)(2,1)S(1)}, u32[]{:S(2)}, u32[]{:S(2)}) async-start(bf16[8,64,1024]{2,1,0:T(8,128)(2,1)} %get-tuple-element.65), calls=%async_computation | async-start | bytes 2097152 | tf_op jit(solution)/shard_map/all_to_all | solution.py:269
  11.2 2.8 %collective-permute-start.1 = (bf16[32,1280]{1,0:T(8,128)(2,1)S(1)}, bf16[32,1280]{1,0:T(8,128)(2,1)S(1)}, u32[]{:S(2)}, u32[]{:S(2)}) collective-permute-start(bf16[32,1280]{1,0:T(8,128)(2,1)S(1)} %copy-done), channel_id=1, source_target_pairs={{2,0},{3,1},{0,2},{1,3},{6,4},{7,5},{4,6},{5,7},{10,8},{11,9},{8,1... | collective-permute-start | bytes 245768 | tf_op jit(solution)/shard_map/ppermute | solution.py:21
  14.1 0.9 collective-permute-start
  14.9 2.9 %collective-permute-start.4 = (bf16[32,1280]{1,0:T(8,128)(2,1)S(1)}, bf16[32,1280]{1,0:T(8,128)(2,1)S(1)}, u32[]{:S(2)}, u32[]{:S(2)}) collective-permute-start(bf16[32,1280]{1,0:T(8,128)(2,1)S(1)} %copy-done.1), channel_id=1, source_target_pairs={{8,0},{12,4},{0,8},{4,12},{9,1},{13,5},{1,9},{5,13},{10,2},{14,6},... | collective-permute-start | bytes 245768 | tf_op jit(solution)/shard_map/ppermute | solution.py:21
  17.8 0.8 collective-permute-start.3
  20.0 1.4 collective-permute-done.3.by1
  21.4 2.0 %collective-permute-done.2.ax3 = bf16[32,1280]{1,0:T(8,128)(2,1)S(1)} collective-permute-done((bf16[32,1280]{1,0:T(8,128)(2,1)S(1)}, bf16[32,1280]{1,0:T(8,128)(2,1)S(1)}, u32[]{:S(2)}, u32[]{:S(2)}) %collective-permute-start.2) | collective-permute-done | bytes 81952 | tf_op jit(solution)/shard_map/ppermute | solution.py:21
  24.1 0.7 collective-permute-start.6
  24.8 2.4 %collective-permute-start.11 = (bf16[4,32,1280]{2,1,0:T(8,128)(2,1)S(1)}, bf16[4,32,1280]{2,1,0:T(8,128)(2,1)S(1)}, u32[]{:S(2)}, u32[]{:S(2)}) collective-permute-start(bf16[4,32,1280]{2,1,0:T(8,128)(2,1)S(1)} %get-tuple-element.63), channel_id=1, source_target_pairs={{8,0},{12,4},{0,8},{4,12},{9,1},{13,5},{1,9},{5,13},{10,2},{14,6},... | collective-permute-start | bytes 983048 | tf_op jit(solution)/shard_map/ppermute | solution.py:21
  27.2 0.8 collective-permute-start.10
  28.1 1.4 collective-permute-start.9
  29.4 2.3 %collective-permute-done.6.x2 = bf16[4,32,1280]{2,1,0:T(8,128)(2,1)S(1)} collective-permute-done((bf16[4,32,1280]{2,1,0:T(8,128)(2,1)S(1)}, bf16[4,32,1280]{2,1,0:T(8,128)(2,1)S(1)}, u32[]{:S(2)}, u32[]{:S(2)}) %collective-permute-start.6) | collective-permute-done | bytes 327712 | tf_op jit(solution)/shard_map/ppermute | solution.py:21
  32.9 6.6 %collective-permute-done.10.y1 = bf16[4,32,1280]{2,1,0:T(8,128)(2,1)S(1)} collective-permute-done((bf16[4,32,1280]{2,1,0:T(8,128)(2,1)S(1)}, bf16[4,32,1280]{2,1,0:T(8,128)(2,1)S(1)}, u32[]{:S(2)}, u32[]{:S(2)}) %collective-permute-start.10) | collective-permute-done | bytes 327712 | tf_op jit(solution)/shard_map/ppermute | solution.py:21
  39.4 1.3 collective-permute-done.8.y3
  41.5 7.5 %collective-permute-start.12 = (bf16[512,1024]{1,0:T(8,128)(2,1)S(1)}, bf16[512,1024]{1,0:T(8,128)(2,1)S(1)}, u32[]{:S(2)}, u32[]{:S(2)}) collective-permute-start(bf16[512,1024]{1,0:T(8,128)(2,1)S(1)} %bitcast.27), channel_id=1, source_target_pairs={{16,0},{0,16},{17,1},{1,17},{18,2},{2,18},{19,3},{3,19},{20,4},{4,... | collective-permute-start | bytes 3145736 | tf_op jit(solution)/shard_map/ppermute | solution.py:21
  49.0 1.0 copy-done.3
  49.9 0.7 shard_map.29
  50.9 1.7 %shard_map.30 = (f32[512,1024]{1,0:T(8,128)S(1)}, f32[4,128]{1,0:T(4,128)S(1)}) custom-call(bf16[512,1024]{1,0:T(8,128)(2,1)S(1)} %bitcast.28, bf16[1024,1024]{1,0:T(8,128)(2,1)S(1)} %get-tuple-element.73.cols, f32[8,128]{1,0:T(8,128)S(1)} %get-tuple-element.74.sq), custom_call_target="tpu_custom_call" | custom-call | flops 1073741824 | bytes 5249024 | tf_op jit(solution)/shard_map/pallas_call | solution.py:37
  52.7 1.7 %shard_map.31 = (f32[512,1024]{1,0:T(8,128)S(1)}, f32[16,24,128]{2,1,0:T(8,128)S(1)}) custom-call(bf16[512,1024]{1,0:T(8,128)(2,1)S(1)} %collective-permute-done.12.rows_ref, bf16[1024,1024]{1,0:T(8,128)(2,1)S(1)} %get-tuple-element.73.cols, f32[8,128]{1,0:T(8,128)S(1)} %get-tuple-element.74.sq, f32[4,128]{1,0:T(4,128)S(1)} %get-tuple-element.76.own_sums, ...), custom_call_target="tpu_custom_call" | custom-call | flops 1073741824 | bytes 5478400 | tf_op jit(solution)/shard_map/pallas_call | solution.py:37
  54.4 17.5 %all_to_all.35.got = f32[16,24,128]{2,1,0:T(8,128)S(1)} all-to-all(f32[16,24,128]{2,1,0:T(8,128)S(1)} %get-tuple-element.78), channel_id=1, replica_groups=mesh['row_0'=8,'row_1'=2,'col_0'=4,'col_1'=4] {'row_0','row_1'}, dimensions={0} | all-to-all | bytes 393216 | tf_op jit(solution)/shard_map/all_to_all | solution.py:319
  72.0 13.4 %all_to_all.36.got = f32[16,40,128]{2,1,0:T(8,128)S(1)} all-to-all(f32[16,40,128]{2,1,0:T(8,128)S(1)} %get-tuple-element.80), channel_id=1, replica_groups=mesh['row_0'=8,'row_1'=2,'col_0'=4,'col_1'=4] {'col_0','col_1'}, dimensions={0} | all-to-all | bytes 655360 | tf_op jit(solution)/shard_map/all_to_all | solution.py:322
  85.4 0.8 shard_map.34
  86.3 1.2 collective-permute-start.14
  87.4 0.9 shard_map.33
  89.1 14.8 %all_to_all.37 = f16[8,64,256]{2,1,0:T(8,128)(2,1)S(1)} all-to-all(f16[8,64,256]{2,1,0:T(8,128)(2,1)S(1)} %bitcast.38), channel_id=1, replica_groups=mesh['row_0'=8,'row_1'=2,'col_0'=4,'col_1'=4] {'row_0'}, dimensions={0} | all-to-all | bytes 524288 | tf_op jit(solution)/shard_map/all_to_all | solution.py:340
  104.2 13.3 %all_to_all.38 = bf16[16,64,256]{2,1,0:T(8,128)(2,1)S(1)} all-to-all(bf16[16,64,256]{2,1,0:T(8,128)(2,1)S(1)} %get-tuple-element.88), channel_id=1, replica_groups=mesh['row_0'=8,'row_1'=2,'col_0'=4,'col_1'=4] {'col_0','col_1'}, dimensions={0} | all-to-all | bytes 1048576 | tf_op jit(solution)/shard_map/all_to_all | solution.py:352
  117.9 2.0 %collective-permute-start.15 = (f32[512,256]{1,0:T(8,128)S(1)}, f32[512,256]{1,0:T(8,128)S(1)}, u32[]{:S(2)}, u32[]{:S(2)}) collective-permute-start(f32[512,256]{1,0:T(8,128)S(1)} %fusion.3), channel_id=1, source_target_pairs={{16,0},{0,16},{17,1},{1,17},{18,2},{2,18},{19,3},{3,19},{20,4},{4,... | collective-permute-start | bytes 1572872 | tf_op jit(solution)/shard_map/ppermute | solution.py:21
  120.4 1.2 collective-permute-done.16
  122.1 16.1 %all_to_all.39 = f16[8,80,256]{2,1,0:T(8,128)(2,1)S(1)} all-to-all(f16[8,80,256]{2,1,0:T(8,128)(2,1)S(1)} %pad_maximum_fusion.2), channel_id=1, replica_groups=mesh['row_0'=8,'row_1'=2,'col_0'=4,'col_1'=4] {'row_0'}, dimensions={0} | all-to-all | bytes 655360 | tf_op jit(solution)/shard_map/all_to_all | solution.py:340
  138.3 10.7 %all_to_all.40 = f32[16,16,256]{2,1,0:T(8,128)S(1)} all-to-all(f32[16,16,256]{2,1,0:T(8,128)S(1)} %broadcast_in_dim.7), channel_id=1, replica_groups=mesh['row_0'=8,'row_1'=2,'col_0'=4,'col_1'=4] {'col_0','col_1'}, dimensions={0} | all-to-all | bytes 524288 | tf_op jit(solution)/shard_map/all_to_all | solution.py:27
  149.0 0.9 shard_map.37
  (44 shorter events, 7.0 us)
Async XLA Ops:
  2.0 9.2 %copy-start = (bf16[32,1280]{1,0:T(8,128)(2,1)S(1)}, bf16[32,1280]{1,0:T(8,128)(2,1)}, u32[]{:S(2)}) copy-start(bf16[32,1280]{1,0:T(8,128)(2,1)} %get-tuple-element.52.ax0) | copy-start | bytes 245764
  2.0 12.9 %copy-start.1 = (bf16[32,1280]{1,0:T(8,128)(2,1)S(1)}, bf16[32,1280]{1,0:T(8,128)(2,1)}, u32[]{:S(2)}) copy-start(bf16[32,1280]{1,0:T(8,128)(2,1)} %get-tuple-element.53.by0) | copy-start | bytes 245764
  2.1 39.4 %all-to-all-start = ((bf16[8,64,1024]{2,1,0:T(8,128)(2,1)}), bf16[8,64,1024]{2,1,0:T(8,128)(2,1)S(1)}, u32[]{:S(2)}, u32[]{:S(2)}) async-start(bf16[8,64,1024]{2,1,0:T(8,128)(2,1)} %get-tuple-element.65), calls=%async_computation | async-start | bytes 2097152 | tf_op jit(solution)/shard_map/all_to_all | solution.py:269
  11.2 7.4 %collective-permute-start.1 = (bf16[32,1280]{1,0:T(8,128)(2,1)S(1)}, bf16[32,1280]{1,0:T(8,128)(2,1)S(1)}, u32[]{:S(2)}, u32[]{:S(2)}) collective-permute-start(bf16[32,1280]{1,0:T(8,128)(2,1)S(1)} %copy-done), channel_id=1, source_target_pairs={{2,0},{3,1},{0,2},{1,3},{6,4},{7,5},{4,6},{5,7},{10,8},{11,9},{8,1... | collective-permute-start | bytes 245768 | tf_op jit(solution)/shard_map/ppermute | solution.py:21
  14.1 5.9 %collective-permute-start = (bf16[32,1280]{1,0:T(8,128)(2,1)S(1)}, bf16[32,1280]{1,0:T(8,128)(2,1)S(1)}, u32[]{:S(2)}, u32[]{:S(2)}) collective-permute-start(bf16[32,1280]{1,0:T(8,128)(2,1)S(1)} %copy-done), channel_id=1, source_target_pairs={{1,0},{2,1},{3,2},{0,3},{5,4},{6,5},{7,6},{4,7},{9,8},{10,9},{11,1... | collective-permute-start | bytes 245768 | tf_op jit(solution)/shard_map/ppermute | solution.py:21
  14.9 5.1 %collective-permute-start.4 = (bf16[32,1280]{1,0:T(8,128)(2,1)S(1)}, bf16[32,1280]{1,0:T(8,128)(2,1)S(1)}, u32[]{:S(2)}, u32[]{:S(2)}) collective-permute-start(bf16[32,1280]{1,0:T(8,128)(2,1)S(1)} %copy-done.1), channel_id=1, source_target_pairs={{8,0},{12,4},{0,8},{4,12},{9,1},{13,5},{1,9},{5,13},{10,2},{14,6},... | collective-permute-start | bytes 245768 | tf_op jit(solution)/shard_map/ppermute | solution.py:21
  17.8 3.6 %collective-permute-start.3 = (bf16[32,1280]{1,0:T(8,128)(2,1)S(1)}, bf16[32,1280]{1,0:T(8,128)(2,1)S(1)}, u32[]{:S(2)}, u32[]{:S(2)}) collective-permute-start(bf16[32,1280]{1,0:T(8,128)(2,1)S(1)} %copy-done.1), channel_id=1, source_target_pairs={{4,0},{8,4},{12,8},{0,12},{5,1},{9,5},{13,9},{1,13},{6,2},{10,6},{... | collective-permute-start | bytes 245768 | tf_op jit(solution)/shard_map/ppermute | solution.py:21
  18.6 4.8 %collective-permute-start.2 = (bf16[32,1280]{1,0:T(8,128)(2,1)S(1)}, bf16[32,1280]{1,0:T(8,128)(2,1)S(1)}, u32[]{:S(2)}, u32[]{:S(2)}) collective-permute-start(bf16[32,1280]{1,0:T(8,128)(2,1)S(1)} %copy-done), channel_id=1, source_target_pairs={{3,0},{0,1},{1,2},{2,3},{7,4},{4,5},{5,6},{6,7},{11,8},{8,9},{9,10... | collective-permute-start | bytes 245768 | tf_op jit(solution)/shard_map/ppermute | solution.py:21
  19.2 4.8 %collective-permute-start.5 = (bf16[32,1280]{1,0:T(8,128)(2,1)S(1)}, bf16[32,1280]{1,0:T(8,128)(2,1)S(1)}, u32[]{:S(2)}, u32[]{:S(2)}) collective-permute-start(bf16[32,1280]{1,0:T(8,128)(2,1)S(1)} %copy-done.1), channel_id=1, source_target_pairs={{12,0},{0,4},{4,8},{8,12},{13,1},{1,5},{5,9},{9,13},{14,2},{2,6},{... | collective-permute-start | bytes 245768 | tf_op jit(solution)/shard_map/ppermute | solution.py:21
  24.1 7.7 %collective-permute-start.6 = (bf16[4,32,1280]{2,1,0:T(8,128)(2,1)S(1)}, bf16[4,32,1280]{2,1,0:T(8,128)(2,1)S(1)}, u32[]{:S(2)}, u32[]{:S(2)}) collective-permute-start(bf16[4,32,1280]{2,1,0:T(8,128)(2,1)S(1)} %get-tuple-element.62), channel_id=1, source_target_pairs={{2,0},{3,1},{0,2},{1,3},{6,4},{7,5},{4,6},{5,7},{10,8},{11,9},{8,1... | collective-permute-start | bytes 983048 | tf_op jit(solution)/shard_map/ppermute | solution.py:21
  24.8 8.0 %collective-permute-start.11 = (bf16[4,32,1280]{2,1,0:T(8,128)(2,1)S(1)}, bf16[4,32,1280]{2,1,0:T(8,128)(2,1)S(1)}, u32[]{:S(2)}, u32[]{:S(2)}) collective-permute-start(bf16[4,32,1280]{2,1,0:T(8,128)(2,1)S(1)} %get-tuple-element.63), channel_id=1, source_target_pairs={{8,0},{12,4},{0,8},{4,12},{9,1},{13,5},{1,9},{5,13},{10,2},{14,6},... | collective-permute-start | bytes 983048 | tf_op jit(solution)/shard_map/ppermute | solution.py:21
  27.2 12.2 %collective-permute-start.10 = (bf16[4,32,1280]{2,1,0:T(8,128)(2,1)S(1)}, bf16[4,32,1280]{2,1,0:T(8,128)(2,1)S(1)}, u32[]{:S(2)}, u32[]{:S(2)}) collective-permute-start(bf16[4,32,1280]{2,1,0:T(8,128)(2,1)S(1)} %get-tuple-element.63), channel_id=1, source_target_pairs={{4,0},{8,4},{12,8},{0,12},{5,1},{9,5},{13,9},{1,13},{6,2},{10,6},{... | collective-permute-start | bytes 983048 | tf_op jit(solution)/shard_map/ppermute | solution.py:21
  28.1 11.3 %collective-permute-start.9 = (bf16[4,32,1280]{2,1,0:T(8,128)(2,1)S(1)}, bf16[4,32,1280]{2,1,0:T(8,128)(2,1)S(1)}, u32[]{:S(2)}, u32[]{:S(2)}) collective-permute-start(bf16[4,32,1280]{2,1,0:T(8,128)(2,1)S(1)} %get-tuple-element.62), channel_id=1, source_target_pairs={{1,0},{2,1},{3,2},{0,3},{5,4},{6,5},{7,6},{4,7},{9,8},{10,9},{11,1... | collective-permute-start | bytes 983048 | tf_op jit(solution)/shard_map/ppermute | solution.py:21
  31.8 7.7 %collective-permute-start.7 = (bf16[4,32,1280]{2,1,0:T(8,128)(2,1)S(1)}, bf16[4,32,1280]{2,1,0:T(8,128)(2,1)S(1)}, u32[]{:S(2)}, u32[]{:S(2)}) collective-permute-start(bf16[4,32,1280]{2,1,0:T(8,128)(2,1)S(1)} %get-tuple-element.62), channel_id=1, source_target_pairs={{3,0},{0,1},{1,2},{2,3},{7,4},{4,5},{5,6},{6,7},{11,8},{8,9},{9,10... | collective-permute-start | bytes 983048 | tf_op jit(solution)/shard_map/ppermute | solution.py:21
  32.2 8.5 %collective-permute-start.8 = (bf16[4,32,1280]{2,1,0:T(8,128)(2,1)S(1)}, bf16[4,32,1280]{2,1,0:T(8,128)(2,1)S(1)}, u32[]{:S(2)}, u32[]{:S(2)}) collective-permute-start(bf16[4,32,1280]{2,1,0:T(8,128)(2,1)S(1)} %get-tuple-element.63), channel_id=1, source_target_pairs={{12,0},{0,4},{4,8},{8,12},{13,1},{1,5},{5,9},{9,13},{14,2},{2,6},{... | collective-permute-start | bytes 983048 | tf_op jit(solution)/shard_map/ppermute | solution.py:21
  40.8 0.7 copy-start.2
  41.5 11.2 %collective-permute-start.12 = (bf16[512,1024]{1,0:T(8,128)(2,1)S(1)}, bf16[512,1024]{1,0:T(8,128)(2,1)S(1)}, u32[]{:S(2)}, u32[]{:S(2)}) collective-permute-start(bf16[512,1024]{1,0:T(8,128)(2,1)S(1)} %bitcast.27), channel_id=1, source_target_pairs={{16,0},{0,16},{17,1},{1,17},{18,2},{2,18},{19,3},{3,19},{20,4},{4,... | collective-permute-start | bytes 3145736 | tf_op jit(solution)/shard_map/ppermute | solution.py:21
  49.0 1.0 copy-start.3
  50.7 2.0 %collective-permute-start.13 = (f32[16,256]{1,0:T(8,128)S(1)}, f32[16,256]{1,0:T(8,128)S(1)}, u32[]{:S(2)}, u32[]{:S(2)}) collective-permute-start(f32[16,256]{1,0:T(8,128)S(1)} %get-tuple-element.77.part), channel_id=1, source_target_pairs={{16,0},{0,16},{17,1},{1,17},{18,2},{2,18},{19,3},{3,19},{20,4},{4,... | collective-permute-start | bytes 49160 | tf_op jit(solution)/shard_map/ppermute | solution.py:21
  86.3 2.7 %collective-permute-start.14 = (f32[512,256]{1,0:T(8,128)S(1)}, f32[512,256]{1,0:T(8,128)S(1)}, u32[]{:S(2)}, u32[]{:S(2)}) collective-permute-start(f32[512,256]{1,0:T(8,128)S(1)} %get-tuple-element.85), channel_id=1, source_target_pairs={{16,0},{0,16},{17,1},{1,17},{18,2},{2,18},{19,3},{3,19},{20,4},{4,... | collective-permute-start | bytes 1572872 | tf_op jit(solution)/shard_map/ppermute | solution.py:21
  87.4 16.5 %copy-start.4 = (f32[64,256]{1,0:T(8,128)S(1)}, f32[64,256]{1,0:T(8,128)}, u32[]{:S(2)}) copy-start(f32[64,256]{1,0:T(8,128)} %h_ref.1) | copy-start | bytes 196612
  117.9 3.6 %collective-permute-start.15 = (f32[512,256]{1,0:T(8,128)S(1)}, f32[512,256]{1,0:T(8,128)S(1)}, u32[]{:S(2)}, u32[]{:S(2)}) collective-permute-start(f32[512,256]{1,0:T(8,128)S(1)} %fusion.3), channel_id=1, source_target_pairs={{16,0},{0,16},{17,1},{1,17},{18,2},{2,18},{19,3},{3,19},{20,4},{4,... | collective-permute-start | bytes 1572872 | tf_op jit(solution)/shard_map/ppermute | solution.py:21
  120.3 1.3 collective-permute-start.16

commit v14 on v11

--- a/solution.py
+++ b/solution.py
@@ -274,9 +274,11 @@
     by_x = jnp.stack([first, x1, x2, x3])
     by_y = jnp.stack([second, y1, y2, y3])
     by_x, by_y = tie((by_x, by_y))
-    y_three, x_three = from_ahead(by_x, Y, 3), from_ahead(by_y, X, 3)
     y_one, x_one = from_ahead(by_x, Y, 1), from_ahead(by_y, X, 1)
     y_two, x_two = from_ahead(by_x, Y, 2), from_ahead(by_y, X, 2)
+    y_three = from_ahead(by_x, Y, 3)
+    by_y, x_two = tie((by_y, x_two))
+    x_three = from_ahead(by_y, X, 3)
     far = [x_three, y_three, x_one, y_one, x_two, y_two]
     far, along_z = tie((far, along_z.reshape(-1, width)))
     other = from_ahead(along_z, CORE, 1)

time: 149 us -> 148 us (level)
  no operation moved by 1% of the time
where the time goes in v14:
time: 148 us; the launch traced here: 147 us
  blocking collectives  85.5 us (58%)
  starting transfers between devices  30.8 us (21%)
  waiting for transfers between devices  18.1 us (12%)
  Pallas kernels  9.58 us (6%)
  local copies, waits for them, and re-layouts  1.75 us (1%)
    all_to_all x2, blocking collectives, over_z(): mine = lax.all_to_all(mine.astype(jnp.float16), Z, 0, 0, tiled=True)  30.9 us
    ppermute x17, starting transfers between devices, from_ahead(): lax.ppermute(value, axis, [((i + steps) % length, i) for i in range(lengt...  21.6 us
    ppermute x17, waiting for transfers between devices, from_ahead(): lax.ppermute(value, axis, [((i + steps) % length, i) for i in range(lengt...  18.1 us
    all_to_all x1, blocking collectives, shards(): lax.all_to_all(message, ROW, 0, 0, tiled=True)  17.2 us
    all_to_all x1, blocking collectives, shards(): gathered = lax.all_to_all(message, COL, 0, 0, tiled=True)  13.5 us
    all_to_all x1, blocking collectives, shards(): lax.all_to_all(hb_cols, COL, 0, 0, tiled=True).reshape(group, rank)  13.3 us
    all_to_all x1, blocking collectives, sent_to_all(): return lax.all_to_all(copies, axes, split_axis=0, concat_axis=0, tiled=True)  10.7 us
    pallas_call x10, Pallas kernels, call(): pl.pallas_call(kernel, out_shape=outs, in_specs=[pl.BlockSpec(memory_spac...  9.58 us
  transfers between devices with their start and end apart: 18, of which 8 were waited for; matrix products, arithmetic and copies ran while one was open for 0% of the time, Pallas kernels for 2%

profile of v14, /device:TPU:1, one launch (start us, length us, event | category | flops | bytes accessed | tf_op | source)
XLA Modules:
  0.0 147.2 jit_solution(4391526034404105128)
XLA Ops:
  0.0 2.0 %shard_map.28 = (bf16[32,1280]{1,0:T(8,128)(2,1)}, bf16[32,1280]{1,0:T(8,128)(2,1)}, bf16[8,64,1024]{2,1,0:T(8,128)(2,1)}) custom-call(bf16[64,1024]{1,0:T(8,128)(2,1)} %points.1, f32[64,256]{1,0:T(8,128)} %h_ref.1), custom_call_target="tpu_custom_call" | custom-call | flops 1 | bytes 1409024 | tf_op jit(solution)/shard_map/pallas_call | solution.py:37
  2.1 9.2 %all-to-all-start = ((bf16[8,64,1024]{2,1,0:T(8,128)(2,1)}), bf16[8,64,1024]{2,1,0:T(8,128)(2,1)S(1)}, u32[]{:S(2)}, u32[]{:S(2)}) async-start(bf16[8,64,1024]{2,1,0:T(8,128)(2,1)} %get-tuple-element.57), calls=%async_computation | async-start | bytes 2097152 | tf_op jit(solution)/shard_map/all_to_all | solution.py:269
  11.2 1.3 collective-permute-start.2
  12.5 2.5 %collective-permute-start.1 = (bf16[32,1280]{1,0:T(8,128)(2,1)S(1)}, bf16[32,1280]{1,0:T(8,128)(2,1)S(1)}, u32[]{:S(2)}, u32[]{:S(2)}) collective-permute-start(bf16[32,1280]{1,0:T(8,128)(2,1)S(1)} %copy-done), channel_id=1, source_target_pairs={{2,0},{3,1},{0,2},{1,3},{6,4},{7,5},{4,6},{5,7},{10,8},{11,9},{8,1... | collective-permute-start | bytes 245768 | tf_op jit(solution)/shard_map/ppermute | solution.py:21
  15.0 1.2 collective-permute-start
  16.1 1.3 collective-permute-start.5
  17.4 2.6 %collective-permute-start.4 = (bf16[32,1280]{1,0:T(8,128)(2,1)S(1)}, bf16[32,1280]{1,0:T(8,128)(2,1)S(1)}, u32[]{:S(2)}, u32[]{:S(2)}) collective-permute-start(bf16[32,1280]{1,0:T(8,128)(2,1)S(1)} %copy-done.1), channel_id=1, source_target_pairs={{8,0},{12,4},{0,8},{4,12},{9,1},{13,5},{1,9},{5,13},{10,2},{14,6},... | collective-permute-start | bytes 245768 | tf_op jit(solution)/shard_map/ppermute | solution.py:21
  20.0 1.1 collective-permute-start.3
  21.1 1.9 %collective-permute-done.4.by2 = bf16[32,1280]{1,0:T(8,128)(2,1)S(1)} collective-permute-done((bf16[32,1280]{1,0:T(8,128)(2,1)S(1)}, bf16[32,1280]{1,0:T(8,128)(2,1)S(1)}, u32[]{:S(2)}, u32[]{:S(2)}) %collective-permute-start.4) | collective-permute-done | bytes 81952 | tf_op jit(solution)/shard_map/ppermute | solution.py:21
  23.0 1.2 collective-permute-done.3.by1
  24.6 2.5 %collective-permute-start.9 = (bf16[4,32,1280]{2,1,0:T(8,128)(2,1)S(1)}, bf16[4,32,1280]{2,1,0:T(8,128)(2,1)S(1)}, u32[]{:S(2)}, u32[]{:S(2)}) collective-permute-start(bf16[4,32,1280]{2,1,0:T(8,128)(2,1)S(1)} %get-tuple-element.54), channel_id=1, source_target_pairs={{1,0},{2,1},{3,2},{0,3},{5,4},{6,5},{7,6},{4,7},{9,8},{10,9},{11,1... | collective-permute-start | bytes 983048 | tf_op jit(solution)/shard_map/ppermute | solution.py:21
  27.1 1.5 collective-permute-start.11
  29.2 0.8 collective-permute-start.8
  30.0 2.4 %collective-permute-done.6.x2 = bf16[4,32,1280]{2,1,0:T(8,128)(2,1)S(1)} collective-permute-done((bf16[4,32,1280]{2,1,0:T(8,128)(2,1)S(1)}, bf16[4,32,1280]{2,1,0:T(8,128)(2,1)S(1)}, u32[]{:S(2)}, u32[]{:S(2)}) %collective-permute-start.6) | collective-permute-done | bytes 327712 | tf_op jit(solution)/shard_map/ppermute | solution.py:21
  32.8 5.9 %collective-permute-done.9.x1 = bf16[4,32,1280]{2,1,0:T(8,128)(2,1)S(1)} collective-permute-done((bf16[4,32,1280]{2,1,0:T(8,128)(2,1)S(1)}, bf16[4,32,1280]{2,1,0:T(8,128)(2,1)S(1)}, u32[]{:S(2)}, u32[]{:S(2)}) %collective-permute-start.9) | collective-permute-done | bytes 327712 | tf_op jit(solution)/shard_map/ppermute | solution.py:21
  38.7 4.3 %collective-permute-done.10.y1 = bf16[4,32,1280]{2,1,0:T(8,128)(2,1)S(1)} collective-permute-done((bf16[4,32,1280]{2,1,0:T(8,128)(2,1)S(1)}, bf16[4,32,1280]{2,1,0:T(8,128)(2,1)S(1)}, u32[]{:S(2)}, u32[]{:S(2)}) %collective-permute-start.10) | collective-permute-done | bytes 327712 | tf_op jit(solution)/shard_map/ppermute | solution.py:21
  44.4 2.1 %collective-permute-start.12 = (bf16[512,1024]{1,0:T(8,128)(2,1)S(1)}, bf16[512,1024]{1,0:T(8,128)(2,1)S(1)}, u32[]{:S(2)}, u32[]{:S(2)}) collective-permute-start(bf16[512,1024]{1,0:T(8,128)(2,1)S(1)} %bitcast.27), channel_id=1, source_target_pairs={{16,0},{0,16},{17,1},{1,17},{18,2},{2,18},{19,3},{3,19},{20,4},{4,... | collective-permute-start | bytes 3145736 | tf_op jit(solution)/shard_map/ppermute | solution.py:21
  46.5 1.0 copy-done.3
  48.4 1.7 %shard_map.30 = (f32[512,1024]{1,0:T(8,128)S(1)}, f32[4,128]{1,0:T(4,128)S(1)}) custom-call(bf16[512,1024]{1,0:T(8,128)(2,1)S(1)} %bitcast.28, bf16[1024,1024]{1,0:T(8,128)(2,1)S(1)} %get-tuple-element.65.cols, f32[8,128]{1,0:T(8,128)S(1)} %get-tuple-element.66.sq), custom_call_target="tpu_custom_call" | custom-call | flops 1073741824 | bytes 5249024 | tf_op jit(solution)/shard_map/pallas_call | solution.py:37
  50.2 1.7 %shard_map.31 = (f32[512,1024]{1,0:T(8,128)S(1)}, f32[16,24,128]{2,1,0:T(8,128)S(1)}) custom-call(bf16[512,1024]{1,0:T(8,128)(2,1)S(1)} %collective-permute-done.12.rows_ref, bf16[1024,1024]{1,0:T(8,128)(2,1)S(1)} %get-tuple-element.65.cols, f32[8,128]{1,0:T(8,128)S(1)} %get-tuple-element.66.sq, f32[4,128]{1,0:T(4,128)S(1)} %get-tuple-element.68.own_sums, ...), custom_call_target="tpu_custom_call" | custom-call | flops 1073741824 | bytes 5478400 | tf_op jit(solution)/shard_map/pallas_call | solution.py:37
  51.9 17.2 %all_to_all.35.got = f32[16,24,128]{2,1,0:T(8,128)S(1)} all-to-all(f32[16,24,128]{2,1,0:T(8,128)S(1)} %get-tuple-element.70), channel_id=1, replica_groups=mesh['row_0'=8,'row_1'=2,'col_0'=4,'col_1'=4] {'row_0','row_1'}, dimensions={0} | all-to-all | bytes 393216 | tf_op jit(solution)/shard_map/all_to_all | solution.py:319
  69.2 13.5 %all_to_all.36.got = f32[16,40,128]{2,1,0:T(8,128)S(1)} all-to-all(f32[16,40,128]{2,1,0:T(8,128)S(1)} %get-tuple-element.72), channel_id=1, replica_groups=mesh['row_0'=8,'row_1'=2,'col_0'=4,'col_1'=4] {'col_0','col_1'}, dimensions={0} | all-to-all | bytes 655360 | tf_op jit(solution)/shard_map/all_to_all | solution.py:322
  82.7 0.8 shard_map.34
  83.5 1.2 collective-permute-start.14
  84.7 0.9 shard_map.33
  86.4 14.8 %all_to_all.37 = f16[8,64,256]{2,1,0:T(8,128)(2,1)S(1)} all-to-all(f16[8,64,256]{2,1,0:T(8,128)(2,1)S(1)} %bitcast.38), channel_id=1, replica_groups=mesh['row_0'=8,'row_1'=2,'col_0'=4,'col_1'=4] {'row_0'}, dimensions={0} | all-to-all | bytes 524288 | tf_op jit(solution)/shard_map/all_to_all | solution.py:340
  101.5 13.3 %all_to_all.38 = bf16[16,64,256]{2,1,0:T(8,128)(2,1)S(1)} all-to-all(bf16[16,64,256]{2,1,0:T(8,128)(2,1)S(1)} %get-tuple-element.80), channel_id=1, replica_groups=mesh['row_0'=8,'row_1'=2,'col_0'=4,'col_1'=4] {'col_0','col_1'}, dimensions={0} | all-to-all | bytes 1048576 | tf_op jit(solution)/shard_map/all_to_all | solution.py:352
  115.2 2.0 %collective-permute-start.15 = (f32[512,256]{1,0:T(8,128)S(1)}, f32[512,256]{1,0:T(8,128)S(1)}, u32[]{:S(2)}, u32[]{:S(2)}) collective-permute-start(f32[512,256]{1,0:T(8,128)S(1)} %fusion.3), channel_id=1, source_target_pairs={{16,0},{0,16},{17,1},{1,17},{18,2},{2,18},{19,3},{3,19},{20,4},{4,... | collective-permute-start | bytes 1572872 | tf_op jit(solution)/shard_map/ppermute | solution.py:21
  117.7 1.2 collective-permute-done.16
  119.4 16.1 %all_to_all.39 = f16[8,80,256]{2,1,0:T(8,128)(2,1)S(1)} all-to-all(f16[8,80,256]{2,1,0:T(8,128)(2,1)S(1)} %pad_maximum_fusion.2), channel_id=1, replica_groups=mesh['row_0'=8,'row_1'=2,'col_0'=4,'col_1'=4] {'row_0'}, dimensions={0} | all-to-all | bytes 655360 | tf_op jit(solution)/shard_map/all_to_all | solution.py:340
  135.6 10.7 %all_to_all.40 = f32[16,16,256]{2,1,0:T(8,128)S(1)} all-to-all(f32[16,16,256]{2,1,0:T(8,128)S(1)} %broadcast_in_dim.7), channel_id=1, replica_groups=mesh['row_0'=8,'row_1'=2,'col_0'=4,'col_1'=4] {'col_0','col_1'}, dimensions={0} | all-to-all | bytes 524288 | tf_op jit(solution)/shard_map/all_to_all | solution.py:27
  146.3 0.9 shard_map.37
  (44 shorter events, 6.7 us)
Async XLA Ops:
  2.0 9.2 %copy-start = (bf16[32,1280]{1,0:T(8,128)(2,1)S(1)}, bf16[32,1280]{1,0:T(8,128)(2,1)}, u32[]{:S(2)}) copy-start(bf16[32,1280]{1,0:T(8,128)(2,1)} %get-tuple-element.45.ax0) | copy-start | bytes 245764
  2.0 14.1 %copy-start.1 = (bf16[32,1280]{1,0:T(8,128)(2,1)S(1)}, bf16[32,1280]{1,0:T(8,128)(2,1)}, u32[]{:S(2)}) copy-start(bf16[32,1280]{1,0:T(8,128)(2,1)} %get-tuple-element.46.by0) | copy-start | bytes 245764
  2.1 42.3 %all-to-all-start = ((bf16[8,64,1024]{2,1,0:T(8,128)(2,1)}), bf16[8,64,1024]{2,1,0:T(8,128)(2,1)S(1)}, u32[]{:S(2)}, u32[]{:S(2)}) async-start(bf16[8,64,1024]{2,1,0:T(8,128)(2,1)} %get-tuple-element.57), calls=%async_computation | async-start | bytes 2097152 | tf_op jit(solution)/shard_map/all_to_all | solution.py:269
  11.2 8.8 %collective-permute-start.2 = (bf16[32,1280]{1,0:T(8,128)(2,1)S(1)}, bf16[32,1280]{1,0:T(8,128)(2,1)S(1)}, u32[]{:S(2)}, u32[]{:S(2)}) collective-permute-start(bf16[32,1280]{1,0:T(8,128)(2,1)S(1)} %copy-done), channel_id=1, source_target_pairs={{3,0},{0,1},{1,2},{2,3},{7,4},{4,5},{5,6},{6,7},{11,8},{8,9},{9,10... | collective-permute-start | bytes 245768 | tf_op jit(solution)/shard_map/ppermute | solution.py:21
  12.5 8.6 %collective-permute-start.1 = (bf16[32,1280]{1,0:T(8,128)(2,1)S(1)}, bf16[32,1280]{1,0:T(8,128)(2,1)S(1)}, u32[]{:S(2)}, u32[]{:S(2)}) collective-permute-start(bf16[32,1280]{1,0:T(8,128)(2,1)S(1)} %copy-done), channel_id=1, source_target_pairs={{2,0},{3,1},{0,2},{1,3},{6,4},{7,5},{4,6},{5,7},{10,8},{11,9},{8,1... | collective-permute-start | bytes 245768 | tf_op jit(solution)/shard_map/ppermute | solution.py:21
  15.0 6.2 %collective-permute-start = (bf16[32,1280]{1,0:T(8,128)(2,1)S(1)}, bf16[32,1280]{1,0:T(8,128)(2,1)S(1)}, u32[]{:S(2)}, u32[]{:S(2)}) collective-permute-start(bf16[32,1280]{1,0:T(8,128)(2,1)S(1)} %copy-done), channel_id=1, source_target_pairs={{1,0},{2,1},{3,2},{0,3},{5,4},{6,5},{7,6},{4,7},{9,8},{10,9},{11,1... | collective-permute-start | bytes 245768 | tf_op jit(solution)/shard_map/ppermute | solution.py:21
  16.1 5.0 %collective-permute-start.5 = (bf16[32,1280]{1,0:T(8,128)(2,1)S(1)}, bf16[32,1280]{1,0:T(8,128)(2,1)S(1)}, u32[]{:S(2)}, u32[]{:S(2)}) collective-permute-start(bf16[32,1280]{1,0:T(8,128)(2,1)S(1)} %copy-done.1), channel_id=1, source_target_pairs={{12,0},{0,4},{4,8},{8,12},{13,1},{1,5},{5,9},{9,13},{14,2},{2,6},{... | collective-permute-start | bytes 245768 | tf_op jit(solution)/shard_map/ppermute | solution.py:21
  17.4 5.6 %collective-permute-start.4 = (bf16[32,1280]{1,0:T(8,128)(2,1)S(1)}, bf16[32,1280]{1,0:T(8,128)(2,1)S(1)}, u32[]{:S(2)}, u32[]{:S(2)}) collective-permute-start(bf16[32,1280]{1,0:T(8,128)(2,1)S(1)} %copy-done.1), channel_id=1, source_target_pairs={{8,0},{12,4},{0,8},{4,12},{9,1},{13,5},{1,9},{5,13},{10,2},{14,6},... | collective-permute-start | bytes 245768 | tf_op jit(solution)/shard_map/ppermute | solution.py:21
  20.0 4.1 %collective-permute-start.3 = (bf16[32,1280]{1,0:T(8,128)(2,1)S(1)}, bf16[32,1280]{1,0:T(8,128)(2,1)S(1)}, u32[]{:S(2)}, u32[]{:S(2)}) collective-permute-start(bf16[32,1280]{1,0:T(8,128)(2,1)S(1)} %copy-done.1), channel_id=1, source_target_pairs={{4,0},{8,4},{12,8},{0,12},{5,1},{9,5},{13,9},{1,13},{6,2},{10,6},{... | collective-permute-start | bytes 245768 | tf_op jit(solution)/shard_map/ppermute | solution.py:21
  24.3 8.1 %collective-permute-start.6 = (bf16[4,32,1280]{2,1,0:T(8,128)(2,1)S(1)}, bf16[4,32,1280]{2,1,0:T(8,128)(2,1)S(1)}, u32[]{:S(2)}, u32[]{:S(2)}) collective-permute-start(bf16[4,32,1280]{2,1,0:T(8,128)(2,1)S(1)} %get-tuple-element.54), channel_id=1, source_target_pairs={{2,0},{3,1},{0,2},{1,3},{6,4},{7,5},{4,6},{5,7},{10,8},{11,9},{8,1... | collective-permute-start | bytes 983048 | tf_op jit(solution)/shard_map/ppermute | solution.py:21
  24.6 14.1 %collective-permute-start.9 = (bf16[4,32,1280]{2,1,0:T(8,128)(2,1)S(1)}, bf16[4,32,1280]{2,1,0:T(8,128)(2,1)S(1)}, u32[]{:S(2)}, u32[]{:S(2)}) collective-permute-start(bf16[4,32,1280]{2,1,0:T(8,128)(2,1)S(1)} %get-tuple-element.54), channel_id=1, source_target_pairs={{1,0},{2,1},{3,2},{0,3},{5,4},{6,5},{7,6},{4,7},{9,8},{10,9},{11,1... | collective-permute-start | bytes 983048 | tf_op jit(solution)/shard_map/ppermute | solution.py:21
  27.1 11.6 %collective-permute-start.11 = (bf16[4,32,1280]{2,1,0:T(8,128)(2,1)S(1)}, bf16[4,32,1280]{2,1,0:T(8,128)(2,1)S(1)}, u32[]{:S(2)}, u32[]{:S(2)}) collective-permute-start(bf16[4,32,1280]{2,1,0:T(8,128)(2,1)S(1)} %get-tuple-element.55), channel_id=1, source_target_pairs={{8,0},{12,4},{0,8},{4,12},{9,1},{13,5},{1,9},{5,13},{10,2},{14,6},... | collective-permute-start | bytes 983048 | tf_op jit(solution)/shard_map/ppermute | solution.py:21
  28.5 14.4 %collective-permute-start.10 = (bf16[4,32,1280]{2,1,0:T(8,128)(2,1)S(1)}, bf16[4,32,1280]{2,1,0:T(8,128)(2,1)S(1)}, u32[]{:S(2)}, u32[]{:S(2)}) collective-permute-start(bf16[4,32,1280]{2,1,0:T(8,128)(2,1)S(1)} %get-tuple-element.55), channel_id=1, source_target_pairs={{4,0},{8,4},{12,8},{0,12},{5,1},{9,5},{13,9},{1,13},{6,2},{10,6},{... | collective-permute-start | bytes 983048 | tf_op jit(solution)/shard_map/ppermute | solution.py:21
  29.2 14.4 %collective-permute-start.8 = (bf16[4,32,1280]{2,1,0:T(8,128)(2,1)S(1)}, bf16[4,32,1280]{2,1,0:T(8,128)(2,1)S(1)}, u32[]{:S(2)}, u32[]{:S(2)}) collective-permute-start(bf16[4,32,1280]{2,1,0:T(8,128)(2,1)S(1)} %get-tuple-element.55), channel_id=1, source_target_pairs={{12,0},{0,4},{4,8},{8,12},{13,1},{1,5},{5,9},{9,13},{14,2},{2,6},{... | collective-permute-start | bytes 983048 | tf_op jit(solution)/shard_map/ppermute | solution.py:21
  32.4 11.2 %collective-permute-start.7 = (bf16[4,32,1280]{2,1,0:T(8,128)(2,1)S(1)}, bf16[4,32,1280]{2,1,0:T(8,128)(2,1)S(1)}, u32[]{:S(2)}, u32[]{:S(2)}) collective-permute-start(bf16[4,32,1280]{2,1,0:T(8,128)(2,1)S(1)} %get-tuple-element.54), channel_id=1, source_target_pairs={{3,0},{0,1},{1,2},{2,3},{7,4},{4,5},{5,6},{6,7},{11,8},{8,9},{9,10... | collective-permute-start | bytes 983048 | tf_op jit(solution)/shard_map/ppermute | solution.py:21
  43.6 0.7 copy-start.2
  44.4 5.8 %collective-permute-start.12 = (bf16[512,1024]{1,0:T(8,128)(2,1)S(1)}, bf16[512,1024]{1,0:T(8,128)(2,1)S(1)}, u32[]{:S(2)}, u32[]{:S(2)}) collective-permute-start(bf16[512,1024]{1,0:T(8,128)(2,1)S(1)} %bitcast.27), channel_id=1, source_target_pairs={{16,0},{0,16},{17,1},{1,17},{18,2},{2,18},{19,3},{3,19},{20,4},{4,... | collective-permute-start | bytes 3145736 | tf_op jit(solution)/shard_map/ppermute | solution.py:21
  46.5 1.0 copy-start.3
  48.2 2.0 %collective-permute-start.13 = (f32[16,256]{1,0:T(8,128)S(1)}, f32[16,256]{1,0:T(8,128)S(1)}, u32[]{:S(2)}, u32[]{:S(2)}) collective-permute-start(f32[16,256]{1,0:T(8,128)S(1)} %get-tuple-element.69.part), channel_id=1, source_target_pairs={{16,0},{0,16},{17,1},{1,17},{18,2},{2,18},{19,3},{3,19},{20,4},{4,... | collective-permute-start | bytes 49160 | tf_op jit(solution)/shard_map/ppermute | solution.py:21
  83.5 2.7 %collective-permute-start.14 = (f32[512,256]{1,0:T(8,128)S(1)}, f32[512,256]{1,0:T(8,128)S(1)}, u32[]{:S(2)}, u32[]{:S(2)}) collective-permute-start(f32[512,256]{1,0:T(8,128)S(1)} %get-tuple-element.77), channel_id=1, source_target_pairs={{16,0},{0,16},{17,1},{1,17},{18,2},{2,18},{19,3},{3,19},{20,4},{4,... | collective-permute-start | bytes 1572872 | tf_op jit(solution)/shard_map/ppermute | solution.py:21
  84.7 16.5 %copy-start.4 = (f32[64,256]{1,0:T(8,128)S(1)}, f32[64,256]{1,0:T(8,128)}, u32[]{:S(2)}) copy-start(f32[64,256]{1,0:T(8,128)} %h_ref.1) | copy-start | bytes 196612
  115.2 3.6 %collective-permute-start.15 = (f32[512,256]{1,0:T(8,128)S(1)}, f32[512,256]{1,0:T(8,128)S(1)}, u32[]{:S(2)}, u32[]{:S(2)}) collective-permute-start(f32[512,256]{1,0:T(8,128)S(1)} %fusion.3), channel_id=1, source_target_pairs={{16,0},{0,16},{17,1},{1,17},{18,2},{2,18},{19,3},{3,19},{20,4},{4,... | collective-permute-start | bytes 1572872 | tf_op jit(solution)/shard_map/ppermute | solution.py:21
  117.6 1.3 collective-permute-start.16
